TPU v7x, 256 devices: a whole 4x4x8 slice. The times are simulated.
256 devices in a mesh: blk: 32 (over z, y_lo, core), rep: 8 (over x, y_hi).
Axes of the slice: x: 4, y: 4 (y_hi: 2, y_lo: 2; y = y_hi * 2 + y_lo), z: 8, core: 2. Of those that a mesh axis runs over, the one named last changes fastest.
Arguments:
- features: bfloat16 [32768, 128], P('blk'), may hold values from -6 to 6
- degrees: int32 [32768], P('blk'), may hold values from 4 to 32
- slot_column_tiles: int32 [256, 32, 6], P('blk', 'rep'), may hold values from 0 to 7
- tile_counts: int32 [256, 32], P('blk', 'rep'), may hold values from 0 to 6, as said below
- slot_edge_weights: bfloat16 [256, 32, 6, 128, 128], P('blk', 'rep'), may hold values from 0 to 0.15234375
- weight: bfloat16 [128, 256], replicated, may hold values from -0.5 to 0.5
- bias: float32 [256], replicated, may hold values from -3 to 3
- cotangent: bfloat16 [32768, 256], P(('blk', 'rep')), may hold values from -1.1953125 to 1.1953125
Outputs:
- activation: bfloat16 [32768, 256], P(('blk', 'rep'))
- grad_weight: float32 [128, 256], replicated
- grad_bias: float32 [256], replicated
- grad_features: float32 [32768, 128], P(('blk', 'rep'))
Inputs may be any that keep to these rules, and one draw needn't show every extreme that they name: slot_column_tiles[i, g, c] names a tile of node block (i // 8 - g) mod 32. Slots c >= tile_counts[i, g] of row tile i at offset g are not part of A; 6 is reached in every draw.
All inputs are finite; a program needn't handle non-finite values.
Results may differ from a plain program's by a relative error of at most 0.025.
Values may be sent and summed in bfloat16 or wider, within the bound.
No kernel may reach another device: no remote copies, remote signals or barrier semaphores. Data moves between devices by JAX's collectives and lax.ppermute only.
A program may use at most 64 MiB of HBM per device.

v0:
```python
import jax
import jax.numpy as jnp
from jax import lax
from jax.sharding import PartitionSpec as P


def passed_along(value, axis, by):
    count = lax.axis_size(axis)
    return lax.ppermute(value, axis, [(i, (i + by) % count) for i in range(count)])


def forward_terms(tiles_now, col_ids, counts, edge_vals):
    slot_count = col_ids.shape[1]
    picked = jnp.take(tiles_now, col_ids, axis=0)
    live_mask = jnp.arange(slot_count, dtype=jnp.int32)[None, :] < counts[:, None]
    picked = jnp.where(live_mask[:, :, None, None], picked, jnp.zeros_like(picked))
    return jnp.einsum("isab,isbf->iaf", edge_vals, picked, preferred_element_type=jnp.float32)


def backward_terms(back_block, col_ids, counts, edge_vals):
    row_tiles, slot_count = col_ids.shape
    initial = jnp.zeros((row_tiles, edge_vals.shape[-1], back_block.shape[-1]), jnp.float32)
    products = jnp.einsum(
        "isab,iaf->isbf", edge_vals, back_block, preferred_element_type=jnp.float32
    )
    live_mask = jnp.arange(slot_count, dtype=jnp.int32)[None, :] < counts[:, None]
    products = jnp.where(live_mask[:, :, None, None], products, jnp.zeros_like(products))
    flat = products.reshape(row_tiles * slot_count, products.shape[2], products.shape[3])
    return initial.at[col_ids.reshape(-1)].add(flat)


def sum_replicas(partial_value, rep_index, share_rows):
    whole = lax.psum(partial_value.astype(jnp.bfloat16), "rep").astype(jnp.float32)
    return lax.dynamic_slice_in_dim(whole, rep_index * share_rows, share_rows, 0)


def on_device(
    features, degrees, slot_column_tiles, tile_counts, slot_edge_weights, weight, bias, cotangent
):
    cycle_size = lax.axis_size("blk")
    rep_size = lax.axis_size("rep")
    cycle_steps = cycle_size // rep_size
    rep_index = lax.axis_index("rep")
    row_tiles = slot_column_tiles.shape[0]
    tile_size = slot_edge_weights.shape[-1]
    feat_width = features.shape[1]
    share_rows = cotangent.shape[0]
    rep_digits = (rep_size - 1).bit_length()
    inv_root = lax.rsqrt(degrees.astype(jnp.float32))
    current = (features * inv_root[:, None]).astype(jnp.bfloat16)
    for bit_pos in range(rep_digits):
        shifted = passed_along(current, "blk", cycle_steps << bit_pos)
        current = jnp.where(rep_index >> bit_pos & 1 == 1, shifted, current)
    partial_value = jnp.zeros((row_tiles, tile_size, feat_width), jnp.float32)
    for step_pos in range(cycle_steps):
        tiles_now = current.reshape(row_tiles, tile_size, feat_width)
        partial_value = partial_value + forward_terms(
            tiles_now,
            slot_column_tiles[:, step_pos],
            tile_counts[:, step_pos],
            slot_edge_weights[:, step_pos],
        )
        if step_pos + 1 < cycle_steps:
            current = passed_along(current, "blk", 1)
    own_rows = sum_replicas(
        partial_value.reshape(row_tiles * tile_size, feat_width), rep_index, share_rows
    )
    row_scale = lax.dynamic_slice_in_dim(inv_root, rep_index * share_rows, share_rows, 0)
    aggregate = (row_scale[:, None] * own_rows).astype(jnp.bfloat16)
    pre_act = jnp.dot(aggregate, weight, preferred_element_type=jnp.float32) + bias
    activation = jax.nn.silu(pre_act).astype(jnp.bfloat16)
    sigma = jax.nn.sigmoid(pre_act)
    grad_pre = cotangent.astype(jnp.float32) * sigma * (1.0 + pre_act * (1.0 - sigma))
    grad_half = grad_pre.astype(jnp.bfloat16)
    weight_term = lax.dot_general(
        aggregate, grad_half, (((0,), (0,)), ((), ())), preferred_element_type=jnp.float32
    )
    grad_weight, grad_bias = lax.psum((weight_term, jnp.sum(grad_pre, axis=0)), ("blk", "rep"))
    back_part = lax.dot_general(
        grad_half, weight, (((1,), (1,)), ((), ())), preferred_element_type=jnp.float32
    )
    back = (row_scale[:, None] * back_part).astype(jnp.bfloat16)
    back_block = lax.all_gather(back, "rep", axis=0, tiled=True).reshape(
        row_tiles, tile_size, feat_width
    )
    column_sums = jnp.zeros((row_tiles, tile_size, feat_width), jnp.float32)
    for turn_pos in range(cycle_steps):
        offset = cycle_steps - 1 - turn_pos
        column_sums = column_sums + backward_terms(
            back_block,
            slot_column_tiles[:, offset],
            tile_counts[:, offset],
            slot_edge_weights[:, offset],
        )
        if turn_pos + 1 < cycle_steps:
            column_sums = passed_along(column_sums.astype(jnp.bfloat16), "blk", -1).astype(
                column_sums.dtype
            )
    for bit_pos in range(rep_digits):
        shifted = passed_along(
            column_sums.astype(jnp.bfloat16), "blk", -(cycle_steps << bit_pos)
        ).astype(column_sums.dtype)
        column_sums = jnp.where(rep_index >> bit_pos & 1 == 1, shifted, column_sums)
    back_rows = sum_replicas(
        column_sums.reshape(row_tiles * tile_size, feat_width), rep_index, share_rows
    )
    grad_features = row_scale[:, None] * back_rows
    return (activation, grad_weight, grad_bias, grad_features)


def solution(mesh):
    return jax.shard_map(
        on_device,
        mesh=mesh,
        in_specs=(
            P("blk", None),
            P("blk"),
            P("blk", "rep", None),
            P("blk", "rep"),
            P("blk", "rep", None, None, None),
            P(),
            P(),
            P(("blk", "rep"), None),
        ),
        out_specs=(P(("blk", "rep"), None), P(), P(), P(("blk", "rep"), None)),
        check_vma=False,
    )
```

profile of v0, /device:TPU:32, one launch (start us, length us, event | category | flops | bytes accessed | tf_op | source)
XLA Modules:
  0.0 647.7 jit_solution(5153493722779816429)
XLA Ops:
  18.4 4.0 collective-permute-start.1
  22.4 8.7 %collective-permute-done.1 = bf16[1024,128]{1,0:T(8,128)(2,1)S(1)} collective-permute-done((bf16[1024,128]{1,0:T(8,128)(2,1)S(1)}, bf16[1024,128]{1,0:T(8,128)(2,1)S(1)}, u32[]{:S(2)}, u32[]{:S(2)}) %collective-permute-start.1) | collective-permute-done | bytes 262176 | tf_op jit(solution)/shard_map/ppermute | solution.py:9
  31.2 4.9 collective-permute-start.2
  36.2 9.5 %collective-permute-done.2 = bf16[1024,128]{1,0:T(8,128)(2,1)S(1)} collective-permute-done((bf16[1024,128]{1,0:T(8,128)(2,1)S(1)}, bf16[1024,128]{1,0:T(8,128)(2,1)S(1)}, u32[]{:S(2)}, u32[]{:S(2)}) %collective-permute-start.2) | collective-permute-done | bytes 262176 | tf_op jit(solution)/shard_map/ppermute | solution.py:9
  46.9 11.8 %collective-permute-done.3 = bf16[1024,128]{1,0:T(8,128)(2,1)S(1)} collective-permute-done((bf16[1024,128]{1,0:T(8,128)(2,1)S(1)}, bf16[1024,128]{1,0:T(8,128)(2,1)S(1)}, u32[]{:S(2)}, u32[]{:S(2)}) %collective-permute-start.3) | collective-permute-done | bytes 262176 | tf_op jit(solution)/shard_map/ppermute | solution.py:9
  65.3 4.6 collective-permute-done.4
  73.0 4.6 collective-permute-done.5
  78.4 2.8 fusion.49
  82.5 92.8 %all-reduce.4.cloned.1.call-done = bf16[1024,128]{1,0:T(8,128)(2,1)} async-done(((bf16[1024,128]{1,0:T(8,128)(2,1)}), bf16[1024,128]{1,0:T(8,128)(2,1)}) %all-reduce.4.cloned.1.call-update) | async-done | bytes 262160 | tf_op jit(solution)/shard_map/psum | solution.py:33
  177.7 34.5 %all_gather.3 = bf16[1024,128]{1,0:T(8,128)(2,1)S(1)} all-gather(bf16[128,128]{1,0:T(8,128)(2,1)S(1)} %fusion.52), channel_id=1, replica_groups=mesh['blk'=32,'rep'=8] {'rep'}, dimensions={0}, use_global_device_ids=true | all-gather | bytes 294912 | tf_op jit(solution)/shard_map/all_gather | solution.py:83
  216.6 7.0 %scatter_fusion = f32[8,128,128]{2,1,0:T(8,128)S(1)} fusion(f32[8,128,128]{2,1,0:T(8,128)S(1)} %broadcast.146, s32[48]{0:T(128)} %fusion.66, f32[48,128,128]{2,1,0:T(8,128)} %copy.37), kind=kCustom, calls=%fused_computation.4 | custom fusion | flops 786432 | bytes 9437376 | tf_op jit(solution)/shard_map/scatter-add | solution.py:29
  229.7 6.7 %scatter_fusion.1 = f32[8,128,128]{2,1,0:T(8,128)S(1)} fusion(f32[8,128,128]{2,1,0:T(8,128)S(1)} %convert_element_type.94, s32[48]{0:T(128)S(1)} %copy-done.4, f32[48,128,128]{2,1,0:T(8,128)} %copy.39), kind=kCustom, calls=%fused_computation.5 | custom fusion | flops 786432 | bytes 9437376 | tf_op jit(solution)/shard_map/scatter-add | solution.py:29
  245.2 6.7 %scatter_fusion.2 = f32[8,128,128]{2,1,0:T(8,128)S(1)} fusion(f32[8,128,128]{2,1,0:T(8,128)S(1)} %convert_element_type.96, s32[48]{0:T(128)S(1)} %copy-done.6, f32[48,128,128]{2,1,0:T(8,128)} %copy.41), kind=kCustom, calls=%fused_computation.6 | custom fusion | flops 786432 | bytes 9437376 | tf_op jit(solution)/shard_map/scatter-add | solution.py:29
  252.7 2.6 collective-permute-start.8
  260.7 6.7 %scatter_fusion.3 = f32[8,128,128]{2,1,0:T(8,128)S(1)} fusion(f32[8,128,128]{2,1,0:T(8,128)S(1)} %convert_element_type.98, s32[48]{0:T(128)S(1)} %copy-done.5, f32[48,128,128]{2,1,0:T(8,128)} %copy.43), kind=kCustom, calls=%fused_computation.7 | custom fusion | flops 786432 | bytes 9437376 | tf_op jit(solution)/shard_map/scatter-add | solution.py:29
  267.5 2.9 collective-permute-start.9
  270.4 4.2 collective-permute-done.9
  274.7 4.5 collective-permute-start.10
  279.2 8.8 %collective-permute-done.10 = bf16[8,128,128]{2,1,0:T(8,128)(2,1)S(1)} collective-permute-done((bf16[8,128,128]{2,1,0:T(8,128)(2,1)S(1)}, bf16[8,128,128]{2,1,0:T(8,128)(2,1)S(1)}, u32[]{:S(2)}, u32[]{:S(2)}) %collective-permute-start.10) | collective-permute-done | bytes 262176 | tf_op jit(solution)/shard_map/ppermute | solution.py:9
  288.0 4.5 collective-permute-start.11
  292.5 9.5 %collective-permute-done.11 = bf16[8,128,128]{2,1,0:T(8,128)(2,1)S(1)} collective-permute-done((bf16[8,128,128]{2,1,0:T(8,128)(2,1)S(1)}, bf16[8,128,128]{2,1,0:T(8,128)(2,1)S(1)}, u32[]{:S(2)}, u32[]{:S(2)}) %collective-permute-start.11) | collective-permute-done | bytes 262176 | tf_op jit(solution)/shard_map/ppermute | solution.py:9
  302.9 80.5 %psum.30 = f32[256]{0:T(256)} all-reduce(f32[256]{0:T(256)S(1)} %copy-done.3), channel_id=1, replica_groups=mesh['blk'=32,'rep'=8] {'blk','rep'}, use_global_device_ids=true, to_apply=%region_3.5 | all-reduce | flops 256 | bytes 2048 | tf_op jit(solution)/shard_map/psum | solution.py:78
  385.1 10.1 %all-reduce.8.cloned.1.call-done = bf16[1024,128]{1,0:T(8,128)(2,1)} async-done(((bf16[1024,128]{1,0:T(8,128)(2,1)}), bf16[1024,128]{1,0:T(8,128)(2,1)}) %all-reduce.8.cloned.1.call-update) | async-done | bytes 262160 | tf_op jit(solution)/shard_map/psum | solution.py:33
  396.7 242.9 %all-reduce.6.cloned.1.call-done = f32[128,256]{1,0:T(8,128)} async-done(((f32[128,256]{1,0:T(8,128)}), f32[128,256]{1,0:T(8,128)}) %all-reduce.6.cloned.1.call-update) | async-done | bytes 131088 | tf_op jit(solution)/shard_map/psum | solution.py:78
  (102 shorter events, 57.8 us)
Async XLA Ops:
  7.2 168.1 %copy-start = (bf16[128,256]{1,0:T(8,128)(2,1)S(1)}, bf16[128,256]{1,0:T(8,128)(2,1)}, u32[]{:S(2)}) copy-start(bf16[128,256]{1,0:T(8,128)(2,1)} %param.15) | copy-start | bytes 196612
  7.2 168.1 %all-reduce.4.cloned.1.call-start = ((), (), s32[]{:S(2)}) async-start(), calls=%async_computation | async-start | bytes 524288 | tf_op jit(solution)/shard_map/psum | solution.py:33
  9.1 8.1 %collective-permute-start = (bf16[1024,128]{1,0:T(8,128)(2,1)S(1)}, bf16[1024,128]{1,0:T(8,128)(2,1)S(1)}, u32[]{:S(2)}, u32[]{:S(2)}) collective-permute-start(bf16[1024,128]{1,0:T(8,128)(2,1)S(1)} %multiply_convert_fusion), channel_id=1, source_target_pairs={{0,32},{8,40},{16,48},{24,56},{32,64},{40,72},{48,80},{56,88},{64,... | collective-permute-start | bytes 786440 | tf_op jit(solution)/shard_map/ppermute | solution.py:9
  18.4 12.8 %collective-permute-start.1 = (bf16[1024,128]{1,0:T(8,128)(2,1)S(1)}, bf16[1024,128]{1,0:T(8,128)(2,1)S(1)}, u32[]{:S(2)}, u32[]{:S(2)}) collective-permute-start(bf16[1024,128]{1,0:T(8,128)(2,1)S(1)} %broadcast_select_fusion), channel_id=1, source_target_pairs={{0,64},{8,72},{16,80},{24,88},{32,96},{40,104},{48,112},{56,120},{... | collective-permute-start | bytes 786440 | tf_op jit(solution)/shard_map/ppermute | solution.py:9
  31.2 14.5 %collective-permute-start.2 = (bf16[1024,128]{1,0:T(8,128)(2,1)S(1)}, bf16[1024,128]{1,0:T(8,128)(2,1)S(1)}, u32[]{:S(2)}, u32[]{:S(2)}) collective-permute-start(bf16[1024,128]{1,0:T(8,128)(2,1)S(1)} %broadcast_select_fusion.1), channel_id=1, source_target_pairs={{0,128},{8,136},{16,144},{24,152},{32,160},{40,168},{48,176},{56,1... | collective-permute-start | bytes 786440 | tf_op jit(solution)/shard_map/ppermute | solution.py:9
  45.8 12.9 %collective-permute-start.3 = (bf16[1024,128]{1,0:T(8,128)(2,1)S(1)}, bf16[1024,128]{1,0:T(8,128)(2,1)S(1)}, u32[]{:S(2)}, u32[]{:S(2)}) collective-permute-start(bf16[1024,128]{1,0:T(8,128)(2,1)S(1)} %broadcast_select_fusion.2), channel_id=1, source_target_pairs={{0,8},{8,16},{16,24},{24,32},{32,40},{40,48},{48,56},{56,64},{64,7... | collective-permute-start | bytes 786440 | tf_op jit(solution)/shard_map/ppermute | solution.py:9
  46.0 24.9 %copy-start.1 = (pred[8,6]{1,0:T(8,128)(4,1)}, pred[8,6]{1,0:T(8,128)(4,1)S(1)}, u32[]{:S(2)}) copy-start(pred[8,6]{1,0:T(8,128)(4,1)S(1)} %get-tuple-element.20) | copy-start | bytes 148
  63.2 6.8 %collective-permute-start.4 = (bf16[1024,128]{1,0:T(8,128)(2,1)S(1)}, bf16[1024,128]{1,0:T(8,128)(2,1)S(1)}, u32[]{:S(2)}, u32[]{:S(2)}) collective-permute-start(bf16[1024,128]{1,0:T(8,128)(2,1)S(1)} %collective-permute-done.3), channel_id=1, source_target_pairs={{0,8},{8,16},{16,24},{24,32},{32,40},{40,48},{48,56},{56,64},{64,7... | collective-permute-start | bytes 786440 | tf_op jit(solution)/shard_map/ppermute | solution.py:9
  70.8 6.8 %collective-permute-start.5 = (bf16[1024,128]{1,0:T(8,128)(2,1)S(1)}, bf16[1024,128]{1,0:T(8,128)(2,1)S(1)}, u32[]{:S(2)}, u32[]{:S(2)}) collective-permute-start(bf16[1024,128]{1,0:T(8,128)(2,1)S(1)} %collective-permute-done.4), channel_id=1, source_target_pairs={{0,8},{8,16},{16,24},{24,32},{32,40},{40,48},{48,56},{56,64},{64,7... | collective-permute-start | bytes 786440 | tf_op jit(solution)/shard_map/ppermute | solution.py:9
  78.4 96.9 %copy-start.7 = (bf16[128,256]{1,0:T(8,128)(2,1)S(1)}, bf16[128,256]{1,0:T(8,128)(2,1)}, u32[]{:S(2)}) copy-start(bf16[128,256]{1,0:T(8,128)(2,1)} %param.17) | copy-start | bytes 196612
  78.4 96.9 %copy-start.8 = (f32[256]{0:T(256)S(1)}, f32[256]{0:T(256)}, u32[]{:S(2)}) copy-start(f32[256]{0:T(256)} %param.16) | copy-start | bytes 3076
  81.3 313.9 %all-reduce.8.cloned.1.call-start = ((), (), s32[]{:S(2)}) async-start(), calls=%async_computation.2 | async-start | bytes 524288 | tf_op jit(solution)/shard_map/psum | solution.py:33
  216.6 7.7 %copy-start.2 = (pred[8,6]{1,0:T(8,128)(4,1)S(1)}, pred[8,6]{1,0:T(8,128)(4,1)}, u32[]{:S(2)}) copy-start(pred[8,6]{1,0:T(8,128)(4,1)} %copy-done.1) | copy-start | bytes 148
  224.3 4.4 collective-permute-start.6
  226.4 3.3 copy-start.4
  237.2 7.0 %collective-permute-start.7 = (bf16[8,128,128]{2,1,0:T(8,128)(2,1)}, bf16[8,128,128]{2,1,0:T(8,128)(2,1)}, u32[]{:S(2)}, u32[]{:S(2)}) collective-permute-start(bf16[8,128,128]{2,1,0:T(8,128)(2,1)} %convert_element_type.95), channel_id=1, source_target_pairs={{0,248},{8,0},{16,8},{24,16},{32,24},{40,32},{48,40},{56,48},{64,5... | collective-permute-start | bytes 786440 | tf_op jit(solution)/shard_map/ppermute | solution.py:9
  241.9 3.3 copy-start.6
  252.7 7.0 %collective-permute-start.8 = (bf16[8,128,128]{2,1,0:T(8,128)(2,1)}, bf16[8,128,128]{2,1,0:T(8,128)(2,1)}, u32[]{:S(2)}, u32[]{:S(2)}) collective-permute-start(bf16[8,128,128]{2,1,0:T(8,128)(2,1)} %convert_element_type.97), channel_id=1, source_target_pairs={{0,248},{8,0},{16,8},{24,16},{32,24},{40,32},{48,40},{56,48},{64,5... | collective-permute-start | bytes 786440 | tf_op jit(solution)/shard_map/ppermute | solution.py:9
  257.3 3.3 copy-start.5
  267.5 7.1 %collective-permute-start.9 = (bf16[8,128,128]{2,1,0:T(8,128)(2,1)S(1)}, bf16[8,128,128]{2,1,0:T(8,128)(2,1)S(1)}, u32[]{:S(2)}, u32[]{:S(2)}) collective-permute-start(bf16[8,128,128]{2,1,0:T(8,128)(2,1)S(1)} %convert_element_type.99), channel_id=1, source_target_pairs={{0,224},{8,232},{16,240},{24,248},{32,0},{40,8},{48,16},{56,24},{6... | collective-permute-start | bytes 786440 | tf_op jit(solution)/shard_map/ppermute | solution.py:9
  274.7 28.3 %copy-start.3 = (f32[256]{0:T(256)S(1)}, f32[256]{0:T(256)}, u32[]{:S(2)}) copy-start(f32[256]{0:T(256)} %get-tuple-element.5) | copy-start | bytes 3076
  274.7 13.3 %collective-permute-start.10 = (bf16[8,128,128]{2,1,0:T(8,128)(2,1)S(1)}, bf16[8,128,128]{2,1,0:T(8,128)(2,1)S(1)}, u32[]{:S(2)}, u32[]{:S(2)}) collective-permute-start(bf16[8,128,128]{2,1,0:T(8,128)(2,1)S(1)} %fusion.61), channel_id=1, source_target_pairs={{0,192},{8,200},{16,208},{24,216},{32,224},{40,232},{48,240},{56,2... | collective-permute-start | bytes 786440 | tf_op jit(solution)/shard_map/ppermute | solution.py:9
  288.0 14.0 %collective-permute-start.11 = (bf16[8,128,128]{2,1,0:T(8,128)(2,1)S(1)}, bf16[8,128,128]{2,1,0:T(8,128)(2,1)S(1)}, u32[]{:S(2)}, u32[]{:S(2)}) collective-permute-start(bf16[8,128,128]{2,1,0:T(8,128)(2,1)S(1)} %fusion.62), channel_id=1, source_target_pairs={{0,128},{8,136},{16,144},{24,152},{32,160},{40,168},{48,176},{56,1... | collective-permute-start | bytes 786440 | tf_op jit(solution)/shard_map/ppermute | solution.py:9
  302.9 336.7 %all-reduce.6.cloned.1.call-start = ((), (), s32[]{:S(2)}) async-start(), calls=%async_computation.1 | async-start | bytes 262144 | tf_op jit(solution)/shard_map/psum | solution.py:78
Sparse Core Ops, SparseCore 0:
  81.4 93.8 all-reduce.3
  303.0 92.1 all-reduce.7
  401.3 238.2 all-reduce.5
where the time goes:
time: 651 us; the launch traced here: 648 us
  waiting for transfers between devices  410 us (63%)
  blocking collectives  115 us (18%)
  other arithmetic  40.3 us (6%)
  starting transfers between devices  28.4 us (4%)
  matrix products  21.6 us (3%)
  local copies, waits for them, and re-layouts  18.2 us (3%)
  between operations  14.1 us (2%)
    psum x1, waiting for transfers between devices, on_device(): lax.psum((weight_term, jnp.sum(grad_pre, axis=0)), ('blk', 'rep'))  243 us
    psum x2, waiting for transfers between devices, sum_replicas(): lax.psum(partial_value.astype(jnp.bfloat16), 'rep').astype(jnp.float32)  103 us
    psum x1, blocking collectives, on_device(): lax.psum((weight_term, jnp.sum(grad_pre, axis=0)), ('blk', 'rep'))  80.5 us
    ppermute x12, waiting for transfers between devices, passed_along(): lax.ppermute(value, axis, [(i, (i + by) % count) for i in range(count)])  64.2 us
    all_gather x1, blocking collectives, on_device(): lax.all_gather(back, 'rep', axis=0, tiled=True)  34.5 us
    ppermute x12, starting transfers between devices, passed_along(): lax.ppermute(value, axis, [(i, (i + by) % count) for i in range(count)])  28.3 us
    scatter-add x4, other arithmetic, backward_terms(): return initial.at[col_ids.reshape(-1)].add(flat)  27.2 us
  transfers between devices with their start and end apart: 15, of which 12 were waited for; matrix products, arithmetic and copies ran while one was open for 4% of the time, Pallas kernels for 0%

commit v1 on v0

v1 whole, which is shorter than its diff:
```python
import jax
import jax.numpy as jnp
from jax import lax
from jax.experimental import pallas as pl
from jax.experimental.pallas import tpu as pltpu
from jax.sharding import Mesh
from jax.sharding import PartitionSpec as P

Z, YL, CORE, X, YH = 8, 2, 2, 4, 2
BLK = ("z", "yl", "core")
REP = ("x", "yh")
T = 128
ROWS = 8
STEPS = 4
SLOTS = 6
GRAD = 48
F32 = jnp.float32
BF16 = jnp.bfloat16

VMEM = pl.BlockSpec(memory_space=pltpu.VMEM)
SMEM = pl.BlockSpec(memory_space=pltpu.SMEM)
PARAMS = pltpu.CompilerParams(vmem_limit_bytes=32 * 1024 * 1024)


def bias_rows(total):
    high = total.astype(BF16)
    low = (total - high.astype(F32)).astype(BF16)
    return jnp.concatenate([high, low, jnp.zeros((12, T), BF16)], axis=0)


def bias_of(rows):
    rows = rows.astype(F32)
    return rows[0:2] + rows[2:4]


def forward_kernel(cols, counts, odd, edges, own, far, near0, near1, out):
    i = pl.program_id(0)
    is_odd = odd[0] == 1
    total = jnp.zeros((T, T), F32)
    for s in range(STEPS):
        picked = []
        for c in range(SLOTS):
            col = cols[i, s, c]
            if s == 0:
                tile = own[col, 0]
            elif s == 2:
                tile = far[col]
            elif s == 1:
                tile = jnp.where(is_odd, near0[col], near1[col])
            else:
                tile = jnp.where(is_odd, near1[col], near0[col])
            picked.append(jnp.where(c < counts[i, s], tile, jnp.zeros_like(tile)))
        left = jnp.concatenate([edges[0, s, c] for c in range(SLOTS)], axis=1)
        total += jnp.dot(left, jnp.concatenate(picked, axis=0), preferred_element_type=F32)
    out[0] = total.astype(BF16)


def dense_kernel(parts, scale, weight, bias, cot, act, send):
    total = parts[0].astype(F32)
    for j in range(1, ROWS):
        total += parts[j].astype(F32)
    agg = (scale[...] * total).astype(BF16)
    pre = jnp.dot(agg, weight[...], preferred_element_type=F32) + bias[...]
    sigma = jax.nn.sigmoid(pre)
    act[...] = (pre * sigma).astype(BF16)
    grad_pre = cot[...].astype(F32) * sigma * (1.0 + pre * (1.0 - sigma))
    half = grad_pre.astype(BF16)
    grad_w = lax.dot_general(agg, half, (((0,), (0,)), ((), ())), preferred_element_type=F32)
    grad_b = jnp.sum(grad_pre, axis=0, keepdims=True)
    grad_b = jnp.concatenate([grad_b[:, :T], grad_b[:, T:]], axis=0)
    back = lax.dot_general(
        half, weight[...], (((1,), (1,)), ((), ())), preferred_element_type=F32
    )
    back = (scale[...] * back).astype(BF16)
    rows_b = bias_rows(grad_b)
    grad_w = grad_w.astype(BF16)
    for j in range(ROWS):
        send[j, 0:T] = back
        send[j, T : T + 16] = grad_w[16 * j : 16 * j + 16, :T]
        send[j, T + 16 : T + 32] = grad_w[16 * j : 16 * j + 16, T:]
        send[j, T + 32 : T + 48] = rows_b


def backward_kernel(cols, counts, odd, edges, got, near, keep, far, grads, sums):
    i = pl.program_id(0)

    @pl.when(i == 0)
    def _():
        sums[...] = jnp.zeros_like(sums)
        total = got[0, T:].astype(F32)
        for j in range(1, ROWS):
            total += got[j, T:].astype(F32)
        grads[0:32] = total[0:32].astype(BF16)
        grads[32:48] = bias_rows(total[32:34] + total[34:36])

    back = got[i, 0:T].T
    for s in range(STEPS):
        right = jnp.concatenate([edges[0, s, c] for c in range(SLOTS)], axis=1)
        prod = jnp.dot(back, right, preferred_element_type=F32)
        for c in range(SLOTS):
            part = prod[:, c * T : (c + 1) * T]
            at = s * ROWS + cols[i, s, c]
            sums[at] += jnp.where(c < counts[i, s], part, jnp.zeros_like(part))

    @pl.when(i == ROWS - 1)
    def _():
        is_odd = odd[0] == 1
        one = sums[ROWS : 2 * ROWS].astype(BF16)
        three = sums[3 * ROWS :].astype(BF16)
        keep[...] = sums[0:ROWS].astype(BF16)
        far[...] = sums[2 * ROWS : 3 * ROWS].astype(BF16)
        near[0:ROWS] = jnp.where(is_odd, one, three)
        near[ROWS:] = jnp.where(is_odd, three, one)


def add_grads(a, b):
    total = a[0:32].astype(F32) + b[0:32].astype(F32)
    return jnp.concatenate([total.astype(BF16), bias_rows(bias_of(a[32:]) + bias_of(b[32:]))], 0)


def near_kernel(far, near_far, grads, near_grads, out, out_grads):
    out[...] = (far[...].astype(F32) + near_far[...].astype(F32)).astype(BF16)
    out_grads[...] = add_grads(grads[...], near_grads[...])


def far_kernel(where_at, keep, near, far, grads, far_grads, out, out_grads):
    even, low = where_at[0] == 0, where_at[1] == 0
    near_f, far_f = near[...].astype(F32), far[...].astype(F32)
    zero = jnp.zeros_like(near_f)
    first = keep[...].astype(F32) + jnp.where(even, near_f, zero) + jnp.where(low, far_f, zero)
    second = jnp.where(even, zero, near_f) + jnp.where(low, zero, far_f)
    total = add_grads(grads[...], far_grads[...])
    out_grads[...] = total
    for j in range(ROWS):
        out[j, 0:T] = first[j].astype(BF16)
        out[j, T : 2 * T] = second[j].astype(BF16)
        out[j, 2 * T :] = total[0:32]


def turn_kernel(where_at, got, grads, out):
    even, z = where_at[0] == 0, where_at[2]
    half = []
    for j in range(ROWS):
        half.append(jnp.where(even, got[j, 2 * T : 2 * T + 16], got[j, 2 * T + 16 :]))
    half = jnp.concatenate(half, axis=0)
    for p in range(Z):
        d = lax.rem(z - p + Z, Z)
        before = lax.rem(d + Z - 1, Z)
        out[p, 0:T] = (got[d, 0:T].astype(F32) + got[before, T : 2 * T].astype(F32)).astype(BF16)
        out[p, T : 2 * T] = half
        out[p, 2 * T :] = grads[32:48]


def last_kernel(got, scale, grad_features, grad_half, grad_bias):
    total = got[0].astype(F32)
    for p in range(1, Z):
        total += got[p].astype(F32)
    grad_features[...] = scale[...] * total[0:T].T
    grad_half[...] = total[T : 2 * T]
    bias = total[2 * T : 2 * T + 2] + total[2 * T + 2 : 2 * T + 4]
    grad_bias[...] = jnp.concatenate([bias[0:1], bias[1:2]], axis=1)


def call(kernel, out, in_specs):
    return pl.pallas_call(
        kernel,
        out_shape=[jax.ShapeDtypeStruct(*o) for o in out],
        in_specs=in_specs,
        out_specs=[VMEM] * len(out),
        compiler_params=PARAMS,
    )


def whole(shape):
    return pl.BlockSpec(shape, lambda i: (0,) * len(shape))


EDGES = pl.BlockSpec((1, STEPS, SLOTS, T, T), lambda i: (i, 0, 0, 0, 0))


def exchange(value, axes):
    return lax.all_to_all(value, axes, 0, 0, tiled=True)


def swap(value, axis):
    return lax.ppermute(value, axis, [(0, 1), (1, 0)])


def on_device(features, degrees, cols, counts, edges, weight, bias, cot):
    z, yl, core = (lax.axis_index(a) for a in BLK)
    rep = lax.axis_index(REP)
    even, low = core == 0, yl == 0
    own_degrees = lax.dynamic_slice_in_dim(degrees, rep * T, T, 0)
    scale = jnp.broadcast_to(lax.rsqrt(own_degrees.astype(F32))[:, None], (T, T))
    own = lax.dynamic_slice_in_dim(features, rep * T, T, 0)
    own = (own * scale).astype(BF16)
    odd = core.astype(jnp.int32)[None]
    where_at = jnp.stack([core, yl, z]).astype(jnp.int32)

    planes = exchange(jnp.broadcast_to(own[None], (Z, T, T)), "z")
    wanted = (z - jnp.arange(ROWS)[:, None] - jnp.arange(2)[None, :]) % Z
    own = exchange(planes[wanted], REP)
    far = swap(jnp.where(low, own[:, 0], own[:, 1]), "yl")
    near0 = swap(jnp.where(even, own[:, 0], own[:, 1]), "core")
    near1 = swap(far, "core")

    tiles = (ROWS, T, T)
    (parts,) = pl.pallas_call(
        forward_kernel,
        grid=(ROWS,),
        out_shape=[jax.ShapeDtypeStruct(tiles, BF16)],
        in_specs=[SMEM, SMEM, SMEM, EDGES, whole((ROWS, 2, T, T))] + [whole(tiles)] * 3,
        out_specs=[pl.BlockSpec((1, T, T), lambda i: (i, 0, 0))],
        compiler_params=PARAMS,
    )(cols, counts, odd, edges, own, far, near0, near1)
    parts = exchange(parts, REP)

    act, send = call(
        dense_kernel,
        [(cot.shape, BF16), ((ROWS, T + GRAD, T), BF16)],
        [VMEM] * 5,
    )(parts, scale, weight, bias[None], cot)
    got = exchange(send, REP)

    near, keep, far, grads = pl.pallas_call(
        backward_kernel,
        grid=(ROWS,),
        out_shape=[
            jax.ShapeDtypeStruct((2 * ROWS, T, T), BF16),
            jax.ShapeDtypeStruct(tiles, BF16),
            jax.ShapeDtypeStruct(tiles, BF16),
            jax.ShapeDtypeStruct((GRAD, T), BF16),
        ],
        in_specs=[SMEM, SMEM, SMEM, EDGES, whole((ROWS, T + GRAD, T))],
        out_specs=[whole((2 * ROWS, T, T)), whole(tiles), whole(tiles), whole((GRAD, T))],
        scratch_shapes=[pltpu.VMEM((STEPS * ROWS, T, T), F32)],
        compiler_params=PARAMS,
    )(cols, counts, odd, edges, got)

    near = swap(near, "core")
    near_grads = swap(grads, "core")
    far, grads = call(near_kernel, [(tiles, BF16), ((GRAD, T), BF16)], [VMEM] * 4)(
        far, near[ROWS:], grads, near_grads
    )
    far_got, far_grads = swap(far, "yl"), swap(grads, "yl")
    send, grads = call(
        far_kernel,
        [((ROWS, 2 * T + 32, T), BF16), ((GRAD, T), BF16)],
        [SMEM] + [VMEM] * 5,
    )(where_at, keep, near[:ROWS], far_got, grads, far_grads)
    got = exchange(send, REP)
    (send,) = call(turn_kernel, [((Z, 2 * T + 16, T), BF16)], [SMEM, VMEM, VMEM])(
        where_at, got, grads
    )
    got = exchange(send, "z")
    grad_features, half, grad_bias = call(
        last_kernel,
        [((T, T), F32), ((T, T), F32), ((1, 2 * T), F32)],
        [VMEM, VMEM],
    )(got, scale)
    other = swap(half, "core")
    grad_weight = jnp.concatenate(
        [jnp.where(even, half, other), jnp.where(even, other, half)], axis=1
    )
    return act, grad_weight, grad_bias[0], grad_features


def solution(mesh):
    fine = Mesh(mesh.devices.reshape(Z, YL, CORE, X, YH), BLK + REP)
    return jax.shard_map(
        on_device,
        mesh=fine,
        in_specs=(
            P(BLK, None),
            P(BLK),
            P(BLK, REP, None),
            P(BLK, REP),
            P(BLK, REP, None, None, None),
            P(),
            P(),
            P(BLK + REP, None),
        ),
        out_specs=(P(BLK + REP, None), P(), P(), P(BLK + REP, None)),
        check_vma=False,
    )
```

time: 651 us -> 140 us (0.22)
  the two profiles are of different devices: /device:TPU:32 before, /device:TPU:1 now
where the time goes in v1:
time: 140 us; the launch traced here: 139 us
  blocking collectives  52 us (37%)
  starting transfers between devices  34.6 us (25%)
  waiting for transfers between devices  28.2 us (20%)
  Pallas kernels  11.9 us (8%)
  local copies, waits for them, and re-layouts  8.53 us (6%)
  other arithmetic  3.22 us (2%)
    all_to_all x4, blocking collectives, exchange(): return lax.all_to_all(value, axes, 0, 0, tiled=True)  52 us
    ppermute x8, starting transfers between devices, swap(): return lax.ppermute(value, axis, [(0, 1), (1, 0)])  18.9 us
    all_to_all x2, waiting for transfers between devices, exchange(): return lax.all_to_all(value, axes, 0, 0, tiled=True)  18.8 us
    all_to_all x2, starting transfers between devices, exchange(): return lax.all_to_all(value, axes, 0, 0, tiled=True)  15.7 us
    ppermute x8, waiting for transfers between devices, swap(): return lax.ppermute(value, axis, [(0, 1), (1, 0)])  9.34 us
    unnamed x22, local copies, waits for them, and re-layouts  6.18 us
    pallas_call x1, Pallas kernels, on_device(): pl.pallas_call(backward_kernel, grid=(ROWS,), out_shape=[jax.ShapeDtypeSt...  4.7 us
    pallas_call x1, Pallas kernels, on_device(): pl.pallas_call(forward_kernel, grid=(ROWS,), out_shape=[jax.ShapeDtypeStr...  4.18 us
  transfers between devices with their start and end apart: 10, of which 6 were waited for; matrix products, arithmetic and copies ran while one was open for 2% of the time, Pallas kernels for 0%

profile of v1, /device:TPU:1, one launch (start us, length us, event | category | flops | bytes accessed | tf_op | source)
XLA Modules:
  0.0 139.1 jit_solution(15443027693946370598)
XLA Ops:
  1.9 0.9 multiply_convert_fusion
  3.6 9.0 %all-to-all-start = ((bf16[8,128,128]{2,1,0:T(8,128)(2,1)}), bf16[8,128,128]{2,1,0:T(8,128)(2,1)S(1)}, u32[]{:S(2)}, u32[]{:S(2)}) async-start(bf16[8,128,128]{2,1,0:T(8,128)(2,1)} %broadcast_in_dim.10), calls=%async_computation | async-start | bytes 524288 | tf_op jit(solution)/shard_map/all_to_all | solution.py:182
  12.7 10.2 %all-to-all-done = bf16[8,128,128]{2,1,0:T(8,128)(2,1)S(1)} async-done(((bf16[8,128,128]{2,1,0:T(8,128)(2,1)}), bf16[8,128,128]{2,1,0:T(8,128)(2,1)S(1)}, u32[]{:S(2)}, u32[]{:S(2)}) %all-to-all-start) | async-done | bytes 262176 | tf_op jit(solution)/shard_map/all_to_all | solution.py:182
  22.9 1.4 %gather_fusion = bf16[16,128,128]{2,1,0:T(8,128)(2,1)} fusion(bf16[8,128,128]{2,1,0:T(8,128)(2,1)S(1)} %all-to-all-done, s32[1024]{0:T(1024)S(1)} %pad_clamp_fusion), kind=kCustom, calls=%fused_computation | custom fusion | bytes 1048640 | tf_op jit(solution)/shard_map/gather | solution.py:202
  24.4 6.7 %all-to-all-start.1 = ((bf16[8,2,128,128]{3,2,1,0:T(8,128)(2,1)}), bf16[8,2,128,128]{3,2,1,0:T(8,128)(2,1)S(1)}, u32[]{:S(2)}, u32[]{:S(2)}) async-start(bf16[8,2,128,128]{3,2,1,0:T(8,128)(2,1)} %bitcast.1), calls=%async_computation.1 | async-start | bytes 1048576 | tf_op jit(solution)/shard_map/all_to_all | solution.py:182
  31.0 8.6 %all-to-all-done.1.own = bf16[8,2,128,128]{3,2,1,0:T(8,128)(2,1)S(1)} async-done(((bf16[8,2,128,128]{3,2,1,0:T(8,128)(2,1)}), bf16[8,2,128,128]{3,2,1,0:T(8,128)(2,1)S(1)}, u32[]{:S(2)}, u32[]{:S(2)}) %all-to-all-start.1) | async-done | bytes 524320 | tf_op jit(solution)/shard_map/all_to_all | solution.py:182
  40.8 4.1 %collective-permute-start.1 = (bf16[8,128,128]{2,1,0:T(8,128)(2,1)}, bf16[8,128,128]{2,1,0:T(8,128)(2,1)S(1)}, u32[]{:S(2)}, u32[]{:S(2)}) collective-permute-start(bf16[8,128,128]{2,1,0:T(8,128)(2,1)} %get-tuple-element.32), channel_id=1, source_target_pairs={{0,8},{8,0},{1,9},{9,1},{2,10},{10,2},{3,11},{11,3},{4,12},{12,4},... | collective-permute-start | bytes 786440 | tf_op jit(solution)/shard_map/ppermute | solution.py:186
  45.6 4.9 %collective-permute-start.2 = (bf16[8,128,128]{2,1,0:T(8,128)(2,1)S(1)}, bf16[8,128,128]{2,1,0:T(8,128)(2,1)S(1)}, u32[]{:S(2)}, u32[]{:S(2)}) collective-permute-start(bf16[8,128,128]{2,1,0:T(8,128)(2,1)S(1)} %collective-permute-done.far), channel_id=1, source_target_pairs={{0,8},{8,0},{1,9},{9,1},{2,10},{10,2},{3,11},{11,3},{4,12},{12,4},... | collective-permute-start | bytes 786440 | tf_op jit(solution)/shard_map/ppermute | solution.py:186
  50.5 0.8 copy.25.cols
  51.4 1.3 copy.26.counts
  52.7 2.8 %copy-done = bf16[8,4,6,128,128]{4,3,2,1,0:T(8,128)(2,1)S(1)} copy-done((bf16[8,4,6,128,128]{4,3,2,1,0:T(8,128)(2,1)S(1)}, bf16[8,4,6,128,128]{4,3,2,1,0:T(8,128)(2,1)}, u32[]{:S(2)}) %copy-start) | copy-done | bytes 6291480
  56.2 4.2 %shard_map.111 = bf16[8,128,128]{2,1,0:T(8,128)(2,1)S(1)} custom-call(s32[8,4,6]{2,1,0:T(4,128)S(1)} %copy.25.cols, s32[8,4]{1,0:T(8,128)S(1)} %copy-done.3, s32[1]{0:T(128)} %bitcast.odd, bf16[8,4,6,128,128]{4,3,2,1,0:T(8,128)(2,1)S(1)} %copy-done, bf16[8,2,128,128]{3,2,1,0:T(8,128)(2,1)S(1)} %all-to-all-done.1.own, ...), custom_call_target="tpu_custom_call" | custom-call | tf_op jit(solution)/shard_map/pallas_call | solution.py:208
  60.4 11.0 %all_to_all.30.parts = bf16[8,128,128]{2,1,0:T(8,128)(2,1)S(1)} all-to-all(bf16[8,128,128]{2,1,0:T(8,128)(2,1)S(1)} %shard_map.111), channel_id=1, replica_groups=mesh['z'=8,'yl'=2,'core'=2,'x'=4,'yh'=2] {'x','yh'}, dimensions={0} | all-to-all | bytes 524288 | tf_op jit(solution)/shard_map/all_to_all | solution.py:182
  71.5 0.8 shard_map.112
  72.3 10.8 %all_to_all.31.got = bf16[8,176,128]{2,1,0:T(8,128)(2,1)S(1)} all-to-all(bf16[8,176,128]{2,1,0:T(8,128)(2,1)S(1)} %get-tuple-element.18), channel_id=1, replica_groups=mesh['z'=8,'yl'=2,'core'=2,'x'=4,'yh'=2] {'x','yh'}, dimensions={0} | all-to-all | bytes 720896 | tf_op jit(solution)/shard_map/all_to_all | solution.py:182
  83.1 4.7 %shard_map.113 = (bf16[16,128,128]{2,1,0:T(8,128)(2,1)S(1)}, bf16[8,128,128]{2,1,0:T(8,128)(2,1)S(1)}, bf16[8,128,128]{2,1,0:T(8,128)(2,1)S(1)}, bf16[48,128]{1,0:T(8,128)(2,1)S(1)}) custom-call(s32[8,4,6]{2,1,0:T(4,128)S(1)} %copy.25.cols, s32[8,4]{1,0:T(8,128)S(1)} %copy-done.4, s32[1]{0:T(128)} %bitcast.odd, bf16[8,4,6,128,128]{4,3,2,1,0:T(8,128)(2,1)S(1)} %bitcast.25, ...), custom_call_target="tpu_custom_call" | custom-call | tf_op jit(solution)/shard_map/pallas_call | solution.py:225
  87.8 2.7 %collective-permute-start.3 = (bf16[16,128,128]{2,1,0:T(8,128)(2,1)S(1)}, bf16[16,128,128]{2,1,0:T(8,128)(2,1)S(1)}, u32[]{:S(2)}, u32[]{:S(2)}) collective-permute-start(bf16[16,128,128]{2,1,0:T(8,128)(2,1)S(1)} %get-tuple-element.20), channel_id=1, source_target_pairs={{0,8},{8,0},{1,9},{9,1},{2,10},{10,2},{3,11},{11,3},{4,12},{12,4},... | collective-permute-start | bytes 1572872 | tf_op jit(solution)/shard_map/ppermute | solution.py:186
  90.6 1.4 %collective-permute-done.3 = bf16[16,128,128]{2,1,0:T(8,128)(2,1)S(1)} collective-permute-done((bf16[16,128,128]{2,1,0:T(8,128)(2,1)S(1)}, bf16[16,128,128]{2,1,0:T(8,128)(2,1)S(1)}, u32[]{:S(2)}, u32[]{:S(2)}) %collective-permute-start.3) | collective-permute-done | bytes 524320 | tf_op jit(solution)/shard_map/ppermute | solution.py:186
  92.6 1.1 collective-permute-start.6
  93.8 6.2 %collective-permute-done.6.far_grads = bf16[48,128]{1,0:T(8,128)(2,1)S(1)} collective-permute-done((bf16[48,128]{1,0:T(8,128)(2,1)S(1)}, bf16[48,128]{1,0:T(8,128)(2,1)S(1)}, u32[]{:S(2)}, u32[]{:S(2)}) %collective-permute-start.6) | collective-permute-done | bytes 12320 | tf_op jit(solution)/shard_map/ppermute | solution.py:186
  100.8 12.8 %all_to_all.32.got = bf16[8,288,128]{2,1,0:T(8,128)(2,1)S(1)} all-to-all(bf16[8,288,128]{2,1,0:T(8,128)(2,1)S(1)} %get-tuple-element.25), channel_id=1, replica_groups=mesh['z'=8,'yl'=2,'core'=2,'x'=4,'yh'=2] {'x','yh'}, dimensions={0} | all-to-all | bytes 1179648 | tf_op jit(solution)/shard_map/all_to_all | solution.py:182
  114.2 17.4 %all_to_all.33.got = bf16[8,272,128]{2,1,0:T(8,128)(2,1)S(1)} all-to-all(bf16[8,272,128]{2,1,0:T(8,128)(2,1)S(1)} %shard_map.116), channel_id=1, replica_groups=mesh['z'=8,'yl'=2,'core'=2,'x'=4,'yh'=2] {'z'}, dimensions={0} | all-to-all | bytes 1114112 | tf_op jit(solution)/shard_map/all_to_all | solution.py:182
  132.4 5.2 %collective-permute-start.7 = (f32[128,128]{1,0:T(8,128)S(1)}, f32[128,128]{1,0:T(8,128)S(1)}, u32[]{:S(2)}, u32[]{:S(2)}) collective-permute-start(f32[128,128]{1,0:T(8,128)S(1)} %get-tuple-element.27), channel_id=1, source_target_pairs={{0,8},{8,0},{1,9},{9,1},{2,10},{10,2},{3,11},{11,3},{4,12},{12,4},... | collective-permute-start | bytes 196616 | tf_op jit(solution)/shard_map/ppermute | solution.py:186
  137.6 0.9 collective-permute-done.7
  (44 shorter events, 8.5 us)
Async XLA Ops:
  1.4 0.5 copy-start.6
  1.9 69.5 %copy-start.1 = (bf16[128,256]{1,0:T(8,128)(2,1)S(1)}, bf16[128,256]{1,0:T(8,128)(2,1)}, u32[]{:S(2)}) copy-start(bf16[128,256]{1,0:T(8,128)(2,1)} %weight.1) | copy-start | bytes 196612
  1.9 69.6 %copy-start.2 = (bf16[128,256]{1,0:T(8,128)(2,1)S(1)}, bf16[128,256]{1,0:T(8,128)(2,1)}, u32[]{:S(2)}) copy-start(bf16[128,256]{1,0:T(8,128)(2,1)} %cot.1) | copy-start | bytes 196612
  2.8 80.3 %slice-start = ((s8[6291456]{0:T(1024)(128)(4,1)}), s8[2097152]{0:T(1024)(128)(4,1)S(1)}, s32[]{:S(2)}) async-start(s8[6291456]{0:T(1024)(128)(4,1)} %bitcast.24), calls=%async_computation.6 | async-start | bytes 4194304
  3.6 19.4 %all-to-all-start = ((bf16[8,128,128]{2,1,0:T(8,128)(2,1)}), bf16[8,128,128]{2,1,0:T(8,128)(2,1)S(1)}, u32[]{:S(2)}, u32[]{:S(2)}) async-start(bf16[8,128,128]{2,1,0:T(8,128)(2,1)} %broadcast_in_dim.10), calls=%async_computation | async-start | bytes 524288 | tf_op jit(solution)/shard_map/all_to_all | solution.py:182
  24.4 15.3 %all-to-all-start.1 = ((bf16[8,2,128,128]{3,2,1,0:T(8,128)(2,1)}), bf16[8,2,128,128]{3,2,1,0:T(8,128)(2,1)S(1)}, u32[]{:S(2)}, u32[]{:S(2)}) async-start(bf16[8,2,128,128]{3,2,1,0:T(8,128)(2,1)} %bitcast.1), calls=%async_computation.1 | async-start | bytes 1048576 | tf_op jit(solution)/shard_map/all_to_all | solution.py:182
  40.4 5.2 %collective-permute-start = (bf16[8,128,128]{2,1,0:T(8,128)(2,1)S(1)}, bf16[8,128,128]{2,1,0:T(8,128)(2,1)S(1)}, u32[]{:S(2)}, u32[]{:S(2)}) collective-permute-start(bf16[8,128,128]{2,1,0:T(8,128)(2,1)S(1)} %get-tuple-element.33), channel_id=1, source_target_pairs={{0,16},{16,0},{1,17},{17,1},{2,18},{18,2},{3,19},{19,3},{4,20},{20... | collective-permute-start | bytes 786440 | tf_op jit(solution)/shard_map/ppermute | solution.py:186
  40.8 11.9 %collective-permute-start.1 = (bf16[8,128,128]{2,1,0:T(8,128)(2,1)}, bf16[8,128,128]{2,1,0:T(8,128)(2,1)S(1)}, u32[]{:S(2)}, u32[]{:S(2)}) collective-permute-start(bf16[8,128,128]{2,1,0:T(8,128)(2,1)} %get-tuple-element.32), channel_id=1, source_target_pairs={{0,8},{8,0},{1,9},{9,1},{2,10},{10,2},{3,11},{11,3},{4,12},{12,4},... | collective-permute-start | bytes 786440 | tf_op jit(solution)/shard_map/ppermute | solution.py:186
  45.6 7.1 %collective-permute-start.2 = (bf16[8,128,128]{2,1,0:T(8,128)(2,1)S(1)}, bf16[8,128,128]{2,1,0:T(8,128)(2,1)S(1)}, u32[]{:S(2)}, u32[]{:S(2)}) collective-permute-start(bf16[8,128,128]{2,1,0:T(8,128)(2,1)S(1)} %collective-permute-done.far), channel_id=1, source_target_pairs={{0,8},{8,0},{1,9},{9,1},{2,10},{10,2},{3,11},{11,3},{4,12},{12,4},... | collective-permute-start | bytes 786440 | tf_op jit(solution)/shard_map/ppermute | solution.py:186
  52.7 18.7 %copy-start.7 = (f32[128]{0:T(128)S(1)}, f32[128]{0:T(128)}, u32[]{:S(2)}) copy-start(f32[128]{0:T(128)} %copy-done.6) | copy-start | bytes 1540
  52.7 18.8 %copy-start.5 = (f32[256]{0:T(256)S(1)}, f32[256]{0:T(256)}, u32[]{:S(2)}) copy-start(f32[256]{0:T(256)} %param.14) | copy-start | bytes 3076
  52.7 2.8 %copy-start = (bf16[8,4,6,128,128]{4,3,2,1,0:T(8,128)(2,1)S(1)}, bf16[8,4,6,128,128]{4,3,2,1,0:T(8,128)(2,1)}, u32[]{:S(2)}) copy-start(bf16[8,4,6,128,128]{4,3,2,1,0:T(8,128)(2,1)} %edges.3) | copy-start | bytes 18874372
  55.5 0.7 copy-start.3
  56.2 26.9 %slice-start.1 = ((s8[6291456]{0:T(1024)(128)(4,1)}), s8[4194304]{0:T(1024)(128)(4,1)S(1)}, s32[]{:S(2)}) async-start(s8[6291456]{0:T(1024)(128)(4,1)} %bitcast.24), calls=%async_computation.7 | async-start | bytes 8388608
  56.2 26.9 %copy-start.4 = (s32[8,4]{1,0:T(8,128)S(1)}, s32[8,4]{1,0:T(8,128)}, u32[]{:S(2)}) copy-start(s32[8,4]{1,0:T(8,128)} %copy.26.counts) | copy-start | bytes 388
  87.8 4.2 %collective-permute-start.3 = (bf16[16,128,128]{2,1,0:T(8,128)(2,1)S(1)}, bf16[16,128,128]{2,1,0:T(8,128)(2,1)S(1)}, u32[]{:S(2)}, u32[]{:S(2)}) collective-permute-start(bf16[16,128,128]{2,1,0:T(8,128)(2,1)S(1)} %get-tuple-element.20), channel_id=1, source_target_pairs={{0,8},{8,0},{1,9},{9,1},{2,10},{10,2},{3,11},{11,3},{4,12},{12,4},... | collective-permute-start | bytes 1572872 | tf_op jit(solution)/shard_map/ppermute | solution.py:186
  90.5 1.6 %collective-permute-start.4 = (bf16[48,128]{1,0:T(8,128)(2,1)S(1)}, bf16[48,128]{1,0:T(8,128)(2,1)S(1)}, u32[]{:S(2)}, u32[]{:S(2)}) collective-permute-start(bf16[48,128]{1,0:T(8,128)(2,1)S(1)} %get-tuple-element.22.grads), channel_id=1, source_target_pairs={{0,8},{8,0},{1,9},{9,1},{2,10},{10,2},{3,11},{11,3},{4,12},{12,4},... | collective-permute-start | bytes 36872 | tf_op jit(solution)/shard_map/ppermute | solution.py:186
  92.1 7.9 %collective-permute-start.5 = (bf16[8,128,128]{2,1,0:T(8,128)(2,1)S(1)}, bf16[8,128,128]{2,1,0:T(8,128)(2,1)S(1)}, u32[]{:S(2)}, u32[]{:S(2)}) collective-permute-start(bf16[8,128,128]{2,1,0:T(8,128)(2,1)S(1)} %get-tuple-element.23), channel_id=1, source_target_pairs={{0,16},{16,0},{1,17},{17,1},{2,18},{18,2},{3,19},{19,3},{4,20},{20... | collective-permute-start | bytes 786440 | tf_op jit(solution)/shard_map/ppermute | solution.py:186
  92.6 7.4 %collective-permute-start.6 = (bf16[48,128]{1,0:T(8,128)(2,1)S(1)}, bf16[48,128]{1,0:T(8,128)(2,1)S(1)}, u32[]{:S(2)}, u32[]{:S(2)}) collective-permute-start(bf16[48,128]{1,0:T(8,128)(2,1)S(1)} %get-tuple-element.24.grads), channel_id=1, source_target_pairs={{0,16},{16,0},{1,17},{17,1},{2,18},{18,2},{3,19},{19,3},{4,20},{20... | collective-permute-start | bytes 36872 | tf_op jit(solution)/shard_map/ppermute | solution.py:186
  132.4 6.1 %collective-permute-start.7 = (f32[128,128]{1,0:T(8,128)S(1)}, f32[128,128]{1,0:T(8,128)S(1)}, u32[]{:S(2)}, u32[]{:S(2)}) collective-permute-start(f32[128,128]{1,0:T(8,128)S(1)} %get-tuple-element.27), channel_id=1, source_target_pairs={{0,8},{8,0},{1,9},{9,1},{2,10},{10,2},{3,11},{11,3},{4,12},{12,4},... | collective-permute-start | bytes 196616 | tf_op jit(solution)/shard_map/ppermute | solution.py:186

commit v2 on v1

v2 whole, which is shorter than its diff:
```python
import functools

import jax
import jax.numpy as jnp
from jax import lax
from jax.experimental import pallas as pl
from jax.experimental.pallas import tpu as pltpu
from jax.sharding import Mesh
from jax.sharding import PartitionSpec as P

Z, YL, CORE, X, YH = 8, 2, 2, 4, 2
BLK = ("z", "yl", "core")
REP = ("x", "yh")
T = 128
ROWS = 8
STEPS = 4
SLOTS = 6
GRAD = 48
F32 = jnp.float32
BF16 = jnp.bfloat16

VMEM = pl.BlockSpec(memory_space=pltpu.VMEM)
SMEM = pl.BlockSpec(memory_space=pltpu.SMEM)
HBM = pl.BlockSpec(memory_space=pltpu.HBM)
PARAMS = pltpu.CompilerParams(vmem_limit_bytes=32 * 1024 * 1024)


def bias_rows(total):
    high = total.astype(BF16)
    low = (total - high.astype(F32)).astype(BF16)
    return jnp.concatenate([high, low, jnp.zeros((12, T), BF16)], axis=0)


def bias_of(rows):
    rows = rows.astype(F32)
    return rows[0:2] + rows[2:4]


def prologue_kernel(rep, features, degrees, planes, scale):
    row = degrees[pl.ds(rep[0], 1), :].astype(F32)
    diagonal = lax.broadcasted_iota(jnp.int32, (T, T), 0) == lax.broadcasted_iota(
        jnp.int32, (T, T), 1
    )
    column = jnp.sum(jnp.where(diagonal, row, jnp.zeros((T, T), F32)), axis=1, keepdims=True)
    inv_root = jnp.broadcast_to(lax.rsqrt(column), (T, T))
    scale[...] = inv_root
    own = (features[...].astype(F32) * inv_root).astype(BF16)
    for p in range(Z):
        planes[p] = own


def planes_kernel(meta, planes, out):
    z = meta[7, 0, 2]
    for j in range(ROWS):
        out[j, 0] = planes[lax.rem(z - j + Z, Z)]
        out[j, 1] = planes[lax.rem(z - j - 1 + Z, Z)]


def pick_kernel(which, meta, own, out):
    at = meta[7, 0, which]
    for j in range(ROWS):
        out[j] = own[j, at]


def product(meta, edges, i, s, tile_at):
    picked = []
    for c in range(SLOTS):
        tile = tile_at(meta[c, s, i])
        picked.append(jnp.where(c < meta[6, s, i], tile, jnp.zeros_like(tile)))
    left = jnp.concatenate([edges[i, s, c] for c in range(SLOTS)], axis=1)
    return jnp.dot(left, jnp.concatenate(picked, axis=0), preferred_element_type=F32)


def first_kernel(meta, edges, own, near, held, out, sems):
    copies = [pltpu.make_async_copy(edges.at[i], held.at[i], sems.at[i]) for i in range(ROWS)]
    for copy in copies:
        copy.start()
    step = 3 - 2 * meta[7, 0, 0]
    for i in range(ROWS):
        copies[i].wait()
        out[i] = product(meta, held, i, 0, lambda col: own[col, 0]) + product(
            meta, held, i, step, lambda col: near[col]
        )


def second_kernel(meta, held, far, total, out):
    for i in range(ROWS):
        out[i] = total[i] + product(meta, held, i, 2, lambda col: far[col])


def third_kernel(meta, held, near, total, out):
    step = 1 + 2 * meta[7, 0, 0]
    for i in range(ROWS):
        out[i] = (total[i] + product(meta, held, i, step, lambda col: near[col])).astype(BF16)


def dense_kernel(parts, scale, weight, bias, cot, act, send):
    total = parts[0].astype(F32)
    for j in range(1, ROWS):
        total += parts[j].astype(F32)
    agg = (scale[...] * total).astype(BF16)
    pre = jnp.dot(agg, weight[...], preferred_element_type=F32) + bias[...]
    sigma = jax.nn.sigmoid(pre)
    act[...] = (pre * sigma).astype(BF16)
    grad_pre = cot[...].astype(F32) * sigma * (1.0 + pre * (1.0 - sigma))
    half = grad_pre.astype(BF16)
    grad_w = lax.dot_general(agg, half, (((0,), (0,)), ((), ())), preferred_element_type=F32)
    grad_b = jnp.sum(grad_pre, axis=0, keepdims=True)
    grad_b = jnp.concatenate([grad_b[:, :T], grad_b[:, T:]], axis=0)
    back = lax.dot_general(
        half, weight[...], (((1,), (1,)), ((), ())), preferred_element_type=F32
    )
    back = (scale[...] * back).astype(BF16)
    rows_b = bias_rows(grad_b)
    grad_w = grad_w.astype(BF16)
    for j in range(ROWS):
        send[j, 0:T] = back
        send[j, T : T + 16] = grad_w[16 * j : 16 * j + 16, :T]
        send[j, T + 16 : T + 32] = grad_w[16 * j : 16 * j + 16, T:]
        send[j, T + 32 : T + 48] = rows_b


def column_sums(meta, held, got, s, sums):
    sums[...] = jnp.zeros_like(sums)
    for i in range(ROWS):
        back = got[i, 0:T].T
        right = jnp.concatenate([held[i, s, c] for c in range(SLOTS)], axis=1)
        prod = jnp.dot(back, right, preferred_element_type=F32)
        for c in range(SLOTS):
            part = prod[:, c * T : (c + 1) * T]
            at = meta[c, s, i]
            sums[at] += jnp.where(c < meta[6, s, i], part, jnp.zeros_like(part))


def near_sums_kernel(meta, held, got, near0, near1, grads, sums):
    total = got[0, T:].astype(F32)
    for j in range(1, ROWS):
        total += got[j, T:].astype(F32)
    grads[0:32] = total[0:32].astype(BF16)
    grads[32:48] = bias_rows(total[32:34] + total[34:36])
    column_sums(meta, held, got, 1 + 2 * meta[7, 0, 0], sums)
    near1[...] = sums[...].astype(BF16)
    column_sums(meta, held, got, 3 - 2 * meta[7, 0, 0], sums)
    near0[...] = sums[...].astype(BF16)


def far_sums_kernel(meta, held, got, far, sums):
    column_sums(meta, held, got, 2, sums)
    far[...] = sums[...].astype(BF16)


def own_sums_kernel(meta, held, got, near, out, sums):
    column_sums(meta, held, got, 0, sums)
    even = meta[7, 0, 0] == 0
    near_f = near[...].astype(F32)
    zero = jnp.zeros_like(near_f)
    out[0] = sums[...] + jnp.where(even, near_f, zero)
    out[1] = jnp.where(even, zero, near_f)


def add_grads(a, b):
    total = a[0:32].astype(F32) + b[0:32].astype(F32)
    return jnp.concatenate([total.astype(BF16), bias_rows(bias_of(a[32:]) + bias_of(b[32:]))], 0)


def near_kernel(far, near_far, grads, near_grads, out, out_grads):
    out[...] = (far[...].astype(F32) + near_far[...].astype(F32)).astype(BF16)
    out_grads[...] = add_grads(grads[...], near_grads[...])


def far_kernel(meta, own, far, grads, far_grads, out, out_grads):
    low = meta[7, 0, 1] == 0
    total = add_grads(grads[...], far_grads[...])
    out_grads[...] = total
    zero = jnp.zeros((T, T), F32)
    for j in range(ROWS):
        far_f = far[j].astype(F32)
        out[j, 0:T] = (own[0, j] + jnp.where(low, far_f, zero)).astype(BF16)
        out[j, T : 2 * T] = (own[1, j] + jnp.where(low, zero, far_f)).astype(BF16)
        out[j, 2 * T :] = total[0:32]


def turn_kernel(meta, got, grads, out):
    even, z = meta[7, 0, 0] == 0, meta[7, 0, 2]
    half = []
    for j in range(ROWS):
        half.append(jnp.where(even, got[j, 2 * T : 2 * T + 16], got[j, 2 * T + 16 :]))
    half = jnp.concatenate(half, axis=0)
    for p in range(Z):
        d = lax.rem(z - p + Z, Z)
        before = lax.rem(d + Z - 1, Z)
        out[p, 0:T] = (got[d, 0:T].astype(F32) + got[before, T : 2 * T].astype(F32)).astype(BF16)
        out[p, T : 2 * T] = half
        out[p, 2 * T :] = grads[32:48]


def last_kernel(got, scale, grad_features, grad_half, grad_bias):
    total = got[0].astype(F32)
    for p in range(1, Z):
        total += got[p].astype(F32)
    grad_features[...] = scale[...] * total[0:T].T
    grad_half[...] = total[T : 2 * T]
    bias = total[2 * T : 2 * T + 2] + total[2 * T + 2 : 2 * T + 4]
    grad_bias[...] = jnp.concatenate([bias[0:1], bias[1:2]], axis=1)


def call(kernel, out, in_specs, scratch=(), flops=0, moved=1 << 20):
    return pl.pallas_call(
        kernel,
        out_shape=[jax.ShapeDtypeStruct(*o) for o in out],
        in_specs=in_specs,
        out_specs=[VMEM] * len(out),
        scratch_shapes=list(scratch),
        cost_estimate=pl.CostEstimate(flops=flops, bytes_accessed=moved, transcendentals=0),
        compiler_params=PARAMS,
    )


def pinned(value):
    return pltpu.with_memory_space_constraint(value, pltpu.HBM)


def exchange(value, axes):
    return lax.all_to_all(value, axes, 0, 0, tiled=True)


def swap(value, axis):
    return lax.ppermute(value, axis, [(0, 1), (1, 0)])


def on_device(features, degrees, cols, counts, edges, weight, bias, cot):
    z, yl, core = (lax.axis_index(a) for a in BLK)
    rep = lax.axis_index(REP)
    even = core == 0
    place = lax.broadcasted_iota(jnp.int32, (1, STEPS, ROWS), 2)
    place = jnp.where(place == 0, core, jnp.where(place == 1, yl, z))
    meta = jnp.concatenate([cols.transpose(2, 1, 0), counts.T[None], place], axis=0)

    tiles = (ROWS, T, T)
    planes, scale = pl.pallas_call(
        prologue_kernel,
        grid_spec=pltpu.PrefetchScalarGridSpec(
            num_scalar_prefetch=1,
            grid=(1,),
            in_specs=[
                pl.BlockSpec((T, T), lambda i, rep: (rep[0], 0)),
                pl.BlockSpec((ROWS, T), lambda i, rep: (0, 0)),
            ],
            out_specs=[
                pl.BlockSpec((Z, T, T), lambda i, rep: (0, 0, 0)),
                pl.BlockSpec((T, T), lambda i, rep: (0, 0)),
            ],
        ),
        out_shape=[jax.ShapeDtypeStruct((Z, T, T), BF16), jax.ShapeDtypeStruct((T, T), F32)],
        compiler_params=PARAMS,
    )(rep.astype(jnp.int32)[None], pinned(features), pinned(degrees.reshape(ROWS, T)))
    planes = exchange(planes, "z")
    (own,) = call(planes_kernel, [((ROWS, 2, T, T), BF16)], [SMEM, VMEM])(meta, planes)
    own = exchange(own, REP)
    pick = [
        call(functools.partial(pick_kernel, which), [(tiles, BF16)], [SMEM, VMEM])
        for which in (0, 1)
    ]
    (far,) = pick[1](meta, own)
    far, own = lax.optimization_barrier((far, own))
    far = swap(far, "yl")
    near0 = swap(pick[0](meta, own)[0], "core")

    work = 2 * ROWS * SLOTS * T * T * T
    held, total = call(
        first_kernel,
        [(edges.shape, BF16), (tiles, F32)],
        [SMEM, HBM, VMEM, VMEM],
        [pltpu.SemaphoreType.DMA((ROWS,))],
        2 * work,
        8 << 20,
    )(meta, pinned(edges), own, near0)
    far, total = lax.optimization_barrier((far, total))
    near1 = swap(far, "core")
    (total,) = call(second_kernel, [(tiles, F32)], [SMEM] + [VMEM] * 3, (), work, 3 << 20)(
        meta, held, far, total
    )
    (parts,) = call(third_kernel, [(tiles, BF16)], [SMEM] + [VMEM] * 3, (), work, 3 << 20)(
        meta, held, near1, total
    )
    parts = exchange(parts, REP)

    act, send = call(
        dense_kernel,
        [(cot.shape, BF16), ((ROWS, T + GRAD, T), BF16)],
        [VMEM] * 5,
    )(parts, scale, weight, bias[None], cot)
    got = exchange(send, REP)

    sums = [pltpu.VMEM(tiles, F32)]
    near0, near1, grads = call(
        near_sums_kernel,
        [(tiles, BF16), (tiles, BF16), ((GRAD, T), BF16)],
        [SMEM, VMEM, VMEM],
        sums,
        2 * work,
        6 << 20,
    )(meta, held, got)
    near0, near1, near_grads = (swap(a, "core") for a in (near0, near1, grads))
    (far,) = call(far_sums_kernel, [(tiles, BF16)], [SMEM, VMEM, VMEM], sums, work, 3 << 20)(
        meta, held, got
    )
    far, grads = call(near_kernel, [(tiles, BF16), ((GRAD, T), BF16)], [VMEM] * 4)(
        far, near1, grads, near_grads
    )
    far, got = lax.optimization_barrier((far, got))
    far_got, far_grads = swap(far, "yl"), swap(grads, "yl")
    (own,) = call(
        own_sums_kernel, [((2, *tiles), F32)], [SMEM] + [VMEM] * 3, sums, work, 3 << 20
    )(meta, held, got, near0)
    send, grads = call(
        far_kernel,
        [((ROWS, 2 * T + 32, T), BF16), ((GRAD, T), BF16)],
        [SMEM] + [VMEM] * 4,
    )(meta, own, far_got, grads, far_grads)
    got = exchange(send, REP)
    (send,) = call(turn_kernel, [((Z, 2 * T + 16, T), BF16)], [SMEM, VMEM, VMEM])(
        meta, got, grads
    )
    got = exchange(send, "z")
    grad_features, half, grad_bias = call(
        last_kernel,
        [((T, T), F32), ((T, T), F32), ((1, 2 * T), F32)],
        [VMEM, VMEM],
    )(got, scale)
    other = swap(half, "core")
    grad_weight = jnp.concatenate(
        [jnp.where(even, half, other), jnp.where(even, other, half)], axis=1
    )
    return act, grad_weight, grad_bias[0], grad_features


def solution(mesh):
    fine = Mesh(mesh.devices.reshape(Z, YL, CORE, X, YH), BLK + REP)
    return jax.shard_map(
        on_device,
        mesh=fine,
        in_specs=(
            P(BLK, None),
            P(BLK),
            P(BLK, REP, None),
            P(BLK, REP),
            P(BLK, REP, None, None, None),
            P(),
            P(),
            P(BLK + REP, None),
        ),
        out_specs=(P(BLK + REP, None), P(), P(), P(BLK + REP, None)),
        check_vma=False,
    )
```

time: 140 us -> 132 us (0.943)
  blocking collectives: 52 us -> 67.6 us
  starting transfers between devices: 34.6 us -> 23 us
  waiting for transfers between devices: 28.2 us -> 18.9 us
  local copies, waits for them, and re-layouts: 8.53 us -> 0.01 us
  Pallas kernels: 11.9 us -> 19.6 us
  other arithmetic: 3.22 us -> 1.42 us
    all_to_all x4 -> x5, blocking collectives: 52 us -> 67.6 us  [exchange(): return lax.all_to_all(value, axes, 0, 0, tiled=True)]
    all_to_all x2 -> x1, waiting for transfers between devices: 18.8 us -> 9.6 us  [exchange(): return lax.all_to_all(value, axes, 0, 0, tiled=True)]
    pallas_call x2 -> x10, Pallas kernels: 8.88 us -> 16.1 us  [the longest x1 4.16 us: on_device(): call(first_kernel, [(edges.shape, BF16), (tiles, F32)], [SMEM, HBM, VMEM,...]
    all_to_all x2 -> x1, starting transfers between devices: 15.7 us -> 9.01 us  [exchange(): return lax.all_to_all(value, axes, 0, 0, tiled=True)]
    unnamed x22 -> x6, local copies, waits for them, and re-layouts: 6.18 us -> 0.01 us
    ppermute x8 -> x9, starting transfers between devices: 18.9 us -> 14 us  [swap(): return lax.ppermute(value, axis, [(0, 1), (1, 0)])]
    gather x1 -> x0, local copies, waits for them, and re-layouts: 1.42 us -> none  [on_device(): own = exchange(planes[wanted], REP)]
    ppermute x8 -> x9, waiting for transfers between devices: 9.34 us -> 9.26 us  [swap(): return lax.ppermute(value, axis, [(0, 1), (1, 0)])]
  transfers between devices with their start and end apart: 10 -> 10, of which waited for: 6 -> 5; matrix products, arithmetic and copies ran while one was open for 2% -> 1% of each run, Pallas kernels for 0% -> 7%
where the time goes in v2:
time: 132 us; the launch traced here: 131 us
  blocking collectives  67.6 us (51%)
  starting transfers between devices  23 us (17%)
  Pallas kernels  19.6 us (15%)
  waiting for transfers between devices  18.9 us (14%)
  other arithmetic  1.42 us (1%)
    all_to_all x5, blocking collectives, exchange(): return lax.all_to_all(value, axes, 0, 0, tiled=True)  67.6 us
    ppermute x9, starting transfers between devices, swap(): return lax.ppermute(value, axis, [(0, 1), (1, 0)])  14 us
    all_to_all x1, waiting for transfers between devices, exchange(): return lax.all_to_all(value, axes, 0, 0, tiled=True)  9.6 us
    ppermute x9, waiting for transfers between devices, swap(): return lax.ppermute(value, axis, [(0, 1), (1, 0)])  9.26 us
    all_to_all x1, starting transfers between devices, exchange(): return lax.all_to_all(value, axes, 0, 0, tiled=True)  9.01 us
    pallas_call x1, Pallas kernels, on_device(): call(first_kernel, [(edges.shape, BF16), (tiles, F32)], [SMEM, HBM, VMEM,...  4.16 us
  transfers between devices with their start and end apart: 10, of which 5 were waited for; matrix products, arithmetic and copies ran while one was open for 1% of the time, Pallas kernels for 7%

profile of v2, /device:TPU:1, one launch (start us, length us, event | category | flops | bytes accessed | tf_op | source)
XLA Modules:
  0.0 131.2 jit_solution(8103044300727749973)
XLA Ops:
  0.6 1.6 %shard_map.111 = (bf16[8,128,128]{2,1,0:T(8,128)(2,1)}, f32[128,128]{1,0:T(8,128)S(1)}) custom-call(s32[1]{0:T(128)} %bitcast.3.rep, bf16[1024,128]{1,0:T(8,128)(2,1)} %features.1, s32[8,128]{1,0:T(8,128)} %bitcast.10), custom_call_target="tpu_custom_call" | custom-call | tf_op jit(solution)/shard_map/pallas_call | solution.py:240
  2.2 9.0 %all-to-all-start = ((bf16[8,128,128]{2,1,0:T(8,128)(2,1)}), bf16[8,128,128]{2,1,0:T(8,128)(2,1)S(1)}, u32[]{:S(2)}, u32[]{:S(2)}) async-start(bf16[8,128,128]{2,1,0:T(8,128)(2,1)} %get-tuple-element.26), calls=%async_computation | async-start | bytes 524288 | tf_op jit(solution)/shard_map/all_to_all | solution.py:224
  12.0 9.6 %all-to-all-done.planes = bf16[8,128,128]{2,1,0:T(8,128)(2,1)S(1)} async-done(((bf16[8,128,128]{2,1,0:T(8,128)(2,1)}), bf16[8,128,128]{2,1,0:T(8,128)(2,1)S(1)}, u32[]{:S(2)}, u32[]{:S(2)}) %all-to-all-start) | async-done | bytes 262176 | tf_op jit(solution)/shard_map/all_to_all | solution.py:224
  21.6 0.9 shard_map.112
  22.5 15.1 %all_to_all.30.own = bf16[8,2,128,128]{3,2,1,0:T(8,128)(2,1)S(1)} all-to-all(bf16[8,2,128,128]{3,2,1,0:T(8,128)(2,1)S(1)} %shard_map.112), channel_id=1, replica_groups=mesh['z'=8,'yl'=2,'core'=2,'x'=4,'yh'=2] {'x','yh'}, dimensions={0} | all-to-all | bytes 1048576 | tf_op jit(solution)/shard_map/all_to_all | solution.py:224
  39.3 4.0 %collective-permute-start = (bf16[8,128,128]{2,1,0:T(8,128)(2,1)S(1)}, bf16[8,128,128]{2,1,0:T(8,128)(2,1)S(1)}, u32[]{:S(2)}, u32[]{:S(2)}) collective-permute-start(bf16[8,128,128]{2,1,0:T(8,128)(2,1)S(1)} %shard_map.114), channel_id=1, source_target_pairs={{0,8},{8,0},{1,9},{9,1},{2,10},{10,2},{3,11},{11,3},{4,12},{12,4},... | collective-permute-start | bytes 786440 | tf_op jit(solution)/shard_map/ppermute | solution.py:228
  44.4 4.2 %shard_map.115 = (bf16[8,4,6,128,128]{4,3,2,1,0:T(8,128)(2,1)S(1)}, f32[8,128,128]{2,1,0:T(8,128)S(1)}) custom-call(s32[8,4,8]{2,1,0:T(4,128)S(1)} %pad_add_fusion.meta, bf16[8,4,6,128,128]{4,3,2,1,0:T(8,128)(2,1)} %edges.1, bf16[8,2,128,128]{3,2,1,0:T(8,128)(2,1)S(1)} %all_to_all.30.own, bf16[8,128,128]{2,1,0:T(8,128)(2,1)S(1)} %collective-permute-done.near), custom_call_target="tpu_custom_call" | custom-call | flops 402653184 | bytes 8388608 | tf_op jit(solution)/shard_map/pallas_call | solution.py:270
  48.6 2.5 %collective-permute-done.1.far = bf16[8,128,128]{2,1,0:T(8,128)(2,1)S(1)} collective-permute-done((bf16[8,128,128]{2,1,0:T(8,128)(2,1)S(1)}, bf16[8,128,128]{2,1,0:T(8,128)(2,1)S(1)}, u32[]{:S(2)}, u32[]{:S(2)}) %collective-permute-start.1) | collective-permute-done | bytes 262176 | tf_op jit(solution)/shard_map/ppermute | solution.py:228
  52.0 1.4 %shard_map.116.total = f32[8,128,128]{2,1,0:T(8,128)S(1)} custom-call(s32[8,4,8]{2,1,0:T(4,128)S(1)} %pad_add_fusion.meta, bf16[8,4,6,128,128]{4,3,2,1,0:T(8,128)(2,1)S(1)} %get-tuple-element.28.held, bf16[8,128,128]{2,1,0:T(8,128)(2,1)S(1)} %collective-permute-done.1.far, f32[8,128,128]{2,1,0:T(8,128)S(1)} %get-tuple-element.32.total), custom_call_target="tpu_custom_call" | custom-call | flops 201326592 | bytes 3145728 | tf_op jit(solution)/shard_map/pallas_call | solution.py:280
  53.4 1.4 %shard_map.117 = bf16[8,128,128]{2,1,0:T(8,128)(2,1)S(1)} custom-call(s32[8,4,8]{2,1,0:T(4,128)S(1)} %pad_add_fusion.meta, bf16[8,4,6,128,128]{4,3,2,1,0:T(8,128)(2,1)S(1)} %get-tuple-element.28.held, bf16[8,128,128]{2,1,0:T(8,128)(2,1)S(1)} %collective-permute-done.2.near, f32[8,128,128]{2,1,0:T(8,128)S(1)} %shard_map.116.total), custom_call_target="tpu_custom_call" | custom-call | flops 201326592 | bytes 3145728 | tf_op jit(solution)/shard_map/pallas_call | solution.py:283
  54.8 10.4 %all_to_all.31.parts = bf16[8,128,128]{2,1,0:T(8,128)(2,1)S(1)} all-to-all(bf16[8,128,128]{2,1,0:T(8,128)(2,1)S(1)} %shard_map.117), channel_id=1, replica_groups=mesh['z'=8,'yl'=2,'core'=2,'x'=4,'yh'=2] {'x','yh'}, dimensions={0} | all-to-all | bytes 524288 | tf_op jit(solution)/shard_map/all_to_all | solution.py:224
  66.1 11.1 %all_to_all.32.got = bf16[8,176,128]{2,1,0:T(8,128)(2,1)S(1)} all-to-all(bf16[8,176,128]{2,1,0:T(8,128)(2,1)S(1)} %get-tuple-element.35), channel_id=1, replica_groups=mesh['z'=8,'yl'=2,'core'=2,'x'=4,'yh'=2] {'x','yh'}, dimensions={0} | all-to-all | bytes 720896 | tf_op jit(solution)/shard_map/all_to_all | solution.py:224
  77.2 2.0 %shard_map.120 = (bf16[8,128,128]{2,1,0:T(8,128)(2,1)S(1)}, bf16[8,128,128]{2,1,0:T(8,128)(2,1)S(1)}, bf16[48,128]{1,0:T(8,128)(2,1)S(1)}) custom-call(s32[8,4,8]{2,1,0:T(4,128)S(1)} %pad_add_fusion.meta, bf16[8,4,6,128,128]{4,3,2,1,0:T(8,128)(2,1)S(1)} %get-tuple-element.28.held, bf16[8,176,128]{2,1,0:T(8,128)(2,1)S(1)} %all_to_all.32.got), custom_call_target="tpu_custom_call" | custom-call | flops 402653184 | bytes 6291456 | tf_op jit(solution)/shard_map/pallas_call | solution.py:296
  79.2 2.7 %collective-permute-start.3 = (bf16[8,128,128]{2,1,0:T(8,128)(2,1)S(1)}, bf16[8,128,128]{2,1,0:T(8,128)(2,1)S(1)}, u32[]{:S(2)}, u32[]{:S(2)}) collective-permute-start(bf16[8,128,128]{2,1,0:T(8,128)(2,1)S(1)} %get-tuple-element.36), channel_id=1, source_target_pairs={{0,8},{8,0},{1,9},{9,1},{2,10},{10,2},{3,11},{11,3},{4,12},{12,4},... | collective-permute-start | bytes 786440 | tf_op jit(solution)/shard_map/ppermute | solution.py:228
  82.4 1.5 %shard_map.119.far = bf16[8,128,128]{2,1,0:T(8,128)(2,1)S(1)} custom-call(s32[8,4,8]{2,1,0:T(4,128)S(1)} %pad_add_fusion.meta, bf16[8,4,6,128,128]{4,3,2,1,0:T(8,128)(2,1)S(1)} %get-tuple-element.28.held, bf16[8,176,128]{2,1,0:T(8,128)(2,1)S(1)} %all_to_all.32.got), custom_call_target="tpu_custom_call" | custom-call | flops 201326592 | bytes 3145728 | tf_op jit(solution)/shard_map/pallas_call | solution.py:305
  84.5 1.1 collective-permute-start.7
  85.6 1.6 %shard_map.122.own = f32[2,8,128,128]{3,2,1,0:T(8,128)S(1)} custom-call(s32[8,4,8]{2,1,0:T(4,128)S(1)} %pad_add_fusion.meta, bf16[8,4,6,128,128]{4,3,2,1,0:T(8,128)(2,1)S(1)} %get-tuple-element.28.held, bf16[8,176,128]{2,1,0:T(8,128)(2,1)S(1)} %all_to_all.32.got, bf16[8,128,128]{2,1,0:T(8,128)(2,1)S(1)} %collective-permute-done.5.near), custom_call_target="tpu_custom_call" | custom-call | flops 201326592 | bytes 3145728 | tf_op jit(solution)/shard_map/pallas_call | solution.py:313
  87.2 5.1 %collective-permute-done.7.far_grads = bf16[48,128]{1,0:T(8,128)(2,1)S(1)} collective-permute-done((bf16[48,128]{1,0:T(8,128)(2,1)S(1)}, bf16[48,128]{1,0:T(8,128)(2,1)S(1)}, u32[]{:S(2)}, u32[]{:S(2)}) %collective-permute-start.7) | collective-permute-done | bytes 12320 | tf_op jit(solution)/shard_map/ppermute | solution.py:228
  92.3 0.9 shard_map.123
  93.2 13.3 %all_to_all.33.got = bf16[8,288,128]{2,1,0:T(8,128)(2,1)S(1)} all-to-all(bf16[8,288,128]{2,1,0:T(8,128)(2,1)S(1)} %get-tuple-element.43), channel_id=1, replica_groups=mesh['z'=8,'yl'=2,'core'=2,'x'=4,'yh'=2] {'x','yh'}, dimensions={0} | all-to-all | bytes 1179648 | tf_op jit(solution)/shard_map/all_to_all | solution.py:224
  106.4 0.9 shard_map.124
  107.3 17.6 %all_to_all.34.got = bf16[8,272,128]{2,1,0:T(8,128)(2,1)S(1)} all-to-all(bf16[8,272,128]{2,1,0:T(8,128)(2,1)S(1)} %shard_map.124), channel_id=1, replica_groups=mesh['z'=8,'yl'=2,'core'=2,'x'=4,'yh'=2] {'z'}, dimensions={0} | all-to-all | bytes 1114112 | tf_op jit(solution)/shard_map/all_to_all | solution.py:224
  125.8 3.9 %collective-permute-start.8 = (f32[128,128]{1,0:T(8,128)S(1)}, f32[128,128]{1,0:T(8,128)S(1)}, u32[]{:S(2)}, u32[]{:S(2)}) collective-permute-start(f32[128,128]{1,0:T(8,128)S(1)} %get-tuple-element.45), channel_id=1, source_target_pairs={{0,8},{8,0},{1,9},{9,1},{2,10},{10,2},{3,11},{11,3},{4,12},{12,4},... | collective-permute-start | bytes 196616 | tf_op jit(solution)/shard_map/ppermute | solution.py:228
  129.6 0.9 collective-permute-done.8
  (28 shorter events, 7.8 us)
Async XLA Ops:
  2.2 19.4 %all-to-all-start = ((bf16[8,128,128]{2,1,0:T(8,128)(2,1)}), bf16[8,128,128]{2,1,0:T(8,128)(2,1)S(1)}, u32[]{:S(2)}, u32[]{:S(2)}) async-start(bf16[8,128,128]{2,1,0:T(8,128)(2,1)} %get-tuple-element.26), calls=%async_computation | async-start | bytes 524288 | tf_op jit(solution)/shard_map/all_to_all | solution.py:224
  39.3 5.1 %collective-permute-start = (bf16[8,128,128]{2,1,0:T(8,128)(2,1)S(1)}, bf16[8,128,128]{2,1,0:T(8,128)(2,1)S(1)}, u32[]{:S(2)}, u32[]{:S(2)}) collective-permute-start(bf16[8,128,128]{2,1,0:T(8,128)(2,1)S(1)} %shard_map.114), channel_id=1, source_target_pairs={{0,8},{8,0},{1,9},{9,1},{2,10},{10,2},{3,11},{11,3},{4,12},{12,4},... | collective-permute-start | bytes 786440 | tf_op jit(solution)/shard_map/ppermute | solution.py:228
  43.3 7.9 %collective-permute-start.1 = (bf16[8,128,128]{2,1,0:T(8,128)(2,1)S(1)}, bf16[8,128,128]{2,1,0:T(8,128)(2,1)S(1)}, u32[]{:S(2)}, u32[]{:S(2)}) collective-permute-start(bf16[8,128,128]{2,1,0:T(8,128)(2,1)S(1)} %shard_map.113), channel_id=1, source_target_pairs={{0,16},{16,0},{1,17},{17,1},{2,18},{18,2},{3,19},{19,3},{4,20},{20... | collective-permute-start | bytes 786440 | tf_op jit(solution)/shard_map/ppermute | solution.py:228
  51.1 2.3 %collective-permute-start.2 = (bf16[8,128,128]{2,1,0:T(8,128)(2,1)S(1)}, bf16[8,128,128]{2,1,0:T(8,128)(2,1)S(1)}, u32[]{:S(2)}, u32[]{:S(2)}) collective-permute-start(bf16[8,128,128]{2,1,0:T(8,128)(2,1)S(1)} %collective-permute-done.1.far), channel_id=1, source_target_pairs={{0,8},{8,0},{1,9},{9,1},{2,10},{10,2},{3,11},{11,3},{4,12},{12,4},... | collective-permute-start | bytes 786440 | tf_op jit(solution)/shard_map/ppermute | solution.py:228
  52.0 13.2 %copy-start = (bf16[128,256]{1,0:T(8,128)(2,1)S(1)}, bf16[128,256]{1,0:T(8,128)(2,1)}, u32[]{:S(2)}) copy-start(bf16[128,256]{1,0:T(8,128)(2,1)} %weight.1) | copy-start | bytes 196612
  52.0 13.2 %copy-start.1 = (bf16[128,256]{1,0:T(8,128)(2,1)S(1)}, bf16[128,256]{1,0:T(8,128)(2,1)}, u32[]{:S(2)}) copy-start(bf16[128,256]{1,0:T(8,128)(2,1)} %cot.1) | copy-start | bytes 196612
  52.0 13.2 %copy-start.2 = (f32[256]{0:T(256)S(1)}, f32[256]{0:T(256)}, u32[]{:S(2)}) copy-start(f32[256]{0:T(256)} %param.14) | copy-start | bytes 3076
  79.2 4.7 %collective-permute-start.3 = (bf16[8,128,128]{2,1,0:T(8,128)(2,1)S(1)}, bf16[8,128,128]{2,1,0:T(8,128)(2,1)S(1)}, u32[]{:S(2)}, u32[]{:S(2)}) collective-permute-start(bf16[8,128,128]{2,1,0:T(8,128)(2,1)S(1)} %get-tuple-element.36), channel_id=1, source_target_pairs={{0,8},{8,0},{1,9},{9,1},{2,10},{10,2},{3,11},{11,3},{4,12},{12,4},... | collective-permute-start | bytes 786440 | tf_op jit(solution)/shard_map/ppermute | solution.py:228
  81.9 2.0 %collective-permute-start.4 = (bf16[48,128]{1,0:T(8,128)(2,1)S(1)}, bf16[48,128]{1,0:T(8,128)(2,1)S(1)}, u32[]{:S(2)}, u32[]{:S(2)}) collective-permute-start(bf16[48,128]{1,0:T(8,128)(2,1)S(1)} %get-tuple-element.37.grads), channel_id=1, source_target_pairs={{0,8},{8,0},{1,9},{9,1},{2,10},{10,2},{3,11},{11,3},{4,12},{12,4},... | collective-permute-start | bytes 36872 | tf_op jit(solution)/shard_map/ppermute | solution.py:228
  82.0 3.6 %collective-permute-start.5 = (bf16[8,128,128]{2,1,0:T(8,128)(2,1)S(1)}, bf16[8,128,128]{2,1,0:T(8,128)(2,1)S(1)}, u32[]{:S(2)}, u32[]{:S(2)}) collective-permute-start(bf16[8,128,128]{2,1,0:T(8,128)(2,1)S(1)} %get-tuple-element.40), channel_id=1, source_target_pairs={{0,8},{8,0},{1,9},{9,1},{2,10},{10,2},{3,11},{11,3},{4,12},{12,4},... | collective-permute-start | bytes 786440 | tf_op jit(solution)/shard_map/ppermute | solution.py:228
  84.0 8.2 %collective-permute-start.6 = (bf16[8,128,128]{2,1,0:T(8,128)(2,1)S(1)}, bf16[8,128,128]{2,1,0:T(8,128)(2,1)S(1)}, u32[]{:S(2)}, u32[]{:S(2)}) collective-permute-start(bf16[8,128,128]{2,1,0:T(8,128)(2,1)S(1)} %get-tuple-element.41), channel_id=1, source_target_pairs={{0,16},{16,0},{1,17},{17,1},{2,18},{18,2},{3,19},{19,3},{4,20},{20... | collective-permute-start | bytes 786440 | tf_op jit(solution)/shard_map/ppermute | solution.py:228
  84.5 7.7 %collective-permute-start.7 = (bf16[48,128]{1,0:T(8,128)(2,1)S(1)}, bf16[48,128]{1,0:T(8,128)(2,1)S(1)}, u32[]{:S(2)}, u32[]{:S(2)}) collective-permute-start(bf16[48,128]{1,0:T(8,128)(2,1)S(1)} %get-tuple-element.42.grads), channel_id=1, source_target_pairs={{0,16},{16,0},{1,17},{17,1},{2,18},{18,2},{3,19},{19,3},{4,20},{20... | collective-permute-start | bytes 36872 | tf_op jit(solution)/shard_map/ppermute | solution.py:228
  125.8 4.8 %collective-permute-start.8 = (f32[128,128]{1,0:T(8,128)S(1)}, f32[128,128]{1,0:T(8,128)S(1)}, u32[]{:S(2)}, u32[]{:S(2)}) collective-permute-start(f32[128,128]{1,0:T(8,128)S(1)} %get-tuple-element.45), channel_id=1, source_target_pairs={{0,8},{8,0},{1,9},{9,1},{2,10},{10,2},{3,11},{11,3},{4,12},{12,4},... | collective-permute-start | bytes 196616 | tf_op jit(solution)/shard_map/ppermute | solution.py:228

commit v3 on v2

v3 whole, which is shorter than its diff:
```python
import functools

import jax
import jax.numpy as jnp
from jax import lax
from jax.experimental import pallas as pl
from jax.experimental.pallas import tpu as pltpu
from jax.sharding import Mesh
from jax.sharding import PartitionSpec as P

Z, YL, CORE, X, YH = 8, 2, 2, 4, 2
BLK = ("z", "yl", "core")
REP = ("x", "yh")
T = 128
ROWS = 8
STEPS = 4
SLOTS = 6
HALF = ROWS // 2
GRAD = 48
F32 = jnp.float32
BF16 = jnp.bfloat16

VMEM = pl.BlockSpec(memory_space=pltpu.VMEM)
SMEM = pl.BlockSpec(memory_space=pltpu.SMEM)
HBM = pl.BlockSpec(memory_space=pltpu.HBM)
PARAMS = pltpu.CompilerParams(vmem_limit_bytes=32 * 1024 * 1024)


def bias_rows(total):
    high = total.astype(BF16)
    low = (total - high.astype(F32)).astype(BF16)
    return jnp.concatenate([high, low, jnp.zeros((12, T), BF16)], axis=0)


def prologue_kernel(rep, features, degrees, low, high, scale):
    rows = jnp.concatenate([degrees[...].astype(F32), jnp.ones((T - ROWS, T), F32)], axis=0)
    columns = lax.rsqrt(rows.T)
    for j in range(ROWS):
        inv_root = jnp.broadcast_to(columns[:, j : j + 1], (T, T))
        tile = (features[j * T : (j + 1) * T].astype(F32) * inv_root).astype(BF16)
        half = low if j < HALF else high
        half[j % HALF] = tile

        @pl.when(rep[0] == j)
        def _():
            scale[...] = inv_root


def tile_of(low, high):
    def tile_at(col):
        at = lax.rem(col, HALF)
        return jnp.where(col < HALF, low[at], high[at])

    return tile_at


def product(meta, edges, i, s, tile_at):
    picked = []
    for c in range(SLOTS):
        tile = tile_at(meta[c, s, i])
        picked.append(jnp.where(c < meta[6, s, i], tile, jnp.zeros_like(tile)))
    left = jnp.concatenate([edges[i, s, c] for c in range(SLOTS)], axis=1)
    return jnp.dot(left, jnp.concatenate(picked, axis=0), preferred_element_type=F32)


def first_kernel(meta, edges, low, high, held, out, sems):
    copies = [pltpu.make_async_copy(edges.at[i], held.at[i], sems.at[i]) for i in range(ROWS)]
    for copy in copies:
        copy.start()
    for i in range(ROWS):
        copies[i].wait()
        out[i] = product(meta, held, i, 0, tile_of(low, high))


def second_kernel(meta, held, far_low, far_high, near_low, near_high, total, out):
    step = 3 - 2 * meta[7, 0, 0]
    for i in range(ROWS):
        out[i] = (
            total[i]
            + product(meta, held, i, 2, tile_of(far_low, far_high))
            + product(meta, held, i, step, tile_of(near_low, near_high))
        )


def third_kernel(meta, held, low, high, total, out):
    step = 1 + 2 * meta[7, 0, 0]
    for i in range(ROWS):
        out[i] = (total[i] + product(meta, held, i, step, tile_of(low, high))).astype(BF16)


def dense_kernel(parts, scale, weight, bias, cot, act, send):
    total = parts[0].astype(F32)
    for j in range(1, ROWS):
        total += parts[j].astype(F32)
    agg = (scale[...] * total).astype(BF16)
    pre = jnp.dot(agg, weight[...], preferred_element_type=F32) + bias[...]
    sigma = jax.nn.sigmoid(pre)
    act[...] = (pre * sigma).astype(BF16)
    grad_pre = cot[...].astype(F32) * sigma * (1.0 + pre * (1.0 - sigma))
    half = grad_pre.astype(BF16)
    grad_w = lax.dot_general(agg, half, (((0,), (0,)), ((), ())), preferred_element_type=F32)
    grad_b = jnp.sum(grad_pre, axis=0, keepdims=True)
    grad_b = jnp.concatenate([grad_b[:, :T], grad_b[:, T:]], axis=0)
    back = lax.dot_general(
        half, weight[...], (((1,), (1,)), ((), ())), preferred_element_type=F32
    )
    back = (scale[...] * back).astype(BF16)
    rows_b = bias_rows(grad_b)
    grad_w = grad_w.astype(BF16)
    for j in range(ROWS):
        send[j, 0:T] = back
        send[j, T : T + 16] = grad_w[16 * j : 16 * j + 16, :T]
        send[j, T + 16 : T + 32] = grad_w[16 * j : 16 * j + 16, T:]
        send[j, T + 32 : T + 48] = rows_b


def column_sums(meta, held, got, s, sums):
    sums[...] = jnp.zeros_like(sums)
    for i in range(ROWS):
        back = got[i, 0:T].T
        right = jnp.concatenate([held[i, s, c] for c in range(SLOTS)], axis=1)
        prod = jnp.dot(back, right, preferred_element_type=F32)
        for c in range(SLOTS):
            part = prod[:, c * T : (c + 1) * T]
            at = meta[c, s, i]
            sums[at] += jnp.where(c < meta[6, s, i], part, jnp.zeros_like(part))


def near_sums_kernel(meta, held, got, near0, near1, grads, sums):
    total = got[0, T:].astype(F32)
    for j in range(1, ROWS):
        total += got[j, T:].astype(F32)
    grads[0:32] = total[0:32]
    grads[32:40] = jnp.concatenate(
        [total[32:34] + total[34:36], jnp.zeros((6, T), F32)], axis=0
    )
    column_sums(meta, held, got, 1 + 2 * meta[7, 0, 0], sums)
    near1[...] = sums[...].astype(BF16)
    column_sums(meta, held, got, 3 - 2 * meta[7, 0, 0], sums)
    near0[...] = sums[...].astype(BF16)


def far_sums_kernel(meta, held, got, far, sums):
    column_sums(meta, held, got, 2, sums)
    far[...] = sums[...].astype(BF16)


def own_sums_kernel(meta, held, got, out, sums):
    column_sums(meta, held, got, 0, sums)
    out[...] = sums[...]


def near_kernel(far, near, low, high):
    low[...] = (far[0:HALF].astype(F32) + near[0:HALF].astype(F32)).astype(BF16)
    high[...] = (far[HALF:].astype(F32) + near[HALF:].astype(F32)).astype(BF16)


def half_kernel(first, own, near, far, out):
    rows = pl.ds(first, HALF)
    total = own[rows] + near[rows].astype(F32) + far[...].astype(F32)
    out[...] = total.astype(BF16)


def gather_kernel(low, high, grads, out):
    mine = grads[0:32].astype(BF16)
    for j in range(ROWS):
        out[j, 0:T] = low[j] if j < HALF else high[j - HALF]
        out[j, T:] = mine


def last_kernel(got, scale, grads, grad_features, grad_weight, grad_bias):
    total = got[0, 0:T].astype(F32)
    for j in range(1, ROWS):
        total += got[j, 0:T].astype(F32)
    grad_features[...] = scale[...] * total.T
    for j in range(ROWS):
        rows = slice(16 * j, 16 * j + 16)
        grad_weight[rows, :T] = got[j, T : T + 16].astype(F32)
        grad_weight[rows, T:] = got[j, T + 16 :].astype(F32)
    grad_bias[...] = jnp.concatenate([grads[32:33], grads[33:34]], axis=1)


def call(kernel, out, in_specs, scratch=(), flops=0, moved=1 << 20):
    return pl.pallas_call(
        kernel,
        out_shape=[jax.ShapeDtypeStruct(*o) for o in out],
        in_specs=in_specs,
        out_specs=[VMEM] * len(out),
        scratch_shapes=list(scratch),
        cost_estimate=pl.CostEstimate(flops=flops, bytes_accessed=moved, transcendentals=0),
        compiler_params=PARAMS,
    )


def pinned(value):
    return pltpu.with_memory_space_constraint(value, pltpu.HBM)


def exchange(value, axes):
    return lax.all_to_all(value, axes, 0, 0, tiled=True)


def move(value, to):
    blk, rep = Z * YL * CORE, X * YH
    pairs = []
    for b in range(blk):
        for r in range(rep):
            to_b, to_r = to(b, r)
            pairs.append((b * rep + r, to_b % blk * rep + to_r))
    return lax.ppermute(value, BLK + REP, pairs)


def swap(value, bit):
    return move(value, lambda b, r: (b ^ bit, r))


def on_device(features, degrees, cols, counts, edges, weight, bias, cot):
    z, yl, core = (lax.axis_index(a) for a in BLK)
    rep = lax.axis_index(REP)
    place = lax.broadcasted_iota(jnp.int32, (1, STEPS, ROWS), 2)
    place = jnp.where(place == 0, core, 0)
    meta = jnp.concatenate([cols.transpose(2, 1, 0), counts.T[None], place], axis=0)

    tiles, half = (ROWS, T, T), (HALF, T, T)
    low, high, scale = call(
        prologue_kernel,
        [(half, BF16), (half, BF16), ((T, T), F32)],
        [SMEM, VMEM, VMEM],
    )(rep.astype(jnp.int32)[None], pinned(features), pinned(degrees.reshape(ROWS, T)))

    low = move(low, lambda b, r: (b + 4 * r, r))
    high = move(high, lambda b, r: (b + 4 * (r ^ 2), r ^ 2))
    far_low, far_high = (move(v, lambda b, r: (b + 2, r)) for v in (low, high))
    near_low, near_high = (move(v, lambda b, r: (b + 1 + 2 * (b % 2), r)) for v in (low, high))

    work = 2 * ROWS * SLOTS * T * T * T
    held, total = call(
        first_kernel,
        [(edges.shape, BF16), (tiles, F32)],
        [SMEM, HBM, VMEM, VMEM],
        [pltpu.SemaphoreType.DMA((ROWS,))],
        work,
        8 << 20,
    )(meta, pinned(edges), low, high)
    far_low, far_high, total = lax.optimization_barrier((far_low, far_high, total))
    last_low, last_high = swap(far_low, 1), swap(far_high, 1)
    (total,) = call(second_kernel, [(tiles, F32)], [SMEM] + [VMEM] * 6, (), 2 * work, 6 << 20)(
        meta, held, far_low, far_high, near_low, near_high, total
    )
    (parts,) = call(third_kernel, [(tiles, BF16)], [SMEM] + [VMEM] * 4, (), work, 3 << 20)(
        meta, held, last_low, last_high, total
    )
    parts = exchange(parts, REP)

    act, send = call(
        dense_kernel,
        [(cot.shape, BF16), ((ROWS, T + GRAD, T), BF16)],
        [VMEM] * 5,
    )(parts, scale, weight, bias[None], cot)
    got = exchange(send, REP)

    sums = [pltpu.VMEM(tiles, F32)]
    near, last, grads = call(
        near_sums_kernel,
        [(tiles, BF16), (tiles, BF16), ((40, T), F32)],
        [SMEM, VMEM, VMEM],
        sums,
        2 * work,
        6 << 20,
    )(meta, held, got)
    last = swap(last, 1)
    near = move(near, lambda b, r: (b - 3 + 2 * (b % 2), r))
    (far,) = call(far_sums_kernel, [(tiles, BF16)], [SMEM, VMEM, VMEM], sums, work, 3 << 20)(
        meta, held, got
    )
    far_low, far_high = call(near_kernel, [(half, BF16), (half, BF16)], [VMEM] * 2)(far, last)
    far_low, far_high, got, grads = lax.optimization_barrier((far_low, far_high, got, grads))
    far_low, far_high = (move(v, lambda b, r: (b - 2, r)) for v in (far_low, far_high))
    (own,) = call(own_sums_kernel, [(tiles, F32)], [SMEM] + [VMEM] * 2, sums, work, 3 << 20)(
        meta, held, got
    )
    grads = grads + swap(grads, 16)
    own, grads = lax.optimization_barrier((own, grads))
    low, high = (
        call(functools.partial(half_kernel, first), [(half, BF16)], [VMEM] * 3)(own, near, far)[0]
        for first, far in ((0, far_low), (HALF, far_high))
    )
    low = move(low, lambda b, r: (b - 4 * r, r))
    high = move(high, lambda b, r: (b - 4 * r, r ^ 2))
    for bit in (8, 4, 2, 1):
        grads = grads + swap(grads, bit)
    (send,) = call(gather_kernel, [((ROWS, T + 32, T), BF16)], [VMEM] * 3)(low, high, grads)
    got = exchange(send, REP)
    grad_features, grad_weight, grad_bias = call(
        last_kernel,
        [((T, T), F32), ((T, 2 * T), F32), ((1, 2 * T), F32)],
        [VMEM] * 3,
    )(got, scale, grads)
    return act, grad_weight, grad_bias[0], grad_features


def solution(mesh):
    fine = Mesh(mesh.devices.reshape(Z, YL, CORE, X, YH), BLK + REP)
    return jax.shard_map(
        on_device,
        mesh=fine,
        in_specs=(
            P(BLK, None),
            P(BLK),
            P(BLK, REP, None),
            P(BLK, REP),
            P(BLK, REP, None, None, None),
            P(),
            P(),
            P(BLK + REP, None),
        ),
        out_specs=(P(BLK + REP, None), P(), P(), P(BLK + REP, None)),
        check_vma=False,
    )
```

time: 132 us -> 123 us (0.932)
  the two profiles are of different devices: /device:TPU:1 before, /device:TPU:32 now
where the time goes in v3:
time: 123 us; the launch traced here: 122 us
  blocking collectives  53.6 us (44%)
  starting transfers between devices  27.6 us (22%)
  waiting for transfers between devices  23.5 us (19%)
  Pallas kernels  16.1 us (13%)
    all_to_all x3, blocking collectives, exchange(): return lax.all_to_all(value, axes, 0, 0, tiled=True)  53.6 us
    ppermute x19, starting transfers between devices, move(): return lax.ppermute(value, BLK + REP, pairs)  27.6 us
    ppermute x19, waiting for transfers between devices, move(): return lax.ppermute(value, BLK + REP, pairs)  23.5 us
    pallas_call x1, Pallas kernels, on_device(): call(first_kernel, [(edges.shape, BF16), (tiles, F32)], [SMEM, HBM, VMEM,...  3.9 us
  transfers between devices with their start and end apart: 19, of which 7 were waited for; matrix products, arithmetic and copies ran while one was open for 1% of the time, Pallas kernels for 8%

profile of v3, /device:TPU:32, one launch (start us, length us, event | category | flops | bytes accessed | tf_op | source)
XLA Modules:
  0.0 122.4 jit_solution(13867631840544394462)
XLA Ops:
  0.6 1.7 %shard_map.111 = (bf16[4,128,128]{2,1,0:T(8,128)(2,1)S(1)}, bf16[4,128,128]{2,1,0:T(8,128)(2,1)S(1)}, f32[128,128]{1,0:T(8,128)S(1)}) custom-call(s32[1]{0:T(128)} %bitcast.3.rep, bf16[1024,128]{1,0:T(8,128)(2,1)} %features.1, s32[8,128]{1,0:T(8,128)} %bitcast.10), custom_call_target="tpu_custom_call" | custom-call | bytes 1048576 | tf_op jit(solution)/shard_map/pallas_call | solution.py:225
  3.0 9.1 %collective-permute-start.1 = (bf16[4,128,128]{2,1,0:T(8,128)(2,1)S(1)}, bf16[4,128,128]{2,1,0:T(8,128)(2,1)S(1)}, u32[]{:S(2)}, u32[]{:S(2)}) collective-permute-start(bf16[4,128,128]{2,1,0:T(8,128)(2,1)S(1)} %get-tuple-element.29), channel_id=1, source_target_pairs={{0,66},{1,99},{2,0},{3,33},{4,198},{5,231},{6,132},{7,165},{8,74},... | collective-permute-start | bytes 393224 | tf_op jit(solution)/shard_map/ppermute | solution.py:210
  12.2 1.7 %collective-permute-start.2 = (bf16[4,128,128]{2,1,0:T(8,128)(2,1)S(1)}, bf16[4,128,128]{2,1,0:T(8,128)(2,1)S(1)}, u32[]{:S(2)}, u32[]{:S(2)}) collective-permute-start(bf16[4,128,128]{2,1,0:T(8,128)(2,1)S(1)} %collective-permute-done.low), channel_id=1, source_target_pairs={{0,16},{1,17},{2,18},{3,19},{4,20},{5,21},{6,22},{7,23},{8,24},{9,... | collective-permute-start | bytes 393224 | tf_op jit(solution)/shard_map/ppermute | solution.py:210
  13.8 3.8 %collective-permute-done.1.high = bf16[4,128,128]{2,1,0:T(8,128)(2,1)S(1)} collective-permute-done((bf16[4,128,128]{2,1,0:T(8,128)(2,1)S(1)}, bf16[4,128,128]{2,1,0:T(8,128)(2,1)S(1)}, u32[]{:S(2)}, u32[]{:S(2)}) %collective-permute-start.1) | collective-permute-done | bytes 131104 | tf_op jit(solution)/shard_map/ppermute | solution.py:210
  17.6 1.6 %collective-permute-start.3 = (bf16[4,128,128]{2,1,0:T(8,128)(2,1)S(1)}, bf16[4,128,128]{2,1,0:T(8,128)(2,1)S(1)}, u32[]{:S(2)}, u32[]{:S(2)}) collective-permute-start(bf16[4,128,128]{2,1,0:T(8,128)(2,1)S(1)} %collective-permute-done.1.high), channel_id=1, source_target_pairs={{0,16},{1,17},{2,18},{3,19},{4,20},{5,21},{6,22},{7,23},{8,24},{9,... | collective-permute-start | bytes 393224 | tf_op jit(solution)/shard_map/ppermute | solution.py:210
  19.9 3.9 %shard_map.112 = (bf16[8,4,6,128,128]{4,3,2,1,0:T(8,128)(2,1)S(1)}, f32[8,128,128]{2,1,0:T(8,128)S(1)}) custom-call(s32[8,4,8]{2,1,0:T(4,128)S(1)} %pad_add_fusion.meta, bf16[8,4,6,128,128]{4,3,2,1,0:T(8,128)(2,1)} %edges.1, bf16[4,128,128]{2,1,0:T(8,128)(2,1)S(1)} %collective-permute-done.low, bf16[4,128,128]{2,1,0:T(8,128)(2,1)S(1)} %collective-permute-done.1.high), custom_call_target="tpu_custom_call" | custom-call | flops 201326592 | bytes 8388608 | tf_op jit(solution)/shard_map/pallas_call | solution.py:237
  23.9 2.6 %collective-permute-done.3.far_high = bf16[4,128,128]{2,1,0:T(8,128)(2,1)S(1)} collective-permute-done((bf16[4,128,128]{2,1,0:T(8,128)(2,1)S(1)}, bf16[4,128,128]{2,1,0:T(8,128)(2,1)S(1)}, u32[]{:S(2)}, u32[]{:S(2)}) %collective-permute-start.3) | collective-permute-done | bytes 131104 | tf_op jit(solution)/shard_map/ppermute | solution.py:210
  26.4 1.7 %collective-permute-start.4 = (bf16[4,128,128]{2,1,0:T(8,128)(2,1)S(1)}, bf16[4,128,128]{2,1,0:T(8,128)(2,1)S(1)}, u32[]{:S(2)}, u32[]{:S(2)}) collective-permute-start(bf16[4,128,128]{2,1,0:T(8,128)(2,1)S(1)} %collective-permute-done.2.far_low), channel_id=1, source_target_pairs={{0,8},{1,9},{2,10},{3,11},{4,12},{5,13},{6,14},{7,15},{8,0},{9,1},... | collective-permute-start | bytes 393224 | tf_op jit(solution)/shard_map/ppermute | solution.py:210
  28.2 2.2 %shard_map.113.total = f32[8,128,128]{2,1,0:T(8,128)S(1)} custom-call(s32[8,4,8]{2,1,0:T(4,128)S(1)} %pad_add_fusion.meta, bf16[8,4,6,128,128]{4,3,2,1,0:T(8,128)(2,1)S(1)} %get-tuple-element.30.held, bf16[4,128,128]{2,1,0:T(8,128)(2,1)S(1)} %collective-permute-done.2.far_low, bf16[4,128,128]{2,1,0:T(8,128)(2,1)S(1)} %collective-permute-done.3.far_high, ...), custom_call_target="tpu_custom_call" | custom-call | flops 402653184 | bytes 6291456 | tf_op jit(solution)/shard_map/pallas_call | solution.py:247
  30.4 1.5 %shard_map.114 = bf16[8,128,128]{2,1,0:T(8,128)(2,1)S(1)} custom-call(s32[8,4,8]{2,1,0:T(4,128)S(1)} %pad_add_fusion.meta, bf16[8,4,6,128,128]{4,3,2,1,0:T(8,128)(2,1)S(1)} %get-tuple-element.30.held, bf16[4,128,128]{2,1,0:T(8,128)(2,1)S(1)} %collective-permute-done.4.low, bf16[4,128,128]{2,1,0:T(8,128)(2,1)S(1)} %collective-permute-done.5.high, ...), custom_call_target="tpu_custom_call" | custom-call | flops 201326592 | bytes 3145728 | tf_op jit(solution)/shard_map/pallas_call | solution.py:250
  31.9 19.7 %all_to_all.15.parts = bf16[8,128,128]{2,1,0:T(8,128)(2,1)S(1)} all-to-all(bf16[8,128,128]{2,1,0:T(8,128)(2,1)S(1)} %shard_map.114), channel_id=1, replica_groups=mesh['z'=8,'yl'=2,'core'=2,'x'=4,'yh'=2] {'x','yh'}, dimensions={0} | all-to-all | bytes 524288 | tf_op jit(solution)/shard_map/all_to_all | solution.py:200
  52.4 12.2 %all_to_all.16.got = bf16[8,176,128]{2,1,0:T(8,128)(2,1)S(1)} all-to-all(bf16[8,176,128]{2,1,0:T(8,128)(2,1)S(1)} %get-tuple-element.37), channel_id=1, replica_groups=mesh['z'=8,'yl'=2,'core'=2,'x'=4,'yh'=2] {'x','yh'}, dimensions={0} | all-to-all | bytes 720896 | tf_op jit(solution)/shard_map/all_to_all | solution.py:200
  64.6 2.0 %shard_map.117 = (bf16[8,128,128]{2,1,0:T(8,128)(2,1)S(1)}, bf16[8,128,128]{2,1,0:T(8,128)(2,1)S(1)}, f32[40,128]{1,0:T(8,128)S(1)}) custom-call(s32[8,4,8]{2,1,0:T(4,128)S(1)} %pad_add_fusion.meta, bf16[8,4,6,128,128]{4,3,2,1,0:T(8,128)(2,1)S(1)} %get-tuple-element.30.held, bf16[8,176,128]{2,1,0:T(8,128)(2,1)S(1)} %all_to_all.16.got), custom_call_target="tpu_custom_call" | custom-call | flops 402653184 | bytes 6291456 | tf_op jit(solution)/shard_map/pallas_call | solution.py:263
  66.7 1.4 %collective-permute-start.10 = (bf16[8,128,128]{2,1,0:T(8,128)(2,1)S(1)}, bf16[8,128,128]{2,1,0:T(8,128)(2,1)S(1)}, u32[]{:S(2)}, u32[]{:S(2)}) collective-permute-start(bf16[8,128,128]{2,1,0:T(8,128)(2,1)S(1)} %get-tuple-element.45), channel_id=1, source_target_pairs={{0,232},{1,233},{2,234},{3,235},{4,236},{5,237},{6,238},{7,239},{8... | collective-permute-start | bytes 786440 | tf_op jit(solution)/shard_map/ppermute | solution.py:210
  68.1 1.5 %shard_map.116.far = bf16[8,128,128]{2,1,0:T(8,128)(2,1)S(1)} custom-call(s32[8,4,8]{2,1,0:T(4,128)S(1)} %pad_add_fusion.meta, bf16[8,4,6,128,128]{4,3,2,1,0:T(8,128)(2,1)S(1)} %get-tuple-element.30.held, bf16[8,176,128]{2,1,0:T(8,128)(2,1)S(1)} %all_to_all.16.got), custom_call_target="tpu_custom_call" | custom-call | flops 201326592 | bytes 3145728 | tf_op jit(solution)/shard_map/pallas_call | solution.py:273
  72.2 3.0 %collective-permute-start.9 = (f32[40,128]{1,0:T(8,128)S(1)}, f32[40,128]{1,0:T(8,128)S(1)}, u32[]{:S(2)}, u32[]{:S(2)}) collective-permute-start(f32[40,128]{1,0:T(8,128)S(1)} %get-tuple-element.43), channel_id=1, source_target_pairs={{0,128},{1,129},{2,130},{3,131},{4,132},{5,133},{6,134},{7,135},{8... | collective-permute-start | bytes 61448 | tf_op jit(solution)/shard_map/ppermute | solution.py:210
  75.2 1.5 %shard_map.119.own = f32[8,128,128]{2,1,0:T(8,128)S(1)} custom-call(s32[8,4,8]{2,1,0:T(4,128)S(1)} %pad_add_fusion.meta, bf16[8,4,6,128,128]{4,3,2,1,0:T(8,128)(2,1)S(1)} %get-tuple-element.30.held, bf16[8,176,128]{2,1,0:T(8,128)(2,1)S(1)} %all_to_all.16.got), custom_call_target="tpu_custom_call" | custom-call | flops 201326592 | bytes 3145728 | tf_op jit(solution)/shard_map/pallas_call | solution.py:279
  76.7 6.3 %collective-permute-done.9 = f32[40,128]{1,0:T(8,128)S(1)} collective-permute-done((f32[40,128]{1,0:T(8,128)S(1)}, f32[40,128]{1,0:T(8,128)S(1)}, u32[]{:S(2)}, u32[]{:S(2)}) %collective-permute-start.9) | collective-permute-done | bytes 20512 | tf_op jit(solution)/shard_map/ppermute | solution.py:210
  83.8 2.6 %collective-permute-start.14 = (bf16[4,128,128]{2,1,0:T(8,128)(2,1)S(1)}, bf16[4,128,128]{2,1,0:T(8,128)(2,1)S(1)}, u32[]{:S(2)}, u32[]{:S(2)}) collective-permute-start(bf16[4,128,128]{2,1,0:T(8,128)(2,1)S(1)} %shard_map.121), channel_id=1, source_target_pairs={{0,2},{1,227},{2,192},{3,161},{4,134},{5,103},{6,68},{7,37},{8,10}... | collective-permute-start | bytes 393224 | tf_op jit(solution)/shard_map/ppermute | solution.py:210
  86.4 2.2 %collective-permute-start.15 = (f32[40,128]{1,0:T(8,128)S(1)}, f32[40,128]{1,0:T(8,128)S(1)}, u32[]{:S(2)}, u32[]{:S(2)}) collective-permute-start(f32[40,128]{1,0:T(8,128)S(1)} %add.19), channel_id=1, source_target_pairs={{0,64},{1,65},{2,66},{3,67},{4,68},{5,69},{6,70},{7,71},{8,72},{9,... | collective-permute-start | bytes 61448 | tf_op jit(solution)/shard_map/ppermute | solution.py:210
  88.7 2.4 %collective-permute-done.15 = f32[40,128]{1,0:T(8,128)S(1)} collective-permute-done((f32[40,128]{1,0:T(8,128)S(1)}, f32[40,128]{1,0:T(8,128)S(1)}, u32[]{:S(2)}, u32[]{:S(2)}) %collective-permute-start.15) | collective-permute-done | bytes 20512 | tf_op jit(solution)/shard_map/ppermute | solution.py:210
  91.5 3.4 %collective-permute-done.16 = f32[40,128]{1,0:T(8,128)S(1)} collective-permute-done((f32[40,128]{1,0:T(8,128)S(1)}, f32[40,128]{1,0:T(8,128)S(1)}, u32[]{:S(2)}, u32[]{:S(2)}) %collective-permute-start.16) | collective-permute-done | bytes 20512 | tf_op jit(solution)/shard_map/ppermute | solution.py:210
  94.9 3.8 %collective-permute-done.17 = f32[40,128]{1,0:T(8,128)S(1)} collective-permute-done((f32[40,128]{1,0:T(8,128)S(1)}, f32[40,128]{1,0:T(8,128)S(1)}, u32[]{:S(2)}, u32[]{:S(2)}) %collective-permute-start.17) | collective-permute-done | bytes 20512 | tf_op jit(solution)/shard_map/ppermute | solution.py:210
  99.9 21.8 %all_to_all.17.got = bf16[8,160,128]{2,1,0:T(8,128)(2,1)S(1)} all-to-all(bf16[8,160,128]{2,1,0:T(8,128)(2,1)S(1)} %shard_map.122), channel_id=1, replica_groups=mesh['z'=8,'yl'=2,'core'=2,'x'=4,'yh'=2] {'x','yh'}, dimensions={0} | all-to-all | bytes 655360 | tf_op jit(solution)/shard_map/all_to_all | solution.py:200
  (44 shorter events, 8.1 us)
Async XLA Ops:
  2.4 9.8 %collective-permute-start = (bf16[4,128,128]{2,1,0:T(8,128)(2,1)S(1)}, bf16[4,128,128]{2,1,0:T(8,128)(2,1)S(1)}, u32[]{:S(2)}, u32[]{:S(2)}) collective-permute-start(bf16[4,128,128]{2,1,0:T(8,128)(2,1)S(1)} %get-tuple-element.28), channel_id=1, source_target_pairs={{0,0},{1,33},{2,66},{3,99},{4,132},{5,165},{6,198},{7,231},{8,8},{... | collective-permute-start | bytes 393224 | tf_op jit(solution)/shard_map/ppermute | solution.py:210
  3.0 14.6 %collective-permute-start.1 = (bf16[4,128,128]{2,1,0:T(8,128)(2,1)S(1)}, bf16[4,128,128]{2,1,0:T(8,128)(2,1)S(1)}, u32[]{:S(2)}, u32[]{:S(2)}) collective-permute-start(bf16[4,128,128]{2,1,0:T(8,128)(2,1)S(1)} %get-tuple-element.29), channel_id=1, source_target_pairs={{0,66},{1,99},{2,0},{3,33},{4,198},{5,231},{6,132},{7,165},{8,74},... | collective-permute-start | bytes 393224 | tf_op jit(solution)/shard_map/ppermute | solution.py:210
  12.2 16.0 %collective-permute-start.6 = (bf16[4,128,128]{2,1,0:T(8,128)(2,1)S(1)}, bf16[4,128,128]{2,1,0:T(8,128)(2,1)S(1)}, u32[]{:S(2)}, u32[]{:S(2)}) collective-permute-start(bf16[4,128,128]{2,1,0:T(8,128)(2,1)S(1)} %collective-permute-done.low), channel_id=1, source_target_pairs={{0,8},{1,9},{2,10},{3,11},{4,12},{5,13},{6,14},{7,15},{8,32},{9,33... | collective-permute-start | bytes 393224 | tf_op jit(solution)/shard_map/ppermute | solution.py:210
  12.2 11.7 %collective-permute-start.2 = (bf16[4,128,128]{2,1,0:T(8,128)(2,1)S(1)}, bf16[4,128,128]{2,1,0:T(8,128)(2,1)S(1)}, u32[]{:S(2)}, u32[]{:S(2)}) collective-permute-start(bf16[4,128,128]{2,1,0:T(8,128)(2,1)S(1)} %collective-permute-done.low), channel_id=1, source_target_pairs={{0,16},{1,17},{2,18},{3,19},{4,20},{5,21},{6,22},{7,23},{8,24},{9,... | collective-permute-start | bytes 393224 | tf_op jit(solution)/shard_map/ppermute | solution.py:210
  17.6 10.5 %collective-permute-start.7 = (bf16[4,128,128]{2,1,0:T(8,128)(2,1)S(1)}, bf16[4,128,128]{2,1,0:T(8,128)(2,1)S(1)}, u32[]{:S(2)}, u32[]{:S(2)}) collective-permute-start(bf16[4,128,128]{2,1,0:T(8,128)(2,1)S(1)} %collective-permute-done.1.high), channel_id=1, source_target_pairs={{0,8},{1,9},{2,10},{3,11},{4,12},{5,13},{6,14},{7,15},{8,32},{9,33... | collective-permute-start | bytes 393224 | tf_op jit(solution)/shard_map/ppermute | solution.py:210
  17.6 8.8 %collective-permute-start.3 = (bf16[4,128,128]{2,1,0:T(8,128)(2,1)S(1)}, bf16[4,128,128]{2,1,0:T(8,128)(2,1)S(1)}, u32[]{:S(2)}, u32[]{:S(2)}) collective-permute-start(bf16[4,128,128]{2,1,0:T(8,128)(2,1)S(1)} %collective-permute-done.1.high), channel_id=1, source_target_pairs={{0,16},{1,17},{2,18},{3,19},{4,20},{5,21},{6,22},{7,23},{8,24},{9,... | collective-permute-start | bytes 393224 | tf_op jit(solution)/shard_map/ppermute | solution.py:210
  26.4 3.9 %collective-permute-start.4 = (bf16[4,128,128]{2,1,0:T(8,128)(2,1)S(1)}, bf16[4,128,128]{2,1,0:T(8,128)(2,1)S(1)}, u32[]{:S(2)}, u32[]{:S(2)}) collective-permute-start(bf16[4,128,128]{2,1,0:T(8,128)(2,1)S(1)} %collective-permute-done.2.far_low), channel_id=1, source_target_pairs={{0,8},{1,9},{2,10},{3,11},{4,12},{5,13},{6,14},{7,15},{8,0},{9,1},... | collective-permute-start | bytes 393224 | tf_op jit(solution)/shard_map/ppermute | solution.py:210
  28.1 2.3 %collective-permute-start.5 = (bf16[4,128,128]{2,1,0:T(8,128)(2,1)S(1)}, bf16[4,128,128]{2,1,0:T(8,128)(2,1)S(1)}, u32[]{:S(2)}, u32[]{:S(2)}) collective-permute-start(bf16[4,128,128]{2,1,0:T(8,128)(2,1)S(1)} %collective-permute-done.3.far_high), channel_id=1, source_target_pairs={{0,8},{1,9},{2,10},{3,11},{4,12},{5,13},{6,14},{7,15},{8,0},{9,1},... | collective-permute-start | bytes 393224 | tf_op jit(solution)/shard_map/ppermute | solution.py:210
  28.1 23.4 %copy-start = (bf16[128,256]{1,0:T(8,128)(2,1)S(1)}, bf16[128,256]{1,0:T(8,128)(2,1)}, u32[]{:S(2)}) copy-start(bf16[128,256]{1,0:T(8,128)(2,1)} %weight.1) | copy-start | bytes 196612
  28.1 23.4 %copy-start.1 = (bf16[128,256]{1,0:T(8,128)(2,1)S(1)}, bf16[128,256]{1,0:T(8,128)(2,1)}, u32[]{:S(2)}) copy-start(bf16[128,256]{1,0:T(8,128)(2,1)} %cot.1) | copy-start | bytes 196612
  28.1 23.4 %copy-start.2 = (f32[256]{0:T(256)S(1)}, f32[256]{0:T(256)}, u32[]{:S(2)}) copy-start(f32[256]{0:T(256)} %param.14) | copy-start | bytes 3076
  66.6 3.0 %collective-permute-start.8 = (bf16[8,128,128]{2,1,0:T(8,128)(2,1)S(1)}, bf16[8,128,128]{2,1,0:T(8,128)(2,1)S(1)}, u32[]{:S(2)}, u32[]{:S(2)}) collective-permute-start(bf16[8,128,128]{2,1,0:T(8,128)(2,1)S(1)} %get-tuple-element.38), channel_id=1, source_target_pairs={{0,8},{1,9},{2,10},{3,11},{4,12},{5,13},{6,14},{7,15},{8,0},{9,1},... | collective-permute-start | bytes 786440 | tf_op jit(solution)/shard_map/ppermute | solution.py:210
  66.7 16.3 %collective-permute-start.10 = (bf16[8,128,128]{2,1,0:T(8,128)(2,1)S(1)}, bf16[8,128,128]{2,1,0:T(8,128)(2,1)S(1)}, u32[]{:S(2)}, u32[]{:S(2)}) collective-permute-start(bf16[8,128,128]{2,1,0:T(8,128)(2,1)S(1)} %get-tuple-element.45), channel_id=1, source_target_pairs={{0,232},{1,233},{2,234},{3,235},{4,236},{5,237},{6,238},{7,239},{8... | collective-permute-start | bytes 786440 | tf_op jit(solution)/shard_map/ppermute | solution.py:210
  69.7 13.3 %collective-permute-start.11 = (bf16[4,128,128]{2,1,0:T(8,128)(2,1)S(1)}, bf16[4,128,128]{2,1,0:T(8,128)(2,1)S(1)}, u32[]{:S(2)}, u32[]{:S(2)}) collective-permute-start(bf16[4,128,128]{2,1,0:T(8,128)(2,1)S(1)} %get-tuple-element.46), channel_id=1, source_target_pairs={{0,240},{1,241},{2,242},{3,243},{4,244},{5,245},{6,246},{7,247},{8... | collective-permute-start | bytes 393224 | tf_op jit(solution)/shard_map/ppermute | solution.py:210
  70.9 12.9 %collective-permute-start.13 = (bf16[4,128,128]{2,1,0:T(8,128)(2,1)S(1)}, bf16[4,128,128]{2,1,0:T(8,128)(2,1)S(1)}, u32[]{:S(2)}, u32[]{:S(2)}) collective-permute-start(bf16[4,128,128]{2,1,0:T(8,128)(2,1)S(1)} %get-tuple-element.47), channel_id=1, source_target_pairs={{0,240},{1,241},{2,242},{3,243},{4,244},{5,245},{6,246},{7,247},{8... | collective-permute-start | bytes 393224 | tf_op jit(solution)/shard_map/ppermute | solution.py:210
  72.2 10.8 %collective-permute-start.9 = (f32[40,128]{1,0:T(8,128)S(1)}, f32[40,128]{1,0:T(8,128)S(1)}, u32[]{:S(2)}, u32[]{:S(2)}) collective-permute-start(f32[40,128]{1,0:T(8,128)S(1)} %get-tuple-element.43), channel_id=1, source_target_pairs={{0,128},{1,129},{2,130},{3,131},{4,132},{5,133},{6,134},{7,135},{8... | collective-permute-start | bytes 61448 | tf_op jit(solution)/shard_map/ppermute | solution.py:210
  83.0 16.8 %collective-permute-start.12 = (bf16[4,128,128]{2,1,0:T(8,128)(2,1)S(1)}, bf16[4,128,128]{2,1,0:T(8,128)(2,1)S(1)}, u32[]{:S(2)}, u32[]{:S(2)}) collective-permute-start(bf16[4,128,128]{2,1,0:T(8,128)(2,1)S(1)} %shard_map.120), channel_id=1, source_target_pairs={{0,0},{1,225},{2,194},{3,163},{4,132},{5,101},{6,70},{7,39},{8,8},... | collective-permute-start | bytes 393224 | tf_op jit(solution)/shard_map/ppermute | solution.py:210
  83.8 16.1 %collective-permute-start.14 = (bf16[4,128,128]{2,1,0:T(8,128)(2,1)S(1)}, bf16[4,128,128]{2,1,0:T(8,128)(2,1)S(1)}, u32[]{:S(2)}, u32[]{:S(2)}) collective-permute-start(bf16[4,128,128]{2,1,0:T(8,128)(2,1)S(1)} %shard_map.121), channel_id=1, source_target_pairs={{0,2},{1,227},{2,192},{3,161},{4,134},{5,103},{6,68},{7,37},{8,10}... | collective-permute-start | bytes 393224 | tf_op jit(solution)/shard_map/ppermute | solution.py:210
  86.4 4.7 %collective-permute-start.15 = (f32[40,128]{1,0:T(8,128)S(1)}, f32[40,128]{1,0:T(8,128)S(1)}, u32[]{:S(2)}, u32[]{:S(2)}) collective-permute-start(f32[40,128]{1,0:T(8,128)S(1)} %add.19), channel_id=1, source_target_pairs={{0,64},{1,65},{2,66},{3,67},{4,68},{5,69},{6,70},{7,71},{8,72},{9,... | collective-permute-start | bytes 61448 | tf_op jit(solution)/shard_map/ppermute | solution.py:210
  91.1 3.8 %collective-permute-start.16 = (f32[40,128]{1,0:T(8,128)S(1)}, f32[40,128]{1,0:T(8,128)S(1)}, u32[]{:S(2)}, u32[]{:S(2)}) collective-permute-start(f32[40,128]{1,0:T(8,128)S(1)} %add.20), channel_id=1, source_target_pairs={{0,32},{1,33},{2,34},{3,35},{4,36},{5,37},{6,38},{7,39},{8,40},{9,... | collective-permute-start | bytes 61448 | tf_op jit(solution)/shard_map/ppermute | solution.py:210
  94.9 3.8 %collective-permute-start.17 = (f32[40,128]{1,0:T(8,128)S(1)}, f32[40,128]{1,0:T(8,128)S(1)}, u32[]{:S(2)}, u32[]{:S(2)}) collective-permute-start(f32[40,128]{1,0:T(8,128)S(1)} %add.21), channel_id=1, source_target_pairs={{0,16},{1,17},{2,18},{3,19},{4,20},{5,21},{6,22},{7,23},{8,24},{9,... | collective-permute-start | bytes 61448 | tf_op jit(solution)/shard_map/ppermute | solution.py:210
  98.7 1.2 collective-permute-start.18

commit v4 on v3

--- a/solution.py
+++ b/solution.py
@@ -63,29 +63,30 @@
     return jnp.dot(left, jnp.concatenate(picked, axis=0), preferred_element_type=F32)
 
 
-def first_kernel(meta, edges, low, high, held, out, sems):
-    copies = [pltpu.make_async_copy(edges.at[i], held.at[i], sems.at[i]) for i in range(ROWS)]
-    for copy in copies:
-        copy.start()
+def load_kernel(edges, held, sem):
+    copy = pltpu.make_async_copy(edges, held, sem)
+    copy.start()
+    copy.wait()
+
+
+def first_kernel(meta, held, low, high, out):
     for i in range(ROWS):
-        copies[i].wait()
         out[i] = product(meta, held, i, 0, tile_of(low, high))
 
 
-def second_kernel(meta, held, far_low, far_high, near_low, near_high, total, out):
-    step = 3 - 2 * meta[7, 0, 0]
+def second_kernel(meta, held, low, high, total, out):
+    for i in range(ROWS):
+        out[i] = total[i] + product(meta, held, i, 2, tile_of(low, high))
+
+
+def third_kernel(meta, held, near_low, near_high, last_low, last_high, total, out):
+    odd = meta[7, 0, 0]
     for i in range(ROWS):
         out[i] = (
             total[i]
-            + product(meta, held, i, 2, tile_of(far_low, far_high))
-            + product(meta, held, i, step, tile_of(near_low, near_high))
-        )
-
-
-def third_kernel(meta, held, low, high, total, out):
-    step = 1 + 2 * meta[7, 0, 0]
-    for i in range(ROWS):
-        out[i] = (total[i] + product(meta, held, i, step, tile_of(low, high))).astype(BF16)
+            + product(meta, held, i, 3 - 2 * odd, tile_of(near_low, near_high))
+            + product(meta, held, i, 1 + 2 * odd, tile_of(last_low, last_high))
+        ).astype(BF16)
 
 
 def dense_kernel(parts, scale, weight, bias, cot, act, send):
@@ -230,25 +231,24 @@
 
     low = move(low, lambda b, r: (b + 4 * r, r))
     high = move(high, lambda b, r: (b + 4 * (r ^ 2), r ^ 2))
+    (held,) = call(
+        load_kernel, [(edges.shape, BF16)], [HBM], [pltpu.SemaphoreType.DMA], 0, 12 << 20
+    )(pinned(edges))
+    low, high, held, meta = lax.optimization_barrier((low, high, held, meta))
     far_low, far_high = (move(v, lambda b, r: (b + 2, r)) for v in (low, high))
+
+    work = 2 * ROWS * SLOTS * T * T * T
+    (total,) = call(first_kernel, [(tiles, F32)], [SMEM] + [VMEM] * 3, (), work, 3 << 20)(
+        meta, held, low, high
+    )
+    low, high, total = lax.optimization_barrier((low, high, total))
     near_low, near_high = (move(v, lambda b, r: (b + 1 + 2 * (b % 2), r)) for v in (low, high))
-
-    work = 2 * ROWS * SLOTS * T * T * T
-    held, total = call(
-        first_kernel,
-        [(edges.shape, BF16), (tiles, F32)],
-        [SMEM, HBM, VMEM, VMEM],
-        [pltpu.SemaphoreType.DMA((ROWS,))],
-        work,
-        8 << 20,
-    )(meta, pinned(edges), low, high)
-    far_low, far_high, total = lax.optimization_barrier((far_low, far_high, total))
     last_low, last_high = swap(far_low, 1), swap(far_high, 1)
-    (total,) = call(second_kernel, [(tiles, F32)], [SMEM] + [VMEM] * 6, (), 2 * work, 6 << 20)(
-        meta, held, far_low, far_high, near_low, near_high, total
-    )
-    (parts,) = call(third_kernel, [(tiles, BF16)], [SMEM] + [VMEM] * 4, (), work, 3 << 20)(
-        meta, held, last_low, last_high, total
+    (total,) = call(second_kernel, [(tiles, F32)], [SMEM] + [VMEM] * 4, (), work, 3 << 20)(
+        meta, held, far_low, far_high, total
+    )
+    (parts,) = call(third_kernel, [(tiles, BF16)], [SMEM] + [VMEM] * 6, (), 2 * work, 6 << 20)(
+        meta, held, near_low, near_high, last_low, last_high, total
     )
     parts = exchange(parts, REP)
 
@@ -274,12 +274,13 @@
         meta, held, got
     )
     far_low, far_high = call(near_kernel, [(half, BF16), (half, BF16)], [VMEM] * 2)(far, last)
+    grads = grads + swap(grads, 4)
     far_low, far_high, got, grads = lax.optimization_barrier((far_low, far_high, got, grads))
     far_low, far_high = (move(v, lambda b, r: (b - 2, r)) for v in (far_low, far_high))
     (own,) = call(own_sums_kernel, [(tiles, F32)], [SMEM] + [VMEM] * 2, sums, work, 3 << 20)(
         meta, held, got
     )
-    grads = grads + swap(grads, 16)
+    grads = grads + swap(grads, 8)
     own, grads = lax.optimization_barrier((own, grads))
     low, high = (
         call(functools.partial(half_kernel, first), [(half, BF16)], [VMEM] * 3)(own, near, far)[0]
@@ -287,7 +288,7 @@
     )
     low = move(low, lambda b, r: (b - 4 * r, r))
     high = move(high, lambda b, r: (b - 4 * r, r ^ 2))
-    for bit in (8, 4, 2, 1):
+    for bit in (2, 1, 16):
         grads = grads + swap(grads, bit)
     (send,) = call(gather_kernel, [((ROWS, T + 32, T), BF16)], [VMEM] * 3)(low, high, grads)
     got = exchange(send, REP)

time: 123 us -> 118 us (0.959)
  waiting for transfers between devices: 23.5 us -> 19.1 us
  blocking collectives: 53.6 us -> 50.2 us
  starting transfers between devices: 27.6 us -> 30.6 us
    ppermute x19, waiting for transfers between devices: 23.5 us -> 19.1 us  [move(): return lax.ppermute(value, BLK + REP, pairs)]
    all_to_all x3, blocking collectives: 53.6 us -> 50.2 us  [exchange(): return lax.all_to_all(value, axes, 0, 0, tiled=True)]
    ppermute x19, starting transfers between devices: 27.6 us -> 30.6 us  [move(): return lax.ppermute(value, BLK + REP, pairs)]
    pallas_call x3 -> x4, Pallas kernels: 7.6 us -> 7.94 us  [the longest x1 2.82 us: on_device(): call(load_kernel, [(edges.shape, BF16)], [HBM], [pltpu.SemaphoreType.DMA]...]
  transfers between devices with their start and end apart: 19 -> 19, of which waited for: 7 -> 9; matrix products, arithmetic and copies ran while one was open for 1% -> 0% of each run, Pallas kernels for 8% -> 8%
where the time goes in v4:
time: 118 us; the launch traced here: 117 us
  blocking collectives  50.2 us (43%)
  starting transfers between devices  30.6 us (26%)
  waiting for transfers between devices  19.1 us (16%)
  Pallas kernels  16.4 us (14%)
    all_to_all x3, blocking collectives, exchange(): return lax.all_to_all(value, axes, 0, 0, tiled=True)  50.2 us
    ppermute x19, starting transfers between devices, move(): return lax.ppermute(value, BLK + REP, pairs)  30.6 us
    ppermute x19, waiting for transfers between devices, move(): return lax.ppermute(value, BLK + REP, pairs)  19.1 us
    pallas_call x1, Pallas kernels, on_device(): call(load_kernel, [(edges.shape, BF16)], [HBM], [pltpu.SemaphoreType.DMA]...  2.82 us
  transfers between devices with their start and end apart: 19, of which 9 were waited for; matrix products, arithmetic and copies ran while one was open for 0% of the time, Pallas kernels for 8%

profile of v4, /device:TPU:32, one launch (start us, length us, event | category | flops | bytes accessed | tf_op | source)
XLA Modules:
  0.0 117.4 jit_solution(17705048091196269292)
XLA Ops:
  0.6 1.7 %shard_map.111 = (bf16[4,128,128]{2,1,0:T(8,128)(2,1)S(1)}, bf16[4,128,128]{2,1,0:T(8,128)(2,1)S(1)}, f32[128,128]{1,0:T(8,128)S(1)}) custom-call(s32[1]{0:T(128)} %bitcast.rep, bf16[1024,128]{1,0:T(8,128)(2,1)} %features.1, s32[8,128]{1,0:T(8,128)} %bitcast.10), custom_call_target="tpu_custom_call" | custom-call | bytes 1048576 | tf_op jit(solution)/shard_map/pallas_call | solution.py:226
  3.0 9.1 %collective-permute-start.1 = (bf16[4,128,128]{2,1,0:T(8,128)(2,1)S(1)}, bf16[4,128,128]{2,1,0:T(8,128)(2,1)S(1)}, u32[]{:S(2)}, u32[]{:S(2)}) collective-permute-start(bf16[4,128,128]{2,1,0:T(8,128)(2,1)S(1)} %get-tuple-element.31), channel_id=1, source_target_pairs={{0,66},{1,99},{2,0},{3,33},{4,198},{5,231},{6,132},{7,165},{8,74},... | collective-permute-start | bytes 393224 | tf_op jit(solution)/shard_map/ppermute | solution.py:211
  12.2 2.8 %shard_map.112.held = bf16[8,4,6,128,128]{4,3,2,1,0:T(8,128)(2,1)S(1)} custom-call(bf16[8,4,6,128,128]{4,3,2,1,0:T(8,128)(2,1)} %edges.1), custom_call_target="tpu_custom_call" | custom-call | bytes 12582912 | tf_op jit(solution)/shard_map/pallas_call | solution.py:234
  15.0 1.6 %collective-permute-done.1.high = bf16[4,128,128]{2,1,0:T(8,128)(2,1)S(1)} collective-permute-done((bf16[4,128,128]{2,1,0:T(8,128)(2,1)S(1)}, bf16[4,128,128]{2,1,0:T(8,128)(2,1)S(1)}, u32[]{:S(2)}, u32[]{:S(2)}) %collective-permute-start.1) | collective-permute-done | bytes 131104 | tf_op jit(solution)/shard_map/ppermute | solution.py:211
  16.7 2.0 %collective-permute-start.4 = (bf16[4,128,128]{2,1,0:T(8,128)(2,1)S(1)}, bf16[4,128,128]{2,1,0:T(8,128)(2,1)S(1)}, u32[]{:S(2)}, u32[]{:S(2)}) collective-permute-start(bf16[4,128,128]{2,1,0:T(8,128)(2,1)S(1)} %collective-permute-done.low), channel_id=1, source_target_pairs={{0,16},{1,17},{2,18},{3,19},{4,20},{5,21},{6,22},{7,23},{8,24},{9,... | collective-permute-start | bytes 393224 | tf_op jit(solution)/shard_map/ppermute | solution.py:211
  19.9 1.5 %shard_map.113.total = f32[8,128,128]{2,1,0:T(8,128)S(1)} custom-call(s32[8,4,8]{2,1,0:T(4,128)S(1)} %pad_add_fusion.meta, bf16[8,4,6,128,128]{4,3,2,1,0:T(8,128)(2,1)S(1)} %shard_map.112.held, bf16[4,128,128]{2,1,0:T(8,128)(2,1)S(1)} %collective-permute-done.low, bf16[4,128,128]{2,1,0:T(8,128)(2,1)S(1)} %collective-permute-done.1.high), custom_call_target="tpu_custom_call" | custom-call | flops 201326592 | bytes 3145728 | tf_op jit(solution)/shard_map/pallas_call | solution.py:241
  22.3 1.8 %collective-permute-done.4.low = bf16[4,128,128]{2,1,0:T(8,128)(2,1)S(1)} collective-permute-done((bf16[4,128,128]{2,1,0:T(8,128)(2,1)S(1)}, bf16[4,128,128]{2,1,0:T(8,128)(2,1)S(1)}, u32[]{:S(2)}, u32[]{:S(2)}) %collective-permute-start.4) | collective-permute-done | bytes 131104 | tf_op jit(solution)/shard_map/ppermute | solution.py:211
  24.1 1.6 %collective-permute-done.6.high = bf16[4,128,128]{2,1,0:T(8,128)(2,1)S(1)} collective-permute-done((bf16[4,128,128]{2,1,0:T(8,128)(2,1)S(1)}, bf16[4,128,128]{2,1,0:T(8,128)(2,1)S(1)}, u32[]{:S(2)}, u32[]{:S(2)}) %collective-permute-start.6) | collective-permute-done | bytes 131104 | tf_op jit(solution)/shard_map/ppermute | solution.py:211
  25.7 1.5 %shard_map.114.total = f32[8,128,128]{2,1,0:T(8,128)S(1)} custom-call(s32[8,4,8]{2,1,0:T(4,128)S(1)} %pad_add_fusion.meta, bf16[8,4,6,128,128]{4,3,2,1,0:T(8,128)(2,1)S(1)} %shard_map.112.held, bf16[4,128,128]{2,1,0:T(8,128)(2,1)S(1)} %collective-permute-done.4.low, bf16[4,128,128]{2,1,0:T(8,128)(2,1)S(1)} %collective-permute-done.6.high, ...), custom_call_target="tpu_custom_call" | custom-call | flops 201326592 | bytes 3145728 | tf_op jit(solution)/shard_map/pallas_call | solution.py:247
  27.3 2.1 %shard_map.115 = bf16[8,128,128]{2,1,0:T(8,128)(2,1)S(1)} custom-call(s32[8,4,8]{2,1,0:T(4,128)S(1)} %pad_add_fusion.meta, bf16[8,4,6,128,128]{4,3,2,1,0:T(8,128)(2,1)S(1)} %shard_map.112.held, bf16[4,128,128]{2,1,0:T(8,128)(2,1)S(1)} %collective-permute-done.2.near_low, bf16[4,128,128]{2,1,0:T(8,128)(2,1)S(1)} %collective-permute-done.3.near_high, ...), custom_call_target="tpu_custom_call" | custom-call | flops 402653184 | bytes 6291456 | tf_op jit(solution)/shard_map/pallas_call | solution.py:250
  29.4 21.9 %all_to_all.15.parts = bf16[8,128,128]{2,1,0:T(8,128)(2,1)S(1)} all-to-all(bf16[8,128,128]{2,1,0:T(8,128)(2,1)S(1)} %shard_map.115), channel_id=1, replica_groups=mesh['z'=8,'yl'=2,'core'=2,'x'=4,'yh'=2] {'x','yh'}, dimensions={0} | all-to-all | bytes 524288 | tf_op jit(solution)/shard_map/all_to_all | solution.py:201
  52.1 12.2 %all_to_all.16.got = bf16[8,176,128]{2,1,0:T(8,128)(2,1)S(1)} all-to-all(bf16[8,176,128]{2,1,0:T(8,128)(2,1)S(1)} %get-tuple-element.41), channel_id=1, replica_groups=mesh['z'=8,'yl'=2,'core'=2,'x'=4,'yh'=2] {'x','yh'}, dimensions={0} | all-to-all | bytes 720896 | tf_op jit(solution)/shard_map/all_to_all | solution.py:201
  64.3 2.0 %shard_map.118 = (bf16[8,128,128]{2,1,0:T(8,128)(2,1)S(1)}, bf16[8,128,128]{2,1,0:T(8,128)(2,1)S(1)}, f32[40,128]{1,0:T(8,128)S(1)}) custom-call(s32[8,4,8]{2,1,0:T(4,128)S(1)} %pad_add_fusion.meta, bf16[8,4,6,128,128]{4,3,2,1,0:T(8,128)(2,1)S(1)} %shard_map.112.held, bf16[8,176,128]{2,1,0:T(8,128)(2,1)S(1)} %all_to_all.16.got), custom_call_target="tpu_custom_call" | custom-call | flops 402653184 | bytes 6291456 | tf_op jit(solution)/shard_map/pallas_call | solution.py:263
  66.5 2.2 %collective-permute-start.11 = (bf16[8,128,128]{2,1,0:T(8,128)(2,1)S(1)}, bf16[8,128,128]{2,1,0:T(8,128)(2,1)S(1)}, u32[]{:S(2)}, u32[]{:S(2)}) collective-permute-start(bf16[8,128,128]{2,1,0:T(8,128)(2,1)S(1)} %get-tuple-element.49), channel_id=1, source_target_pairs={{0,232},{1,233},{2,234},{3,235},{4,236},{5,237},{6,238},{7,239},{8... | collective-permute-start | bytes 786440 | tf_op jit(solution)/shard_map/ppermute | solution.py:211
  68.7 2.2 %collective-permute-start.9 = (f32[40,128]{1,0:T(8,128)S(1)}, f32[40,128]{1,0:T(8,128)S(1)}, u32[]{:S(2)}, u32[]{:S(2)}) collective-permute-start(f32[40,128]{1,0:T(8,128)S(1)} %get-tuple-element.45), channel_id=1, source_target_pairs={{0,32},{1,33},{2,34},{3,35},{4,36},{5,37},{6,38},{7,39},{8,40},{9,... | collective-permute-start | bytes 61448 | tf_op jit(solution)/shard_map/ppermute | solution.py:211
  73.5 2.1 %collective-permute-start.14 = (bf16[4,128,128]{2,1,0:T(8,128)(2,1)S(1)}, bf16[4,128,128]{2,1,0:T(8,128)(2,1)S(1)}, u32[]{:S(2)}, u32[]{:S(2)}) collective-permute-start(bf16[4,128,128]{2,1,0:T(8,128)(2,1)S(1)} %get-tuple-element.51), channel_id=1, source_target_pairs={{0,240},{1,241},{2,242},{3,243},{4,244},{5,245},{6,246},{7,247},{8... | collective-permute-start | bytes 393224 | tf_op jit(solution)/shard_map/ppermute | solution.py:211
  75.6 1.9 %collective-permute-start.12 = (bf16[4,128,128]{2,1,0:T(8,128)(2,1)S(1)}, bf16[4,128,128]{2,1,0:T(8,128)(2,1)S(1)}, u32[]{:S(2)}, u32[]{:S(2)}) collective-permute-start(bf16[4,128,128]{2,1,0:T(8,128)(2,1)S(1)} %get-tuple-element.50), channel_id=1, source_target_pairs={{0,240},{1,241},{2,242},{3,243},{4,244},{5,245},{6,246},{7,247},{8... | collective-permute-start | bytes 393224 | tf_op jit(solution)/shard_map/ppermute | solution.py:211
  77.5 2.8 %collective-permute-start.10 = (f32[40,128]{1,0:T(8,128)S(1)}, f32[40,128]{1,0:T(8,128)S(1)}, u32[]{:S(2)}, u32[]{:S(2)}) collective-permute-start(f32[40,128]{1,0:T(8,128)S(1)} %add.19), channel_id=1, source_target_pairs={{0,64},{1,65},{2,66},{3,67},{4,68},{5,69},{6,70},{7,71},{8,72},{9,... | collective-permute-start | bytes 61448 | tf_op jit(solution)/shard_map/ppermute | solution.py:211
  80.3 1.5 %shard_map.120.own = f32[8,128,128]{2,1,0:T(8,128)S(1)} custom-call(s32[8,4,8]{2,1,0:T(4,128)S(1)} %pad_add_fusion.meta, bf16[8,4,6,128,128]{4,3,2,1,0:T(8,128)(2,1)S(1)} %shard_map.112.held, bf16[8,176,128]{2,1,0:T(8,128)(2,1)S(1)} %all_to_all.16.got), custom_call_target="tpu_custom_call" | custom-call | flops 201326592 | bytes 3145728 | tf_op jit(solution)/shard_map/pallas_call | solution.py:280
  81.8 1.7 %collective-permute-done.10 = f32[40,128]{1,0:T(8,128)S(1)} collective-permute-done((f32[40,128]{1,0:T(8,128)S(1)}, f32[40,128]{1,0:T(8,128)S(1)}, u32[]{:S(2)}, u32[]{:S(2)}) %collective-permute-start.10) | collective-permute-done | bytes 20512 | tf_op jit(solution)/shard_map/ppermute | solution.py:211
  83.5 3.3 %collective-permute-start.15 = (bf16[4,128,128]{2,1,0:T(8,128)(2,1)S(1)}, bf16[4,128,128]{2,1,0:T(8,128)(2,1)S(1)}, u32[]{:S(2)}, u32[]{:S(2)}) collective-permute-start(bf16[4,128,128]{2,1,0:T(8,128)(2,1)S(1)} %shard_map.122), channel_id=1, source_target_pairs={{0,2},{1,227},{2,192},{3,161},{4,134},{5,103},{6,68},{7,37},{8,10}... | collective-permute-start | bytes 393224 | tf_op jit(solution)/shard_map/ppermute | solution.py:211
  87.7 3.8 %collective-permute-done.16 = f32[40,128]{1,0:T(8,128)S(1)} collective-permute-done((f32[40,128]{1,0:T(8,128)S(1)}, f32[40,128]{1,0:T(8,128)S(1)}, u32[]{:S(2)}, u32[]{:S(2)}) %collective-permute-start.16) | collective-permute-done | bytes 20512 | tf_op jit(solution)/shard_map/ppermute | solution.py:211
  94.0 6.3 %collective-permute-done.18 = f32[40,128]{1,0:T(8,128)S(1)} collective-permute-done((f32[40,128]{1,0:T(8,128)S(1)}, f32[40,128]{1,0:T(8,128)S(1)}, u32[]{:S(2)}, u32[]{:S(2)}) %collective-permute-start.18) | collective-permute-done | bytes 20512 | tf_op jit(solution)/shard_map/ppermute | solution.py:211
  100.4 16.2 %all_to_all.17.got = bf16[8,160,128]{2,1,0:T(8,128)(2,1)S(1)} all-to-all(bf16[8,160,128]{2,1,0:T(8,128)(2,1)S(1)} %shard_map.123), channel_id=1, replica_groups=mesh['z'=8,'yl'=2,'core'=2,'x'=4,'yh'=2] {'x','yh'}, dimensions={0} | all-to-all | bytes 655360 | tf_op jit(solution)/shard_map/all_to_all | solution.py:201
  (49 shorter events, 10.5 us)
Async XLA Ops:
  2.4 12.7 %collective-permute-start = (bf16[4,128,128]{2,1,0:T(8,128)(2,1)S(1)}, bf16[4,128,128]{2,1,0:T(8,128)(2,1)S(1)}, u32[]{:S(2)}, u32[]{:S(2)}) collective-permute-start(bf16[4,128,128]{2,1,0:T(8,128)(2,1)S(1)} %get-tuple-element.30), channel_id=1, source_target_pairs={{0,0},{1,33},{2,66},{3,99},{4,132},{5,165},{6,198},{7,231},{8,8},{... | collective-permute-start | bytes 393224 | tf_op jit(solution)/shard_map/ppermute | solution.py:211
  3.0 13.6 %collective-permute-start.1 = (bf16[4,128,128]{2,1,0:T(8,128)(2,1)S(1)}, bf16[4,128,128]{2,1,0:T(8,128)(2,1)S(1)}, u32[]{:S(2)}, u32[]{:S(2)}) collective-permute-start(bf16[4,128,128]{2,1,0:T(8,128)(2,1)S(1)} %get-tuple-element.31), channel_id=1, source_target_pairs={{0,66},{1,99},{2,0},{3,33},{4,198},{5,231},{6,132},{7,165},{8,74},... | collective-permute-start | bytes 393224 | tf_op jit(solution)/shard_map/ppermute | solution.py:211
  12.1 2.8 %copy-start.3 = (s32[8,4,6]{0,1,2:T(4,128)S(1)}, s32[8,4,6]{0,1,2:T(4,128)}, u32[]{:S(2)}) copy-start(s32[8,4,6]{0,1,2:T(4,128)} %param.10) | copy-start | bytes 2308
  12.2 2.9 %copy-start.4 = (s32[8,4]{0,1:T(4,128)S(1)}, s32[8,4]{0,1:T(4,128)}, u32[]{:S(2)}) copy-start(s32[8,4]{0,1:T(4,128)} %param.11) | copy-start | bytes 388
  16.7 7.4 %collective-permute-start.4 = (bf16[4,128,128]{2,1,0:T(8,128)(2,1)S(1)}, bf16[4,128,128]{2,1,0:T(8,128)(2,1)S(1)}, u32[]{:S(2)}, u32[]{:S(2)}) collective-permute-start(bf16[4,128,128]{2,1,0:T(8,128)(2,1)S(1)} %collective-permute-done.low), channel_id=1, source_target_pairs={{0,16},{1,17},{2,18},{3,19},{4,20},{5,21},{6,22},{7,23},{8,24},{9,... | collective-permute-start | bytes 393224 | tf_op jit(solution)/shard_map/ppermute | solution.py:211
  18.7 7.0 %collective-permute-start.6 = (bf16[4,128,128]{2,1,0:T(8,128)(2,1)S(1)}, bf16[4,128,128]{2,1,0:T(8,128)(2,1)S(1)}, u32[]{:S(2)}, u32[]{:S(2)}) collective-permute-start(bf16[4,128,128]{2,1,0:T(8,128)(2,1)S(1)} %collective-permute-done.1.high), channel_id=1, source_target_pairs={{0,16},{1,17},{2,18},{3,19},{4,20},{5,21},{6,22},{7,23},{8,24},{9,... | collective-permute-start | bytes 393224 | tf_op jit(solution)/shard_map/ppermute | solution.py:211
  21.4 29.9 %copy-start = (bf16[128,256]{1,0:T(8,128)(2,1)S(1)}, bf16[128,256]{1,0:T(8,128)(2,1)}, u32[]{:S(2)}) copy-start(bf16[128,256]{1,0:T(8,128)(2,1)} %weight.1) | copy-start | bytes 196612
  21.4 29.9 %copy-start.1 = (bf16[128,256]{1,0:T(8,128)(2,1)S(1)}, bf16[128,256]{1,0:T(8,128)(2,1)}, u32[]{:S(2)}) copy-start(bf16[128,256]{1,0:T(8,128)(2,1)} %cot.1) | copy-start | bytes 196612
  21.5 29.9 %copy-start.2 = (f32[256]{0:T(256)S(1)}, f32[256]{0:T(256)}, u32[]{:S(2)}) copy-start(f32[256]{0:T(256)} %param.14) | copy-start | bytes 3076
  21.5 5.7 %collective-permute-start.2 = (bf16[4,128,128]{2,1,0:T(8,128)(2,1)S(1)}, bf16[4,128,128]{2,1,0:T(8,128)(2,1)S(1)}, u32[]{:S(2)}, u32[]{:S(2)}) collective-permute-start(bf16[4,128,128]{2,1,0:T(8,128)(2,1)S(1)} %collective-permute-done.low), channel_id=1, source_target_pairs={{0,8},{1,9},{2,10},{3,11},{4,12},{5,13},{6,14},{7,15},{8,32},{9,33... | collective-permute-start | bytes 393224 | tf_op jit(solution)/shard_map/ppermute | solution.py:211
  21.5 5.8 %collective-permute-start.3 = (bf16[4,128,128]{2,1,0:T(8,128)(2,1)S(1)}, bf16[4,128,128]{2,1,0:T(8,128)(2,1)S(1)}, u32[]{:S(2)}, u32[]{:S(2)}) collective-permute-start(bf16[4,128,128]{2,1,0:T(8,128)(2,1)S(1)} %collective-permute-done.1.high), channel_id=1, source_target_pairs={{0,8},{1,9},{2,10},{3,11},{4,12},{5,13},{6,14},{7,15},{8,32},{9,33... | collective-permute-start | bytes 393224 | tf_op jit(solution)/shard_map/ppermute | solution.py:211
  24.1 3.2 %collective-permute-start.5 = (bf16[4,128,128]{2,1,0:T(8,128)(2,1)S(1)}, bf16[4,128,128]{2,1,0:T(8,128)(2,1)S(1)}, u32[]{:S(2)}, u32[]{:S(2)}) collective-permute-start(bf16[4,128,128]{2,1,0:T(8,128)(2,1)S(1)} %collective-permute-done.4.low), channel_id=1, source_target_pairs={{0,8},{1,9},{2,10},{3,11},{4,12},{5,13},{6,14},{7,15},{8,0},{9,1},... | collective-permute-start | bytes 393224 | tf_op jit(solution)/shard_map/ppermute | solution.py:211
  25.7 1.6 %collective-permute-start.7 = (bf16[4,128,128]{2,1,0:T(8,128)(2,1)S(1)}, bf16[4,128,128]{2,1,0:T(8,128)(2,1)S(1)}, u32[]{:S(2)}, u32[]{:S(2)}) collective-permute-start(bf16[4,128,128]{2,1,0:T(8,128)(2,1)S(1)} %collective-permute-done.6.high), channel_id=1, source_target_pairs={{0,8},{1,9},{2,10},{3,11},{4,12},{5,13},{6,14},{7,15},{8,0},{9,1},... | collective-permute-start | bytes 393224 | tf_op jit(solution)/shard_map/ppermute | solution.py:211
  66.4 7.0 %collective-permute-start.8 = (bf16[8,128,128]{2,1,0:T(8,128)(2,1)S(1)}, bf16[8,128,128]{2,1,0:T(8,128)(2,1)S(1)}, u32[]{:S(2)}, u32[]{:S(2)}) collective-permute-start(bf16[8,128,128]{2,1,0:T(8,128)(2,1)S(1)} %get-tuple-element.42), channel_id=1, source_target_pairs={{0,8},{1,9},{2,10},{3,11},{4,12},{5,13},{6,14},{7,15},{8,0},{9,1},... | collective-permute-start | bytes 786440 | tf_op jit(solution)/shard_map/ppermute | solution.py:211
  66.5 17.0 %collective-permute-start.11 = (bf16[8,128,128]{2,1,0:T(8,128)(2,1)S(1)}, bf16[8,128,128]{2,1,0:T(8,128)(2,1)S(1)}, u32[]{:S(2)}, u32[]{:S(2)}) collective-permute-start(bf16[8,128,128]{2,1,0:T(8,128)(2,1)S(1)} %get-tuple-element.49), channel_id=1, source_target_pairs={{0,232},{1,233},{2,234},{3,235},{4,236},{5,237},{6,238},{7,239},{8... | collective-permute-start | bytes 786440 | tf_op jit(solution)/shard_map/ppermute | solution.py:211
  68.7 4.7 %collective-permute-start.9 = (f32[40,128]{1,0:T(8,128)S(1)}, f32[40,128]{1,0:T(8,128)S(1)}, u32[]{:S(2)}, u32[]{:S(2)}) collective-permute-start(f32[40,128]{1,0:T(8,128)S(1)} %get-tuple-element.45), channel_id=1, source_target_pairs={{0,32},{1,33},{2,34},{3,35},{4,36},{5,37},{6,38},{7,39},{8,40},{9,... | collective-permute-start | bytes 61448 | tf_op jit(solution)/shard_map/ppermute | solution.py:211
  73.5 10.0 %collective-permute-start.14 = (bf16[4,128,128]{2,1,0:T(8,128)(2,1)S(1)}, bf16[4,128,128]{2,1,0:T(8,128)(2,1)S(1)}, u32[]{:S(2)}, u32[]{:S(2)}) collective-permute-start(bf16[4,128,128]{2,1,0:T(8,128)(2,1)S(1)} %get-tuple-element.51), channel_id=1, source_target_pairs={{0,240},{1,241},{2,242},{3,243},{4,244},{5,245},{6,246},{7,247},{8... | collective-permute-start | bytes 393224 | tf_op jit(solution)/shard_map/ppermute | solution.py:211
  75.6 11.3 %collective-permute-start.12 = (bf16[4,128,128]{2,1,0:T(8,128)(2,1)S(1)}, bf16[4,128,128]{2,1,0:T(8,128)(2,1)S(1)}, u32[]{:S(2)}, u32[]{:S(2)}) collective-permute-start(bf16[4,128,128]{2,1,0:T(8,128)(2,1)S(1)} %get-tuple-element.50), channel_id=1, source_target_pairs={{0,240},{1,241},{2,242},{3,243},{4,244},{5,245},{6,246},{7,247},{8... | collective-permute-start | bytes 393224 | tf_op jit(solution)/shard_map/ppermute | solution.py:211
  77.5 6.0 %collective-permute-start.10 = (f32[40,128]{1,0:T(8,128)S(1)}, f32[40,128]{1,0:T(8,128)S(1)}, u32[]{:S(2)}, u32[]{:S(2)}) collective-permute-start(f32[40,128]{1,0:T(8,128)S(1)} %add.19), channel_id=1, source_target_pairs={{0,64},{1,65},{2,66},{3,67},{4,68},{5,69},{6,70},{7,71},{8,72},{9,... | collective-permute-start | bytes 61448 | tf_op jit(solution)/shard_map/ppermute | solution.py:211
  83.5 16.8 %collective-permute-start.15 = (bf16[4,128,128]{2,1,0:T(8,128)(2,1)S(1)}, bf16[4,128,128]{2,1,0:T(8,128)(2,1)S(1)}, u32[]{:S(2)}, u32[]{:S(2)}) collective-permute-start(bf16[4,128,128]{2,1,0:T(8,128)(2,1)S(1)} %shard_map.122), channel_id=1, source_target_pairs={{0,2},{1,227},{2,192},{3,161},{4,134},{5,103},{6,68},{7,37},{8,10}... | collective-permute-start | bytes 393224 | tf_op jit(solution)/shard_map/ppermute | solution.py:211
  86.9 13.5 %collective-permute-start.13 = (bf16[4,128,128]{2,1,0:T(8,128)(2,1)S(1)}, bf16[4,128,128]{2,1,0:T(8,128)(2,1)S(1)}, u32[]{:S(2)}, u32[]{:S(2)}) collective-permute-start(bf16[4,128,128]{2,1,0:T(8,128)(2,1)S(1)} %shard_map.121), channel_id=1, source_target_pairs={{0,0},{1,225},{2,194},{3,163},{4,132},{5,101},{6,70},{7,39},{8,8},... | collective-permute-start | bytes 393224 | tf_op jit(solution)/shard_map/ppermute | solution.py:211
  87.6 3.9 %collective-permute-start.16 = (f32[40,128]{1,0:T(8,128)S(1)}, f32[40,128]{1,0:T(8,128)S(1)}, u32[]{:S(2)}, u32[]{:S(2)}) collective-permute-start(f32[40,128]{1,0:T(8,128)S(1)} %add.20), channel_id=1, source_target_pairs={{0,16},{1,17},{2,18},{3,19},{4,20},{5,21},{6,22},{7,23},{8,24},{9,... | collective-permute-start | bytes 61448 | tf_op jit(solution)/shard_map/ppermute | solution.py:211
  91.5 1.2 %collective-permute-start.17 = (f32[40,128]{1,0:T(8,128)S(1)}, f32[40,128]{1,0:T(8,128)S(1)}, u32[]{:S(2)}, u32[]{:S(2)}) collective-permute-start(f32[40,128]{1,0:T(8,128)S(1)} %add.21), channel_id=1, source_target_pairs={{0,8},{1,9},{2,10},{3,11},{4,12},{5,13},{6,14},{7,15},{8,0},{9,1},... | collective-permute-start | bytes 61448 | tf_op jit(solution)/shard_map/ppermute | solution.py:211
  92.7 7.7 %collective-permute-start.18 = (f32[40,128]{1,0:T(8,128)S(1)}, f32[40,128]{1,0:T(8,128)S(1)}, u32[]{:S(2)}, u32[]{:S(2)}) collective-permute-start(f32[40,128]{1,0:T(8,128)S(1)} %add.22), channel_id=1, source_target_pairs={{0,128},{1,129},{2,130},{3,131},{4,132},{5,133},{6,134},{7,135},{8... | collective-permute-start | bytes 61448 | tf_op jit(solution)/shard_map/ppermute | solution.py:211

commit v5 on v4

--- a/solution.py
+++ b/solution.py
@@ -16,6 +16,7 @@
 STEPS = 4
 SLOTS = 6
 HALF = ROWS // 2
+NODES = ROWS * T
 GRAD = 48
 F32 = jnp.float32
 BF16 = jnp.bfloat16
@@ -127,18 +128,20 @@
             sums[at] += jnp.where(c < meta[6, s, i], part, jnp.zeros_like(part))
 
 
-def near_sums_kernel(meta, held, got, near0, near1, grads, sums):
+def near_sums_kernel(meta, held, got, near, last, sums):
     total = got[0, T:].astype(F32)
     for j in range(1, ROWS):
         total += got[j, T:].astype(F32)
-    grads[0:32] = total[0:32]
-    grads[32:40] = jnp.concatenate(
-        [total[32:34] + total[34:36], jnp.zeros((6, T), F32)], axis=0
-    )
+    total = jnp.concatenate(
+        [total[0:32], total[32:34] + total[34:36], jnp.zeros((14, T), F32)], axis=0
+    )
+    high = total.astype(BF16)
+    last[NODES : NODES + GRAD] = high
+    last[NODES + GRAD :] = (total - high.astype(F32)).astype(BF16)
     column_sums(meta, held, got, 1 + 2 * meta[7, 0, 0], sums)
-    near1[...] = sums[...].astype(BF16)
+    last[0:NODES] = sums[...].astype(BF16).reshape(NODES, T)
     column_sums(meta, held, got, 3 - 2 * meta[7, 0, 0], sums)
-    near0[...] = sums[...].astype(BF16)
+    near[...] = sums[...].astype(BF16)
 
 
 def far_sums_kernel(meta, held, got, far, sums):
@@ -151,9 +154,16 @@
     out[...] = sums[...]
 
 
-def near_kernel(far, near, low, high):
-    low[...] = (far[0:HALF].astype(F32) + near[0:HALF].astype(F32)).astype(BF16)
-    high[...] = (far[HALF:].astype(F32) + near[HALF:].astype(F32)).astype(BF16)
+def grads_of(rows):
+    return rows[NODES : NODES + GRAD].astype(F32) + rows[NODES + GRAD :].astype(F32)
+
+
+def near_kernel(far, mine, other, low, high, grads):
+    for j in range(ROWS):
+        half = low if j < HALF else high
+        rows = other[j * T : (j + 1) * T].astype(F32)
+        half[j % HALF] = (far[j].astype(F32) + rows).astype(BF16)
+    grads[...] = grads_of(mine) + grads_of(other)
 
 
 def half_kernel(first, own, near, far, out):
@@ -162,8 +172,12 @@
     out[...] = total.astype(BF16)
 
 
-def gather_kernel(low, high, grads, out):
-    mine = grads[0:32].astype(BF16)
+def gather_kernel(low, high, planes, out, grads):
+    total = planes[0]
+    for p in range(1, Z):
+        total += planes[p]
+    grads[...] = total
+    mine = total[0:32].astype(BF16)
     for j in range(ROWS):
         out[j, 0:T] = low[j] if j < HALF else high[j - HALF]
         out[j, T:] = mine
@@ -234,15 +248,16 @@
     (held,) = call(
         load_kernel, [(edges.shape, BF16)], [HBM], [pltpu.SemaphoreType.DMA], 0, 12 << 20
     )(pinned(edges))
-    low, high, held, meta = lax.optimization_barrier((low, high, held, meta))
+    low, held, meta = lax.optimization_barrier((low, held, meta))
     far_low, far_high = (move(v, lambda b, r: (b + 2, r)) for v in (low, high))
+    near_low = move(low, lambda b, r: (b + 1 + 2 * (b % 2), r))
 
     work = 2 * ROWS * SLOTS * T * T * T
     (total,) = call(first_kernel, [(tiles, F32)], [SMEM] + [VMEM] * 3, (), work, 3 << 20)(
         meta, held, low, high
     )
-    low, high, total = lax.optimization_barrier((low, high, total))
-    near_low, near_high = (move(v, lambda b, r: (b + 1 + 2 * (b % 2), r)) for v in (low, high))
+    high, total = lax.optimization_barrier((high, total))
+    near_high = move(high, lambda b, r: (b + 1 + 2 * (b % 2), r))
     last_low, last_high = swap(far_low, 1), swap(far_high, 1)
     (total,) = call(second_kernel, [(tiles, F32)], [SMEM] + [VMEM] * 4, (), work, 3 << 20)(
         meta, held, far_low, far_high, total
@@ -260,37 +275,40 @@
     got = exchange(send, REP)
 
     sums = [pltpu.VMEM(tiles, F32)]
-    near, last, grads = call(
+    near, mine = call(
         near_sums_kernel,
-        [(tiles, BF16), (tiles, BF16), ((40, T), F32)],
+        [(tiles, BF16), ((NODES + 2 * GRAD, T), BF16)],
         [SMEM, VMEM, VMEM],
         sums,
         2 * work,
         6 << 20,
     )(meta, held, got)
-    last = swap(last, 1)
+    other = swap(mine, 1)
     near = move(near, lambda b, r: (b - 3 + 2 * (b % 2), r))
     (far,) = call(far_sums_kernel, [(tiles, BF16)], [SMEM, VMEM, VMEM], sums, work, 3 << 20)(
         meta, held, got
     )
-    far_low, far_high = call(near_kernel, [(half, BF16), (half, BF16)], [VMEM] * 2)(far, last)
-    grads = grads + swap(grads, 4)
+    far_low, far_high, grads = call(
+        near_kernel, [(half, BF16), (half, BF16), ((GRAD, T), F32)], [VMEM] * 3
+    )(far, mine, other)
     far_low, far_high, got, grads = lax.optimization_barrier((far_low, far_high, got, grads))
     far_low, far_high = (move(v, lambda b, r: (b - 2, r)) for v in (far_low, far_high))
     (own,) = call(own_sums_kernel, [(tiles, F32)], [SMEM] + [VMEM] * 2, sums, work, 3 << 20)(
         meta, held, got
     )
-    grads = grads + swap(grads, 8)
+    grads = grads + swap(grads, 2)
     own, grads = lax.optimization_barrier((own, grads))
     low, high = (
         call(functools.partial(half_kernel, first), [(half, BF16)], [VMEM] * 3)(own, near, far)[0]
         for first, far in ((0, far_low), (HALF, far_high))
     )
+    high, grads = lax.optimization_barrier((high, grads))
     low = move(low, lambda b, r: (b - 4 * r, r))
     high = move(high, lambda b, r: (b - 4 * r, r ^ 2))
-    for bit in (2, 1, 16):
-        grads = grads + swap(grads, bit)
-    (send,) = call(gather_kernel, [((ROWS, T + 32, T), BF16)], [VMEM] * 3)(low, high, grads)
+    planes = exchange(jnp.broadcast_to(grads[None], (Z, GRAD, T)), "z")
+    send, grads = call(
+        gather_kernel, [((ROWS, T + 32, T), BF16), ((GRAD, T), F32)], [VMEM] * 3
+    )(low, high, planes)
     got = exchange(send, REP)
     grad_features, grad_weight, grad_bias = call(
         last_kernel,

time: 118 us -> 121 us (1.025)
  blocking collectives: 50.2 us -> 57.2 us
  starting transfers between devices: 30.6 us -> 24.6 us
  waiting for transfers between devices: 19.1 us -> 20.6 us
    ppermute x19 -> x15, starting transfers between devices: 30.6 us -> 19.1 us  [move(): return lax.ppermute(value, BLK + REP, pairs)]
    all_to_all x3, blocking collectives: 50.2 us -> 57.2 us  [exchange(): return lax.all_to_all(value, axes, 0, 0, tiled=True)]
    all_to_all x0 -> x1, starting transfers between devices: none -> 5.59 us  [exchange(): return lax.all_to_all(value, axes, 0, 0, tiled=True)]
    ppermute x19 -> x15, waiting for transfers between devices: 19.1 us -> 20.6 us  [move(): return lax.ppermute(value, BLK + REP, pairs)]
  transfers between devices with their start and end apart: 19 -> 16, of which waited for: 9 -> 5; matrix products, arithmetic and copies ran while one was open for 0% -> 0% of each run, Pallas kernels for 8% -> 7%
where the time goes in v5:
time: 121 us; the launch traced here: 120 us
  blocking collectives  57.2 us (47%)
  starting transfers between devices  24.6 us (20%)
  waiting for transfers between devices  20.6 us (17%)
  Pallas kernels  16.3 us (13%)
    all_to_all x3, blocking collectives, exchange(): return lax.all_to_all(value, axes, 0, 0, tiled=True)  57.2 us
    ppermute x15, waiting for transfers between devices, move(): return lax.ppermute(value, BLK + REP, pairs)  20.6 us
    ppermute x15, starting transfers between devices, move(): return lax.ppermute(value, BLK + REP, pairs)  19.1 us
    all_to_all x1, starting transfers between devices, exchange(): return lax.all_to_all(value, axes, 0, 0, tiled=True)  5.59 us
    pallas_call x1, Pallas kernels, on_device(): call(load_kernel, [(edges.shape, BF16)], [HBM], [pltpu.SemaphoreType.DMA]...  2.82 us
  transfers between devices with their start and end apart: 16, of which 5 were waited for; matrix products, arithmetic and copies ran while one was open for 0% of the time, Pallas kernels for 7%

profile of v5, /device:TPU:32, one launch (start us, length us, event | category | flops | bytes accessed | tf_op | source)
XLA Modules:
  0.0 120.3 jit_solution(11909066741663526181)
XLA Ops:
  0.6 1.7 %shard_map.111 = (bf16[4,128,128]{2,1,0:T(8,128)(2,1)S(1)}, bf16[4,128,128]{2,1,0:T(8,128)(2,1)S(1)}, f32[128,128]{1,0:T(8,128)S(1)}) custom-call(s32[1]{0:T(128)} %bitcast.rep, bf16[1024,128]{1,0:T(8,128)(2,1)} %features.1, s32[8,128]{1,0:T(8,128)} %bitcast.10), custom_call_target="tpu_custom_call" | custom-call | bytes 1048576 | tf_op jit(solution)/shard_map/pallas_call | solution.py:240
  3.0 9.1 %collective-permute-start.2 = (bf16[4,128,128]{2,1,0:T(8,128)(2,1)S(1)}, bf16[4,128,128]{2,1,0:T(8,128)(2,1)S(1)}, u32[]{:S(2)}, u32[]{:S(2)}) collective-permute-start(bf16[4,128,128]{2,1,0:T(8,128)(2,1)S(1)} %get-tuple-element.36), channel_id=1, source_target_pairs={{0,66},{1,99},{2,0},{3,33},{4,198},{5,231},{6,132},{7,165},{8,74},... | collective-permute-start | bytes 393224 | tf_op jit(solution)/shard_map/ppermute | solution.py:225
  12.2 2.8 %shard_map.112.held = bf16[8,4,6,128,128]{4,3,2,1,0:T(8,128)(2,1)S(1)} custom-call(bf16[8,4,6,128,128]{4,3,2,1,0:T(8,128)(2,1)} %edges.1), custom_call_target="tpu_custom_call" | custom-call | bytes 12582912 | tf_op jit(solution)/shard_map/pallas_call | solution.py:248
  15.0 1.7 %collective-permute-start.4 = (bf16[4,128,128]{2,1,0:T(8,128)(2,1)S(1)}, bf16[4,128,128]{2,1,0:T(8,128)(2,1)S(1)}, u32[]{:S(2)}, u32[]{:S(2)}) collective-permute-start(bf16[4,128,128]{2,1,0:T(8,128)(2,1)S(1)} %collective-permute-done.low), channel_id=1, source_target_pairs={{0,16},{1,17},{2,18},{3,19},{4,20},{5,21},{6,22},{7,23},{8,24},{9,... | collective-permute-start | bytes 393224 | tf_op jit(solution)/shard_map/ppermute | solution.py:225
  16.7 2.7 %collective-permute-start.6 = (bf16[4,128,128]{2,1,0:T(8,128)(2,1)S(1)}, bf16[4,128,128]{2,1,0:T(8,128)(2,1)S(1)}, u32[]{:S(2)}, u32[]{:S(2)}) collective-permute-start(bf16[4,128,128]{2,1,0:T(8,128)(2,1)S(1)} %collective-permute-done.2.high), channel_id=1, source_target_pairs={{0,16},{1,17},{2,18},{3,19},{4,20},{5,21},{6,22},{7,23},{8,24},{9,... | collective-permute-start | bytes 393224 | tf_op jit(solution)/shard_map/ppermute | solution.py:225
  19.4 1.5 %shard_map.113.total = f32[8,128,128]{2,1,0:T(8,128)S(1)} custom-call(s32[8,4,8]{2,1,0:T(4,128)S(1)} %pad_add_fusion.meta, bf16[8,4,6,128,128]{4,3,2,1,0:T(8,128)(2,1)S(1)} %shard_map.112.held, bf16[4,128,128]{2,1,0:T(8,128)(2,1)S(1)} %collective-permute-done.low, bf16[4,128,128]{2,1,0:T(8,128)(2,1)S(1)} %collective-permute-done.2.high), custom_call_target="tpu_custom_call" | custom-call | flops 201326592 | bytes 3145728 | tf_op jit(solution)/shard_map/pallas_call | solution.py:256
  21.0 2.4 %collective-permute-done.4.low = bf16[4,128,128]{2,1,0:T(8,128)(2,1)S(1)} collective-permute-done((bf16[4,128,128]{2,1,0:T(8,128)(2,1)S(1)}, bf16[4,128,128]{2,1,0:T(8,128)(2,1)S(1)}, u32[]{:S(2)}, u32[]{:S(2)}) %collective-permute-start.4) | collective-permute-done | bytes 131104 | tf_op jit(solution)/shard_map/ppermute | solution.py:225
  23.4 2.8 %collective-permute-done.6.high = bf16[4,128,128]{2,1,0:T(8,128)(2,1)S(1)} collective-permute-done((bf16[4,128,128]{2,1,0:T(8,128)(2,1)S(1)}, bf16[4,128,128]{2,1,0:T(8,128)(2,1)S(1)}, u32[]{:S(2)}, u32[]{:S(2)}) %collective-permute-start.6) | collective-permute-done | bytes 131104 | tf_op jit(solution)/shard_map/ppermute | solution.py:225
  26.2 1.5 %shard_map.114.total = f32[8,128,128]{2,1,0:T(8,128)S(1)} custom-call(s32[8,4,8]{2,1,0:T(4,128)S(1)} %pad_add_fusion.meta, bf16[8,4,6,128,128]{4,3,2,1,0:T(8,128)(2,1)S(1)} %shard_map.112.held, bf16[4,128,128]{2,1,0:T(8,128)(2,1)S(1)} %collective-permute-done.4.low, bf16[4,128,128]{2,1,0:T(8,128)(2,1)S(1)} %collective-permute-done.6.high, ...), custom_call_target="tpu_custom_call" | custom-call | flops 201326592 | bytes 3145728 | tf_op jit(solution)/shard_map/pallas_call | solution.py:262
  27.7 2.1 %shard_map.115 = bf16[8,128,128]{2,1,0:T(8,128)(2,1)S(1)} custom-call(s32[8,4,8]{2,1,0:T(4,128)S(1)} %pad_add_fusion.meta, bf16[8,4,6,128,128]{4,3,2,1,0:T(8,128)(2,1)S(1)} %shard_map.112.held, bf16[4,128,128]{2,1,0:T(8,128)(2,1)S(1)} %collective-permute-done.1.near_low, bf16[4,128,128]{2,1,0:T(8,128)(2,1)S(1)} %collective-permute-done.3.near_high, ...), custom_call_target="tpu_custom_call" | custom-call | flops 402653184 | bytes 6291456 | tf_op jit(solution)/shard_map/pallas_call | solution.py:265
  29.8 21.0 %all_to_all.20.parts = bf16[8,128,128]{2,1,0:T(8,128)(2,1)S(1)} all-to-all(bf16[8,128,128]{2,1,0:T(8,128)(2,1)S(1)} %shard_map.115), channel_id=1, replica_groups=mesh['z'=8,'yl'=2,'core'=2,'x'=4,'yh'=2] {'x','yh'}, dimensions={0} | all-to-all | bytes 524288 | tf_op jit(solution)/shard_map/all_to_all | solution.py:215
  50.8 0.8 shard_map.116
  51.7 12.2 %all_to_all.21.got = bf16[8,176,128]{2,1,0:T(8,128)(2,1)S(1)} all-to-all(bf16[8,176,128]{2,1,0:T(8,128)(2,1)S(1)} %get-tuple-element.41), channel_id=1, replica_groups=mesh['z'=8,'yl'=2,'core'=2,'x'=4,'yh'=2] {'x','yh'}, dimensions={0} | all-to-all | bytes 720896 | tf_op jit(solution)/shard_map/all_to_all | solution.py:215
  63.8 2.0 %shard_map.118 = (bf16[8,128,128]{2,1,0:T(8,128)(2,1)S(1)}, bf16[1120,128]{1,0:T(8,128)(2,1)S(1)}) custom-call(s32[8,4,8]{2,1,0:T(4,128)S(1)} %pad_add_fusion.meta, bf16[8,4,6,128,128]{4,3,2,1,0:T(8,128)(2,1)S(1)} %shard_map.112.held, bf16[8,176,128]{2,1,0:T(8,128)(2,1)S(1)} %all_to_all.21.got), custom_call_target="tpu_custom_call" | custom-call | flops 402653184 | bytes 6291456 | tf_op jit(solution)/shard_map/pallas_call | solution.py:278
  66.0 1.5 %shard_map.117.far = bf16[8,128,128]{2,1,0:T(8,128)(2,1)S(1)} custom-call(s32[8,4,8]{2,1,0:T(4,128)S(1)} %pad_add_fusion.meta, bf16[8,4,6,128,128]{4,3,2,1,0:T(8,128)(2,1)S(1)} %shard_map.112.held, bf16[8,176,128]{2,1,0:T(8,128)(2,1)S(1)} %all_to_all.21.got), custom_call_target="tpu_custom_call" | custom-call | flops 201326592 | bytes 3145728 | tf_op jit(solution)/shard_map/pallas_call | solution.py:288
  68.1 1.6 %collective-permute-start.9 = (f32[48,128]{1,0:T(8,128)S(1)}, f32[48,128]{1,0:T(8,128)S(1)}, u32[]{:S(2)}, u32[]{:S(2)}) collective-permute-start(f32[48,128]{1,0:T(8,128)S(1)} %get-tuple-element.47), channel_id=1, source_target_pairs={{0,16},{1,17},{2,18},{3,19},{4,20},{5,21},{6,22},{7,23},{8,24},{9,... | collective-permute-start | bytes 73736 | tf_op jit(solution)/shard_map/ppermute | solution.py:225
  69.7 1.5 %shard_map.120.own = f32[8,128,128]{2,1,0:T(8,128)S(1)} custom-call(s32[8,4,8]{2,1,0:T(4,128)S(1)} %pad_add_fusion.meta, bf16[8,4,6,128,128]{4,3,2,1,0:T(8,128)(2,1)S(1)} %shard_map.112.held, bf16[8,176,128]{2,1,0:T(8,128)(2,1)S(1)} %all_to_all.21.got), custom_call_target="tpu_custom_call" | custom-call | flops 201326592 | bytes 3145728 | tf_op jit(solution)/shard_map/pallas_call | solution.py:296
  71.2 2.9 %collective-permute-done.9 = f32[48,128]{1,0:T(8,128)S(1)} collective-permute-done((f32[48,128]{1,0:T(8,128)S(1)}, f32[48,128]{1,0:T(8,128)S(1)}, u32[]{:S(2)}, u32[]{:S(2)}) %collective-permute-start.9) | collective-permute-done | bytes 24608 | tf_op jit(solution)/shard_map/ppermute | solution.py:225
  74.8 5.6 %all-to-all-start.2 = ((f32[8,48,128]{2,1,0:T(8,128)}), f32[8,48,128]{2,1,0:T(8,128)S(1)}, u32[]{:S(2)}, u32[]{:S(2)}) async-start(f32[8,48,128]{2,1,0:T(8,128)} %broadcast_in_dim.25), calls=%async_computation.2 | async-start | bytes 393216 | tf_op jit(solution)/shard_map/all_to_all | solution.py:215
  80.4 1.4 %collective-permute-start.11 = (bf16[4,128,128]{2,1,0:T(8,128)(2,1)S(1)}, bf16[4,128,128]{2,1,0:T(8,128)(2,1)S(1)}, u32[]{:S(2)}, u32[]{:S(2)}) collective-permute-start(bf16[4,128,128]{2,1,0:T(8,128)(2,1)S(1)} %get-tuple-element.50), channel_id=1, source_target_pairs={{0,240},{1,241},{2,242},{3,243},{4,244},{5,245},{6,246},{7,247},{8... | collective-permute-start | bytes 393224 | tf_op jit(solution)/shard_map/ppermute | solution.py:225
  82.4 4.8 %collective-permute-done.11.far = bf16[4,128,128]{2,1,0:T(8,128)(2,1)S(1)} collective-permute-done((bf16[4,128,128]{2,1,0:T(8,128)(2,1)S(1)}, bf16[4,128,128]{2,1,0:T(8,128)(2,1)S(1)}, u32[]{:S(2)}, u32[]{:S(2)}) %collective-permute-start.11) | collective-permute-done | bytes 131104 | tf_op jit(solution)/shard_map/ppermute | solution.py:225
  87.9 7.7 %collective-permute-done.14.high = bf16[4,128,128]{2,1,0:T(8,128)(2,1)S(1)} collective-permute-done((bf16[4,128,128]{2,1,0:T(8,128)(2,1)S(1)}, bf16[4,128,128]{2,1,0:T(8,128)(2,1)S(1)}, u32[]{:S(2)}, u32[]{:S(2)}) %collective-permute-start.14) | collective-permute-done | bytes 131104 | tf_op jit(solution)/shard_map/ppermute | solution.py:225
  95.6 24.0 %all_to_all.22.got = bf16[8,160,128]{2,1,0:T(8,128)(2,1)S(1)} all-to-all(bf16[8,160,128]{2,1,0:T(8,128)(2,1)S(1)} %get-tuple-element.55), channel_id=1, replica_groups=mesh['z'=8,'yl'=2,'core'=2,'x'=4,'yh'=2] {'x','yh'}, dimensions={0} | all-to-all | bytes 655360 | tf_op jit(solution)/shard_map/all_to_all | solution.py:215
  119.6 0.7 shard_map.124
  (40 shorter events, 3.6 us)
Async XLA Ops:
  2.4 12.7 %collective-permute-start = (bf16[4,128,128]{2,1,0:T(8,128)(2,1)S(1)}, bf16[4,128,128]{2,1,0:T(8,128)(2,1)S(1)}, u32[]{:S(2)}, u32[]{:S(2)}) collective-permute-start(bf16[4,128,128]{2,1,0:T(8,128)(2,1)S(1)} %get-tuple-element.32), channel_id=1, source_target_pairs={{0,0},{1,33},{2,66},{3,99},{4,132},{5,165},{6,198},{7,231},{8,8},{... | collective-permute-start | bytes 393224 | tf_op jit(solution)/shard_map/ppermute | solution.py:225
  3.0 13.6 %collective-permute-start.2 = (bf16[4,128,128]{2,1,0:T(8,128)(2,1)S(1)}, bf16[4,128,128]{2,1,0:T(8,128)(2,1)S(1)}, u32[]{:S(2)}, u32[]{:S(2)}) collective-permute-start(bf16[4,128,128]{2,1,0:T(8,128)(2,1)S(1)} %get-tuple-element.36), channel_id=1, source_target_pairs={{0,66},{1,99},{2,0},{3,33},{4,198},{5,231},{6,132},{7,165},{8,74},... | collective-permute-start | bytes 393224 | tf_op jit(solution)/shard_map/ppermute | solution.py:225
  12.1 2.8 %copy-start.3 = (s32[8,4,6]{0,1,2:T(4,128)S(1)}, s32[8,4,6]{0,1,2:T(4,128)}, u32[]{:S(2)}) copy-start(s32[8,4,6]{0,1,2:T(4,128)} %param.10) | copy-start | bytes 2308
  12.2 2.9 %copy-start.4 = (s32[8,4]{0,1:T(4,128)S(1)}, s32[8,4]{0,1:T(4,128)}, u32[]{:S(2)}) copy-start(s32[8,4]{0,1:T(4,128)} %param.11) | copy-start | bytes 388
  15.0 8.3 %collective-permute-start.4 = (bf16[4,128,128]{2,1,0:T(8,128)(2,1)S(1)}, bf16[4,128,128]{2,1,0:T(8,128)(2,1)S(1)}, u32[]{:S(2)}, u32[]{:S(2)}) collective-permute-start(bf16[4,128,128]{2,1,0:T(8,128)(2,1)S(1)} %collective-permute-done.low), channel_id=1, source_target_pairs={{0,16},{1,17},{2,18},{3,19},{4,20},{5,21},{6,22},{7,23},{8,24},{9,... | collective-permute-start | bytes 393224 | tf_op jit(solution)/shard_map/ppermute | solution.py:225
  16.7 9.5 %collective-permute-start.6 = (bf16[4,128,128]{2,1,0:T(8,128)(2,1)S(1)}, bf16[4,128,128]{2,1,0:T(8,128)(2,1)S(1)}, u32[]{:S(2)}, u32[]{:S(2)}) collective-permute-start(bf16[4,128,128]{2,1,0:T(8,128)(2,1)S(1)} %collective-permute-done.2.high), channel_id=1, source_target_pairs={{0,16},{1,17},{2,18},{3,19},{4,20},{5,21},{6,22},{7,23},{8,24},{9,... | collective-permute-start | bytes 393224 | tf_op jit(solution)/shard_map/ppermute | solution.py:225
  19.4 8.3 %collective-permute-start.1 = (bf16[4,128,128]{2,1,0:T(8,128)(2,1)S(1)}, bf16[4,128,128]{2,1,0:T(8,128)(2,1)S(1)}, u32[]{:S(2)}, u32[]{:S(2)}) collective-permute-start(bf16[4,128,128]{2,1,0:T(8,128)(2,1)S(1)} %collective-permute-done.low), channel_id=1, source_target_pairs={{0,8},{1,9},{2,10},{3,11},{4,12},{5,13},{6,14},{7,15},{8,32},{9,33... | collective-permute-start | bytes 393224 | tf_op jit(solution)/shard_map/ppermute | solution.py:225
  20.9 29.9 %copy-start = (bf16[128,256]{1,0:T(8,128)(2,1)S(1)}, bf16[128,256]{1,0:T(8,128)(2,1)}, u32[]{:S(2)}) copy-start(bf16[128,256]{1,0:T(8,128)(2,1)} %weight.1) | copy-start | bytes 196612
  20.9 29.9 %copy-start.1 = (bf16[128,256]{1,0:T(8,128)(2,1)S(1)}, bf16[128,256]{1,0:T(8,128)(2,1)}, u32[]{:S(2)}) copy-start(bf16[128,256]{1,0:T(8,128)(2,1)} %cot.1) | copy-start | bytes 196612
  20.9 29.9 %copy-start.2 = (f32[256]{0:T(256)S(1)}, f32[256]{0:T(256)}, u32[]{:S(2)}) copy-start(f32[256]{0:T(256)} %param.14) | copy-start | bytes 3076
  20.9 6.7 %collective-permute-start.3 = (bf16[4,128,128]{2,1,0:T(8,128)(2,1)S(1)}, bf16[4,128,128]{2,1,0:T(8,128)(2,1)S(1)}, u32[]{:S(2)}, u32[]{:S(2)}) collective-permute-start(bf16[4,128,128]{2,1,0:T(8,128)(2,1)S(1)} %collective-permute-done.2.high), channel_id=1, source_target_pairs={{0,8},{1,9},{2,10},{3,11},{4,12},{5,13},{6,14},{7,15},{8,32},{9,33... | collective-permute-start | bytes 393224 | tf_op jit(solution)/shard_map/ppermute | solution.py:225
  23.4 4.3 %collective-permute-start.5 = (bf16[4,128,128]{2,1,0:T(8,128)(2,1)S(1)}, bf16[4,128,128]{2,1,0:T(8,128)(2,1)S(1)}, u32[]{:S(2)}, u32[]{:S(2)}) collective-permute-start(bf16[4,128,128]{2,1,0:T(8,128)(2,1)S(1)} %collective-permute-done.4.low), channel_id=1, source_target_pairs={{0,8},{1,9},{2,10},{3,11},{4,12},{5,13},{6,14},{7,15},{8,0},{9,1},... | collective-permute-start | bytes 393224 | tf_op jit(solution)/shard_map/ppermute | solution.py:225
  26.2 1.5 %collective-permute-start.7 = (bf16[4,128,128]{2,1,0:T(8,128)(2,1)S(1)}, bf16[4,128,128]{2,1,0:T(8,128)(2,1)S(1)}, u32[]{:S(2)}, u32[]{:S(2)}) collective-permute-start(bf16[4,128,128]{2,1,0:T(8,128)(2,1)S(1)} %collective-permute-done.6.high), channel_id=1, source_target_pairs={{0,8},{1,9},{2,10},{3,11},{4,12},{5,13},{6,14},{7,15},{8,0},{9,1},... | collective-permute-start | bytes 393224 | tf_op jit(solution)/shard_map/ppermute | solution.py:225
  65.9 1.7 %collective-permute-start.8 = (bf16[1120,128]{1,0:T(8,128)(2,1)S(1)}, bf16[1120,128]{1,0:T(8,128)(2,1)S(1)}, u32[]{:S(2)}, u32[]{:S(2)}) collective-permute-start(bf16[1120,128]{1,0:T(8,128)(2,1)S(1)} %get-tuple-element.42.mine), channel_id=1, source_target_pairs={{0,8},{1,9},{2,10},{3,11},{4,12},{5,13},{6,14},{7,15},{8,0},{9,1},... | collective-permute-start | bytes 860168 | tf_op jit(solution)/shard_map/ppermute | solution.py:225
  66.0 8.1 %collective-permute-start.10 = (bf16[8,128,128]{2,1,0:T(8,128)(2,1)S(1)}, bf16[8,128,128]{2,1,0:T(8,128)(2,1)S(1)}, u32[]{:S(2)}, u32[]{:S(2)}) collective-permute-start(bf16[8,128,128]{2,1,0:T(8,128)(2,1)S(1)} %get-tuple-element.49), channel_id=1, source_target_pairs={{0,232},{1,233},{2,234},{3,235},{4,236},{5,237},{6,238},{7,239},{8... | collective-permute-start | bytes 786440 | tf_op jit(solution)/shard_map/ppermute | solution.py:225
  67.6 6.5 %collective-permute-start.13 = (bf16[4,128,128]{2,1,0:T(8,128)(2,1)S(1)}, bf16[4,128,128]{2,1,0:T(8,128)(2,1)S(1)}, u32[]{:S(2)}, u32[]{:S(2)}) collective-permute-start(bf16[4,128,128]{2,1,0:T(8,128)(2,1)S(1)} %get-tuple-element.51), channel_id=1, source_target_pairs={{0,240},{1,241},{2,242},{3,243},{4,244},{5,245},{6,246},{7,247},{8... | collective-permute-start | bytes 393224 | tf_op jit(solution)/shard_map/ppermute | solution.py:225
  68.1 6.0 %collective-permute-start.9 = (f32[48,128]{1,0:T(8,128)S(1)}, f32[48,128]{1,0:T(8,128)S(1)}, u32[]{:S(2)}, u32[]{:S(2)}) collective-permute-start(f32[48,128]{1,0:T(8,128)S(1)} %get-tuple-element.47), channel_id=1, source_target_pairs={{0,16},{1,17},{2,18},{3,19},{4,20},{5,21},{6,22},{7,23},{8,24},{9,... | collective-permute-start | bytes 73736 | tf_op jit(solution)/shard_map/ppermute | solution.py:225
  74.8 20.8 %all-to-all-start.2 = ((f32[8,48,128]{2,1,0:T(8,128)}), f32[8,48,128]{2,1,0:T(8,128)S(1)}, u32[]{:S(2)}, u32[]{:S(2)}) async-start(f32[8,48,128]{2,1,0:T(8,128)} %broadcast_in_dim.25), calls=%async_computation.2 | async-start | bytes 393216 | tf_op jit(solution)/shard_map/all_to_all | solution.py:215
  80.4 6.7 %collective-permute-start.11 = (bf16[4,128,128]{2,1,0:T(8,128)(2,1)S(1)}, bf16[4,128,128]{2,1,0:T(8,128)(2,1)S(1)}, u32[]{:S(2)}, u32[]{:S(2)}) collective-permute-start(bf16[4,128,128]{2,1,0:T(8,128)(2,1)S(1)} %get-tuple-element.50), channel_id=1, source_target_pairs={{0,240},{1,241},{2,242},{3,243},{4,244},{5,245},{6,246},{7,247},{8... | collective-permute-start | bytes 393224 | tf_op jit(solution)/shard_map/ppermute | solution.py:225
  81.8 13.7 %collective-permute-start.14 = (bf16[4,128,128]{2,1,0:T(8,128)(2,1)S(1)}, bf16[4,128,128]{2,1,0:T(8,128)(2,1)S(1)}, u32[]{:S(2)}, u32[]{:S(2)}) collective-permute-start(bf16[4,128,128]{2,1,0:T(8,128)(2,1)S(1)} %shard_map.122), channel_id=1, source_target_pairs={{0,2},{1,227},{2,192},{3,161},{4,134},{5,103},{6,68},{7,37},{8,10}... | collective-permute-start | bytes 393224 | tf_op jit(solution)/shard_map/ppermute | solution.py:225
  87.2 8.4 %collective-permute-start.12 = (bf16[4,128,128]{2,1,0:T(8,128)(2,1)S(1)}, bf16[4,128,128]{2,1,0:T(8,128)(2,1)S(1)}, u32[]{:S(2)}, u32[]{:S(2)}) collective-permute-start(bf16[4,128,128]{2,1,0:T(8,128)(2,1)S(1)} %shard_map.121), channel_id=1, source_target_pairs={{0,0},{1,225},{2,194},{3,163},{4,132},{5,101},{6,70},{7,39},{8,8},... | collective-permute-start | bytes 393224 | tf_op jit(solution)/shard_map/ppermute | solution.py:225

commit v6 on v5

--- a/solution.py
+++ b/solution.py
@@ -18,6 +18,7 @@
 HALF = ROWS // 2
 NODES = ROWS * T
 GRAD = 48
+SWAP = 96
 F32 = jnp.float32
 BF16 = jnp.bfloat16
 
@@ -163,7 +164,8 @@
         half = low if j < HALF else high
         rows = other[j * T : (j + 1) * T].astype(F32)
         half[j % HALF] = (far[j].astype(F32) + rows).astype(BF16)
-    grads[...] = grads_of(mine) + grads_of(other)
+    grads[0:GRAD] = grads_of(mine) + grads_of(other)
+    grads[GRAD:] = jnp.zeros((SWAP - GRAD, T), F32)
 
 
 def half_kernel(first, own, near, far, out):
@@ -172,12 +174,8 @@
     out[...] = total.astype(BF16)
 
 
-def gather_kernel(low, high, planes, out, grads):
-    total = planes[0]
-    for p in range(1, Z):
-        total += planes[p]
-    grads[...] = total
-    mine = total[0:32].astype(BF16)
+def gather_kernel(low, high, grads, out):
+    mine = grads[0:32].astype(BF16)
     for j in range(ROWS):
         out[j, 0:T] = low[j] if j < HALF else high[j - HALF]
         out[j, T:] = mine
@@ -289,7 +287,7 @@
         meta, held, got
     )
     far_low, far_high, grads = call(
-        near_kernel, [(half, BF16), (half, BF16), ((GRAD, T), F32)], [VMEM] * 3
+        near_kernel, [(half, BF16), (half, BF16), ((SWAP, T), F32)], [VMEM] * 3
     )(far, mine, other)
     far_low, far_high, got, grads = lax.optimization_barrier((far_low, far_high, got, grads))
     far_low, far_high = (move(v, lambda b, r: (b - 2, r)) for v in (far_low, far_high))
@@ -302,13 +300,11 @@
         call(functools.partial(half_kernel, first), [(half, BF16)], [VMEM] * 3)(own, near, far)[0]
         for first, far in ((0, far_low), (HALF, far_high))
     )
-    high, grads = lax.optimization_barrier((high, grads))
     low = move(low, lambda b, r: (b - 4 * r, r))
     high = move(high, lambda b, r: (b - 4 * r, r ^ 2))
-    planes = exchange(jnp.broadcast_to(grads[None], (Z, GRAD, T)), "z")
-    send, grads = call(
-        gather_kernel, [((ROWS, T + 32, T), BF16), ((GRAD, T), F32)], [VMEM] * 3
-    )(low, high, planes)
+    for bit in (16, 4, 8):
+        grads = grads + swap(grads, bit)
+    (send,) = call(gather_kernel, [((ROWS, T + 32, T), BF16)], [VMEM] * 3)(low, high, grads)
     got = exchange(send, REP)
     grad_features, grad_weight, grad_bias = call(
         last_kernel,

time: 121 us -> 122 us (level)
  starting transfers between devices: 24.6 us -> 28.2 us
    ppermute x15 -> x18, starting transfers between devices: 19.1 us -> 28.2 us  [move(): return lax.ppermute(value, BLK + REP, pairs)]
    all_to_all x1 -> x0, starting transfers between devices: 5.59 us -> none  [exchange(): return lax.all_to_all(value, axes, 0, 0, tiled=True)]
    ppermute x15 -> x18, waiting for transfers between devices: 20.6 us -> 19.8 us  [move(): return lax.ppermute(value, BLK + REP, pairs)]
  transfers between devices with their start and end apart: 16 -> 18, of which waited for: 5 -> 8; matrix products, arithmetic and copies ran while one was open for 0% -> 0% of each run, Pallas kernels for 7% -> 7%
where the time goes in v6:
time: 122 us; the launch traced here: 121 us
  blocking collectives  56 us (46%)
  starting transfers between devices  28.2 us (23%)
  waiting for transfers between devices  19.8 us (16%)
  Pallas kernels  16.3 us (13%)
    all_to_all x3, blocking collectives, exchange(): return lax.all_to_all(value, axes, 0, 0, tiled=True)  56 us
    ppermute x18, starting transfers between devices, move(): return lax.ppermute(value, BLK + REP, pairs)  28.2 us
    ppermute x18, waiting for transfers between devices, move(): return lax.ppermute(value, BLK + REP, pairs)  19.8 us
    pallas_call x1, Pallas kernels, on_device(): call(load_kernel, [(edges.shape, BF16)], [HBM], [pltpu.SemaphoreType.DMA]...  2.82 us
  transfers between devices with their start and end apart: 18, of which 8 were waited for; matrix products, arithmetic and copies ran while one was open for 0% of the time, Pallas kernels for 7%

profile of v6, /device:TPU:32, one launch (start us, length us, event | category | flops | bytes accessed | tf_op | source)
XLA Modules:
  0.0 121.2 jit_solution(6306936390529245639)
XLA Ops:
  0.6 1.7 %shard_map.111 = (bf16[4,128,128]{2,1,0:T(8,128)(2,1)S(1)}, bf16[4,128,128]{2,1,0:T(8,128)(2,1)S(1)}, f32[128,128]{1,0:T(8,128)S(1)}) custom-call(s32[1]{0:T(128)} %bitcast.rep, bf16[1024,128]{1,0:T(8,128)(2,1)} %features.1, s32[8,128]{1,0:T(8,128)} %bitcast.10), custom_call_target="tpu_custom_call" | custom-call | bytes 1048576 | tf_op jit(solution)/shard_map/pallas_call | solution.py:238
  3.0 9.1 %collective-permute-start.2 = (bf16[4,128,128]{2,1,0:T(8,128)(2,1)S(1)}, bf16[4,128,128]{2,1,0:T(8,128)(2,1)S(1)}, u32[]{:S(2)}, u32[]{:S(2)}) collective-permute-start(bf16[4,128,128]{2,1,0:T(8,128)(2,1)S(1)} %get-tuple-element.32), channel_id=1, source_target_pairs={{0,66},{1,99},{2,0},{3,33},{4,198},{5,231},{6,132},{7,165},{8,74},... | collective-permute-start | bytes 393224 | tf_op jit(solution)/shard_map/ppermute | solution.py:223
  12.2 2.8 %shard_map.112.held = bf16[8,4,6,128,128]{4,3,2,1,0:T(8,128)(2,1)S(1)} custom-call(bf16[8,4,6,128,128]{4,3,2,1,0:T(8,128)(2,1)} %edges.1), custom_call_target="tpu_custom_call" | custom-call | bytes 12582912 | tf_op jit(solution)/shard_map/pallas_call | solution.py:246
  15.0 1.6 %collective-permute-done.2.high = bf16[4,128,128]{2,1,0:T(8,128)(2,1)S(1)} collective-permute-done((bf16[4,128,128]{2,1,0:T(8,128)(2,1)S(1)}, bf16[4,128,128]{2,1,0:T(8,128)(2,1)S(1)}, u32[]{:S(2)}, u32[]{:S(2)}) %collective-permute-start.2) | collective-permute-done | bytes 131104 | tf_op jit(solution)/shard_map/ppermute | solution.py:223
  16.7 2.0 %collective-permute-start.6 = (bf16[4,128,128]{2,1,0:T(8,128)(2,1)S(1)}, bf16[4,128,128]{2,1,0:T(8,128)(2,1)S(1)}, u32[]{:S(2)}, u32[]{:S(2)}) collective-permute-start(bf16[4,128,128]{2,1,0:T(8,128)(2,1)S(1)} %collective-permute-done.2.high), channel_id=1, source_target_pairs={{0,16},{1,17},{2,18},{3,19},{4,20},{5,21},{6,22},{7,23},{8,24},{9,... | collective-permute-start | bytes 393224 | tf_op jit(solution)/shard_map/ppermute | solution.py:223
  19.9 1.5 %shard_map.113.total = f32[8,128,128]{2,1,0:T(8,128)S(1)} custom-call(s32[8,4,8]{2,1,0:T(4,128)S(1)} %pad_add_fusion.meta, bf16[8,4,6,128,128]{4,3,2,1,0:T(8,128)(2,1)S(1)} %shard_map.112.held, bf16[4,128,128]{2,1,0:T(8,128)(2,1)S(1)} %collective-permute-done.low, bf16[4,128,128]{2,1,0:T(8,128)(2,1)S(1)} %collective-permute-done.2.high), custom_call_target="tpu_custom_call" | custom-call | flops 201326592 | bytes 3145728 | tf_op jit(solution)/shard_map/pallas_call | solution.py:254
  22.3 2.1 %collective-permute-done.6.high = bf16[4,128,128]{2,1,0:T(8,128)(2,1)S(1)} collective-permute-done((bf16[4,128,128]{2,1,0:T(8,128)(2,1)S(1)}, bf16[4,128,128]{2,1,0:T(8,128)(2,1)S(1)}, u32[]{:S(2)}, u32[]{:S(2)}) %collective-permute-start.6) | collective-permute-done | bytes 131104 | tf_op jit(solution)/shard_map/ppermute | solution.py:223
  24.3 2.8 %collective-permute-done.4.low = bf16[4,128,128]{2,1,0:T(8,128)(2,1)S(1)} collective-permute-done((bf16[4,128,128]{2,1,0:T(8,128)(2,1)S(1)}, bf16[4,128,128]{2,1,0:T(8,128)(2,1)S(1)}, u32[]{:S(2)}, u32[]{:S(2)}) %collective-permute-start.4) | collective-permute-done | bytes 131104 | tf_op jit(solution)/shard_map/ppermute | solution.py:223
  27.1 1.5 %shard_map.114.total = f32[8,128,128]{2,1,0:T(8,128)S(1)} custom-call(s32[8,4,8]{2,1,0:T(4,128)S(1)} %pad_add_fusion.meta, bf16[8,4,6,128,128]{4,3,2,1,0:T(8,128)(2,1)S(1)} %shard_map.112.held, bf16[4,128,128]{2,1,0:T(8,128)(2,1)S(1)} %collective-permute-done.4.low, bf16[4,128,128]{2,1,0:T(8,128)(2,1)S(1)} %collective-permute-done.6.high, ...), custom_call_target="tpu_custom_call" | custom-call | flops 201326592 | bytes 3145728 | tf_op jit(solution)/shard_map/pallas_call | solution.py:260
  28.7 2.1 %shard_map.115 = bf16[8,128,128]{2,1,0:T(8,128)(2,1)S(1)} custom-call(s32[8,4,8]{2,1,0:T(4,128)S(1)} %pad_add_fusion.meta, bf16[8,4,6,128,128]{4,3,2,1,0:T(8,128)(2,1)S(1)} %shard_map.112.held, bf16[4,128,128]{2,1,0:T(8,128)(2,1)S(1)} %collective-permute-done.1.near_low, bf16[4,128,128]{2,1,0:T(8,128)(2,1)S(1)} %collective-permute-done.3.near_high, ...), custom_call_target="tpu_custom_call" | custom-call | flops 402653184 | bytes 6291456 | tf_op jit(solution)/shard_map/pallas_call | solution.py:263
  30.8 22.1 %all_to_all.15.parts = bf16[8,128,128]{2,1,0:T(8,128)(2,1)S(1)} all-to-all(bf16[8,128,128]{2,1,0:T(8,128)(2,1)S(1)} %shard_map.115), channel_id=1, replica_groups=mesh['z'=8,'yl'=2,'core'=2,'x'=4,'yh'=2] {'x','yh'}, dimensions={0} | all-to-all | bytes 524288 | tf_op jit(solution)/shard_map/all_to_all | solution.py:213
  53.7 12.2 %all_to_all.16.got = bf16[8,176,128]{2,1,0:T(8,128)(2,1)S(1)} all-to-all(bf16[8,176,128]{2,1,0:T(8,128)(2,1)S(1)} %get-tuple-element.37), channel_id=1, replica_groups=mesh['z'=8,'yl'=2,'core'=2,'x'=4,'yh'=2] {'x','yh'}, dimensions={0} | all-to-all | bytes 720896 | tf_op jit(solution)/shard_map/all_to_all | solution.py:213
  65.9 2.0 %shard_map.118 = (bf16[8,128,128]{2,1,0:T(8,128)(2,1)S(1)}, bf16[1120,128]{1,0:T(8,128)(2,1)S(1)}) custom-call(s32[8,4,8]{2,1,0:T(4,128)S(1)} %pad_add_fusion.meta, bf16[8,4,6,128,128]{4,3,2,1,0:T(8,128)(2,1)S(1)} %shard_map.112.held, bf16[8,176,128]{2,1,0:T(8,128)(2,1)S(1)} %all_to_all.16.got), custom_call_target="tpu_custom_call" | custom-call | flops 402653184 | bytes 6291456 | tf_op jit(solution)/shard_map/pallas_call | solution.py:276
  68.6 1.5 %shard_map.117.far = bf16[8,128,128]{2,1,0:T(8,128)(2,1)S(1)} custom-call(s32[8,4,8]{2,1,0:T(4,128)S(1)} %pad_add_fusion.meta, bf16[8,4,6,128,128]{4,3,2,1,0:T(8,128)(2,1)S(1)} %shard_map.112.held, bf16[8,176,128]{2,1,0:T(8,128)(2,1)S(1)} %all_to_all.16.got), custom_call_target="tpu_custom_call" | custom-call | flops 201326592 | bytes 3145728 | tf_op jit(solution)/shard_map/pallas_call | solution.py:286
  70.9 3.0 %collective-permute-start.13 = (bf16[4,128,128]{2,1,0:T(8,128)(2,1)S(1)}, bf16[4,128,128]{2,1,0:T(8,128)(2,1)S(1)}, u32[]{:S(2)}, u32[]{:S(2)}) collective-permute-start(bf16[4,128,128]{2,1,0:T(8,128)(2,1)S(1)} %get-tuple-element.47), channel_id=1, source_target_pairs={{0,240},{1,241},{2,242},{3,243},{4,244},{5,245},{6,246},{7,247},{8... | collective-permute-start | bytes 393224 | tf_op jit(solution)/shard_map/ppermute | solution.py:223
  73.9 1.5 %shard_map.120.own = f32[8,128,128]{2,1,0:T(8,128)S(1)} custom-call(s32[8,4,8]{2,1,0:T(4,128)S(1)} %pad_add_fusion.meta, bf16[8,4,6,128,128]{4,3,2,1,0:T(8,128)(2,1)S(1)} %shard_map.112.held, bf16[8,176,128]{2,1,0:T(8,128)(2,1)S(1)} %all_to_all.16.got), custom_call_target="tpu_custom_call" | custom-call | flops 201326592 | bytes 3145728 | tf_op jit(solution)/shard_map/pallas_call | solution.py:294
  75.5 4.0 %collective-permute-done.9 = f32[96,128]{1,0:T(8,128)S(1)} collective-permute-done((f32[96,128]{1,0:T(8,128)S(1)}, f32[96,128]{1,0:T(8,128)S(1)}, u32[]{:S(2)}, u32[]{:S(2)}) %collective-permute-start.9) | collective-permute-done | bytes 49184 | tf_op jit(solution)/shard_map/ppermute | solution.py:223
  79.5 2.7 %collective-permute-start.15 = (f32[96,128]{1,0:T(8,128)S(1)}, f32[96,128]{1,0:T(8,128)S(1)}, u32[]{:S(2)}, u32[]{:S(2)}) collective-permute-start(f32[96,128]{1,0:T(8,128)S(1)} %add.16), channel_id=1, source_target_pairs={{0,128},{1,129},{2,130},{3,131},{4,132},{5,133},{6,134},{7,135},{8... | collective-permute-start | bytes 147464 | tf_op jit(solution)/shard_map/ppermute | solution.py:223
  83.0 4.0 %collective-permute-start.14 = (bf16[4,128,128]{2,1,0:T(8,128)(2,1)S(1)}, bf16[4,128,128]{2,1,0:T(8,128)(2,1)S(1)}, u32[]{:S(2)}, u32[]{:S(2)}) collective-permute-start(bf16[4,128,128]{2,1,0:T(8,128)(2,1)S(1)} %shard_map.122), channel_id=1, source_target_pairs={{0,2},{1,227},{2,192},{3,161},{4,134},{5,103},{6,68},{7,37},{8,10}... | collective-permute-start | bytes 393224 | tf_op jit(solution)/shard_map/ppermute | solution.py:223
  88.4 3.6 %collective-permute-done.16 = f32[96,128]{1,0:T(8,128)S(1)} collective-permute-done((f32[96,128]{1,0:T(8,128)S(1)}, f32[96,128]{1,0:T(8,128)S(1)}, u32[]{:S(2)}, u32[]{:S(2)}) %collective-permute-start.16) | collective-permute-done | bytes 49184 | tf_op jit(solution)/shard_map/ppermute | solution.py:223
  92.0 1.5 %collective-permute-start.17 = (f32[96,128]{1,0:T(8,128)S(1)}, f32[96,128]{1,0:T(8,128)S(1)}, u32[]{:S(2)}, u32[]{:S(2)}) collective-permute-start(f32[96,128]{1,0:T(8,128)S(1)} %add.18), channel_id=1, source_target_pairs={{0,64},{1,65},{2,66},{3,67},{4,68},{5,69},{6,70},{7,71},{8,72},{9,... | collective-permute-start | bytes 147464 | tf_op jit(solution)/shard_map/ppermute | solution.py:223
  93.6 3.5 %collective-permute-done.17 = f32[96,128]{1,0:T(8,128)S(1)} collective-permute-done((f32[96,128]{1,0:T(8,128)S(1)}, f32[96,128]{1,0:T(8,128)S(1)}, u32[]{:S(2)}, u32[]{:S(2)}) %collective-permute-start.17) | collective-permute-done | bytes 49184 | tf_op jit(solution)/shard_map/ppermute | solution.py:223
  97.1 1.6 %collective-permute-done.14.high = bf16[4,128,128]{2,1,0:T(8,128)(2,1)S(1)} collective-permute-done((bf16[4,128,128]{2,1,0:T(8,128)(2,1)S(1)}, bf16[4,128,128]{2,1,0:T(8,128)(2,1)S(1)}, u32[]{:S(2)}, u32[]{:S(2)}) %collective-permute-start.14) | collective-permute-done | bytes 131104 | tf_op jit(solution)/shard_map/ppermute | solution.py:223
  98.8 21.7 %all_to_all.17.got = bf16[8,160,128]{2,1,0:T(8,128)(2,1)S(1)} all-to-all(bf16[8,160,128]{2,1,0:T(8,128)(2,1)S(1)} %shard_map.123), channel_id=1, replica_groups=mesh['z'=8,'yl'=2,'core'=2,'x'=4,'yh'=2] {'x','yh'}, dimensions={0} | all-to-all | bytes 655360 | tf_op jit(solution)/shard_map/all_to_all | solution.py:213
  (46 shorter events, 8.1 us)
Async XLA Ops:
  2.4 12.7 %collective-permute-start = (bf16[4,128,128]{2,1,0:T(8,128)(2,1)S(1)}, bf16[4,128,128]{2,1,0:T(8,128)(2,1)S(1)}, u32[]{:S(2)}, u32[]{:S(2)}) collective-permute-start(bf16[4,128,128]{2,1,0:T(8,128)(2,1)S(1)} %get-tuple-element.28), channel_id=1, source_target_pairs={{0,0},{1,33},{2,66},{3,99},{4,132},{5,165},{6,198},{7,231},{8,8},{... | collective-permute-start | bytes 393224 | tf_op jit(solution)/shard_map/ppermute | solution.py:223
  3.0 13.6 %collective-permute-start.2 = (bf16[4,128,128]{2,1,0:T(8,128)(2,1)S(1)}, bf16[4,128,128]{2,1,0:T(8,128)(2,1)S(1)}, u32[]{:S(2)}, u32[]{:S(2)}) collective-permute-start(bf16[4,128,128]{2,1,0:T(8,128)(2,1)S(1)} %get-tuple-element.32), channel_id=1, source_target_pairs={{0,66},{1,99},{2,0},{3,33},{4,198},{5,231},{6,132},{7,165},{8,74},... | collective-permute-start | bytes 393224 | tf_op jit(solution)/shard_map/ppermute | solution.py:223
  12.1 2.8 %copy-start.3 = (s32[8,4,6]{0,1,2:T(4,128)S(1)}, s32[8,4,6]{0,1,2:T(4,128)}, u32[]{:S(2)}) copy-start(s32[8,4,6]{0,1,2:T(4,128)} %param.10) | copy-start | bytes 2308
  12.2 2.9 %copy-start.4 = (s32[8,4]{0,1:T(4,128)S(1)}, s32[8,4]{0,1:T(4,128)}, u32[]{:S(2)}) copy-start(s32[8,4]{0,1:T(4,128)} %param.11) | copy-start | bytes 388
  16.7 7.7 %collective-permute-start.6 = (bf16[4,128,128]{2,1,0:T(8,128)(2,1)S(1)}, bf16[4,128,128]{2,1,0:T(8,128)(2,1)S(1)}, u32[]{:S(2)}, u32[]{:S(2)}) collective-permute-start(bf16[4,128,128]{2,1,0:T(8,128)(2,1)S(1)} %collective-permute-done.2.high), channel_id=1, source_target_pairs={{0,16},{1,17},{2,18},{3,19},{4,20},{5,21},{6,22},{7,23},{8,24},{9,... | collective-permute-start | bytes 393224 | tf_op jit(solution)/shard_map/ppermute | solution.py:223
  18.7 8.5 %collective-permute-start.4 = (bf16[4,128,128]{2,1,0:T(8,128)(2,1)S(1)}, bf16[4,128,128]{2,1,0:T(8,128)(2,1)S(1)}, u32[]{:S(2)}, u32[]{:S(2)}) collective-permute-start(bf16[4,128,128]{2,1,0:T(8,128)(2,1)S(1)} %collective-permute-done.low), channel_id=1, source_target_pairs={{0,16},{1,17},{2,18},{3,19},{4,20},{5,21},{6,22},{7,23},{8,24},{9,... | collective-permute-start | bytes 393224 | tf_op jit(solution)/shard_map/ppermute | solution.py:223
  19.9 8.7 %collective-permute-start.1 = (bf16[4,128,128]{2,1,0:T(8,128)(2,1)S(1)}, bf16[4,128,128]{2,1,0:T(8,128)(2,1)S(1)}, u32[]{:S(2)}, u32[]{:S(2)}) collective-permute-start(bf16[4,128,128]{2,1,0:T(8,128)(2,1)S(1)} %collective-permute-done.low), channel_id=1, source_target_pairs={{0,8},{1,9},{2,10},{3,11},{4,12},{5,13},{6,14},{7,15},{8,32},{9,33... | collective-permute-start | bytes 393224 | tf_op jit(solution)/shard_map/ppermute | solution.py:223
  21.4 31.4 %copy-start = (bf16[128,256]{1,0:T(8,128)(2,1)S(1)}, bf16[128,256]{1,0:T(8,128)(2,1)}, u32[]{:S(2)}) copy-start(bf16[128,256]{1,0:T(8,128)(2,1)} %weight.1) | copy-start | bytes 196612
  21.5 31.4 %copy-start.1 = (bf16[128,256]{1,0:T(8,128)(2,1)S(1)}, bf16[128,256]{1,0:T(8,128)(2,1)}, u32[]{:S(2)}) copy-start(bf16[128,256]{1,0:T(8,128)(2,1)} %cot.1) | copy-start | bytes 196612
  21.5 31.4 %copy-start.2 = (f32[256]{0:T(256)S(1)}, f32[256]{0:T(256)}, u32[]{:S(2)}) copy-start(f32[256]{0:T(256)} %param.14) | copy-start | bytes 3076
  21.5 7.2 %collective-permute-start.3 = (bf16[4,128,128]{2,1,0:T(8,128)(2,1)S(1)}, bf16[4,128,128]{2,1,0:T(8,128)(2,1)S(1)}, u32[]{:S(2)}, u32[]{:S(2)}) collective-permute-start(bf16[4,128,128]{2,1,0:T(8,128)(2,1)S(1)} %collective-permute-done.2.high), channel_id=1, source_target_pairs={{0,8},{1,9},{2,10},{3,11},{4,12},{5,13},{6,14},{7,15},{8,32},{9,33... | collective-permute-start | bytes 393224 | tf_op jit(solution)/shard_map/ppermute | solution.py:223
  24.3 4.3 %collective-permute-start.7 = (bf16[4,128,128]{2,1,0:T(8,128)(2,1)S(1)}, bf16[4,128,128]{2,1,0:T(8,128)(2,1)S(1)}, u32[]{:S(2)}, u32[]{:S(2)}) collective-permute-start(bf16[4,128,128]{2,1,0:T(8,128)(2,1)S(1)} %collective-permute-done.6.high), channel_id=1, source_target_pairs={{0,8},{1,9},{2,10},{3,11},{4,12},{5,13},{6,14},{7,15},{8,0},{9,1},... | collective-permute-start | bytes 393224 | tf_op jit(solution)/shard_map/ppermute | solution.py:223
  27.1 1.5 %collective-permute-start.5 = (bf16[4,128,128]{2,1,0:T(8,128)(2,1)S(1)}, bf16[4,128,128]{2,1,0:T(8,128)(2,1)S(1)}, u32[]{:S(2)}, u32[]{:S(2)}) collective-permute-start(bf16[4,128,128]{2,1,0:T(8,128)(2,1)S(1)} %collective-permute-done.4.low), channel_id=1, source_target_pairs={{0,8},{1,9},{2,10},{3,11},{4,12},{5,13},{6,14},{7,15},{8,0},{9,1},... | collective-permute-start | bytes 393224 | tf_op jit(solution)/shard_map/ppermute | solution.py:223
  67.9 2.2 %collective-permute-start.8 = (bf16[1120,128]{1,0:T(8,128)(2,1)S(1)}, bf16[1120,128]{1,0:T(8,128)(2,1)S(1)}, u32[]{:S(2)}, u32[]{:S(2)}) collective-permute-start(bf16[1120,128]{1,0:T(8,128)(2,1)S(1)} %get-tuple-element.38.mine), channel_id=1, source_target_pairs={{0,8},{1,9},{2,10},{3,11},{4,12},{5,13},{6,14},{7,15},{8,0},{9,1},... | collective-permute-start | bytes 860168 | tf_op jit(solution)/shard_map/ppermute | solution.py:223
  68.0 14.2 %collective-permute-start.10 = (bf16[8,128,128]{2,1,0:T(8,128)(2,1)S(1)}, bf16[8,128,128]{2,1,0:T(8,128)(2,1)S(1)}, u32[]{:S(2)}, u32[]{:S(2)}) collective-permute-start(bf16[8,128,128]{2,1,0:T(8,128)(2,1)S(1)} %get-tuple-element.45), channel_id=1, source_target_pairs={{0,232},{1,233},{2,234},{3,235},{4,236},{5,237},{6,238},{7,239},{8... | collective-permute-start | bytes 786440 | tf_op jit(solution)/shard_map/ppermute | solution.py:223
  70.2 12.0 %collective-permute-start.11 = (bf16[4,128,128]{2,1,0:T(8,128)(2,1)S(1)}, bf16[4,128,128]{2,1,0:T(8,128)(2,1)S(1)}, u32[]{:S(2)}, u32[]{:S(2)}) collective-permute-start(bf16[4,128,128]{2,1,0:T(8,128)(2,1)S(1)} %get-tuple-element.46), channel_id=1, source_target_pairs={{0,240},{1,241},{2,242},{3,243},{4,244},{5,245},{6,246},{7,247},{8... | collective-permute-start | bytes 393224 | tf_op jit(solution)/shard_map/ppermute | solution.py:223
  70.9 12.0 %collective-permute-start.13 = (bf16[4,128,128]{2,1,0:T(8,128)(2,1)S(1)}, bf16[4,128,128]{2,1,0:T(8,128)(2,1)S(1)}, u32[]{:S(2)}, u32[]{:S(2)}) collective-permute-start(bf16[4,128,128]{2,1,0:T(8,128)(2,1)S(1)} %get-tuple-element.47), channel_id=1, source_target_pairs={{0,240},{1,241},{2,242},{3,243},{4,244},{5,245},{6,246},{7,247},{8... | collective-permute-start | bytes 393224 | tf_op jit(solution)/shard_map/ppermute | solution.py:223
  73.9 5.5 %collective-permute-start.9 = (f32[96,128]{1,0:T(8,128)S(1)}, f32[96,128]{1,0:T(8,128)S(1)}, u32[]{:S(2)}, u32[]{:S(2)}) collective-permute-start(f32[96,128]{1,0:T(8,128)S(1)} %get-tuple-element.43), channel_id=1, source_target_pairs={{0,16},{1,17},{2,18},{3,19},{4,20},{5,21},{6,22},{7,23},{8,24},{9,... | collective-permute-start | bytes 147464 | tf_op jit(solution)/shard_map/ppermute | solution.py:223
  79.5 8.1 %collective-permute-start.15 = (f32[96,128]{1,0:T(8,128)S(1)}, f32[96,128]{1,0:T(8,128)S(1)}, u32[]{:S(2)}, u32[]{:S(2)}) collective-permute-start(f32[96,128]{1,0:T(8,128)S(1)} %add.16), channel_id=1, source_target_pairs={{0,128},{1,129},{2,130},{3,131},{4,132},{5,133},{6,134},{7,135},{8... | collective-permute-start | bytes 147464 | tf_op jit(solution)/shard_map/ppermute | solution.py:223
  82.2 14.9 %collective-permute-start.12 = (bf16[4,128,128]{2,1,0:T(8,128)(2,1)S(1)}, bf16[4,128,128]{2,1,0:T(8,128)(2,1)S(1)}, u32[]{:S(2)}, u32[]{:S(2)}) collective-permute-start(bf16[4,128,128]{2,1,0:T(8,128)(2,1)S(1)} %shard_map.121), channel_id=1, source_target_pairs={{0,0},{1,225},{2,194},{3,163},{4,132},{5,101},{6,70},{7,39},{8,8},... | collective-permute-start | bytes 393224 | tf_op jit(solution)/shard_map/ppermute | solution.py:223
  83.0 15.7 %collective-permute-start.14 = (bf16[4,128,128]{2,1,0:T(8,128)(2,1)S(1)}, bf16[4,128,128]{2,1,0:T(8,128)(2,1)S(1)}, u32[]{:S(2)}, u32[]{:S(2)}) collective-permute-start(bf16[4,128,128]{2,1,0:T(8,128)(2,1)S(1)} %shard_map.122), channel_id=1, source_target_pairs={{0,2},{1,227},{2,192},{3,161},{4,134},{5,103},{6,68},{7,37},{8,10}... | collective-permute-start | bytes 393224 | tf_op jit(solution)/shard_map/ppermute | solution.py:223
  87.5 4.5 %collective-permute-start.16 = (f32[96,128]{1,0:T(8,128)S(1)}, f32[96,128]{1,0:T(8,128)S(1)}, u32[]{:S(2)}, u32[]{:S(2)}) collective-permute-start(f32[96,128]{1,0:T(8,128)S(1)} %add.17), channel_id=1, source_target_pairs={{0,32},{1,33},{2,34},{3,35},{4,36},{5,37},{6,38},{7,39},{8,40},{9,... | collective-permute-start | bytes 147464 | tf_op jit(solution)/shard_map/ppermute | solution.py:223
  92.0 5.1 %collective-permute-start.17 = (f32[96,128]{1,0:T(8,128)S(1)}, f32[96,128]{1,0:T(8,128)S(1)}, u32[]{:S(2)}, u32[]{:S(2)}) collective-permute-start(f32[96,128]{1,0:T(8,128)S(1)} %add.18), channel_id=1, source_target_pairs={{0,64},{1,65},{2,66},{3,67},{4,68},{5,69},{6,70},{7,71},{8,72},{9,... | collective-permute-start | bytes 147464 | tf_op jit(solution)/shard_map/ppermute | solution.py:223

commit v7 on v6

--- a/solution.py
+++ b/solution.py
@@ -17,8 +17,8 @@
 SLOTS = 6
 HALF = ROWS // 2
 NODES = ROWS * T
+PAIR_FLOPS, GROUP_FLOPS = 5 * 10**9, 2 * 10**10
 GRAD = 48
-SWAP = 96
 F32 = jnp.float32
 BF16 = jnp.bfloat16
 
@@ -159,13 +159,19 @@
     return rows[NODES : NODES + GRAD].astype(F32) + rows[NODES + GRAD :].astype(F32)
 
 
-def near_kernel(far, mine, other, low, high, grads):
+def near_kernel(far, other, low, high):
     for j in range(ROWS):
         half = low if j < HALF else high
         rows = other[j * T : (j + 1) * T].astype(F32)
         half[j % HALF] = (far[j].astype(F32) + rows).astype(BF16)
-    grads[0:GRAD] = grads_of(mine) + grads_of(other)
-    grads[GRAD:] = jnp.zeros((SWAP - GRAD, T), F32)
+
+
+def pair_kernel(mine, other, grads):
+    grads[...] = grads_of(mine) + grads_of(other)
+
+
+def group_kernel(grads, one, two, three, low, high, out):
+    out[...] = (grads[...] + one[...]) + (two[...] + three[...])
 
 
 def half_kernel(first, own, near, far, out):
@@ -286,23 +292,26 @@
     (far,) = call(far_sums_kernel, [(tiles, BF16)], [SMEM, VMEM, VMEM], sums, work, 3 << 20)(
         meta, held, got
     )
-    far_low, far_high, grads = call(
-        near_kernel, [(half, BF16), (half, BF16), ((SWAP, T), F32)], [VMEM] * 3
-    )(far, mine, other)
-    far_low, far_high, got, grads = lax.optimization_barrier((far_low, far_high, got, grads))
+    far_low, far_high = call(near_kernel, [(half, BF16), (half, BF16)], [VMEM] * 2)(far, other)
+    far_low, far_high, got, other = lax.optimization_barrier((far_low, far_high, got, other))
     far_low, far_high = (move(v, lambda b, r: (b - 2, r)) for v in (far_low, far_high))
     (own,) = call(own_sums_kernel, [(tiles, F32)], [SMEM] + [VMEM] * 2, sums, work, 3 << 20)(
         meta, held, got
     )
-    grads = grads + swap(grads, 2)
-    own, grads = lax.optimization_barrier((own, grads))
+    (grads,) = call(pair_kernel, [((GRAD, T), F32)], [VMEM] * 2, (), PAIR_FLOPS)(mine, other)
+    groups = [swap(grads, bits) for bits in (4, 8, 12)]
     low, high = (
         call(functools.partial(half_kernel, first), [(half, BF16)], [VMEM] * 3)(own, near, far)[0]
         for first, far in ((0, far_low), (HALF, far_high))
     )
+    sent_low, sent_high = low, high
     low = move(low, lambda b, r: (b - 4 * r, r))
     high = move(high, lambda b, r: (b - 4 * r, r ^ 2))
-    for bit in (16, 4, 8):
+    anywhere = pl.BlockSpec(memory_space=pl.ANY)
+    (grads,) = call(
+        group_kernel, [((GRAD, T), F32)], [VMEM] * 4 + [anywhere] * 2, (), GROUP_FLOPS
+    )(grads, *groups, sent_low, sent_high)
+    for bit in (2, 16):
         grads = grads + swap(grads, bit)
     (send,) = call(gather_kernel, [((ROWS, T + 32, T), BF16)], [VMEM] * 3)(low, high, grads)
     got = exchange(send, REP)

time: 122 us -> 114 us (0.934)
  waiting for transfers between devices: 19.8 us -> 14.4 us
    ppermute x18 -> x19, waiting for transfers between devices: 19.8 us -> 14.4 us  [move(): return lax.ppermute(value, BLK + REP, pairs)]
    ppermute x18 -> x19, starting transfers between devices: 28.2 us -> 27.2 us  [move(): return lax.ppermute(value, BLK + REP, pairs)]
  transfers between devices with their start and end apart: 18 -> 19, of which waited for: 8 -> 6; matrix products, arithmetic and copies ran while one was open for 0% -> 0% of each run, Pallas kernels for 7% -> 8%
where the time goes in v7:
time: 114 us
  blocking collectives  54.9 us (48%)
  starting transfers between devices  27.2 us (24%)
  Pallas kernels  16.4 us (14%)
  waiting for transfers between devices  14.4 us (13%)
    all_to_all x3, blocking collectives, exchange(): return lax.all_to_all(value, axes, 0, 0, tiled=True)  54.9 us
    ppermute x19, starting transfers between devices, move(): return lax.ppermute(value, BLK + REP, pairs)  27.2 us
    ppermute x19, waiting for transfers between devices, move(): return lax.ppermute(value, BLK + REP, pairs)  14.4 us
    pallas_call x1, Pallas kernels, on_device(): call(load_kernel, [(edges.shape, BF16)], [HBM], [pltpu.SemaphoreType.DMA]...  2.82 us
  transfers between devices with their start and end apart: 19, of which 6 were waited for; matrix products, arithmetic and copies ran while one was open for 0% of the time, Pallas kernels for 8%

profile of v7, /device:TPU:32, one launch (start us, length us, event | category | flops | bytes accessed | tf_op | source)
XLA Modules:
  0.0 113.8 jit_solution(3980371504792543010)
XLA Ops:
  0.6 1.7 %shard_map.111 = (bf16[4,128,128]{2,1,0:T(8,128)(2,1)S(1)}, bf16[4,128,128]{2,1,0:T(8,128)(2,1)S(1)}, f32[128,128]{1,0:T(8,128)S(1)}) custom-call(s32[1]{0:T(128)} %bitcast.rep, bf16[1024,128]{1,0:T(8,128)(2,1)} %features.1, s32[8,128]{1,0:T(8,128)} %bitcast.10), custom_call_target="tpu_custom_call" | custom-call | bytes 1048576 | tf_op jit(solution)/shard_map/pallas_call | solution.py:244
  3.0 9.1 %collective-permute-start.2 = (bf16[4,128,128]{2,1,0:T(8,128)(2,1)S(1)}, bf16[4,128,128]{2,1,0:T(8,128)(2,1)S(1)}, u32[]{:S(2)}, u32[]{:S(2)}) collective-permute-start(bf16[4,128,128]{2,1,0:T(8,128)(2,1)S(1)} %get-tuple-element.29), channel_id=1, source_target_pairs={{0,66},{1,99},{2,0},{3,33},{4,198},{5,231},{6,132},{7,165},{8,74},... | collective-permute-start | bytes 393224 | tf_op jit(solution)/shard_map/ppermute | solution.py:229
  12.2 2.8 %shard_map.112.held = bf16[8,4,6,128,128]{4,3,2,1,0:T(8,128)(2,1)S(1)} custom-call(bf16[8,4,6,128,128]{4,3,2,1,0:T(8,128)(2,1)} %edges.1), custom_call_target="tpu_custom_call" | custom-call | bytes 12582912 | tf_op jit(solution)/shard_map/pallas_call | solution.py:252
  15.0 1.7 %collective-permute-start.4 = (bf16[4,128,128]{2,1,0:T(8,128)(2,1)S(1)}, bf16[4,128,128]{2,1,0:T(8,128)(2,1)S(1)}, u32[]{:S(2)}, u32[]{:S(2)}) collective-permute-start(bf16[4,128,128]{2,1,0:T(8,128)(2,1)S(1)} %collective-permute-done.low), channel_id=1, source_target_pairs={{0,16},{1,17},{2,18},{3,19},{4,20},{5,21},{6,22},{7,23},{8,24},{9,... | collective-permute-start | bytes 393224 | tf_op jit(solution)/shard_map/ppermute | solution.py:229
  16.7 2.7 %collective-permute-start.6 = (bf16[4,128,128]{2,1,0:T(8,128)(2,1)S(1)}, bf16[4,128,128]{2,1,0:T(8,128)(2,1)S(1)}, u32[]{:S(2)}, u32[]{:S(2)}) collective-permute-start(bf16[4,128,128]{2,1,0:T(8,128)(2,1)S(1)} %collective-permute-done.2.high), channel_id=1, source_target_pairs={{0,16},{1,17},{2,18},{3,19},{4,20},{5,21},{6,22},{7,23},{8,24},{9,... | collective-permute-start | bytes 393224 | tf_op jit(solution)/shard_map/ppermute | solution.py:229
  19.4 1.5 %shard_map.113.total = f32[8,128,128]{2,1,0:T(8,128)S(1)} custom-call(s32[8,4,8]{2,1,0:T(4,128)S(1)} %pad_add_fusion.meta, bf16[8,4,6,128,128]{4,3,2,1,0:T(8,128)(2,1)S(1)} %shard_map.112.held, bf16[4,128,128]{2,1,0:T(8,128)(2,1)S(1)} %collective-permute-done.low, bf16[4,128,128]{2,1,0:T(8,128)(2,1)S(1)} %collective-permute-done.2.high), custom_call_target="tpu_custom_call" | custom-call | flops 201326592 | bytes 3145728 | tf_op jit(solution)/shard_map/pallas_call | solution.py:260
  21.0 2.4 %collective-permute-done.4.low = bf16[4,128,128]{2,1,0:T(8,128)(2,1)S(1)} collective-permute-done((bf16[4,128,128]{2,1,0:T(8,128)(2,1)S(1)}, bf16[4,128,128]{2,1,0:T(8,128)(2,1)S(1)}, u32[]{:S(2)}, u32[]{:S(2)}) %collective-permute-start.4) | collective-permute-done | bytes 131104 | tf_op jit(solution)/shard_map/ppermute | solution.py:229
  23.4 2.8 %collective-permute-done.6.high = bf16[4,128,128]{2,1,0:T(8,128)(2,1)S(1)} collective-permute-done((bf16[4,128,128]{2,1,0:T(8,128)(2,1)S(1)}, bf16[4,128,128]{2,1,0:T(8,128)(2,1)S(1)}, u32[]{:S(2)}, u32[]{:S(2)}) %collective-permute-start.6) | collective-permute-done | bytes 131104 | tf_op jit(solution)/shard_map/ppermute | solution.py:229
  26.2 1.5 %shard_map.114.total = f32[8,128,128]{2,1,0:T(8,128)S(1)} custom-call(s32[8,4,8]{2,1,0:T(4,128)S(1)} %pad_add_fusion.meta, bf16[8,4,6,128,128]{4,3,2,1,0:T(8,128)(2,1)S(1)} %shard_map.112.held, bf16[4,128,128]{2,1,0:T(8,128)(2,1)S(1)} %collective-permute-done.4.low, bf16[4,128,128]{2,1,0:T(8,128)(2,1)S(1)} %collective-permute-done.6.high, ...), custom_call_target="tpu_custom_call" | custom-call | flops 201326592 | bytes 3145728 | tf_op jit(solution)/shard_map/pallas_call | solution.py:266
  27.7 2.1 %shard_map.115 = bf16[8,128,128]{2,1,0:T(8,128)(2,1)S(1)} custom-call(s32[8,4,8]{2,1,0:T(4,128)S(1)} %pad_add_fusion.meta, bf16[8,4,6,128,128]{4,3,2,1,0:T(8,128)(2,1)S(1)} %shard_map.112.held, bf16[4,128,128]{2,1,0:T(8,128)(2,1)S(1)} %collective-permute-done.1.near_low, bf16[4,128,128]{2,1,0:T(8,128)(2,1)S(1)} %collective-permute-done.3.near_high, ...), custom_call_target="tpu_custom_call" | custom-call | flops 402653184 | bytes 6291456 | tf_op jit(solution)/shard_map/pallas_call | solution.py:269
  29.9 21.0 %all_to_all.15.parts = bf16[8,128,128]{2,1,0:T(8,128)(2,1)S(1)} all-to-all(bf16[8,128,128]{2,1,0:T(8,128)(2,1)S(1)} %shard_map.115), channel_id=1, replica_groups=mesh['z'=8,'yl'=2,'core'=2,'x'=4,'yh'=2] {'x','yh'}, dimensions={0} | all-to-all | bytes 524288 | tf_op jit(solution)/shard_map/all_to_all | solution.py:219
  51.7 12.2 %all_to_all.16.got = bf16[8,176,128]{2,1,0:T(8,128)(2,1)S(1)} all-to-all(bf16[8,176,128]{2,1,0:T(8,128)(2,1)S(1)} %get-tuple-element.34), channel_id=1, replica_groups=mesh['z'=8,'yl'=2,'core'=2,'x'=4,'yh'=2] {'x','yh'}, dimensions={0} | all-to-all | bytes 720896 | tf_op jit(solution)/shard_map/all_to_all | solution.py:219
  63.9 2.0 %shard_map.118 = (bf16[8,128,128]{2,1,0:T(8,128)(2,1)S(1)}, bf16[1120,128]{1,0:T(8,128)(2,1)S(1)}) custom-call(s32[8,4,8]{2,1,0:T(4,128)S(1)} %pad_add_fusion.meta, bf16[8,4,6,128,128]{4,3,2,1,0:T(8,128)(2,1)S(1)} %shard_map.112.held, bf16[8,176,128]{2,1,0:T(8,128)(2,1)S(1)} %all_to_all.16.got), custom_call_target="tpu_custom_call" | custom-call | flops 402653184 | bytes 6291456 | tf_op jit(solution)/shard_map/pallas_call | solution.py:282
  66.1 1.5 %shard_map.117.far = bf16[8,128,128]{2,1,0:T(8,128)(2,1)S(1)} custom-call(s32[8,4,8]{2,1,0:T(4,128)S(1)} %pad_add_fusion.meta, bf16[8,4,6,128,128]{4,3,2,1,0:T(8,128)(2,1)S(1)} %shard_map.112.held, bf16[8,176,128]{2,1,0:T(8,128)(2,1)S(1)} %all_to_all.16.got), custom_call_target="tpu_custom_call" | custom-call | flops 201326592 | bytes 3145728 | tf_op jit(solution)/shard_map/pallas_call | solution.py:292
  68.2 3.0 %collective-permute-start.10 = (bf16[4,128,128]{2,1,0:T(8,128)(2,1)S(1)}, bf16[4,128,128]{2,1,0:T(8,128)(2,1)S(1)}, u32[]{:S(2)}, u32[]{:S(2)}) collective-permute-start(bf16[4,128,128]{2,1,0:T(8,128)(2,1)S(1)} %get-tuple-element.40), channel_id=1, source_target_pairs={{0,240},{1,241},{2,242},{3,243},{4,244},{5,245},{6,246},{7,247},{8... | collective-permute-start | bytes 393224 | tf_op jit(solution)/shard_map/ppermute | solution.py:229
  71.9 1.2 %collective-permute-start.15 = (f32[48,128]{1,0:T(8,128)S(1)}, f32[48,128]{1,0:T(8,128)S(1)}, u32[]{:S(2)}, u32[]{:S(2)}) collective-permute-start(f32[48,128]{1,0:T(8,128)S(1)} %shard_map.123.grads), channel_id=1, source_target_pairs={{0,64},{1,65},{2,66},{3,67},{4,68},{5,69},{6,70},{7,71},{8,72},{9,... | collective-permute-start | bytes 73736 | tf_op jit(solution)/shard_map/ppermute | solution.py:229
  73.1 1.7 %collective-permute-start.16 = (f32[48,128]{1,0:T(8,128)S(1)}, f32[48,128]{1,0:T(8,128)S(1)}, u32[]{:S(2)}, u32[]{:S(2)}) collective-permute-start(f32[48,128]{1,0:T(8,128)S(1)} %shard_map.123.grads), channel_id=1, source_target_pairs={{0,96},{1,97},{2,98},{3,99},{4,100},{5,101},{6,102},{7,103},{8,104... | collective-permute-start | bytes 73736 | tf_op jit(solution)/shard_map/ppermute | solution.py:229
  74.8 1.5 %shard_map.120.own = f32[8,128,128]{2,1,0:T(8,128)S(1)} custom-call(s32[8,4,8]{2,1,0:T(4,128)S(1)} %pad_add_fusion.meta, bf16[8,4,6,128,128]{4,3,2,1,0:T(8,128)(2,1)S(1)} %shard_map.112.held, bf16[8,176,128]{2,1,0:T(8,128)(2,1)S(1)} %all_to_all.16.got), custom_call_target="tpu_custom_call" | custom-call | flops 201326592 | bytes 3145728 | tf_op jit(solution)/shard_map/pallas_call | solution.py:298
  77.7 1.4 %collective-permute-done.15.two = f32[48,128]{1,0:T(8,128)S(1)} collective-permute-done((f32[48,128]{1,0:T(8,128)S(1)}, f32[48,128]{1,0:T(8,128)S(1)}, u32[]{:S(2)}, u32[]{:S(2)}) %collective-permute-start.15) | collective-permute-done | bytes 24608 | tf_op jit(solution)/shard_map/ppermute | solution.py:229
  79.7 1.3 %collective-permute-start.17 = (f32[48,128]{1,0:T(8,128)S(1)}, f32[48,128]{1,0:T(8,128)S(1)}, u32[]{:S(2)}, u32[]{:S(2)}) collective-permute-start(f32[48,128]{1,0:T(8,128)S(1)} %shard_map.124), channel_id=1, source_target_pairs={{0,16},{1,17},{2,18},{3,19},{4,20},{5,21},{6,22},{7,23},{8,24},{9,... | collective-permute-start | bytes 73736 | tf_op jit(solution)/shard_map/ppermute | solution.py:229
  81.0 2.6 %collective-permute-done.17 = f32[48,128]{1,0:T(8,128)S(1)} collective-permute-done((f32[48,128]{1,0:T(8,128)S(1)}, f32[48,128]{1,0:T(8,128)S(1)}, u32[]{:S(2)}, u32[]{:S(2)}) %collective-permute-start.17) | collective-permute-done | bytes 24608 | tf_op jit(solution)/shard_map/ppermute | solution.py:229
  83.7 3.2 %collective-permute-start.18 = (f32[48,128]{1,0:T(8,128)S(1)}, f32[48,128]{1,0:T(8,128)S(1)}, u32[]{:S(2)}, u32[]{:S(2)}) collective-permute-start(f32[48,128]{1,0:T(8,128)S(1)} %add.10), channel_id=1, source_target_pairs={{0,128},{1,129},{2,130},{3,131},{4,132},{5,133},{6,134},{7,135},{8... | collective-permute-start | bytes 73736 | tf_op jit(solution)/shard_map/ppermute | solution.py:229
  86.9 4.5 %collective-permute-done.18 = f32[48,128]{1,0:T(8,128)S(1)} collective-permute-done((f32[48,128]{1,0:T(8,128)S(1)}, f32[48,128]{1,0:T(8,128)S(1)}, u32[]{:S(2)}, u32[]{:S(2)}) %collective-permute-start.18) | collective-permute-done | bytes 24608 | tf_op jit(solution)/shard_map/ppermute | solution.py:229
  91.5 21.6 %all_to_all.17.got = bf16[8,160,128]{2,1,0:T(8,128)(2,1)S(1)} all-to-all(bf16[8,160,128]{2,1,0:T(8,128)(2,1)S(1)} %shard_map.125), channel_id=1, replica_groups=mesh['z'=8,'yl'=2,'core'=2,'x'=4,'yh'=2] {'x','yh'}, dimensions={0} | all-to-all | bytes 655360 | tf_op jit(solution)/shard_map/all_to_all | solution.py:219
  (48 shorter events, 5.8 us)
Async XLA Ops:
  2.4 12.7 %collective-permute-start = (bf16[4,128,128]{2,1,0:T(8,128)(2,1)S(1)}, bf16[4,128,128]{2,1,0:T(8,128)(2,1)S(1)}, u32[]{:S(2)}, u32[]{:S(2)}) collective-permute-start(bf16[4,128,128]{2,1,0:T(8,128)(2,1)S(1)} %get-tuple-element.25), channel_id=1, source_target_pairs={{0,0},{1,33},{2,66},{3,99},{4,132},{5,165},{6,198},{7,231},{8,8},{... | collective-permute-start | bytes 393224 | tf_op jit(solution)/shard_map/ppermute | solution.py:229
  3.0 13.6 %collective-permute-start.2 = (bf16[4,128,128]{2,1,0:T(8,128)(2,1)S(1)}, bf16[4,128,128]{2,1,0:T(8,128)(2,1)S(1)}, u32[]{:S(2)}, u32[]{:S(2)}) collective-permute-start(bf16[4,128,128]{2,1,0:T(8,128)(2,1)S(1)} %get-tuple-element.29), channel_id=1, source_target_pairs={{0,66},{1,99},{2,0},{3,33},{4,198},{5,231},{6,132},{7,165},{8,74},... | collective-permute-start | bytes 393224 | tf_op jit(solution)/shard_map/ppermute | solution.py:229
  12.1 2.8 %copy-start.3 = (s32[8,4,6]{0,1,2:T(4,128)S(1)}, s32[8,4,6]{0,1,2:T(4,128)}, u32[]{:S(2)}) copy-start(s32[8,4,6]{0,1,2:T(4,128)} %param.10) | copy-start | bytes 2308
  12.2 2.9 %copy-start.4 = (s32[8,4]{0,1:T(4,128)S(1)}, s32[8,4]{0,1:T(4,128)}, u32[]{:S(2)}) copy-start(s32[8,4]{0,1:T(4,128)} %param.11) | copy-start | bytes 388
  15.0 8.3 %collective-permute-start.4 = (bf16[4,128,128]{2,1,0:T(8,128)(2,1)S(1)}, bf16[4,128,128]{2,1,0:T(8,128)(2,1)S(1)}, u32[]{:S(2)}, u32[]{:S(2)}) collective-permute-start(bf16[4,128,128]{2,1,0:T(8,128)(2,1)S(1)} %collective-permute-done.low), channel_id=1, source_target_pairs={{0,16},{1,17},{2,18},{3,19},{4,20},{5,21},{6,22},{7,23},{8,24},{9,... | collective-permute-start | bytes 393224 | tf_op jit(solution)/shard_map/ppermute | solution.py:229
  16.7 9.5 %collective-permute-start.6 = (bf16[4,128,128]{2,1,0:T(8,128)(2,1)S(1)}, bf16[4,128,128]{2,1,0:T(8,128)(2,1)S(1)}, u32[]{:S(2)}, u32[]{:S(2)}) collective-permute-start(bf16[4,128,128]{2,1,0:T(8,128)(2,1)S(1)} %collective-permute-done.2.high), channel_id=1, source_target_pairs={{0,16},{1,17},{2,18},{3,19},{4,20},{5,21},{6,22},{7,23},{8,24},{9,... | collective-permute-start | bytes 393224 | tf_op jit(solution)/shard_map/ppermute | solution.py:229
  19.4 8.3 %collective-permute-start.1 = (bf16[4,128,128]{2,1,0:T(8,128)(2,1)S(1)}, bf16[4,128,128]{2,1,0:T(8,128)(2,1)S(1)}, u32[]{:S(2)}, u32[]{:S(2)}) collective-permute-start(bf16[4,128,128]{2,1,0:T(8,128)(2,1)S(1)} %collective-permute-done.low), channel_id=1, source_target_pairs={{0,8},{1,9},{2,10},{3,11},{4,12},{5,13},{6,14},{7,15},{8,32},{9,33... | collective-permute-start | bytes 393224 | tf_op jit(solution)/shard_map/ppermute | solution.py:229
  20.9 30.0 %copy-start = (bf16[128,256]{1,0:T(8,128)(2,1)S(1)}, bf16[128,256]{1,0:T(8,128)(2,1)}, u32[]{:S(2)}) copy-start(bf16[128,256]{1,0:T(8,128)(2,1)} %weight.1) | copy-start | bytes 196612
  20.9 30.0 %copy-start.1 = (bf16[128,256]{1,0:T(8,128)(2,1)S(1)}, bf16[128,256]{1,0:T(8,128)(2,1)}, u32[]{:S(2)}) copy-start(bf16[128,256]{1,0:T(8,128)(2,1)} %cot.1) | copy-start | bytes 196612
  20.9 30.0 %copy-start.2 = (f32[256]{0:T(256)S(1)}, f32[256]{0:T(256)}, u32[]{:S(2)}) copy-start(f32[256]{0:T(256)} %param.14) | copy-start | bytes 3076
  20.9 6.7 %collective-permute-start.3 = (bf16[4,128,128]{2,1,0:T(8,128)(2,1)S(1)}, bf16[4,128,128]{2,1,0:T(8,128)(2,1)S(1)}, u32[]{:S(2)}, u32[]{:S(2)}) collective-permute-start(bf16[4,128,128]{2,1,0:T(8,128)(2,1)S(1)} %collective-permute-done.2.high), channel_id=1, source_target_pairs={{0,8},{1,9},{2,10},{3,11},{4,12},{5,13},{6,14},{7,15},{8,32},{9,33... | collective-permute-start | bytes 393224 | tf_op jit(solution)/shard_map/ppermute | solution.py:229
  23.4 4.3 %collective-permute-start.5 = (bf16[4,128,128]{2,1,0:T(8,128)(2,1)S(1)}, bf16[4,128,128]{2,1,0:T(8,128)(2,1)S(1)}, u32[]{:S(2)}, u32[]{:S(2)}) collective-permute-start(bf16[4,128,128]{2,1,0:T(8,128)(2,1)S(1)} %collective-permute-done.4.low), channel_id=1, source_target_pairs={{0,8},{1,9},{2,10},{3,11},{4,12},{5,13},{6,14},{7,15},{8,0},{9,1},... | collective-permute-start | bytes 393224 | tf_op jit(solution)/shard_map/ppermute | solution.py:229
  26.2 1.5 %collective-permute-start.7 = (bf16[4,128,128]{2,1,0:T(8,128)(2,1)S(1)}, bf16[4,128,128]{2,1,0:T(8,128)(2,1)S(1)}, u32[]{:S(2)}, u32[]{:S(2)}) collective-permute-start(bf16[4,128,128]{2,1,0:T(8,128)(2,1)S(1)} %collective-permute-done.6.high), channel_id=1, source_target_pairs={{0,8},{1,9},{2,10},{3,11},{4,12},{5,13},{6,14},{7,15},{8,0},{9,1},... | collective-permute-start | bytes 393224 | tf_op jit(solution)/shard_map/ppermute | solution.py:229
  65.9 1.7 %collective-permute-start.8 = (bf16[1120,128]{1,0:T(8,128)(2,1)S(1)}, bf16[1120,128]{1,0:T(8,128)(2,1)S(1)}, u32[]{:S(2)}, u32[]{:S(2)}) collective-permute-start(bf16[1120,128]{1,0:T(8,128)(2,1)S(1)} %get-tuple-element.35.mine), channel_id=1, source_target_pairs={{0,8},{1,9},{2,10},{3,11},{4,12},{5,13},{6,14},{7,15},{8,0},{9,1},... | collective-permute-start | bytes 860168 | tf_op jit(solution)/shard_map/ppermute | solution.py:229
  66.0 7.1 %collective-permute-start.9 = (bf16[8,128,128]{2,1,0:T(8,128)(2,1)S(1)}, bf16[8,128,128]{2,1,0:T(8,128)(2,1)S(1)}, u32[]{:S(2)}, u32[]{:S(2)}) collective-permute-start(bf16[8,128,128]{2,1,0:T(8,128)(2,1)S(1)} %get-tuple-element.39), channel_id=1, source_target_pairs={{0,232},{1,233},{2,234},{3,235},{4,236},{5,237},{6,238},{7,239},{8... | collective-permute-start | bytes 786440 | tf_op jit(solution)/shard_map/ppermute | solution.py:229
  67.7 8.6 %collective-permute-start.12 = (bf16[4,128,128]{2,1,0:T(8,128)(2,1)S(1)}, bf16[4,128,128]{2,1,0:T(8,128)(2,1)S(1)}, u32[]{:S(2)}, u32[]{:S(2)}) collective-permute-start(bf16[4,128,128]{2,1,0:T(8,128)(2,1)S(1)} %get-tuple-element.41), channel_id=1, source_target_pairs={{0,240},{1,241},{2,242},{3,243},{4,244},{5,245},{6,246},{7,247},{8... | collective-permute-start | bytes 393224 | tf_op jit(solution)/shard_map/ppermute | solution.py:229
  68.2 8.8 %collective-permute-start.10 = (bf16[4,128,128]{2,1,0:T(8,128)(2,1)S(1)}, bf16[4,128,128]{2,1,0:T(8,128)(2,1)S(1)}, u32[]{:S(2)}, u32[]{:S(2)}) collective-permute-start(bf16[4,128,128]{2,1,0:T(8,128)(2,1)S(1)} %get-tuple-element.40), channel_id=1, source_target_pairs={{0,240},{1,241},{2,242},{3,243},{4,244},{5,245},{6,246},{7,247},{8... | collective-permute-start | bytes 393224 | tf_op jit(solution)/shard_map/ppermute | solution.py:229
  71.2 6.5 %collective-permute-start.14 = (f32[48,128]{1,0:T(8,128)S(1)}, f32[48,128]{1,0:T(8,128)S(1)}, u32[]{:S(2)}, u32[]{:S(2)}) collective-permute-start(f32[48,128]{1,0:T(8,128)S(1)} %shard_map.123.grads), channel_id=1, source_target_pairs={{0,32},{1,33},{2,34},{3,35},{4,36},{5,37},{6,38},{7,39},{8,40},{9,... | collective-permute-start | bytes 73736 | tf_op jit(solution)/shard_map/ppermute | solution.py:229
  71.9 7.2 %collective-permute-start.15 = (f32[48,128]{1,0:T(8,128)S(1)}, f32[48,128]{1,0:T(8,128)S(1)}, u32[]{:S(2)}, u32[]{:S(2)}) collective-permute-start(f32[48,128]{1,0:T(8,128)S(1)} %shard_map.123.grads), channel_id=1, source_target_pairs={{0,64},{1,65},{2,66},{3,67},{4,68},{5,69},{6,70},{7,71},{8,72},{9,... | collective-permute-start | bytes 73736 | tf_op jit(solution)/shard_map/ppermute | solution.py:229
  73.1 6.6 %collective-permute-start.16 = (f32[48,128]{1,0:T(8,128)S(1)}, f32[48,128]{1,0:T(8,128)S(1)}, u32[]{:S(2)}, u32[]{:S(2)}) collective-permute-start(f32[48,128]{1,0:T(8,128)S(1)} %shard_map.123.grads), channel_id=1, source_target_pairs={{0,96},{1,97},{2,98},{3,99},{4,100},{5,101},{6,102},{7,103},{8,104... | collective-permute-start | bytes 73736 | tf_op jit(solution)/shard_map/ppermute | solution.py:229
  76.3 15.1 %collective-permute-start.13 = (bf16[4,128,128]{2,1,0:T(8,128)(2,1)S(1)}, bf16[4,128,128]{2,1,0:T(8,128)(2,1)S(1)}, u32[]{:S(2)}, u32[]{:S(2)}) collective-permute-start(bf16[4,128,128]{2,1,0:T(8,128)(2,1)S(1)} %shard_map.122.high), channel_id=1, source_target_pairs={{0,2},{1,227},{2,192},{3,161},{4,134},{5,103},{6,68},{7,37},{8,10}... | collective-permute-start | bytes 393224 | tf_op jit(solution)/shard_map/ppermute | solution.py:229
  77.0 14.4 %collective-permute-start.11 = (bf16[4,128,128]{2,1,0:T(8,128)(2,1)S(1)}, bf16[4,128,128]{2,1,0:T(8,128)(2,1)S(1)}, u32[]{:S(2)}, u32[]{:S(2)}) collective-permute-start(bf16[4,128,128]{2,1,0:T(8,128)(2,1)S(1)} %shard_map.121.low), channel_id=1, source_target_pairs={{0,0},{1,225},{2,194},{3,163},{4,132},{5,101},{6,70},{7,39},{8,8},... | collective-permute-start | bytes 393224 | tf_op jit(solution)/shard_map/ppermute | solution.py:229
  79.7 3.9 %collective-permute-start.17 = (f32[48,128]{1,0:T(8,128)S(1)}, f32[48,128]{1,0:T(8,128)S(1)}, u32[]{:S(2)}, u32[]{:S(2)}) collective-permute-start(f32[48,128]{1,0:T(8,128)S(1)} %shard_map.124), channel_id=1, source_target_pairs={{0,16},{1,17},{2,18},{3,19},{4,20},{5,21},{6,22},{7,23},{8,24},{9,... | collective-permute-start | bytes 73736 | tf_op jit(solution)/shard_map/ppermute | solution.py:229
  83.7 7.7 %collective-permute-start.18 = (f32[48,128]{1,0:T(8,128)S(1)}, f32[48,128]{1,0:T(8,128)S(1)}, u32[]{:S(2)}, u32[]{:S(2)}) collective-permute-start(f32[48,128]{1,0:T(8,128)S(1)} %add.10), channel_id=1, source_target_pairs={{0,128},{1,129},{2,130},{3,131},{4,132},{5,133},{6,134},{7,135},{8... | collective-permute-start | bytes 73736 | tf_op jit(solution)/shard_map/ppermute | solution.py:229

commit v8 on v7

--- a/solution.py
+++ b/solution.py
@@ -159,11 +159,10 @@
     return rows[NODES : NODES + GRAD].astype(F32) + rows[NODES + GRAD :].astype(F32)
 
 
-def near_kernel(far, other, low, high):
-    for j in range(ROWS):
-        half = low if j < HALF else high
+def near_kernel(far, other, out):
+    for j in range(ROWS):
         rows = other[j * T : (j + 1) * T].astype(F32)
-        half[j % HALF] = (far[j].astype(F32) + rows).astype(BF16)
+        out[j] = (far[j].astype(F32) + rows).astype(BF16)
 
 
 def pair_kernel(mine, other, grads):
@@ -174,10 +173,11 @@
     out[...] = (grads[...] + one[...]) + (two[...] + three[...])
 
 
-def half_kernel(first, own, near, far, out):
-    rows = pl.ds(first, HALF)
-    total = own[rows] + near[rows].astype(F32) + far[...].astype(F32)
-    out[...] = total.astype(BF16)
+def total_kernel(own, near, far, one, two, three, low, high):
+    for half, first in ((low, 0), (high, HALF)):
+        rows = pl.ds(first, HALF)
+        total = own[rows] + near[rows].astype(F32) + far[rows].astype(F32)
+        half[...] = total.astype(BF16)
 
 
 def gather_kernel(low, high, grads, out):
@@ -229,6 +229,10 @@
     return lax.ppermute(value, BLK + REP, pairs)
 
 
+def column(r):
+    return r ^ (6 if r % 2 else 2)
+
+
 def swap(value, bit):
     return move(value, lambda b, r: (b ^ bit, r))
 
@@ -248,7 +252,7 @@
     )(rep.astype(jnp.int32)[None], pinned(features), pinned(degrees.reshape(ROWS, T)))
 
     low = move(low, lambda b, r: (b + 4 * r, r))
-    high = move(high, lambda b, r: (b + 4 * (r ^ 2), r ^ 2))
+    high = move(high, lambda b, r: (b + 4 * column(r), column(r)))
     (held,) = call(
         load_kernel, [(edges.shape, BF16)], [HBM], [pltpu.SemaphoreType.DMA], 0, 12 << 20
     )(pinned(edges))
@@ -292,22 +296,22 @@
     (far,) = call(far_sums_kernel, [(tiles, BF16)], [SMEM, VMEM, VMEM], sums, work, 3 << 20)(
         meta, held, got
     )
-    far_low, far_high = call(near_kernel, [(half, BF16), (half, BF16)], [VMEM] * 2)(far, other)
-    far_low, far_high, got, other = lax.optimization_barrier((far_low, far_high, got, other))
-    far_low, far_high = (move(v, lambda b, r: (b - 2, r)) for v in (far_low, far_high))
+    (far,) = call(near_kernel, [(tiles, BF16)], [VMEM] * 2)(far, other)
+    far, got, other = lax.optimization_barrier((far, got, other))
+    far = move(far, lambda b, r: (b - 2, r))
     (own,) = call(own_sums_kernel, [(tiles, F32)], [SMEM] + [VMEM] * 2, sums, work, 3 << 20)(
         meta, held, got
     )
     (grads,) = call(pair_kernel, [((GRAD, T), F32)], [VMEM] * 2, (), PAIR_FLOPS)(mine, other)
     groups = [swap(grads, bits) for bits in (4, 8, 12)]
-    low, high = (
-        call(functools.partial(half_kernel, first), [(half, BF16)], [VMEM] * 3)(own, near, far)[0]
-        for first, far in ((0, far_low), (HALF, far_high))
+    anywhere = pl.BlockSpec(memory_space=pl.ANY)
+    low, high = call(total_kernel, [(half, BF16), (half, BF16)], [VMEM] * 3 + [anywhere] * 3)(
+        own, near, far, *groups
     )
     sent_low, sent_high = low, high
     low = move(low, lambda b, r: (b - 4 * r, r))
-    high = move(high, lambda b, r: (b - 4 * r, r ^ 2))
-    anywhere = pl.BlockSpec(memory_space=pl.ANY)
+    high = move(high, lambda b, r: (b, column(r)))
+    high = move(high, lambda b, r: (b - 4 * column(r), r))
     (grads,) = call(
         group_kernel, [((GRAD, T), F32)], [VMEM] * 4 + [anywhere] * 2, (), GROUP_FLOPS
     )(grads, *groups, sent_low, sent_high)

time: 114 us -> 115 us (level)
  waiting for transfers between devices: 14.4 us -> 21.6 us
  blocking collectives: 54.9 us -> 47.8 us
    ppermute x19, waiting for transfers between devices: 14.4 us -> 21.6 us  [move(): return lax.ppermute(value, BLK + REP, pairs)]
    all_to_all x3, blocking collectives: 54.9 us -> 47.8 us  [exchange(): return lax.all_to_all(value, axes, 0, 0, tiled=True)]
  transfers between devices with their start and end apart: 19 -> 19, of which waited for: 6 -> 8; matrix products, arithmetic and copies ran while one was open for 0% -> 0% of each run, Pallas kernels for 8% -> 8%
where the time goes in v8:
time: 115 us; the launch traced here: 114 us
  blocking collectives  47.8 us (42%)
  starting transfers between devices  27.7 us (24%)
  waiting for transfers between devices  21.6 us (19%)
  Pallas kernels  16.4 us (14%)
    all_to_all x3, blocking collectives, exchange(): return lax.all_to_all(value, axes, 0, 0, tiled=True)  47.8 us
    ppermute x19, starting transfers between devices, move(): return lax.ppermute(value, BLK + REP, pairs)  27.7 us
    ppermute x19, waiting for transfers between devices, move(): return lax.ppermute(value, BLK + REP, pairs)  21.6 us
    pallas_call x1, Pallas kernels, on_device(): call(load_kernel, [(edges.shape, BF16)], [HBM], [pltpu.SemaphoreType.DMA]...  2.82 us
  transfers between devices with their start and end apart: 19, of which 8 were waited for; matrix products, arithmetic and copies ran while one was open for 0% of the time, Pallas kernels for 8%

profile of v8, /device:TPU:32, one launch (start us, length us, event | category | flops | bytes accessed | tf_op | source)
XLA Modules:
  0.0 114.5 jit_solution(7473979735881052374)
XLA Ops:
  0.6 1.7 %shard_map.111 = (bf16[4,128,128]{2,1,0:T(8,128)(2,1)S(1)}, bf16[4,128,128]{2,1,0:T(8,128)(2,1)S(1)}, f32[128,128]{1,0:T(8,128)S(1)}) custom-call(s32[1]{0:T(128)} %bitcast.rep, bf16[1024,128]{1,0:T(8,128)(2,1)} %features.1, s32[8,128]{1,0:T(8,128)} %bitcast.10), custom_call_target="tpu_custom_call" | custom-call | bytes 1048576 | tf_op jit(solution)/shard_map/pallas_call | solution.py:248
  3.0 9.1 %collective-permute-start.2 = (bf16[4,128,128]{2,1,0:T(8,128)(2,1)S(1)}, bf16[4,128,128]{2,1,0:T(8,128)(2,1)S(1)}, u32[]{:S(2)}, u32[]{:S(2)}) collective-permute-start(bf16[4,128,128]{2,1,0:T(8,128)(2,1)S(1)} %get-tuple-element.28), channel_id=1, source_target_pairs={{0,66},{1,231},{2,0},{3,165},{4,198},{5,99},{6,132},{7,33},{8,74},... | collective-permute-start | bytes 393224 | tf_op jit(solution)/shard_map/ppermute | solution.py:229
  12.2 2.8 %shard_map.112.held = bf16[8,4,6,128,128]{4,3,2,1,0:T(8,128)(2,1)S(1)} custom-call(bf16[8,4,6,128,128]{4,3,2,1,0:T(8,128)(2,1)} %edges.1), custom_call_target="tpu_custom_call" | custom-call | bytes 12582912 | tf_op jit(solution)/shard_map/pallas_call | solution.py:256
  15.1 1.7 %collective-permute-start.4 = (bf16[4,128,128]{2,1,0:T(8,128)(2,1)S(1)}, bf16[4,128,128]{2,1,0:T(8,128)(2,1)S(1)}, u32[]{:S(2)}, u32[]{:S(2)}) collective-permute-start(bf16[4,128,128]{2,1,0:T(8,128)(2,1)S(1)} %collective-permute-done.low), channel_id=1, source_target_pairs={{0,16},{1,17},{2,18},{3,19},{4,20},{5,21},{6,22},{7,23},{8,24},{9,... | collective-permute-start | bytes 393224 | tf_op jit(solution)/shard_map/ppermute | solution.py:229
  16.7 2.7 %collective-permute-start.6 = (bf16[4,128,128]{2,1,0:T(8,128)(2,1)S(1)}, bf16[4,128,128]{2,1,0:T(8,128)(2,1)S(1)}, u32[]{:S(2)}, u32[]{:S(2)}) collective-permute-start(bf16[4,128,128]{2,1,0:T(8,128)(2,1)S(1)} %collective-permute-done.2.high), channel_id=1, source_target_pairs={{0,16},{1,17},{2,18},{3,19},{4,20},{5,21},{6,22},{7,23},{8,24},{9,... | collective-permute-start | bytes 393224 | tf_op jit(solution)/shard_map/ppermute | solution.py:229
  21.0 2.4 %collective-permute-done.4.low = bf16[4,128,128]{2,1,0:T(8,128)(2,1)S(1)} collective-permute-done((bf16[4,128,128]{2,1,0:T(8,128)(2,1)S(1)}, bf16[4,128,128]{2,1,0:T(8,128)(2,1)S(1)}, u32[]{:S(2)}, u32[]{:S(2)}) %collective-permute-start.4) | collective-permute-done | bytes 131104 | tf_op jit(solution)/shard_map/ppermute | solution.py:229
  23.4 2.8 %collective-permute-done.6.high = bf16[4,128,128]{2,1,0:T(8,128)(2,1)S(1)} collective-permute-done((bf16[4,128,128]{2,1,0:T(8,128)(2,1)S(1)}, bf16[4,128,128]{2,1,0:T(8,128)(2,1)S(1)}, u32[]{:S(2)}, u32[]{:S(2)}) %collective-permute-start.6) | collective-permute-done | bytes 131104 | tf_op jit(solution)/shard_map/ppermute | solution.py:229
  26.2 1.5 %shard_map.114.total = f32[8,128,128]{2,1,0:T(8,128)S(1)} custom-call(s32[8,4,8]{2,1,0:T(4,128)S(1)} %pad_add_fusion.meta, bf16[8,4,6,128,128]{4,3,2,1,0:T(8,128)(2,1)S(1)} %shard_map.112.held, bf16[4,128,128]{2,1,0:T(8,128)(2,1)S(1)} %collective-permute-done.4.low, bf16[4,128,128]{2,1,0:T(8,128)(2,1)S(1)} %collective-permute-done.6.high, ...), custom_call_target="tpu_custom_call" | custom-call | flops 201326592 | bytes 3145728 | tf_op jit(solution)/shard_map/pallas_call | solution.py:270
  27.7 2.2 %shard_map.115 = bf16[8,128,128]{2,1,0:T(8,128)(2,1)S(1)} custom-call(s32[8,4,8]{2,1,0:T(4,128)S(1)} %pad_add_fusion.meta, bf16[8,4,6,128,128]{4,3,2,1,0:T(8,128)(2,1)S(1)} %shard_map.112.held, bf16[4,128,128]{2,1,0:T(8,128)(2,1)S(1)} %collective-permute-done.1.near_low, bf16[4,128,128]{2,1,0:T(8,128)(2,1)S(1)} %collective-permute-done.3.near_high, ...), custom_call_target="tpu_custom_call" | custom-call | flops 402653184 | bytes 6291456 | tf_op jit(solution)/shard_map/pallas_call | solution.py:273
  29.9 20.2 %all_to_all.15.parts = bf16[8,128,128]{2,1,0:T(8,128)(2,1)S(1)} all-to-all(bf16[8,128,128]{2,1,0:T(8,128)(2,1)S(1)} %shard_map.115), channel_id=1, replica_groups=mesh['z'=8,'yl'=2,'core'=2,'x'=4,'yh'=2] {'x','yh'}, dimensions={0} | all-to-all | bytes 524288 | tf_op jit(solution)/shard_map/all_to_all | solution.py:219
  50.9 12.2 %all_to_all.16.got = bf16[8,176,128]{2,1,0:T(8,128)(2,1)S(1)} all-to-all(bf16[8,176,128]{2,1,0:T(8,128)(2,1)S(1)} %get-tuple-element.33), channel_id=1, replica_groups=mesh['z'=8,'yl'=2,'core'=2,'x'=4,'yh'=2] {'x','yh'}, dimensions={0} | all-to-all | bytes 720896 | tf_op jit(solution)/shard_map/all_to_all | solution.py:219
  63.1 2.0 %shard_map.118 = (bf16[8,128,128]{2,1,0:T(8,128)(2,1)S(1)}, bf16[1120,128]{1,0:T(8,128)(2,1)S(1)}) custom-call(s32[8,4,8]{2,1,0:T(4,128)S(1)} %pad_add_fusion.meta, bf16[8,4,6,128,128]{4,3,2,1,0:T(8,128)(2,1)S(1)} %shard_map.112.held, bf16[8,176,128]{2,1,0:T(8,128)(2,1)S(1)} %all_to_all.16.got), custom_call_target="tpu_custom_call" | custom-call | flops 402653184 | bytes 6291456 | tf_op jit(solution)/shard_map/pallas_call | solution.py:286
  65.3 1.5 %shard_map.117.far = bf16[8,128,128]{2,1,0:T(8,128)(2,1)S(1)} custom-call(s32[8,4,8]{2,1,0:T(4,128)S(1)} %pad_add_fusion.meta, bf16[8,4,6,128,128]{4,3,2,1,0:T(8,128)(2,1)S(1)} %shard_map.112.held, bf16[8,176,128]{2,1,0:T(8,128)(2,1)S(1)} %all_to_all.16.got), custom_call_target="tpu_custom_call" | custom-call | flops 201326592 | bytes 3145728 | tf_op jit(solution)/shard_map/pallas_call | solution.py:296
  67.9 1.9 %collective-permute-start.11 = (f32[48,128]{1,0:T(8,128)S(1)}, f32[48,128]{1,0:T(8,128)S(1)}, u32[]{:S(2)}, u32[]{:S(2)}) collective-permute-start(f32[48,128]{1,0:T(8,128)S(1)} %shard_map.121.grads), channel_id=1, source_target_pairs={{0,32},{1,33},{2,34},{3,35},{4,36},{5,37},{6,38},{7,39},{8,40},{9,... | collective-permute-start | bytes 73736 | tf_op jit(solution)/shard_map/ppermute | solution.py:229
  71.5 1.5 %shard_map.120.own = f32[8,128,128]{2,1,0:T(8,128)S(1)} custom-call(s32[8,4,8]{2,1,0:T(4,128)S(1)} %pad_add_fusion.meta, bf16[8,4,6,128,128]{4,3,2,1,0:T(8,128)(2,1)S(1)} %shard_map.112.held, bf16[8,176,128]{2,1,0:T(8,128)(2,1)S(1)} %all_to_all.16.got), custom_call_target="tpu_custom_call" | custom-call | flops 201326592 | bytes 3145728 | tf_op jit(solution)/shard_map/pallas_call | solution.py:302
  73.0 2.8 %collective-permute-done.11.one = f32[48,128]{1,0:T(8,128)S(1)} collective-permute-done((f32[48,128]{1,0:T(8,128)S(1)}, f32[48,128]{1,0:T(8,128)S(1)}, u32[]{:S(2)}, u32[]{:S(2)}) %collective-permute-start.11) | collective-permute-done | bytes 24608 | tf_op jit(solution)/shard_map/ppermute | solution.py:229
  75.8 3.2 %collective-permute-done.12.two = f32[48,128]{1,0:T(8,128)S(1)} collective-permute-done((f32[48,128]{1,0:T(8,128)S(1)}, f32[48,128]{1,0:T(8,128)S(1)}, u32[]{:S(2)}, u32[]{:S(2)}) %collective-permute-start.12) | collective-permute-done | bytes 24608 | tf_op jit(solution)/shard_map/ppermute | solution.py:229
  80.8 3.7 %collective-permute-done.15 = bf16[4,128,128]{2,1,0:T(8,128)(2,1)S(1)} collective-permute-done((bf16[4,128,128]{2,1,0:T(8,128)(2,1)S(1)}, bf16[4,128,128]{2,1,0:T(8,128)(2,1)S(1)}, u32[]{:S(2)}, u32[]{:S(2)}) %collective-permute-start.15) | collective-permute-done | bytes 131104 | tf_op jit(solution)/shard_map/ppermute | solution.py:229
  84.6 2.0 %collective-permute-start.16 = (bf16[4,128,128]{2,1,0:T(8,128)(2,1)S(1)}, bf16[4,128,128]{2,1,0:T(8,128)(2,1)S(1)}, u32[]{:S(2)}, u32[]{:S(2)}) collective-permute-start(bf16[4,128,128]{2,1,0:T(8,128)(2,1)S(1)} %collective-permute-done.15), channel_id=1, source_target_pairs={{0,192},{1,33},{2,2},{3,99},{4,68},{5,165},{6,134},{7,231},{8,200}... | collective-permute-start | bytes 393224 | tf_op jit(solution)/shard_map/ppermute | solution.py:229
  86.6 2.0 %collective-permute-start.17 = (f32[48,128]{1,0:T(8,128)S(1)}, f32[48,128]{1,0:T(8,128)S(1)}, u32[]{:S(2)}, u32[]{:S(2)}) collective-permute-start(f32[48,128]{1,0:T(8,128)S(1)} %shard_map.123), channel_id=1, source_target_pairs={{0,16},{1,17},{2,18},{3,19},{4,20},{5,21},{6,22},{7,23},{8,24},{9,... | collective-permute-start | bytes 73736 | tf_op jit(solution)/shard_map/ppermute | solution.py:229
  88.6 1.9 %collective-permute-done.17 = f32[48,128]{1,0:T(8,128)S(1)} collective-permute-done((f32[48,128]{1,0:T(8,128)S(1)}, f32[48,128]{1,0:T(8,128)S(1)}, u32[]{:S(2)}, u32[]{:S(2)}) %collective-permute-start.17) | collective-permute-done | bytes 24608 | tf_op jit(solution)/shard_map/ppermute | solution.py:229
  90.5 3.4 %collective-permute-start.18 = (f32[48,128]{1,0:T(8,128)S(1)}, f32[48,128]{1,0:T(8,128)S(1)}, u32[]{:S(2)}, u32[]{:S(2)}) collective-permute-start(f32[48,128]{1,0:T(8,128)S(1)} %add.10), channel_id=1, source_target_pairs={{0,128},{1,129},{2,130},{3,131},{4,132},{5,133},{6,134},{7,135},{8... | collective-permute-start | bytes 73736 | tf_op jit(solution)/shard_map/ppermute | solution.py:229
  94.0 4.3 %collective-permute-done.18 = f32[48,128]{1,0:T(8,128)S(1)} collective-permute-done((f32[48,128]{1,0:T(8,128)S(1)}, f32[48,128]{1,0:T(8,128)S(1)}, u32[]{:S(2)}, u32[]{:S(2)}) %collective-permute-start.18) | collective-permute-done | bytes 24608 | tf_op jit(solution)/shard_map/ppermute | solution.py:229
  98.3 15.4 %all_to_all.17.got = bf16[8,160,128]{2,1,0:T(8,128)(2,1)S(1)} all-to-all(bf16[8,160,128]{2,1,0:T(8,128)(2,1)S(1)} %shard_map.124), channel_id=1, replica_groups=mesh['z'=8,'yl'=2,'core'=2,'x'=4,'yh'=2] {'x','yh'}, dimensions={0} | all-to-all | bytes 655360 | tf_op jit(solution)/shard_map/all_to_all | solution.py:219
  (47 shorter events, 8.6 us)
Async XLA Ops:
  2.4 12.7 %collective-permute-start = (bf16[4,128,128]{2,1,0:T(8,128)(2,1)S(1)}, bf16[4,128,128]{2,1,0:T(8,128)(2,1)S(1)}, u32[]{:S(2)}, u32[]{:S(2)}) collective-permute-start(bf16[4,128,128]{2,1,0:T(8,128)(2,1)S(1)} %get-tuple-element.24), channel_id=1, source_target_pairs={{0,0},{1,33},{2,66},{3,99},{4,132},{5,165},{6,198},{7,231},{8,8},{... | collective-permute-start | bytes 393224 | tf_op jit(solution)/shard_map/ppermute | solution.py:229
  3.0 13.7 %collective-permute-start.2 = (bf16[4,128,128]{2,1,0:T(8,128)(2,1)S(1)}, bf16[4,128,128]{2,1,0:T(8,128)(2,1)S(1)}, u32[]{:S(2)}, u32[]{:S(2)}) collective-permute-start(bf16[4,128,128]{2,1,0:T(8,128)(2,1)S(1)} %get-tuple-element.28), channel_id=1, source_target_pairs={{0,66},{1,231},{2,0},{3,165},{4,198},{5,99},{6,132},{7,33},{8,74},... | collective-permute-start | bytes 393224 | tf_op jit(solution)/shard_map/ppermute | solution.py:229
  12.2 2.8 %copy-start.3 = (s32[8,4,6]{0,1,2:T(4,128)S(1)}, s32[8,4,6]{0,1,2:T(4,128)}, u32[]{:S(2)}) copy-start(s32[8,4,6]{0,1,2:T(4,128)} %param.10) | copy-start | bytes 2308
  12.2 2.9 %copy-start.4 = (s32[8,4]{0,1:T(4,128)S(1)}, s32[8,4]{0,1:T(4,128)}, u32[]{:S(2)}) copy-start(s32[8,4]{0,1:T(4,128)} %param.11) | copy-start | bytes 388
  15.1 8.3 %collective-permute-start.4 = (bf16[4,128,128]{2,1,0:T(8,128)(2,1)S(1)}, bf16[4,128,128]{2,1,0:T(8,128)(2,1)S(1)}, u32[]{:S(2)}, u32[]{:S(2)}) collective-permute-start(bf16[4,128,128]{2,1,0:T(8,128)(2,1)S(1)} %collective-permute-done.low), channel_id=1, source_target_pairs={{0,16},{1,17},{2,18},{3,19},{4,20},{5,21},{6,22},{7,23},{8,24},{9,... | collective-permute-start | bytes 393224 | tf_op jit(solution)/shard_map/ppermute | solution.py:229
  16.7 9.5 %collective-permute-start.6 = (bf16[4,128,128]{2,1,0:T(8,128)(2,1)S(1)}, bf16[4,128,128]{2,1,0:T(8,128)(2,1)S(1)}, u32[]{:S(2)}, u32[]{:S(2)}) collective-permute-start(bf16[4,128,128]{2,1,0:T(8,128)(2,1)S(1)} %collective-permute-done.2.high), channel_id=1, source_target_pairs={{0,16},{1,17},{2,18},{3,19},{4,20},{5,21},{6,22},{7,23},{8,24},{9,... | collective-permute-start | bytes 393224 | tf_op jit(solution)/shard_map/ppermute | solution.py:229
  19.4 8.3 %collective-permute-start.1 = (bf16[4,128,128]{2,1,0:T(8,128)(2,1)S(1)}, bf16[4,128,128]{2,1,0:T(8,128)(2,1)S(1)}, u32[]{:S(2)}, u32[]{:S(2)}) collective-permute-start(bf16[4,128,128]{2,1,0:T(8,128)(2,1)S(1)} %collective-permute-done.low), channel_id=1, source_target_pairs={{0,8},{1,9},{2,10},{3,11},{4,12},{5,13},{6,14},{7,15},{8,32},{9,33... | collective-permute-start | bytes 393224 | tf_op jit(solution)/shard_map/ppermute | solution.py:229
  20.9 29.2 %copy-start = (bf16[128,256]{1,0:T(8,128)(2,1)S(1)}, bf16[128,256]{1,0:T(8,128)(2,1)}, u32[]{:S(2)}) copy-start(bf16[128,256]{1,0:T(8,128)(2,1)} %weight.1) | copy-start | bytes 196612
  20.9 29.1 %copy-start.1 = (bf16[128,256]{1,0:T(8,128)(2,1)S(1)}, bf16[128,256]{1,0:T(8,128)(2,1)}, u32[]{:S(2)}) copy-start(bf16[128,256]{1,0:T(8,128)(2,1)} %cot.1) | copy-start | bytes 196612
  20.9 29.1 %copy-start.2 = (f32[256]{0:T(256)S(1)}, f32[256]{0:T(256)}, u32[]{:S(2)}) copy-start(f32[256]{0:T(256)} %param.14) | copy-start | bytes 3076
  21.0 6.7 %collective-permute-start.3 = (bf16[4,128,128]{2,1,0:T(8,128)(2,1)S(1)}, bf16[4,128,128]{2,1,0:T(8,128)(2,1)S(1)}, u32[]{:S(2)}, u32[]{:S(2)}) collective-permute-start(bf16[4,128,128]{2,1,0:T(8,128)(2,1)S(1)} %collective-permute-done.2.high), channel_id=1, source_target_pairs={{0,8},{1,9},{2,10},{3,11},{4,12},{5,13},{6,14},{7,15},{8,32},{9,33... | collective-permute-start | bytes 393224 | tf_op jit(solution)/shard_map/ppermute | solution.py:229
  23.4 4.3 %collective-permute-start.5 = (bf16[4,128,128]{2,1,0:T(8,128)(2,1)S(1)}, bf16[4,128,128]{2,1,0:T(8,128)(2,1)S(1)}, u32[]{:S(2)}, u32[]{:S(2)}) collective-permute-start(bf16[4,128,128]{2,1,0:T(8,128)(2,1)S(1)} %collective-permute-done.4.low), channel_id=1, source_target_pairs={{0,8},{1,9},{2,10},{3,11},{4,12},{5,13},{6,14},{7,15},{8,0},{9,1},... | collective-permute-start | bytes 393224 | tf_op jit(solution)/shard_map/ppermute | solution.py:229
  26.2 1.5 %collective-permute-start.7 = (bf16[4,128,128]{2,1,0:T(8,128)(2,1)S(1)}, bf16[4,128,128]{2,1,0:T(8,128)(2,1)S(1)}, u32[]{:S(2)}, u32[]{:S(2)}) collective-permute-start(bf16[4,128,128]{2,1,0:T(8,128)(2,1)S(1)} %collective-permute-done.6.high), channel_id=1, source_target_pairs={{0,8},{1,9},{2,10},{3,11},{4,12},{5,13},{6,14},{7,15},{8,0},{9,1},... | collective-permute-start | bytes 393224 | tf_op jit(solution)/shard_map/ppermute | solution.py:229
  65.1 1.7 %collective-permute-start.8 = (bf16[1120,128]{1,0:T(8,128)(2,1)S(1)}, bf16[1120,128]{1,0:T(8,128)(2,1)S(1)}, u32[]{:S(2)}, u32[]{:S(2)}) collective-permute-start(bf16[1120,128]{1,0:T(8,128)(2,1)S(1)} %get-tuple-element.34.mine), channel_id=1, source_target_pairs={{0,8},{1,9},{2,10},{3,11},{4,12},{5,13},{6,14},{7,15},{8,0},{9,1},... | collective-permute-start | bytes 860168 | tf_op jit(solution)/shard_map/ppermute | solution.py:229
  65.2 7.8 %collective-permute-start.9 = (bf16[8,128,128]{2,1,0:T(8,128)(2,1)S(1)}, bf16[8,128,128]{2,1,0:T(8,128)(2,1)S(1)}, u32[]{:S(2)}, u32[]{:S(2)}) collective-permute-start(bf16[8,128,128]{2,1,0:T(8,128)(2,1)S(1)} %get-tuple-element.36), channel_id=1, source_target_pairs={{0,232},{1,233},{2,234},{3,235},{4,236},{5,237},{6,238},{7,239},{8... | collective-permute-start | bytes 786440 | tf_op jit(solution)/shard_map/ppermute | solution.py:229
  66.9 12.6 %collective-permute-start.10 = (bf16[8,128,128]{2,1,0:T(8,128)(2,1)S(1)}, bf16[8,128,128]{2,1,0:T(8,128)(2,1)S(1)}, u32[]{:S(2)}, u32[]{:S(2)}) collective-permute-start(bf16[8,128,128]{2,1,0:T(8,128)(2,1)S(1)} %shard_map.119), channel_id=1, source_target_pairs={{0,240},{1,241},{2,242},{3,243},{4,244},{5,245},{6,246},{7,247},{8... | collective-permute-start | bytes 786440 | tf_op jit(solution)/shard_map/ppermute | solution.py:229
  67.9 7.9 %collective-permute-start.11 = (f32[48,128]{1,0:T(8,128)S(1)}, f32[48,128]{1,0:T(8,128)S(1)}, u32[]{:S(2)}, u32[]{:S(2)}) collective-permute-start(f32[48,128]{1,0:T(8,128)S(1)} %shard_map.121.grads), channel_id=1, source_target_pairs={{0,32},{1,33},{2,34},{3,35},{4,36},{5,37},{6,38},{7,39},{8,40},{9,... | collective-permute-start | bytes 73736 | tf_op jit(solution)/shard_map/ppermute | solution.py:229
  69.8 9.2 %collective-permute-start.12 = (f32[48,128]{1,0:T(8,128)S(1)}, f32[48,128]{1,0:T(8,128)S(1)}, u32[]{:S(2)}, u32[]{:S(2)}) collective-permute-start(f32[48,128]{1,0:T(8,128)S(1)} %shard_map.121.grads), channel_id=1, source_target_pairs={{0,64},{1,65},{2,66},{3,67},{4,68},{5,69},{6,70},{7,71},{8,72},{9,... | collective-permute-start | bytes 73736 | tf_op jit(solution)/shard_map/ppermute | solution.py:229
  70.6 8.8 %collective-permute-start.13 = (f32[48,128]{1,0:T(8,128)S(1)}, f32[48,128]{1,0:T(8,128)S(1)}, u32[]{:S(2)}, u32[]{:S(2)}) collective-permute-start(f32[48,128]{1,0:T(8,128)S(1)} %shard_map.121.grads), channel_id=1, source_target_pairs={{0,96},{1,97},{2,98},{3,99},{4,100},{5,101},{6,102},{7,103},{8,104... | collective-permute-start | bytes 73736 | tf_op jit(solution)/shard_map/ppermute | solution.py:229
  79.5 5.1 %collective-permute-start.15 = (bf16[4,128,128]{2,1,0:T(8,128)(2,1)S(1)}, bf16[4,128,128]{2,1,0:T(8,128)(2,1)S(1)}, u32[]{:S(2)}, u32[]{:S(2)}) collective-permute-start(bf16[4,128,128]{2,1,0:T(8,128)(2,1)S(1)} %get-tuple-element.40.high), channel_id=1, source_target_pairs={{0,2},{1,7},{2,0},{3,5},{4,6},{5,3},{6,4},{7,1},{8,10},{9,15},{10,... | collective-permute-start | bytes 393224 | tf_op jit(solution)/shard_map/ppermute | solution.py:229
  80.2 18.1 %collective-permute-start.14 = (bf16[4,128,128]{2,1,0:T(8,128)(2,1)S(1)}, bf16[4,128,128]{2,1,0:T(8,128)(2,1)S(1)}, u32[]{:S(2)}, u32[]{:S(2)}) collective-permute-start(bf16[4,128,128]{2,1,0:T(8,128)(2,1)S(1)} %get-tuple-element.39.low), channel_id=1, source_target_pairs={{0,0},{1,225},{2,194},{3,163},{4,132},{5,101},{6,70},{7,39},{8,8},... | collective-permute-start | bytes 393224 | tf_op jit(solution)/shard_map/ppermute | solution.py:229
  84.6 13.7 %collective-permute-start.16 = (bf16[4,128,128]{2,1,0:T(8,128)(2,1)S(1)}, bf16[4,128,128]{2,1,0:T(8,128)(2,1)S(1)}, u32[]{:S(2)}, u32[]{:S(2)}) collective-permute-start(bf16[4,128,128]{2,1,0:T(8,128)(2,1)S(1)} %collective-permute-done.15), channel_id=1, source_target_pairs={{0,192},{1,33},{2,2},{3,99},{4,68},{5,165},{6,134},{7,231},{8,200}... | collective-permute-start | bytes 393224 | tf_op jit(solution)/shard_map/ppermute | solution.py:229
  86.6 3.9 %collective-permute-start.17 = (f32[48,128]{1,0:T(8,128)S(1)}, f32[48,128]{1,0:T(8,128)S(1)}, u32[]{:S(2)}, u32[]{:S(2)}) collective-permute-start(f32[48,128]{1,0:T(8,128)S(1)} %shard_map.123), channel_id=1, source_target_pairs={{0,16},{1,17},{2,18},{3,19},{4,20},{5,21},{6,22},{7,23},{8,24},{9,... | collective-permute-start | bytes 73736 | tf_op jit(solution)/shard_map/ppermute | solution.py:229
  90.5 7.7 %collective-permute-start.18 = (f32[48,128]{1,0:T(8,128)S(1)}, f32[48,128]{1,0:T(8,128)S(1)}, u32[]{:S(2)}, u32[]{:S(2)}) collective-permute-start(f32[48,128]{1,0:T(8,128)S(1)} %add.10), channel_id=1, source_target_pairs={{0,128},{1,129},{2,130},{3,131},{4,132},{5,133},{6,134},{7,135},{8... | collective-permute-start | bytes 73736 | tf_op jit(solution)/shard_map/ppermute | solution.py:229

commit v9 on v8

--- a/solution.py
+++ b/solution.py
@@ -173,7 +173,7 @@
     out[...] = (grads[...] + one[...]) + (two[...] + three[...])
 
 
-def total_kernel(own, near, far, one, two, three, low, high):
+def total_kernel(own, near, far, low, high):
     for half, first in ((low, 0), (high, HALF)):
         rows = pl.ds(first, HALF)
         total = own[rows] + near[rows].astype(F32) + far[rows].astype(F32)
@@ -304,14 +304,11 @@
     )
     (grads,) = call(pair_kernel, [((GRAD, T), F32)], [VMEM] * 2, (), PAIR_FLOPS)(mine, other)
     groups = [swap(grads, bits) for bits in (4, 8, 12)]
-    anywhere = pl.BlockSpec(memory_space=pl.ANY)
-    low, high = call(total_kernel, [(half, BF16), (half, BF16)], [VMEM] * 3 + [anywhere] * 3)(
-        own, near, far, *groups
-    )
+    low, high = call(total_kernel, [(half, BF16), (half, BF16)], [VMEM] * 3)(own, near, far)
     sent_low, sent_high = low, high
     low = move(low, lambda b, r: (b - 4 * r, r))
-    high = move(high, lambda b, r: (b, column(r)))
-    high = move(high, lambda b, r: (b - 4 * column(r), r))
+    high = move(high, lambda b, r: (b - 4 * r, r ^ 2))
+    anywhere = pl.BlockSpec(memory_space=pl.ANY)
     (grads,) = call(
         group_kernel, [((GRAD, T), F32)], [VMEM] * 4 + [anywhere] * 2, (), GROUP_FLOPS
     )(grads, *groups, sent_low, sent_high)

time: 115 us -> 113 us (0.983)
  waiting for transfers between devices: 21.6 us -> 14.3 us
  starting transfers between devices: 27.7 us -> 30.5 us
  blocking collectives: 47.8 us -> 50.5 us
    ppermute x19 -> x18, waiting for transfers between devices: 21.6 us -> 14.3 us  [move(): return lax.ppermute(value, BLK + REP, pairs)]
    ppermute x19 -> x18, starting transfers between devices: 27.7 us -> 30.5 us  [move(): return lax.ppermute(value, BLK + REP, pairs)]
    all_to_all x3, blocking collectives: 47.8 us -> 50.5 us  [exchange(): return lax.all_to_all(value, axes, 0, 0, tiled=True)]
  transfers between devices with their start and end apart: 19 -> 18, of which waited for: 8 -> 5; matrix products, arithmetic and copies ran while one was open for 0% -> 0% of each run, Pallas kernels for 8% -> 8%
where the time goes in v9:
time: 113 us
  blocking collectives  50.5 us (45%)
  starting transfers between devices  30.5 us (27%)
  Pallas kernels  16.4 us (15%)
  waiting for transfers between devices  14.3 us (13%)
    all_to_all x3, blocking collectives, exchange(): return lax.all_to_all(value, axes, 0, 0, tiled=True)  50.5 us
    ppermute x18, starting transfers between devices, move(): return lax.ppermute(value, BLK + REP, pairs)  30.5 us
    ppermute x18, waiting for transfers between devices, move(): return lax.ppermute(value, BLK + REP, pairs)  14.3 us
    pallas_call x1, Pallas kernels, on_device(): call(load_kernel, [(edges.shape, BF16)], [HBM], [pltpu.SemaphoreType.DMA]...  2.82 us
  transfers between devices with their start and end apart: 18, of which 5 were waited for; matrix products, arithmetic and copies ran while one was open for 0% of the time, Pallas kernels for 8%

profile of v9, /device:TPU:32, one launch (start us, length us, event | category | flops | bytes accessed | tf_op | source)
XLA Modules:
  0.0 112.7 jit_solution(1015606703522350548)
XLA Ops:
  0.6 1.7 %shard_map.111 = (bf16[4,128,128]{2,1,0:T(8,128)(2,1)S(1)}, bf16[4,128,128]{2,1,0:T(8,128)(2,1)S(1)}, f32[128,128]{1,0:T(8,128)S(1)}) custom-call(s32[1]{0:T(128)} %bitcast.rep, bf16[1024,128]{1,0:T(8,128)(2,1)} %features.1, s32[8,128]{1,0:T(8,128)} %bitcast.10), custom_call_target="tpu_custom_call" | custom-call | bytes 1048576 | tf_op jit(solution)/shard_map/pallas_call | solution.py:248
  3.0 9.1 %collective-permute-start.2 = (bf16[4,128,128]{2,1,0:T(8,128)(2,1)S(1)}, bf16[4,128,128]{2,1,0:T(8,128)(2,1)S(1)}, u32[]{:S(2)}, u32[]{:S(2)}) collective-permute-start(bf16[4,128,128]{2,1,0:T(8,128)(2,1)S(1)} %get-tuple-element.28), channel_id=1, source_target_pairs={{0,66},{1,231},{2,0},{3,165},{4,198},{5,99},{6,132},{7,33},{8,74},... | collective-permute-start | bytes 393224 | tf_op jit(solution)/shard_map/ppermute | solution.py:229
  12.2 2.8 %shard_map.112.held = bf16[8,4,6,128,128]{4,3,2,1,0:T(8,128)(2,1)S(1)} custom-call(bf16[8,4,6,128,128]{4,3,2,1,0:T(8,128)(2,1)} %edges.1), custom_call_target="tpu_custom_call" | custom-call | bytes 12582912 | tf_op jit(solution)/shard_map/pallas_call | solution.py:256
  15.1 1.7 %collective-permute-start.4 = (bf16[4,128,128]{2,1,0:T(8,128)(2,1)S(1)}, bf16[4,128,128]{2,1,0:T(8,128)(2,1)S(1)}, u32[]{:S(2)}, u32[]{:S(2)}) collective-permute-start(bf16[4,128,128]{2,1,0:T(8,128)(2,1)S(1)} %collective-permute-done.low), channel_id=1, source_target_pairs={{0,16},{1,17},{2,18},{3,19},{4,20},{5,21},{6,22},{7,23},{8,24},{9,... | collective-permute-start | bytes 393224 | tf_op jit(solution)/shard_map/ppermute | solution.py:229
  16.7 2.7 %collective-permute-start.6 = (bf16[4,128,128]{2,1,0:T(8,128)(2,1)S(1)}, bf16[4,128,128]{2,1,0:T(8,128)(2,1)S(1)}, u32[]{:S(2)}, u32[]{:S(2)}) collective-permute-start(bf16[4,128,128]{2,1,0:T(8,128)(2,1)S(1)} %collective-permute-done.2.high), channel_id=1, source_target_pairs={{0,16},{1,17},{2,18},{3,19},{4,20},{5,21},{6,22},{7,23},{8,24},{9,... | collective-permute-start | bytes 393224 | tf_op jit(solution)/shard_map/ppermute | solution.py:229
  19.4 1.5 %shard_map.113.total = f32[8,128,128]{2,1,0:T(8,128)S(1)} custom-call(s32[8,4,8]{2,1,0:T(4,128)S(1)} %pad_add_fusion.meta, bf16[8,4,6,128,128]{4,3,2,1,0:T(8,128)(2,1)S(1)} %shard_map.112.held, bf16[4,128,128]{2,1,0:T(8,128)(2,1)S(1)} %collective-permute-done.low, bf16[4,128,128]{2,1,0:T(8,128)(2,1)S(1)} %collective-permute-done.2.high), custom_call_target="tpu_custom_call" | custom-call | flops 201326592 | bytes 3145728 | tf_op jit(solution)/shard_map/pallas_call | solution.py:264
  21.0 2.4 %collective-permute-done.4.low = bf16[4,128,128]{2,1,0:T(8,128)(2,1)S(1)} collective-permute-done((bf16[4,128,128]{2,1,0:T(8,128)(2,1)S(1)}, bf16[4,128,128]{2,1,0:T(8,128)(2,1)S(1)}, u32[]{:S(2)}, u32[]{:S(2)}) %collective-permute-start.4) | collective-permute-done | bytes 131104 | tf_op jit(solution)/shard_map/ppermute | solution.py:229
  23.4 2.8 %collective-permute-done.6.high = bf16[4,128,128]{2,1,0:T(8,128)(2,1)S(1)} collective-permute-done((bf16[4,128,128]{2,1,0:T(8,128)(2,1)S(1)}, bf16[4,128,128]{2,1,0:T(8,128)(2,1)S(1)}, u32[]{:S(2)}, u32[]{:S(2)}) %collective-permute-start.6) | collective-permute-done | bytes 131104 | tf_op jit(solution)/shard_map/ppermute | solution.py:229
  26.2 1.5 %shard_map.114.total = f32[8,128,128]{2,1,0:T(8,128)S(1)} custom-call(s32[8,4,8]{2,1,0:T(4,128)S(1)} %pad_add_fusion.meta, bf16[8,4,6,128,128]{4,3,2,1,0:T(8,128)(2,1)S(1)} %shard_map.112.held, bf16[4,128,128]{2,1,0:T(8,128)(2,1)S(1)} %collective-permute-done.4.low, bf16[4,128,128]{2,1,0:T(8,128)(2,1)S(1)} %collective-permute-done.6.high, ...), custom_call_target="tpu_custom_call" | custom-call | flops 201326592 | bytes 3145728 | tf_op jit(solution)/shard_map/pallas_call | solution.py:270
  27.7 2.2 %shard_map.115 = bf16[8,128,128]{2,1,0:T(8,128)(2,1)S(1)} custom-call(s32[8,4,8]{2,1,0:T(4,128)S(1)} %pad_add_fusion.meta, bf16[8,4,6,128,128]{4,3,2,1,0:T(8,128)(2,1)S(1)} %shard_map.112.held, bf16[4,128,128]{2,1,0:T(8,128)(2,1)S(1)} %collective-permute-done.1.near_low, bf16[4,128,128]{2,1,0:T(8,128)(2,1)S(1)} %collective-permute-done.3.near_high, ...), custom_call_target="tpu_custom_call" | custom-call | flops 402653184 | bytes 6291456 | tf_op jit(solution)/shard_map/pallas_call | solution.py:273
  29.9 20.2 %all_to_all.15.parts = bf16[8,128,128]{2,1,0:T(8,128)(2,1)S(1)} all-to-all(bf16[8,128,128]{2,1,0:T(8,128)(2,1)S(1)} %shard_map.115), channel_id=1, replica_groups=mesh['z'=8,'yl'=2,'core'=2,'x'=4,'yh'=2] {'x','yh'}, dimensions={0} | all-to-all | bytes 524288 | tf_op jit(solution)/shard_map/all_to_all | solution.py:219
  50.9 12.2 %all_to_all.16.got = bf16[8,176,128]{2,1,0:T(8,128)(2,1)S(1)} all-to-all(bf16[8,176,128]{2,1,0:T(8,128)(2,1)S(1)} %get-tuple-element.33), channel_id=1, replica_groups=mesh['z'=8,'yl'=2,'core'=2,'x'=4,'yh'=2] {'x','yh'}, dimensions={0} | all-to-all | bytes 720896 | tf_op jit(solution)/shard_map/all_to_all | solution.py:219
  63.1 2.0 %shard_map.118 = (bf16[8,128,128]{2,1,0:T(8,128)(2,1)S(1)}, bf16[1120,128]{1,0:T(8,128)(2,1)S(1)}) custom-call(s32[8,4,8]{2,1,0:T(4,128)S(1)} %pad_add_fusion.meta, bf16[8,4,6,128,128]{4,3,2,1,0:T(8,128)(2,1)S(1)} %shard_map.112.held, bf16[8,176,128]{2,1,0:T(8,128)(2,1)S(1)} %all_to_all.16.got), custom_call_target="tpu_custom_call" | custom-call | flops 402653184 | bytes 6291456 | tf_op jit(solution)/shard_map/pallas_call | solution.py:286
  65.3 1.5 %shard_map.117.far = bf16[8,128,128]{2,1,0:T(8,128)(2,1)S(1)} custom-call(s32[8,4,8]{2,1,0:T(4,128)S(1)} %pad_add_fusion.meta, bf16[8,4,6,128,128]{4,3,2,1,0:T(8,128)(2,1)S(1)} %shard_map.112.held, bf16[8,176,128]{2,1,0:T(8,128)(2,1)S(1)} %all_to_all.16.got), custom_call_target="tpu_custom_call" | custom-call | flops 201326592 | bytes 3145728 | tf_op jit(solution)/shard_map/pallas_call | solution.py:296
  66.9 1.1 collective-permute-start.10
  67.9 1.9 %collective-permute-start.13 = (f32[48,128]{1,0:T(8,128)S(1)}, f32[48,128]{1,0:T(8,128)S(1)}, u32[]{:S(2)}, u32[]{:S(2)}) collective-permute-start(f32[48,128]{1,0:T(8,128)S(1)} %shard_map.122.grads), channel_id=1, source_target_pairs={{0,32},{1,33},{2,34},{3,35},{4,36},{5,37},{6,38},{7,39},{8,40},{9,... | collective-permute-start | bytes 73736 | tf_op jit(solution)/shard_map/ppermute | solution.py:229
  71.5 1.5 %shard_map.120.own = f32[8,128,128]{2,1,0:T(8,128)S(1)} custom-call(s32[8,4,8]{2,1,0:T(4,128)S(1)} %pad_add_fusion.meta, bf16[8,4,6,128,128]{4,3,2,1,0:T(8,128)(2,1)S(1)} %shard_map.112.held, bf16[8,176,128]{2,1,0:T(8,128)(2,1)S(1)} %all_to_all.16.got), custom_call_target="tpu_custom_call" | custom-call | flops 201326592 | bytes 3145728 | tf_op jit(solution)/shard_map/pallas_call | solution.py:302
  73.0 2.6 %collective-permute-done.10.far = bf16[8,128,128]{2,1,0:T(8,128)(2,1)S(1)} collective-permute-done((bf16[8,128,128]{2,1,0:T(8,128)(2,1)S(1)}, bf16[8,128,128]{2,1,0:T(8,128)(2,1)S(1)}, u32[]{:S(2)}, u32[]{:S(2)}) %collective-permute-start.10) | collective-permute-done | bytes 262176 | tf_op jit(solution)/shard_map/ppermute | solution.py:229
  76.4 5.0 %collective-permute-start.12 = (bf16[4,128,128]{2,1,0:T(8,128)(2,1)S(1)}, bf16[4,128,128]{2,1,0:T(8,128)(2,1)S(1)}, u32[]{:S(2)}, u32[]{:S(2)}) collective-permute-start(bf16[4,128,128]{2,1,0:T(8,128)(2,1)S(1)} %get-tuple-element.39.high), channel_id=1, source_target_pairs={{0,2},{1,227},{2,192},{3,161},{4,134},{5,103},{6,68},{7,37},{8,10}... | collective-permute-start | bytes 393224 | tf_op jit(solution)/shard_map/ppermute | solution.py:229
  81.4 2.8 %collective-permute-start.16 = (f32[48,128]{1,0:T(8,128)S(1)}, f32[48,128]{1,0:T(8,128)S(1)}, u32[]{:S(2)}, u32[]{:S(2)}) collective-permute-start(f32[48,128]{1,0:T(8,128)S(1)} %shard_map.123), channel_id=1, source_target_pairs={{0,16},{1,17},{2,18},{3,19},{4,20},{5,21},{6,22},{7,23},{8,24},{9,... | collective-permute-start | bytes 73736 | tf_op jit(solution)/shard_map/ppermute | solution.py:229
  84.2 1.8 %collective-permute-done.16 = f32[48,128]{1,0:T(8,128)S(1)} collective-permute-done((f32[48,128]{1,0:T(8,128)S(1)}, f32[48,128]{1,0:T(8,128)S(1)}, u32[]{:S(2)}, u32[]{:S(2)}) %collective-permute-start.16) | collective-permute-done | bytes 24608 | tf_op jit(solution)/shard_map/ppermute | solution.py:229
  86.0 3.0 %collective-permute-start.17 = (f32[48,128]{1,0:T(8,128)S(1)}, f32[48,128]{1,0:T(8,128)S(1)}, u32[]{:S(2)}, u32[]{:S(2)}) collective-permute-start(f32[48,128]{1,0:T(8,128)S(1)} %add.10), channel_id=1, source_target_pairs={{0,128},{1,129},{2,130},{3,131},{4,132},{5,133},{6,134},{7,135},{8... | collective-permute-start | bytes 73736 | tf_op jit(solution)/shard_map/ppermute | solution.py:229
  89.0 4.7 %collective-permute-done.17 = f32[48,128]{1,0:T(8,128)S(1)} collective-permute-done((f32[48,128]{1,0:T(8,128)S(1)}, f32[48,128]{1,0:T(8,128)S(1)}, u32[]{:S(2)}, u32[]{:S(2)}) %collective-permute-start.17) | collective-permute-done | bytes 24608 | tf_op jit(solution)/shard_map/ppermute | solution.py:229
  93.8 18.2 %all_to_all.17.got = bf16[8,160,128]{2,1,0:T(8,128)(2,1)S(1)} all-to-all(bf16[8,160,128]{2,1,0:T(8,128)(2,1)S(1)} %shard_map.124), channel_id=1, replica_groups=mesh['z'=8,'yl'=2,'core'=2,'x'=4,'yh'=2] {'x','yh'}, dimensions={0} | all-to-all | bytes 655360 | tf_op jit(solution)/shard_map/all_to_all | solution.py:219
  (45 shorter events, 5.1 us)
Async XLA Ops:
  2.4 12.7 %collective-permute-start = (bf16[4,128,128]{2,1,0:T(8,128)(2,1)S(1)}, bf16[4,128,128]{2,1,0:T(8,128)(2,1)S(1)}, u32[]{:S(2)}, u32[]{:S(2)}) collective-permute-start(bf16[4,128,128]{2,1,0:T(8,128)(2,1)S(1)} %get-tuple-element.24), channel_id=1, source_target_pairs={{0,0},{1,33},{2,66},{3,99},{4,132},{5,165},{6,198},{7,231},{8,8},{... | collective-permute-start | bytes 393224 | tf_op jit(solution)/shard_map/ppermute | solution.py:229
  3.0 13.7 %collective-permute-start.2 = (bf16[4,128,128]{2,1,0:T(8,128)(2,1)S(1)}, bf16[4,128,128]{2,1,0:T(8,128)(2,1)S(1)}, u32[]{:S(2)}, u32[]{:S(2)}) collective-permute-start(bf16[4,128,128]{2,1,0:T(8,128)(2,1)S(1)} %get-tuple-element.28), channel_id=1, source_target_pairs={{0,66},{1,231},{2,0},{3,165},{4,198},{5,99},{6,132},{7,33},{8,74},... | collective-permute-start | bytes 393224 | tf_op jit(solution)/shard_map/ppermute | solution.py:229
  12.2 2.8 %copy-start.3 = (s32[8,4,6]{0,1,2:T(4,128)S(1)}, s32[8,4,6]{0,1,2:T(4,128)}, u32[]{:S(2)}) copy-start(s32[8,4,6]{0,1,2:T(4,128)} %param.10) | copy-start | bytes 2308
  12.2 2.9 %copy-start.4 = (s32[8,4]{0,1:T(4,128)S(1)}, s32[8,4]{0,1:T(4,128)}, u32[]{:S(2)}) copy-start(s32[8,4]{0,1:T(4,128)} %param.11) | copy-start | bytes 388
  15.1 8.3 %collective-permute-start.4 = (bf16[4,128,128]{2,1,0:T(8,128)(2,1)S(1)}, bf16[4,128,128]{2,1,0:T(8,128)(2,1)S(1)}, u32[]{:S(2)}, u32[]{:S(2)}) collective-permute-start(bf16[4,128,128]{2,1,0:T(8,128)(2,1)S(1)} %collective-permute-done.low), channel_id=1, source_target_pairs={{0,16},{1,17},{2,18},{3,19},{4,20},{5,21},{6,22},{7,23},{8,24},{9,... | collective-permute-start | bytes 393224 | tf_op jit(solution)/shard_map/ppermute | solution.py:229
  16.7 9.5 %collective-permute-start.6 = (bf16[4,128,128]{2,1,0:T(8,128)(2,1)S(1)}, bf16[4,128,128]{2,1,0:T(8,128)(2,1)S(1)}, u32[]{:S(2)}, u32[]{:S(2)}) collective-permute-start(bf16[4,128,128]{2,1,0:T(8,128)(2,1)S(1)} %collective-permute-done.2.high), channel_id=1, source_target_pairs={{0,16},{1,17},{2,18},{3,19},{4,20},{5,21},{6,22},{7,23},{8,24},{9,... | collective-permute-start | bytes 393224 | tf_op jit(solution)/shard_map/ppermute | solution.py:229
  19.4 8.3 %collective-permute-start.1 = (bf16[4,128,128]{2,1,0:T(8,128)(2,1)S(1)}, bf16[4,128,128]{2,1,0:T(8,128)(2,1)S(1)}, u32[]{:S(2)}, u32[]{:S(2)}) collective-permute-start(bf16[4,128,128]{2,1,0:T(8,128)(2,1)S(1)} %collective-permute-done.low), channel_id=1, source_target_pairs={{0,8},{1,9},{2,10},{3,11},{4,12},{5,13},{6,14},{7,15},{8,32},{9,33... | collective-permute-start | bytes 393224 | tf_op jit(solution)/shard_map/ppermute | solution.py:229
  20.9 29.2 %copy-start = (bf16[128,256]{1,0:T(8,128)(2,1)S(1)}, bf16[128,256]{1,0:T(8,128)(2,1)}, u32[]{:S(2)}) copy-start(bf16[128,256]{1,0:T(8,128)(2,1)} %weight.1) | copy-start | bytes 196612
  20.9 29.1 %copy-start.1 = (bf16[128,256]{1,0:T(8,128)(2,1)S(1)}, bf16[128,256]{1,0:T(8,128)(2,1)}, u32[]{:S(2)}) copy-start(bf16[128,256]{1,0:T(8,128)(2,1)} %cot.1) | copy-start | bytes 196612
  20.9 29.1 %copy-start.2 = (f32[256]{0:T(256)S(1)}, f32[256]{0:T(256)}, u32[]{:S(2)}) copy-start(f32[256]{0:T(256)} %param.14) | copy-start | bytes 3076
  21.0 6.7 %collective-permute-start.3 = (bf16[4,128,128]{2,1,0:T(8,128)(2,1)S(1)}, bf16[4,128,128]{2,1,0:T(8,128)(2,1)S(1)}, u32[]{:S(2)}, u32[]{:S(2)}) collective-permute-start(bf16[4,128,128]{2,1,0:T(8,128)(2,1)S(1)} %collective-permute-done.2.high), channel_id=1, source_target_pairs={{0,8},{1,9},{2,10},{3,11},{4,12},{5,13},{6,14},{7,15},{8,32},{9,33... | collective-permute-start | bytes 393224 | tf_op jit(solution)/shard_map/ppermute | solution.py:229
  23.4 4.3 %collective-permute-start.5 = (bf16[4,128,128]{2,1,0:T(8,128)(2,1)S(1)}, bf16[4,128,128]{2,1,0:T(8,128)(2,1)S(1)}, u32[]{:S(2)}, u32[]{:S(2)}) collective-permute-start(bf16[4,128,128]{2,1,0:T(8,128)(2,1)S(1)} %collective-permute-done.4.low), channel_id=1, source_target_pairs={{0,8},{1,9},{2,10},{3,11},{4,12},{5,13},{6,14},{7,15},{8,0},{9,1},... | collective-permute-start | bytes 393224 | tf_op jit(solution)/shard_map/ppermute | solution.py:229
  26.2 1.5 %collective-permute-start.7 = (bf16[4,128,128]{2,1,0:T(8,128)(2,1)S(1)}, bf16[4,128,128]{2,1,0:T(8,128)(2,1)S(1)}, u32[]{:S(2)}, u32[]{:S(2)}) collective-permute-start(bf16[4,128,128]{2,1,0:T(8,128)(2,1)S(1)} %collective-permute-done.6.high), channel_id=1, source_target_pairs={{0,8},{1,9},{2,10},{3,11},{4,12},{5,13},{6,14},{7,15},{8,0},{9,1},... | collective-permute-start | bytes 393224 | tf_op jit(solution)/shard_map/ppermute | solution.py:229
  65.1 1.7 %collective-permute-start.8 = (bf16[1120,128]{1,0:T(8,128)(2,1)S(1)}, bf16[1120,128]{1,0:T(8,128)(2,1)S(1)}, u32[]{:S(2)}, u32[]{:S(2)}) collective-permute-start(bf16[1120,128]{1,0:T(8,128)(2,1)S(1)} %get-tuple-element.34.mine), channel_id=1, source_target_pairs={{0,8},{1,9},{2,10},{3,11},{4,12},{5,13},{6,14},{7,15},{8,0},{9,1},... | collective-permute-start | bytes 860168 | tf_op jit(solution)/shard_map/ppermute | solution.py:229
  65.2 7.8 %collective-permute-start.9 = (bf16[8,128,128]{2,1,0:T(8,128)(2,1)S(1)}, bf16[8,128,128]{2,1,0:T(8,128)(2,1)S(1)}, u32[]{:S(2)}, u32[]{:S(2)}) collective-permute-start(bf16[8,128,128]{2,1,0:T(8,128)(2,1)S(1)} %get-tuple-element.36), channel_id=1, source_target_pairs={{0,232},{1,233},{2,234},{3,235},{4,236},{5,237},{6,238},{7,239},{8... | collective-permute-start | bytes 786440 | tf_op jit(solution)/shard_map/ppermute | solution.py:229
  66.9 8.8 %collective-permute-start.10 = (bf16[8,128,128]{2,1,0:T(8,128)(2,1)S(1)}, bf16[8,128,128]{2,1,0:T(8,128)(2,1)S(1)}, u32[]{:S(2)}, u32[]{:S(2)}) collective-permute-start(bf16[8,128,128]{2,1,0:T(8,128)(2,1)S(1)} %shard_map.119), channel_id=1, source_target_pairs={{0,240},{1,241},{2,242},{3,243},{4,244},{5,245},{6,246},{7,247},{8... | collective-permute-start | bytes 786440 | tf_op jit(solution)/shard_map/ppermute | solution.py:229
  67.9 13.4 %collective-permute-start.13 = (f32[48,128]{1,0:T(8,128)S(1)}, f32[48,128]{1,0:T(8,128)S(1)}, u32[]{:S(2)}, u32[]{:S(2)}) collective-permute-start(f32[48,128]{1,0:T(8,128)S(1)} %shard_map.122.grads), channel_id=1, source_target_pairs={{0,32},{1,33},{2,34},{3,35},{4,36},{5,37},{6,38},{7,39},{8,40},{9,... | collective-permute-start | bytes 73736 | tf_op jit(solution)/shard_map/ppermute | solution.py:229
  69.8 11.6 %collective-permute-start.14 = (f32[48,128]{1,0:T(8,128)S(1)}, f32[48,128]{1,0:T(8,128)S(1)}, u32[]{:S(2)}, u32[]{:S(2)}) collective-permute-start(f32[48,128]{1,0:T(8,128)S(1)} %shard_map.122.grads), channel_id=1, source_target_pairs={{0,64},{1,65},{2,66},{3,67},{4,68},{5,69},{6,70},{7,71},{8,72},{9,... | collective-permute-start | bytes 73736 | tf_op jit(solution)/shard_map/ppermute | solution.py:229
  70.6 10.8 %collective-permute-start.15 = (f32[48,128]{1,0:T(8,128)S(1)}, f32[48,128]{1,0:T(8,128)S(1)}, u32[]{:S(2)}, u32[]{:S(2)}) collective-permute-start(f32[48,128]{1,0:T(8,128)S(1)} %shard_map.122.grads), channel_id=1, source_target_pairs={{0,96},{1,97},{2,98},{3,99},{4,100},{5,101},{6,102},{7,103},{8,104... | collective-permute-start | bytes 73736 | tf_op jit(solution)/shard_map/ppermute | solution.py:229
  75.7 18.1 %collective-permute-start.11 = (bf16[4,128,128]{2,1,0:T(8,128)(2,1)S(1)}, bf16[4,128,128]{2,1,0:T(8,128)(2,1)S(1)}, u32[]{:S(2)}, u32[]{:S(2)}) collective-permute-start(bf16[4,128,128]{2,1,0:T(8,128)(2,1)S(1)} %get-tuple-element.38.low), channel_id=1, source_target_pairs={{0,0},{1,225},{2,194},{3,163},{4,132},{5,101},{6,70},{7,39},{8,8},... | collective-permute-start | bytes 393224 | tf_op jit(solution)/shard_map/ppermute | solution.py:229
  76.4 17.4 %collective-permute-start.12 = (bf16[4,128,128]{2,1,0:T(8,128)(2,1)S(1)}, bf16[4,128,128]{2,1,0:T(8,128)(2,1)S(1)}, u32[]{:S(2)}, u32[]{:S(2)}) collective-permute-start(bf16[4,128,128]{2,1,0:T(8,128)(2,1)S(1)} %get-tuple-element.39.high), channel_id=1, source_target_pairs={{0,2},{1,227},{2,192},{3,161},{4,134},{5,103},{6,68},{7,37},{8,10}... | collective-permute-start | bytes 393224 | tf_op jit(solution)/shard_map/ppermute | solution.py:229
  81.4 4.6 %collective-permute-start.16 = (f32[48,128]{1,0:T(8,128)S(1)}, f32[48,128]{1,0:T(8,128)S(1)}, u32[]{:S(2)}, u32[]{:S(2)}) collective-permute-start(f32[48,128]{1,0:T(8,128)S(1)} %shard_map.123), channel_id=1, source_target_pairs={{0,16},{1,17},{2,18},{3,19},{4,20},{5,21},{6,22},{7,23},{8,24},{9,... | collective-permute-start | bytes 73736 | tf_op jit(solution)/shard_map/ppermute | solution.py:229
  86.0 7.8 %collective-permute-start.17 = (f32[48,128]{1,0:T(8,128)S(1)}, f32[48,128]{1,0:T(8,128)S(1)}, u32[]{:S(2)}, u32[]{:S(2)}) collective-permute-start(f32[48,128]{1,0:T(8,128)S(1)} %add.10), channel_id=1, source_target_pairs={{0,128},{1,129},{2,130},{3,131},{4,132},{5,133},{6,134},{7,135},{8... | collective-permute-start | bytes 73736 | tf_op jit(solution)/shard_map/ppermute | solution.py:229

commit v10 on v9

--- a/solution.py
+++ b/solution.py
@@ -225,12 +225,20 @@
     for b in range(blk):
         for r in range(rep):
             to_b, to_r = to(b, r)
-            pairs.append((b * rep + r, to_b % blk * rep + to_r))
+            pairs.append((b * rep + r, to_b % blk * rep + to_r % rep))
     return lax.ppermute(value, BLK + REP, pairs)
 
 
 def column(r):
     return r ^ (6 if r % 2 else 2)
+
+
+def far_out(b, r):
+    return (b + 2, r) if b % 4 < 2 else (b - 2, r - 1)
+
+
+def far_back(b, r):
+    return (b - 2, r) if b % 4 >= 2 else (b + 2, r + 1)
 
 
 def swap(value, bit):
@@ -257,7 +265,7 @@
         load_kernel, [(edges.shape, BF16)], [HBM], [pltpu.SemaphoreType.DMA], 0, 12 << 20
     )(pinned(edges))
     low, held, meta = lax.optimization_barrier((low, held, meta))
-    far_low, far_high = (move(v, lambda b, r: (b + 2, r)) for v in (low, high))
+    far_low, far_high = (move(v, far_out) for v in (low, high))
     near_low = move(low, lambda b, r: (b + 1 + 2 * (b % 2), r))
 
     work = 2 * ROWS * SLOTS * T * T * T
@@ -298,7 +306,7 @@
     )
     (far,) = call(near_kernel, [(tiles, BF16)], [VMEM] * 2)(far, other)
     far, got, other = lax.optimization_barrier((far, got, other))
-    far = move(far, lambda b, r: (b - 2, r))
+    far = move(far, far_back)
     (own,) = call(own_sums_kernel, [(tiles, F32)], [SMEM] + [VMEM] * 2, sums, work, 3 << 20)(
         meta, held, got
     )

time: 113 us -> 112 us (level)
  starting transfers between devices: 30.5 us -> 28 us
  blocking collectives: 50.5 us -> 52.6 us
    ppermute x18, starting transfers between devices: 30.5 us -> 28 us  [move(): return lax.ppermute(value, BLK + REP, pairs)]
    all_to_all x3, blocking collectives: 50.5 us -> 52.6 us  [exchange(): return lax.all_to_all(value, axes, 0, 0, tiled=True)]
    ppermute x18, waiting for transfers between devices: 14.3 us -> 13.2 us  [move(): return lax.ppermute(value, BLK + REP, pairs)]
  transfers between devices with their start and end apart: 18 -> 18, of which waited for: 5 -> 6; matrix products, arithmetic and copies ran while one was open for 0% -> 0% of each run, Pallas kernels for 8% -> 8%
where the time goes in v10:
time: 112 us; the launch traced here: 111 us
  blocking collectives  52.6 us (47%)
  starting transfers between devices  28 us (25%)
  Pallas kernels  16.4 us (15%)
  waiting for transfers between devices  13.2 us (12%)
    all_to_all x3, blocking collectives, exchange(): return lax.all_to_all(value, axes, 0, 0, tiled=True)  52.6 us
    ppermute x18, starting transfers between devices, move(): return lax.ppermute(value, BLK + REP, pairs)  28 us
    ppermute x18, waiting for transfers between devices, move(): return lax.ppermute(value, BLK + REP, pairs)  13.2 us
    pallas_call x1, Pallas kernels, on_device(): call(load_kernel, [(edges.shape, BF16)], [HBM], [pltpu.SemaphoreType.DMA]...  2.82 us
  transfers between devices with their start and end apart: 18, of which 6 were waited for; matrix products, arithmetic and copies ran while one was open for 0% of the time, Pallas kernels for 8%

profile of v10, /device:TPU:32, one launch (start us, length us, event | category | flops | bytes accessed | tf_op | source)
XLA Modules:
  0.0 111.2 jit_solution(14911836925524046836)
XLA Ops:
  0.6 1.7 %shard_map.111 = (bf16[4,128,128]{2,1,0:T(8,128)(2,1)S(1)}, bf16[4,128,128]{2,1,0:T(8,128)(2,1)S(1)}, f32[128,128]{1,0:T(8,128)S(1)}) custom-call(s32[1]{0:T(128)} %bitcast.rep, bf16[1024,128]{1,0:T(8,128)(2,1)} %features.1, s32[8,128]{1,0:T(8,128)} %bitcast.10), custom_call_target="tpu_custom_call" | custom-call | bytes 1048576 | tf_op jit(solution)/shard_map/pallas_call | solution.py:256
  3.0 9.1 %collective-permute-start.2 = (bf16[4,128,128]{2,1,0:T(8,128)(2,1)S(1)}, bf16[4,128,128]{2,1,0:T(8,128)(2,1)S(1)}, u32[]{:S(2)}, u32[]{:S(2)}) collective-permute-start(bf16[4,128,128]{2,1,0:T(8,128)(2,1)S(1)} %get-tuple-element.28), channel_id=1, source_target_pairs={{0,66},{1,231},{2,0},{3,165},{4,198},{5,99},{6,132},{7,33},{8,74},... | collective-permute-start | bytes 393224 | tf_op jit(solution)/shard_map/ppermute | solution.py:229
  12.2 2.8 %shard_map.112.held = bf16[8,4,6,128,128]{4,3,2,1,0:T(8,128)(2,1)S(1)} custom-call(bf16[8,4,6,128,128]{4,3,2,1,0:T(8,128)(2,1)} %edges.1), custom_call_target="tpu_custom_call" | custom-call | bytes 12582912 | tf_op jit(solution)/shard_map/pallas_call | solution.py:264
  15.1 1.7 %collective-permute-start.4 = (bf16[4,128,128]{2,1,0:T(8,128)(2,1)S(1)}, bf16[4,128,128]{2,1,0:T(8,128)(2,1)S(1)}, u32[]{:S(2)}, u32[]{:S(2)}) collective-permute-start(bf16[4,128,128]{2,1,0:T(8,128)(2,1)S(1)} %collective-permute-done.low), channel_id=1, source_target_pairs={{0,16},{1,17},{2,18},{3,19},{4,20},{5,21},{6,22},{7,23},{8,24},{9,... | collective-permute-start | bytes 393224 | tf_op jit(solution)/shard_map/ppermute | solution.py:229
  16.7 1.5 %collective-permute-start.6 = (bf16[4,128,128]{2,1,0:T(8,128)(2,1)S(1)}, bf16[4,128,128]{2,1,0:T(8,128)(2,1)S(1)}, u32[]{:S(2)}, u32[]{:S(2)}) collective-permute-start(bf16[4,128,128]{2,1,0:T(8,128)(2,1)S(1)} %collective-permute-done.2.high), channel_id=1, source_target_pairs={{0,16},{1,17},{2,18},{3,19},{4,20},{5,21},{6,22},{7,23},{8,24},{9,... | collective-permute-start | bytes 393224 | tf_op jit(solution)/shard_map/ppermute | solution.py:229
  18.3 1.5 %shard_map.113.total = f32[8,128,128]{2,1,0:T(8,128)S(1)} custom-call(s32[8,4,8]{2,1,0:T(4,128)S(1)} %pad_add_fusion.meta, bf16[8,4,6,128,128]{4,3,2,1,0:T(8,128)(2,1)S(1)} %shard_map.112.held, bf16[4,128,128]{2,1,0:T(8,128)(2,1)S(1)} %collective-permute-done.low, bf16[4,128,128]{2,1,0:T(8,128)(2,1)S(1)} %collective-permute-done.2.high), custom_call_target="tpu_custom_call" | custom-call | flops 201326592 | bytes 3145728 | tf_op jit(solution)/shard_map/pallas_call | solution.py:272
  19.8 1.9 %collective-permute-start.3 = (bf16[4,128,128]{2,1,0:T(8,128)(2,1)S(1)}, bf16[4,128,128]{2,1,0:T(8,128)(2,1)S(1)}, u32[]{:S(2)}, u32[]{:S(2)}) collective-permute-start(bf16[4,128,128]{2,1,0:T(8,128)(2,1)S(1)} %collective-permute-done.2.high), channel_id=1, source_target_pairs={{0,8},{1,9},{2,10},{3,11},{4,12},{5,13},{6,14},{7,15},{8,32},{9,33... | collective-permute-start | bytes 393224 | tf_op jit(solution)/shard_map/ppermute | solution.py:229
  21.7 1.1 collective-permute-done.4.low
  22.8 1.4 %collective-permute-done.6.high = bf16[4,128,128]{2,1,0:T(8,128)(2,1)S(1)} collective-permute-done((bf16[4,128,128]{2,1,0:T(8,128)(2,1)S(1)}, bf16[4,128,128]{2,1,0:T(8,128)(2,1)S(1)}, u32[]{:S(2)}, u32[]{:S(2)}) %collective-permute-start.6) | collective-permute-done | bytes 131104 | tf_op jit(solution)/shard_map/ppermute | solution.py:229
  24.2 1.5 %shard_map.114.total = f32[8,128,128]{2,1,0:T(8,128)S(1)} custom-call(s32[8,4,8]{2,1,0:T(4,128)S(1)} %pad_add_fusion.meta, bf16[8,4,6,128,128]{4,3,2,1,0:T(8,128)(2,1)S(1)} %shard_map.112.held, bf16[4,128,128]{2,1,0:T(8,128)(2,1)S(1)} %collective-permute-done.4.low, bf16[4,128,128]{2,1,0:T(8,128)(2,1)S(1)} %collective-permute-done.6.high, ...), custom_call_target="tpu_custom_call" | custom-call | flops 201326592 | bytes 3145728 | tf_op jit(solution)/shard_map/pallas_call | solution.py:278
  25.8 2.2 %shard_map.115 = bf16[8,128,128]{2,1,0:T(8,128)(2,1)S(1)} custom-call(s32[8,4,8]{2,1,0:T(4,128)S(1)} %pad_add_fusion.meta, bf16[8,4,6,128,128]{4,3,2,1,0:T(8,128)(2,1)S(1)} %shard_map.112.held, bf16[4,128,128]{2,1,0:T(8,128)(2,1)S(1)} %collective-permute-done.1.near_low, bf16[4,128,128]{2,1,0:T(8,128)(2,1)S(1)} %collective-permute-done.3.near_high, ...), custom_call_target="tpu_custom_call" | custom-call | flops 402653184 | bytes 6291456 | tf_op jit(solution)/shard_map/pallas_call | solution.py:281
  27.9 20.7 %all_to_all.15.parts = bf16[8,128,128]{2,1,0:T(8,128)(2,1)S(1)} all-to-all(bf16[8,128,128]{2,1,0:T(8,128)(2,1)S(1)} %shard_map.115), channel_id=1, replica_groups=mesh['z'=8,'yl'=2,'core'=2,'x'=4,'yh'=2] {'x','yh'}, dimensions={0} | all-to-all | bytes 524288 | tf_op jit(solution)/shard_map/all_to_all | solution.py:219
  49.4 12.2 %all_to_all.16.got = bf16[8,176,128]{2,1,0:T(8,128)(2,1)S(1)} all-to-all(bf16[8,176,128]{2,1,0:T(8,128)(2,1)S(1)} %get-tuple-element.33), channel_id=1, replica_groups=mesh['z'=8,'yl'=2,'core'=2,'x'=4,'yh'=2] {'x','yh'}, dimensions={0} | all-to-all | bytes 720896 | tf_op jit(solution)/shard_map/all_to_all | solution.py:219
  61.6 2.0 %shard_map.118 = (bf16[8,128,128]{2,1,0:T(8,128)(2,1)S(1)}, bf16[1120,128]{1,0:T(8,128)(2,1)S(1)}) custom-call(s32[8,4,8]{2,1,0:T(4,128)S(1)} %pad_add_fusion.meta, bf16[8,4,6,128,128]{4,3,2,1,0:T(8,128)(2,1)S(1)} %shard_map.112.held, bf16[8,176,128]{2,1,0:T(8,128)(2,1)S(1)} %all_to_all.16.got), custom_call_target="tpu_custom_call" | custom-call | flops 402653184 | bytes 6291456 | tf_op jit(solution)/shard_map/pallas_call | solution.py:294
  63.9 1.5 %shard_map.117.far = bf16[8,128,128]{2,1,0:T(8,128)(2,1)S(1)} custom-call(s32[8,4,8]{2,1,0:T(4,128)S(1)} %pad_add_fusion.meta, bf16[8,4,6,128,128]{4,3,2,1,0:T(8,128)(2,1)S(1)} %shard_map.112.held, bf16[8,176,128]{2,1,0:T(8,128)(2,1)S(1)} %all_to_all.16.got), custom_call_target="tpu_custom_call" | custom-call | flops 201326592 | bytes 3145728 | tf_op jit(solution)/shard_map/pallas_call | solution.py:304
  66.5 1.6 %collective-permute-start.13 = (f32[48,128]{1,0:T(8,128)S(1)}, f32[48,128]{1,0:T(8,128)S(1)}, u32[]{:S(2)}, u32[]{:S(2)}) collective-permute-start(f32[48,128]{1,0:T(8,128)S(1)} %shard_map.122.grads), channel_id=1, source_target_pairs={{0,32},{1,33},{2,34},{3,35},{4,36},{5,37},{6,38},{7,39},{8,40},{9,... | collective-permute-start | bytes 73736 | tf_op jit(solution)/shard_map/ppermute | solution.py:229
  70.1 1.5 %shard_map.120.own = f32[8,128,128]{2,1,0:T(8,128)S(1)} custom-call(s32[8,4,8]{2,1,0:T(4,128)S(1)} %pad_add_fusion.meta, bf16[8,4,6,128,128]{4,3,2,1,0:T(8,128)(2,1)S(1)} %shard_map.112.held, bf16[8,176,128]{2,1,0:T(8,128)(2,1)S(1)} %all_to_all.16.got), custom_call_target="tpu_custom_call" | custom-call | flops 201326592 | bytes 3145728 | tf_op jit(solution)/shard_map/pallas_call | solution.py:310
  71.6 2.6 %collective-permute-done.10.far = bf16[8,128,128]{2,1,0:T(8,128)(2,1)S(1)} collective-permute-done((bf16[8,128,128]{2,1,0:T(8,128)(2,1)S(1)}, bf16[8,128,128]{2,1,0:T(8,128)(2,1)S(1)}, u32[]{:S(2)}, u32[]{:S(2)}) %collective-permute-start.10) | collective-permute-done | bytes 262176 | tf_op jit(solution)/shard_map/ppermute | solution.py:229
  74.9 3.9 %collective-permute-start.12 = (bf16[4,128,128]{2,1,0:T(8,128)(2,1)S(1)}, bf16[4,128,128]{2,1,0:T(8,128)(2,1)S(1)}, u32[]{:S(2)}, u32[]{:S(2)}) collective-permute-start(bf16[4,128,128]{2,1,0:T(8,128)(2,1)S(1)} %get-tuple-element.39.high), channel_id=1, source_target_pairs={{0,2},{1,227},{2,192},{3,161},{4,134},{5,103},{6,68},{7,37},{8,10}... | collective-permute-start | bytes 393224 | tf_op jit(solution)/shard_map/ppermute | solution.py:229
  78.8 1.8 %collective-permute-start.16 = (f32[48,128]{1,0:T(8,128)S(1)}, f32[48,128]{1,0:T(8,128)S(1)}, u32[]{:S(2)}, u32[]{:S(2)}) collective-permute-start(f32[48,128]{1,0:T(8,128)S(1)} %shard_map.123), channel_id=1, source_target_pairs={{0,16},{1,17},{2,18},{3,19},{4,20},{5,21},{6,22},{7,23},{8,24},{9,... | collective-permute-start | bytes 73736 | tf_op jit(solution)/shard_map/ppermute | solution.py:229
  80.6 2.2 %collective-permute-done.16 = f32[48,128]{1,0:T(8,128)S(1)} collective-permute-done((f32[48,128]{1,0:T(8,128)S(1)}, f32[48,128]{1,0:T(8,128)S(1)}, u32[]{:S(2)}, u32[]{:S(2)}) %collective-permute-start.16) | collective-permute-done | bytes 24608 | tf_op jit(solution)/shard_map/ppermute | solution.py:229
  82.8 2.0 %collective-permute-start.17 = (f32[48,128]{1,0:T(8,128)S(1)}, f32[48,128]{1,0:T(8,128)S(1)}, u32[]{:S(2)}, u32[]{:S(2)}) collective-permute-start(f32[48,128]{1,0:T(8,128)S(1)} %add.10), channel_id=1, source_target_pairs={{0,128},{1,129},{2,130},{3,131},{4,132},{5,133},{6,134},{7,135},{8... | collective-permute-start | bytes 73736 | tf_op jit(solution)/shard_map/ppermute | solution.py:229
  84.7 5.8 %collective-permute-done.17 = f32[48,128]{1,0:T(8,128)S(1)} collective-permute-done((f32[48,128]{1,0:T(8,128)S(1)}, f32[48,128]{1,0:T(8,128)S(1)}, u32[]{:S(2)}, u32[]{:S(2)}) %collective-permute-start.17) | collective-permute-done | bytes 24608 | tf_op jit(solution)/shard_map/ppermute | solution.py:229
  90.7 19.8 %all_to_all.17.got = bf16[8,160,128]{2,1,0:T(8,128)(2,1)S(1)} all-to-all(bf16[8,160,128]{2,1,0:T(8,128)(2,1)S(1)} %shard_map.124), channel_id=1, replica_groups=mesh['z'=8,'yl'=2,'core'=2,'x'=4,'yh'=2] {'x','yh'}, dimensions={0} | all-to-all | bytes 655360 | tf_op jit(solution)/shard_map/all_to_all | solution.py:219
  (45 shorter events, 6.6 us)
Async XLA Ops:
  2.4 12.7 %collective-permute-start = (bf16[4,128,128]{2,1,0:T(8,128)(2,1)S(1)}, bf16[4,128,128]{2,1,0:T(8,128)(2,1)S(1)}, u32[]{:S(2)}, u32[]{:S(2)}) collective-permute-start(bf16[4,128,128]{2,1,0:T(8,128)(2,1)S(1)} %get-tuple-element.24), channel_id=1, source_target_pairs={{0,0},{1,33},{2,66},{3,99},{4,132},{5,165},{6,198},{7,231},{8,8},{... | collective-permute-start | bytes 393224 | tf_op jit(solution)/shard_map/ppermute | solution.py:229
  3.0 13.7 %collective-permute-start.2 = (bf16[4,128,128]{2,1,0:T(8,128)(2,1)S(1)}, bf16[4,128,128]{2,1,0:T(8,128)(2,1)S(1)}, u32[]{:S(2)}, u32[]{:S(2)}) collective-permute-start(bf16[4,128,128]{2,1,0:T(8,128)(2,1)S(1)} %get-tuple-element.28), channel_id=1, source_target_pairs={{0,66},{1,231},{2,0},{3,165},{4,198},{5,99},{6,132},{7,33},{8,74},... | collective-permute-start | bytes 393224 | tf_op jit(solution)/shard_map/ppermute | solution.py:229
  12.2 2.8 %copy-start.3 = (s32[8,4,6]{0,1,2:T(4,128)S(1)}, s32[8,4,6]{0,1,2:T(4,128)}, u32[]{:S(2)}) copy-start(s32[8,4,6]{0,1,2:T(4,128)} %param.10) | copy-start | bytes 2308
  12.2 2.9 %copy-start.4 = (s32[8,4]{0,1:T(4,128)S(1)}, s32[8,4]{0,1:T(4,128)}, u32[]{:S(2)}) copy-start(s32[8,4]{0,1:T(4,128)} %param.11) | copy-start | bytes 388
  15.1 7.8 %collective-permute-start.4 = (bf16[4,128,128]{2,1,0:T(8,128)(2,1)S(1)}, bf16[4,128,128]{2,1,0:T(8,128)(2,1)S(1)}, u32[]{:S(2)}, u32[]{:S(2)}) collective-permute-start(bf16[4,128,128]{2,1,0:T(8,128)(2,1)S(1)} %collective-permute-done.low), channel_id=1, source_target_pairs={{0,16},{1,17},{2,18},{3,19},{4,20},{5,21},{6,22},{7,23},{8,24},{9,... | collective-permute-start | bytes 393224 | tf_op jit(solution)/shard_map/ppermute | solution.py:229
  16.7 7.5 %collective-permute-start.6 = (bf16[4,128,128]{2,1,0:T(8,128)(2,1)S(1)}, bf16[4,128,128]{2,1,0:T(8,128)(2,1)S(1)}, u32[]{:S(2)}, u32[]{:S(2)}) collective-permute-start(bf16[4,128,128]{2,1,0:T(8,128)(2,1)S(1)} %collective-permute-done.2.high), channel_id=1, source_target_pairs={{0,16},{1,17},{2,18},{3,19},{4,20},{5,21},{6,22},{7,23},{8,24},{9,... | collective-permute-start | bytes 393224 | tf_op jit(solution)/shard_map/ppermute | solution.py:229
  18.3 7.5 %collective-permute-start.1 = (bf16[4,128,128]{2,1,0:T(8,128)(2,1)S(1)}, bf16[4,128,128]{2,1,0:T(8,128)(2,1)S(1)}, u32[]{:S(2)}, u32[]{:S(2)}) collective-permute-start(bf16[4,128,128]{2,1,0:T(8,128)(2,1)S(1)} %collective-permute-done.low), channel_id=1, source_target_pairs={{0,8},{1,9},{2,10},{3,11},{4,12},{5,13},{6,14},{7,15},{8,32},{9,33... | collective-permute-start | bytes 393224 | tf_op jit(solution)/shard_map/ppermute | solution.py:229
  19.8 28.9 %copy-start = (bf16[128,256]{1,0:T(8,128)(2,1)S(1)}, bf16[128,256]{1,0:T(8,128)(2,1)}, u32[]{:S(2)}) copy-start(bf16[128,256]{1,0:T(8,128)(2,1)} %weight.1) | copy-start | bytes 196612
  19.8 28.8 %copy-start.1 = (bf16[128,256]{1,0:T(8,128)(2,1)S(1)}, bf16[128,256]{1,0:T(8,128)(2,1)}, u32[]{:S(2)}) copy-start(bf16[128,256]{1,0:T(8,128)(2,1)} %cot.1) | copy-start | bytes 196612
  19.8 28.8 %copy-start.2 = (f32[256]{0:T(256)S(1)}, f32[256]{0:T(256)}, u32[]{:S(2)}) copy-start(f32[256]{0:T(256)} %param.14) | copy-start | bytes 3076
  19.8 6.0 %collective-permute-start.3 = (bf16[4,128,128]{2,1,0:T(8,128)(2,1)S(1)}, bf16[4,128,128]{2,1,0:T(8,128)(2,1)S(1)}, u32[]{:S(2)}, u32[]{:S(2)}) collective-permute-start(bf16[4,128,128]{2,1,0:T(8,128)(2,1)S(1)} %collective-permute-done.2.high), channel_id=1, source_target_pairs={{0,8},{1,9},{2,10},{3,11},{4,12},{5,13},{6,14},{7,15},{8,32},{9,33... | collective-permute-start | bytes 393224 | tf_op jit(solution)/shard_map/ppermute | solution.py:229
  22.8 2.9 %collective-permute-start.5 = (bf16[4,128,128]{2,1,0:T(8,128)(2,1)S(1)}, bf16[4,128,128]{2,1,0:T(8,128)(2,1)S(1)}, u32[]{:S(2)}, u32[]{:S(2)}) collective-permute-start(bf16[4,128,128]{2,1,0:T(8,128)(2,1)S(1)} %collective-permute-done.4.low), channel_id=1, source_target_pairs={{0,8},{1,9},{2,10},{3,11},{4,12},{5,13},{6,14},{7,15},{8,0},{9,1},... | collective-permute-start | bytes 393224 | tf_op jit(solution)/shard_map/ppermute | solution.py:229
  24.2 1.5 %collective-permute-start.7 = (bf16[4,128,128]{2,1,0:T(8,128)(2,1)S(1)}, bf16[4,128,128]{2,1,0:T(8,128)(2,1)S(1)}, u32[]{:S(2)}, u32[]{:S(2)}) collective-permute-start(bf16[4,128,128]{2,1,0:T(8,128)(2,1)S(1)} %collective-permute-done.6.high), channel_id=1, source_target_pairs={{0,8},{1,9},{2,10},{3,11},{4,12},{5,13},{6,14},{7,15},{8,0},{9,1},... | collective-permute-start | bytes 393224 | tf_op jit(solution)/shard_map/ppermute | solution.py:229
  63.7 1.8 %collective-permute-start.8 = (bf16[1120,128]{1,0:T(8,128)(2,1)S(1)}, bf16[1120,128]{1,0:T(8,128)(2,1)S(1)}, u32[]{:S(2)}, u32[]{:S(2)}) collective-permute-start(bf16[1120,128]{1,0:T(8,128)(2,1)S(1)} %get-tuple-element.34.mine), channel_id=1, source_target_pairs={{0,8},{1,9},{2,10},{3,11},{4,12},{5,13},{6,14},{7,15},{8,0},{9,1},... | collective-permute-start | bytes 860168 | tf_op jit(solution)/shard_map/ppermute | solution.py:229
  63.8 7.8 %collective-permute-start.9 = (bf16[8,128,128]{2,1,0:T(8,128)(2,1)S(1)}, bf16[8,128,128]{2,1,0:T(8,128)(2,1)S(1)}, u32[]{:S(2)}, u32[]{:S(2)}) collective-permute-start(bf16[8,128,128]{2,1,0:T(8,128)(2,1)S(1)} %get-tuple-element.36), channel_id=1, source_target_pairs={{0,232},{1,233},{2,234},{3,235},{4,236},{5,237},{6,238},{7,239},{8... | collective-permute-start | bytes 786440 | tf_op jit(solution)/shard_map/ppermute | solution.py:229
  65.5 8.6 %collective-permute-start.10 = (bf16[8,128,128]{2,1,0:T(8,128)(2,1)S(1)}, bf16[8,128,128]{2,1,0:T(8,128)(2,1)S(1)}, u32[]{:S(2)}, u32[]{:S(2)}) collective-permute-start(bf16[8,128,128]{2,1,0:T(8,128)(2,1)S(1)} %shard_map.119), channel_id=1, source_target_pairs={{0,17},{1,18},{2,19},{3,20},{4,21},{5,22},{6,23},{7,16},{8,25},{9,... | collective-permute-start | bytes 786440 | tf_op jit(solution)/shard_map/ppermute | solution.py:229
  66.5 12.3 %collective-permute-start.13 = (f32[48,128]{1,0:T(8,128)S(1)}, f32[48,128]{1,0:T(8,128)S(1)}, u32[]{:S(2)}, u32[]{:S(2)}) collective-permute-start(f32[48,128]{1,0:T(8,128)S(1)} %shard_map.122.grads), channel_id=1, source_target_pairs={{0,32},{1,33},{2,34},{3,35},{4,36},{5,37},{6,38},{7,39},{8,40},{9,... | collective-permute-start | bytes 73736 | tf_op jit(solution)/shard_map/ppermute | solution.py:229
  68.0 10.8 %collective-permute-start.14 = (f32[48,128]{1,0:T(8,128)S(1)}, f32[48,128]{1,0:T(8,128)S(1)}, u32[]{:S(2)}, u32[]{:S(2)}) collective-permute-start(f32[48,128]{1,0:T(8,128)S(1)} %shard_map.122.grads), channel_id=1, source_target_pairs={{0,64},{1,65},{2,66},{3,67},{4,68},{5,69},{6,70},{7,71},{8,72},{9,... | collective-permute-start | bytes 73736 | tf_op jit(solution)/shard_map/ppermute | solution.py:229
  69.1 9.7 %collective-permute-start.15 = (f32[48,128]{1,0:T(8,128)S(1)}, f32[48,128]{1,0:T(8,128)S(1)}, u32[]{:S(2)}, u32[]{:S(2)}) collective-permute-start(f32[48,128]{1,0:T(8,128)S(1)} %shard_map.122.grads), channel_id=1, source_target_pairs={{0,96},{1,97},{2,98},{3,99},{4,100},{5,101},{6,102},{7,103},{8,104... | collective-permute-start | bytes 73736 | tf_op jit(solution)/shard_map/ppermute | solution.py:229
  74.2 16.3 %collective-permute-start.11 = (bf16[4,128,128]{2,1,0:T(8,128)(2,1)S(1)}, bf16[4,128,128]{2,1,0:T(8,128)(2,1)S(1)}, u32[]{:S(2)}, u32[]{:S(2)}) collective-permute-start(bf16[4,128,128]{2,1,0:T(8,128)(2,1)S(1)} %get-tuple-element.38.low), channel_id=1, source_target_pairs={{0,0},{1,225},{2,194},{3,163},{4,132},{5,101},{6,70},{7,39},{8,8},... | collective-permute-start | bytes 393224 | tf_op jit(solution)/shard_map/ppermute | solution.py:229
  74.9 15.7 %collective-permute-start.12 = (bf16[4,128,128]{2,1,0:T(8,128)(2,1)S(1)}, bf16[4,128,128]{2,1,0:T(8,128)(2,1)S(1)}, u32[]{:S(2)}, u32[]{:S(2)}) collective-permute-start(bf16[4,128,128]{2,1,0:T(8,128)(2,1)S(1)} %get-tuple-element.39.high), channel_id=1, source_target_pairs={{0,2},{1,227},{2,192},{3,161},{4,134},{5,103},{6,68},{7,37},{8,10}... | collective-permute-start | bytes 393224 | tf_op jit(solution)/shard_map/ppermute | solution.py:229
  78.8 3.9 %collective-permute-start.16 = (f32[48,128]{1,0:T(8,128)S(1)}, f32[48,128]{1,0:T(8,128)S(1)}, u32[]{:S(2)}, u32[]{:S(2)}) collective-permute-start(f32[48,128]{1,0:T(8,128)S(1)} %shard_map.123), channel_id=1, source_target_pairs={{0,16},{1,17},{2,18},{3,19},{4,20},{5,21},{6,22},{7,23},{8,24},{9,... | collective-permute-start | bytes 73736 | tf_op jit(solution)/shard_map/ppermute | solution.py:229
  82.8 7.7 %collective-permute-start.17 = (f32[48,128]{1,0:T(8,128)S(1)}, f32[48,128]{1,0:T(8,128)S(1)}, u32[]{:S(2)}, u32[]{:S(2)}) collective-permute-start(f32[48,128]{1,0:T(8,128)S(1)} %add.10), channel_id=1, source_target_pairs={{0,128},{1,129},{2,130},{3,131},{4,132},{5,133},{6,134},{7,135},{8... | collective-permute-start | bytes 73736 | tf_op jit(solution)/shard_map/ppermute | solution.py:229

commit v11 on v10

--- a/solution.py
+++ b/solution.py
@@ -48,19 +48,18 @@
             scale[...] = inv_root
 
 
-def tile_of(low, high):
-    def tile_at(col):
-        at = lax.rem(col, HALF)
-        return jnp.where(col < HALF, low[at], high[at])
-
-    return tile_at
-
-
-def product(meta, edges, i, s, tile_at):
-    picked = []
-    for c in range(SLOTS):
-        tile = tile_at(meta[c, s, i])
-        picked.append(jnp.where(c < meta[6, s, i], tile, jnp.zeros_like(tile)))
+def fill(tiles, low, high):
+    tiles[0:HALF] = low[...]
+    tiles[HALF:ROWS] = high[...]
+    tiles[ROWS] = jnp.zeros((T, T), BF16)
+
+
+def tile_id(meta, i, s, c):
+    return jnp.where(c < meta[6, s, i], meta[c, s, i], ROWS)
+
+
+def product(meta, edges, i, s, tiles):
+    picked = [tiles[tile_id(meta, i, s, c)] for c in range(SLOTS)]
     left = jnp.concatenate([edges[i, s, c] for c in range(SLOTS)], axis=1)
     return jnp.dot(left, jnp.concatenate(picked, axis=0), preferred_element_type=F32)
 
@@ -71,23 +70,27 @@
     copy.wait()
 
 
-def first_kernel(meta, held, low, high, out):
+def first_kernel(meta, held, low, high, out, tiles):
+    fill(tiles, low, high)
     for i in range(ROWS):
-        out[i] = product(meta, held, i, 0, tile_of(low, high))
-
-
-def second_kernel(meta, held, low, high, total, out):
+        out[i] = product(meta, held, i, 0, tiles)
+
+
+def second_kernel(meta, held, low, high, total, out, tiles):
+    fill(tiles, low, high)
     for i in range(ROWS):
-        out[i] = total[i] + product(meta, held, i, 2, tile_of(low, high))
-
-
-def third_kernel(meta, held, near_low, near_high, last_low, last_high, total, out):
+        out[i] = total[i] + product(meta, held, i, 2, tiles)
+
+
+def third_kernel(meta, held, near_low, near_high, last_low, last_high, total, out, near, last):
     odd = meta[7, 0, 0]
+    fill(near, near_low, near_high)
+    fill(last, last_low, last_high)
     for i in range(ROWS):
         out[i] = (
             total[i]
-            + product(meta, held, i, 3 - 2 * odd, tile_of(near_low, near_high))
-            + product(meta, held, i, 1 + 2 * odd, tile_of(last_low, last_high))
+            + product(meta, held, i, 3 - 2 * odd, near)
+            + product(meta, held, i, 1 + 2 * odd, last)
         ).astype(BF16)
 
 
@@ -125,8 +128,7 @@
         prod = jnp.dot(back, right, preferred_element_type=F32)
         for c in range(SLOTS):
             part = prod[:, c * T : (c + 1) * T]
-            at = meta[c, s, i]
-            sums[at] += jnp.where(c < meta[6, s, i], part, jnp.zeros_like(part))
+            sums[tile_id(meta, i, s, c)] += part
 
 
 def near_sums_kernel(meta, held, got, near, last, sums):
@@ -140,19 +142,19 @@
     last[NODES : NODES + GRAD] = high
     last[NODES + GRAD :] = (total - high.astype(F32)).astype(BF16)
     column_sums(meta, held, got, 1 + 2 * meta[7, 0, 0], sums)
-    last[0:NODES] = sums[...].astype(BF16).reshape(NODES, T)
+    last[0:NODES] = sums[0:ROWS].astype(BF16).reshape(NODES, T)
     column_sums(meta, held, got, 3 - 2 * meta[7, 0, 0], sums)
-    near[...] = sums[...].astype(BF16)
+    near[...] = sums[0:ROWS].astype(BF16)
 
 
 def far_sums_kernel(meta, held, got, far, sums):
     column_sums(meta, held, got, 2, sums)
-    far[...] = sums[...].astype(BF16)
+    far[...] = sums[0:ROWS].astype(BF16)
 
 
 def own_sums_kernel(meta, held, got, out, sums):
     column_sums(meta, held, got, 0, sums)
-    out[...] = sums[...]
+    out[...] = sums[0:ROWS]
 
 
 def grads_of(rows):
@@ -269,16 +271,17 @@
     near_low = move(low, lambda b, r: (b + 1 + 2 * (b % 2), r))
 
     work = 2 * ROWS * SLOTS * T * T * T
-    (total,) = call(first_kernel, [(tiles, F32)], [SMEM] + [VMEM] * 3, (), work, 3 << 20)(
+    block = pltpu.VMEM((ROWS + 1, T, T), BF16)
+    (total,) = call(first_kernel, [(tiles, F32)], [SMEM] + [VMEM] * 3, [block], work, 3 << 20)(
         meta, held, low, high
     )
     high, total = lax.optimization_barrier((high, total))
     near_high = move(high, lambda b, r: (b + 1 + 2 * (b % 2), r))
     last_low, last_high = swap(far_low, 1), swap(far_high, 1)
-    (total,) = call(second_kernel, [(tiles, F32)], [SMEM] + [VMEM] * 4, (), work, 3 << 20)(
+    (total,) = call(second_kernel, [(tiles, F32)], [SMEM] + [VMEM] * 4, [block], work, 3 << 20)(
         meta, held, far_low, far_high, total
     )
-    (parts,) = call(third_kernel, [(tiles, BF16)], [SMEM] + [VMEM] * 6, (), 2 * work, 6 << 20)(
+    (parts,) = call(third_kernel, [(tiles, BF16)], [SMEM] + [VMEM] * 6, [block] * 2, 2 * work, 6 << 20)(
         meta, held, near_low, near_high, last_low, last_high, total
     )
     parts = exchange(parts, REP)
@@ -290,7 +293,7 @@
     )(parts, scale, weight, bias[None], cot)
     got = exchange(send, REP)
 
-    sums = [pltpu.VMEM(tiles, F32)]
+    sums = [pltpu.VMEM((ROWS + 1, T, T), F32)]
     near, mine = call(
         near_sums_kernel,
         [(tiles, BF16), ((NODES + 2 * GRAD, T), BF16)],

time: 112 us -> 111 us (level)
  no operation moved by 1% of the time
where the time goes in v11:
time: 111 us
  blocking collectives  52.7 us (47%)
  starting transfers between devices  28 us (25%)
  Pallas kernels  16 us (14%)
  waiting for transfers between devices  13.3 us (12%)
    all_to_all x3, blocking collectives, exchange(): return lax.all_to_all(value, axes, 0, 0, tiled=True)  52.7 us
    ppermute x18, starting transfers between devices, move(): return lax.ppermute(value, BLK + REP, pairs)  28 us
    ppermute x18, waiting for transfers between devices, move(): return lax.ppermute(value, BLK + REP, pairs)  13.3 us
    pallas_call x1, Pallas kernels, on_device(): call(load_kernel, [(edges.shape, BF16)], [HBM], [pltpu.SemaphoreType.DMA]...  2.82 us
  transfers between devices with their start and end apart: 18, of which 6 were waited for; matrix products, arithmetic and copies ran while one was open for 0% of the time, Pallas kernels for 8%

profile of v11, /device:TPU:32, one launch (start us, length us, event | category | flops | bytes accessed | tf_op | source)
XLA Modules:
  0.0 110.9 jit_solution(8648205864441903308)
XLA Ops:
  0.6 1.7 %shard_map.111 = (bf16[4,128,128]{2,1,0:T(8,128)(2,1)S(1)}, bf16[4,128,128]{2,1,0:T(8,128)(2,1)S(1)}, f32[128,128]{1,0:T(8,128)S(1)}) custom-call(s32[1]{0:T(128)} %bitcast.rep, bf16[1024,128]{1,0:T(8,128)(2,1)} %features.1, s32[8,128]{1,0:T(8,128)} %bitcast.10), custom_call_target="tpu_custom_call" | custom-call | bytes 1048576 | tf_op jit(solution)/shard_map/pallas_call | solution.py:258
  3.0 9.1 %collective-permute-start.2 = (bf16[4,128,128]{2,1,0:T(8,128)(2,1)S(1)}, bf16[4,128,128]{2,1,0:T(8,128)(2,1)S(1)}, u32[]{:S(2)}, u32[]{:S(2)}) collective-permute-start(bf16[4,128,128]{2,1,0:T(8,128)(2,1)S(1)} %get-tuple-element.28), channel_id=1, source_target_pairs={{0,66},{1,231},{2,0},{3,165},{4,198},{5,99},{6,132},{7,33},{8,74},... | collective-permute-start | bytes 393224 | tf_op jit(solution)/shard_map/ppermute | solution.py:231
  12.2 2.8 %shard_map.112.held = bf16[8,4,6,128,128]{4,3,2,1,0:T(8,128)(2,1)S(1)} custom-call(bf16[8,4,6,128,128]{4,3,2,1,0:T(8,128)(2,1)} %edges.1), custom_call_target="tpu_custom_call" | custom-call | bytes 12582912 | tf_op jit(solution)/shard_map/pallas_call | solution.py:266
  15.1 1.7 %collective-permute-start.4 = (bf16[4,128,128]{2,1,0:T(8,128)(2,1)S(1)}, bf16[4,128,128]{2,1,0:T(8,128)(2,1)S(1)}, u32[]{:S(2)}, u32[]{:S(2)}) collective-permute-start(bf16[4,128,128]{2,1,0:T(8,128)(2,1)S(1)} %collective-permute-done.low), channel_id=1, source_target_pairs={{0,16},{1,17},{2,18},{3,19},{4,20},{5,21},{6,22},{7,23},{8,24},{9,... | collective-permute-start | bytes 393224 | tf_op jit(solution)/shard_map/ppermute | solution.py:231
  16.7 1.5 %collective-permute-start.6 = (bf16[4,128,128]{2,1,0:T(8,128)(2,1)S(1)}, bf16[4,128,128]{2,1,0:T(8,128)(2,1)S(1)}, u32[]{:S(2)}, u32[]{:S(2)}) collective-permute-start(bf16[4,128,128]{2,1,0:T(8,128)(2,1)S(1)} %collective-permute-done.2.high), channel_id=1, source_target_pairs={{0,16},{1,17},{2,18},{3,19},{4,20},{5,21},{6,22},{7,23},{8,24},{9,... | collective-permute-start | bytes 393224 | tf_op jit(solution)/shard_map/ppermute | solution.py:231
  18.3 1.4 %shard_map.113.total = f32[8,128,128]{2,1,0:T(8,128)S(1)} custom-call(s32[8,4,8]{2,1,0:T(4,128)S(1)} %pad_add_fusion.meta, bf16[8,4,6,128,128]{4,3,2,1,0:T(8,128)(2,1)S(1)} %shard_map.112.held, bf16[4,128,128]{2,1,0:T(8,128)(2,1)S(1)} %collective-permute-done.low, bf16[4,128,128]{2,1,0:T(8,128)(2,1)S(1)} %collective-permute-done.2.high), custom_call_target="tpu_custom_call" | custom-call | flops 201326592 | bytes 3145728 | tf_op jit(solution)/shard_map/pallas_call | solution.py:275
  19.7 1.9 %collective-permute-start.3 = (bf16[4,128,128]{2,1,0:T(8,128)(2,1)S(1)}, bf16[4,128,128]{2,1,0:T(8,128)(2,1)S(1)}, u32[]{:S(2)}, u32[]{:S(2)}) collective-permute-start(bf16[4,128,128]{2,1,0:T(8,128)(2,1)S(1)} %collective-permute-done.2.high), channel_id=1, source_target_pairs={{0,8},{1,9},{2,10},{3,11},{4,12},{5,13},{6,14},{7,15},{8,32},{9,33... | collective-permute-start | bytes 393224 | tf_op jit(solution)/shard_map/ppermute | solution.py:231
  21.6 1.2 %collective-permute-done.4.low = bf16[4,128,128]{2,1,0:T(8,128)(2,1)S(1)} collective-permute-done((bf16[4,128,128]{2,1,0:T(8,128)(2,1)S(1)}, bf16[4,128,128]{2,1,0:T(8,128)(2,1)S(1)}, u32[]{:S(2)}, u32[]{:S(2)}) %collective-permute-start.4) | collective-permute-done | bytes 131104 | tf_op jit(solution)/shard_map/ppermute | solution.py:231
  22.8 1.4 %collective-permute-done.6.high = bf16[4,128,128]{2,1,0:T(8,128)(2,1)S(1)} collective-permute-done((bf16[4,128,128]{2,1,0:T(8,128)(2,1)S(1)}, bf16[4,128,128]{2,1,0:T(8,128)(2,1)S(1)}, u32[]{:S(2)}, u32[]{:S(2)}) %collective-permute-start.6) | collective-permute-done | bytes 131104 | tf_op jit(solution)/shard_map/ppermute | solution.py:231
  24.2 1.4 %shard_map.114.total = f32[8,128,128]{2,1,0:T(8,128)S(1)} custom-call(s32[8,4,8]{2,1,0:T(4,128)S(1)} %pad_add_fusion.meta, bf16[8,4,6,128,128]{4,3,2,1,0:T(8,128)(2,1)S(1)} %shard_map.112.held, bf16[4,128,128]{2,1,0:T(8,128)(2,1)S(1)} %collective-permute-done.4.low, bf16[4,128,128]{2,1,0:T(8,128)(2,1)S(1)} %collective-permute-done.6.high, ...), custom_call_target="tpu_custom_call" | custom-call | flops 201326592 | bytes 3145728 | tf_op jit(solution)/shard_map/pallas_call | solution.py:281
  25.7 1.8 %shard_map.115 = bf16[8,128,128]{2,1,0:T(8,128)(2,1)S(1)} custom-call(s32[8,4,8]{2,1,0:T(4,128)S(1)} %pad_add_fusion.meta, bf16[8,4,6,128,128]{4,3,2,1,0:T(8,128)(2,1)S(1)} %shard_map.112.held, bf16[4,128,128]{2,1,0:T(8,128)(2,1)S(1)} %collective-permute-done.1.near_low, bf16[4,128,128]{2,1,0:T(8,128)(2,1)S(1)} %collective-permute-done.3.near_high, ...), custom_call_target="tpu_custom_call" | custom-call | flops 402653184 | bytes 6291456 | tf_op jit(solution)/shard_map/pallas_call | solution.py:284
  27.5 20.7 %all_to_all.15.parts = bf16[8,128,128]{2,1,0:T(8,128)(2,1)S(1)} all-to-all(bf16[8,128,128]{2,1,0:T(8,128)(2,1)S(1)} %shard_map.115), channel_id=1, replica_groups=mesh['z'=8,'yl'=2,'core'=2,'x'=4,'yh'=2] {'x','yh'}, dimensions={0} | all-to-all | bytes 524288 | tf_op jit(solution)/shard_map/all_to_all | solution.py:221
  49.0 12.2 %all_to_all.16.got = bf16[8,176,128]{2,1,0:T(8,128)(2,1)S(1)} all-to-all(bf16[8,176,128]{2,1,0:T(8,128)(2,1)S(1)} %get-tuple-element.33), channel_id=1, replica_groups=mesh['z'=8,'yl'=2,'core'=2,'x'=4,'yh'=2] {'x','yh'}, dimensions={0} | all-to-all | bytes 720896 | tf_op jit(solution)/shard_map/all_to_all | solution.py:221
  61.2 2.1 %shard_map.118 = (bf16[8,128,128]{2,1,0:T(8,128)(2,1)S(1)}, bf16[1120,128]{1,0:T(8,128)(2,1)S(1)}) custom-call(s32[8,4,8]{2,1,0:T(4,128)S(1)} %pad_add_fusion.meta, bf16[8,4,6,128,128]{4,3,2,1,0:T(8,128)(2,1)S(1)} %shard_map.112.held, bf16[8,176,128]{2,1,0:T(8,128)(2,1)S(1)} %all_to_all.16.got), custom_call_target="tpu_custom_call" | custom-call | flops 402653184 | bytes 6291456 | tf_op jit(solution)/shard_map/pallas_call | solution.py:297
  63.5 1.5 %shard_map.117.far = bf16[8,128,128]{2,1,0:T(8,128)(2,1)S(1)} custom-call(s32[8,4,8]{2,1,0:T(4,128)S(1)} %pad_add_fusion.meta, bf16[8,4,6,128,128]{4,3,2,1,0:T(8,128)(2,1)S(1)} %shard_map.112.held, bf16[8,176,128]{2,1,0:T(8,128)(2,1)S(1)} %all_to_all.16.got), custom_call_target="tpu_custom_call" | custom-call | flops 201326592 | bytes 3145728 | tf_op jit(solution)/shard_map/pallas_call | solution.py:307
  66.1 1.6 %collective-permute-start.13 = (f32[48,128]{1,0:T(8,128)S(1)}, f32[48,128]{1,0:T(8,128)S(1)}, u32[]{:S(2)}, u32[]{:S(2)}) collective-permute-start(f32[48,128]{1,0:T(8,128)S(1)} %shard_map.122.grads), channel_id=1, source_target_pairs={{0,32},{1,33},{2,34},{3,35},{4,36},{5,37},{6,38},{7,39},{8,40},{9,... | collective-permute-start | bytes 73736 | tf_op jit(solution)/shard_map/ppermute | solution.py:231
  69.7 1.5 %shard_map.120.own = f32[8,128,128]{2,1,0:T(8,128)S(1)} custom-call(s32[8,4,8]{2,1,0:T(4,128)S(1)} %pad_add_fusion.meta, bf16[8,4,6,128,128]{4,3,2,1,0:T(8,128)(2,1)S(1)} %shard_map.112.held, bf16[8,176,128]{2,1,0:T(8,128)(2,1)S(1)} %all_to_all.16.got), custom_call_target="tpu_custom_call" | custom-call | flops 201326592 | bytes 3145728 | tf_op jit(solution)/shard_map/pallas_call | solution.py:313
  71.2 2.6 %collective-permute-done.10.far = bf16[8,128,128]{2,1,0:T(8,128)(2,1)S(1)} collective-permute-done((bf16[8,128,128]{2,1,0:T(8,128)(2,1)S(1)}, bf16[8,128,128]{2,1,0:T(8,128)(2,1)S(1)}, u32[]{:S(2)}, u32[]{:S(2)}) %collective-permute-start.10) | collective-permute-done | bytes 262176 | tf_op jit(solution)/shard_map/ppermute | solution.py:231
  74.5 3.9 %collective-permute-start.12 = (bf16[4,128,128]{2,1,0:T(8,128)(2,1)S(1)}, bf16[4,128,128]{2,1,0:T(8,128)(2,1)S(1)}, u32[]{:S(2)}, u32[]{:S(2)}) collective-permute-start(bf16[4,128,128]{2,1,0:T(8,128)(2,1)S(1)} %get-tuple-element.39.high), channel_id=1, source_target_pairs={{0,2},{1,227},{2,192},{3,161},{4,134},{5,103},{6,68},{7,37},{8,10}... | collective-permute-start | bytes 393224 | tf_op jit(solution)/shard_map/ppermute | solution.py:231
  78.5 1.8 %collective-permute-start.16 = (f32[48,128]{1,0:T(8,128)S(1)}, f32[48,128]{1,0:T(8,128)S(1)}, u32[]{:S(2)}, u32[]{:S(2)}) collective-permute-start(f32[48,128]{1,0:T(8,128)S(1)} %shard_map.123), channel_id=1, source_target_pairs={{0,16},{1,17},{2,18},{3,19},{4,20},{5,21},{6,22},{7,23},{8,24},{9,... | collective-permute-start | bytes 73736 | tf_op jit(solution)/shard_map/ppermute | solution.py:231
  80.2 2.1 %collective-permute-done.16 = f32[48,128]{1,0:T(8,128)S(1)} collective-permute-done((f32[48,128]{1,0:T(8,128)S(1)}, f32[48,128]{1,0:T(8,128)S(1)}, u32[]{:S(2)}, u32[]{:S(2)}) %collective-permute-start.16) | collective-permute-done | bytes 24608 | tf_op jit(solution)/shard_map/ppermute | solution.py:231
  82.4 1.9 %collective-permute-start.17 = (f32[48,128]{1,0:T(8,128)S(1)}, f32[48,128]{1,0:T(8,128)S(1)}, u32[]{:S(2)}, u32[]{:S(2)}) collective-permute-start(f32[48,128]{1,0:T(8,128)S(1)} %add.10), channel_id=1, source_target_pairs={{0,128},{1,129},{2,130},{3,131},{4,132},{5,133},{6,134},{7,135},{8... | collective-permute-start | bytes 73736 | tf_op jit(solution)/shard_map/ppermute | solution.py:231
  84.3 5.8 %collective-permute-done.17 = f32[48,128]{1,0:T(8,128)S(1)} collective-permute-done((f32[48,128]{1,0:T(8,128)S(1)}, f32[48,128]{1,0:T(8,128)S(1)}, u32[]{:S(2)}, u32[]{:S(2)}) %collective-permute-start.17) | collective-permute-done | bytes 24608 | tf_op jit(solution)/shard_map/ppermute | solution.py:231
  90.3 19.8 %all_to_all.17.got = bf16[8,160,128]{2,1,0:T(8,128)(2,1)S(1)} all-to-all(bf16[8,160,128]{2,1,0:T(8,128)(2,1)S(1)} %shard_map.124), channel_id=1, replica_groups=mesh['z'=8,'yl'=2,'core'=2,'x'=4,'yh'=2] {'x','yh'}, dimensions={0} | all-to-all | bytes 655360 | tf_op jit(solution)/shard_map/all_to_all | solution.py:221
  (45 shorter events, 6.5 us)
Async XLA Ops:
  2.4 12.7 %collective-permute-start = (bf16[4,128,128]{2,1,0:T(8,128)(2,1)S(1)}, bf16[4,128,128]{2,1,0:T(8,128)(2,1)S(1)}, u32[]{:S(2)}, u32[]{:S(2)}) collective-permute-start(bf16[4,128,128]{2,1,0:T(8,128)(2,1)S(1)} %get-tuple-element.24), channel_id=1, source_target_pairs={{0,0},{1,33},{2,66},{3,99},{4,132},{5,165},{6,198},{7,231},{8,8},{... | collective-permute-start | bytes 393224 | tf_op jit(solution)/shard_map/ppermute | solution.py:231
  3.0 13.7 %collective-permute-start.2 = (bf16[4,128,128]{2,1,0:T(8,128)(2,1)S(1)}, bf16[4,128,128]{2,1,0:T(8,128)(2,1)S(1)}, u32[]{:S(2)}, u32[]{:S(2)}) collective-permute-start(bf16[4,128,128]{2,1,0:T(8,128)(2,1)S(1)} %get-tuple-element.28), channel_id=1, source_target_pairs={{0,66},{1,231},{2,0},{3,165},{4,198},{5,99},{6,132},{7,33},{8,74},... | collective-permute-start | bytes 393224 | tf_op jit(solution)/shard_map/ppermute | solution.py:231
  12.2 2.8 %copy-start.3 = (s32[8,4,6]{0,1,2:T(4,128)S(1)}, s32[8,4,6]{0,1,2:T(4,128)}, u32[]{:S(2)}) copy-start(s32[8,4,6]{0,1,2:T(4,128)} %param.10) | copy-start | bytes 2308
  12.2 2.9 %copy-start.4 = (s32[8,4]{0,1:T(4,128)S(1)}, s32[8,4]{0,1:T(4,128)}, u32[]{:S(2)}) copy-start(s32[8,4]{0,1:T(4,128)} %param.11) | copy-start | bytes 388
  15.1 7.8 %collective-permute-start.4 = (bf16[4,128,128]{2,1,0:T(8,128)(2,1)S(1)}, bf16[4,128,128]{2,1,0:T(8,128)(2,1)S(1)}, u32[]{:S(2)}, u32[]{:S(2)}) collective-permute-start(bf16[4,128,128]{2,1,0:T(8,128)(2,1)S(1)} %collective-permute-done.low), channel_id=1, source_target_pairs={{0,16},{1,17},{2,18},{3,19},{4,20},{5,21},{6,22},{7,23},{8,24},{9,... | collective-permute-start | bytes 393224 | tf_op jit(solution)/shard_map/ppermute | solution.py:231
  16.7 7.5 %collective-permute-start.6 = (bf16[4,128,128]{2,1,0:T(8,128)(2,1)S(1)}, bf16[4,128,128]{2,1,0:T(8,128)(2,1)S(1)}, u32[]{:S(2)}, u32[]{:S(2)}) collective-permute-start(bf16[4,128,128]{2,1,0:T(8,128)(2,1)S(1)} %collective-permute-done.2.high), channel_id=1, source_target_pairs={{0,16},{1,17},{2,18},{3,19},{4,20},{5,21},{6,22},{7,23},{8,24},{9,... | collective-permute-start | bytes 393224 | tf_op jit(solution)/shard_map/ppermute | solution.py:231
  18.3 7.4 %collective-permute-start.1 = (bf16[4,128,128]{2,1,0:T(8,128)(2,1)S(1)}, bf16[4,128,128]{2,1,0:T(8,128)(2,1)S(1)}, u32[]{:S(2)}, u32[]{:S(2)}) collective-permute-start(bf16[4,128,128]{2,1,0:T(8,128)(2,1)S(1)} %collective-permute-done.low), channel_id=1, source_target_pairs={{0,8},{1,9},{2,10},{3,11},{4,12},{5,13},{6,14},{7,15},{8,32},{9,33... | collective-permute-start | bytes 393224 | tf_op jit(solution)/shard_map/ppermute | solution.py:231
  19.7 28.5 %copy-start = (bf16[128,256]{1,0:T(8,128)(2,1)S(1)}, bf16[128,256]{1,0:T(8,128)(2,1)}, u32[]{:S(2)}) copy-start(bf16[128,256]{1,0:T(8,128)(2,1)} %weight.1) | copy-start | bytes 196612
  19.7 28.5 %copy-start.1 = (bf16[128,256]{1,0:T(8,128)(2,1)S(1)}, bf16[128,256]{1,0:T(8,128)(2,1)}, u32[]{:S(2)}) copy-start(bf16[128,256]{1,0:T(8,128)(2,1)} %cot.1) | copy-start | bytes 196612
  19.7 28.5 %copy-start.2 = (f32[256]{0:T(256)S(1)}, f32[256]{0:T(256)}, u32[]{:S(2)}) copy-start(f32[256]{0:T(256)} %param.14) | copy-start | bytes 3076
  19.7 5.9 %collective-permute-start.3 = (bf16[4,128,128]{2,1,0:T(8,128)(2,1)S(1)}, bf16[4,128,128]{2,1,0:T(8,128)(2,1)S(1)}, u32[]{:S(2)}, u32[]{:S(2)}) collective-permute-start(bf16[4,128,128]{2,1,0:T(8,128)(2,1)S(1)} %collective-permute-done.2.high), channel_id=1, source_target_pairs={{0,8},{1,9},{2,10},{3,11},{4,12},{5,13},{6,14},{7,15},{8,32},{9,33... | collective-permute-start | bytes 393224 | tf_op jit(solution)/shard_map/ppermute | solution.py:231
  22.8 2.8 %collective-permute-start.5 = (bf16[4,128,128]{2,1,0:T(8,128)(2,1)S(1)}, bf16[4,128,128]{2,1,0:T(8,128)(2,1)S(1)}, u32[]{:S(2)}, u32[]{:S(2)}) collective-permute-start(bf16[4,128,128]{2,1,0:T(8,128)(2,1)S(1)} %collective-permute-done.4.low), channel_id=1, source_target_pairs={{0,8},{1,9},{2,10},{3,11},{4,12},{5,13},{6,14},{7,15},{8,0},{9,1},... | collective-permute-start | bytes 393224 | tf_op jit(solution)/shard_map/ppermute | solution.py:231
  24.2 1.4 %collective-permute-start.7 = (bf16[4,128,128]{2,1,0:T(8,128)(2,1)S(1)}, bf16[4,128,128]{2,1,0:T(8,128)(2,1)S(1)}, u32[]{:S(2)}, u32[]{:S(2)}) collective-permute-start(bf16[4,128,128]{2,1,0:T(8,128)(2,1)S(1)} %collective-permute-done.6.high), channel_id=1, source_target_pairs={{0,8},{1,9},{2,10},{3,11},{4,12},{5,13},{6,14},{7,15},{8,0},{9,1},... | collective-permute-start | bytes 393224 | tf_op jit(solution)/shard_map/ppermute | solution.py:231
  63.3 1.8 %collective-permute-start.8 = (bf16[1120,128]{1,0:T(8,128)(2,1)S(1)}, bf16[1120,128]{1,0:T(8,128)(2,1)S(1)}, u32[]{:S(2)}, u32[]{:S(2)}) collective-permute-start(bf16[1120,128]{1,0:T(8,128)(2,1)S(1)} %get-tuple-element.34.mine), channel_id=1, source_target_pairs={{0,8},{1,9},{2,10},{3,11},{4,12},{5,13},{6,14},{7,15},{8,0},{9,1},... | collective-permute-start | bytes 860168 | tf_op jit(solution)/shard_map/ppermute | solution.py:231
  63.4 7.8 %collective-permute-start.9 = (bf16[8,128,128]{2,1,0:T(8,128)(2,1)S(1)}, bf16[8,128,128]{2,1,0:T(8,128)(2,1)S(1)}, u32[]{:S(2)}, u32[]{:S(2)}) collective-permute-start(bf16[8,128,128]{2,1,0:T(8,128)(2,1)S(1)} %get-tuple-element.36), channel_id=1, source_target_pairs={{0,232},{1,233},{2,234},{3,235},{4,236},{5,237},{6,238},{7,239},{8... | collective-permute-start | bytes 786440 | tf_op jit(solution)/shard_map/ppermute | solution.py:231
  65.1 8.7 %collective-permute-start.10 = (bf16[8,128,128]{2,1,0:T(8,128)(2,1)S(1)}, bf16[8,128,128]{2,1,0:T(8,128)(2,1)S(1)}, u32[]{:S(2)}, u32[]{:S(2)}) collective-permute-start(bf16[8,128,128]{2,1,0:T(8,128)(2,1)S(1)} %shard_map.119), channel_id=1, source_target_pairs={{0,17},{1,18},{2,19},{3,20},{4,21},{5,22},{6,23},{7,16},{8,25},{9,... | collective-permute-start | bytes 786440 | tf_op jit(solution)/shard_map/ppermute | solution.py:231
  66.1 12.4 %collective-permute-start.13 = (f32[48,128]{1,0:T(8,128)S(1)}, f32[48,128]{1,0:T(8,128)S(1)}, u32[]{:S(2)}, u32[]{:S(2)}) collective-permute-start(f32[48,128]{1,0:T(8,128)S(1)} %shard_map.122.grads), channel_id=1, source_target_pairs={{0,32},{1,33},{2,34},{3,35},{4,36},{5,37},{6,38},{7,39},{8,40},{9,... | collective-permute-start | bytes 73736 | tf_op jit(solution)/shard_map/ppermute | solution.py:231
  67.7 10.8 %collective-permute-start.14 = (f32[48,128]{1,0:T(8,128)S(1)}, f32[48,128]{1,0:T(8,128)S(1)}, u32[]{:S(2)}, u32[]{:S(2)}) collective-permute-start(f32[48,128]{1,0:T(8,128)S(1)} %shard_map.122.grads), channel_id=1, source_target_pairs={{0,64},{1,65},{2,66},{3,67},{4,68},{5,69},{6,70},{7,71},{8,72},{9,... | collective-permute-start | bytes 73736 | tf_op jit(solution)/shard_map/ppermute | solution.py:231
  68.7 9.7 %collective-permute-start.15 = (f32[48,128]{1,0:T(8,128)S(1)}, f32[48,128]{1,0:T(8,128)S(1)}, u32[]{:S(2)}, u32[]{:S(2)}) collective-permute-start(f32[48,128]{1,0:T(8,128)S(1)} %shard_map.122.grads), channel_id=1, source_target_pairs={{0,96},{1,97},{2,98},{3,99},{4,100},{5,101},{6,102},{7,103},{8,104... | collective-permute-start | bytes 73736 | tf_op jit(solution)/shard_map/ppermute | solution.py:231
  73.9 16.3 %collective-permute-start.11 = (bf16[4,128,128]{2,1,0:T(8,128)(2,1)S(1)}, bf16[4,128,128]{2,1,0:T(8,128)(2,1)S(1)}, u32[]{:S(2)}, u32[]{:S(2)}) collective-permute-start(bf16[4,128,128]{2,1,0:T(8,128)(2,1)S(1)} %get-tuple-element.38.low), channel_id=1, source_target_pairs={{0,0},{1,225},{2,194},{3,163},{4,132},{5,101},{6,70},{7,39},{8,8},... | collective-permute-start | bytes 393224 | tf_op jit(solution)/shard_map/ppermute | solution.py:231
  74.5 15.8 %collective-permute-start.12 = (bf16[4,128,128]{2,1,0:T(8,128)(2,1)S(1)}, bf16[4,128,128]{2,1,0:T(8,128)(2,1)S(1)}, u32[]{:S(2)}, u32[]{:S(2)}) collective-permute-start(bf16[4,128,128]{2,1,0:T(8,128)(2,1)S(1)} %get-tuple-element.39.high), channel_id=1, source_target_pairs={{0,2},{1,227},{2,192},{3,161},{4,134},{5,103},{6,68},{7,37},{8,10}... | collective-permute-start | bytes 393224 | tf_op jit(solution)/shard_map/ppermute | solution.py:231
  78.5 3.9 %collective-permute-start.16 = (f32[48,128]{1,0:T(8,128)S(1)}, f32[48,128]{1,0:T(8,128)S(1)}, u32[]{:S(2)}, u32[]{:S(2)}) collective-permute-start(f32[48,128]{1,0:T(8,128)S(1)} %shard_map.123), channel_id=1, source_target_pairs={{0,16},{1,17},{2,18},{3,19},{4,20},{5,21},{6,22},{7,23},{8,24},{9,... | collective-permute-start | bytes 73736 | tf_op jit(solution)/shard_map/ppermute | solution.py:231
  82.4 7.7 %collective-permute-start.17 = (f32[48,128]{1,0:T(8,128)S(1)}, f32[48,128]{1,0:T(8,128)S(1)}, u32[]{:S(2)}, u32[]{:S(2)}) collective-permute-start(f32[48,128]{1,0:T(8,128)S(1)} %add.10), channel_id=1, source_target_pairs={{0,128},{1,129},{2,130},{3,131},{4,132},{5,133},{6,134},{7,135},{8... | collective-permute-start | bytes 73736 | tf_op jit(solution)/shard_map/ppermute | solution.py:231

commit v12 on v11

--- a/solution.py
+++ b/solution.py
@@ -167,12 +167,28 @@
         out[j] = (far[j].astype(F32) + rows).astype(BF16)
 
 
+def bias_of(rows):
+    return rows[32:34].astype(F32) + rows[34:36].astype(F32)
+
+
+def slice_rows(weights, bias):
+    return jnp.concatenate([weights.astype(BF16), bias_rows(bias)], axis=0)
+
+
 def pair_kernel(mine, other, grads):
-    grads[...] = grads_of(mine) + grads_of(other)
+    total = grads_of(mine) + grads_of(other)
+    grads[...] = slice_rows(total[0:32], total[32:34])
 
 
 def group_kernel(grads, one, two, three, low, high, out):
-    out[...] = (grads[...] + one[...]) + (two[...] + three[...])
+    a, b, c, d = (v[0:32].astype(F32) for v in (grads, one, two, three))
+    bias = (bias_of(grads) + bias_of(one)) + (bias_of(two) + bias_of(three))
+    out[...] = slice_rows((a + b) + (c + d), bias)
+
+
+def add_kernel(grads, other, out):
+    total = grads[0:32].astype(F32) + other[0:32].astype(F32)
+    out[...] = slice_rows(total, bias_of(grads) + bias_of(other))
 
 
 def total_kernel(own, near, far, low, high):
@@ -183,7 +199,7 @@
 
 
 def gather_kernel(low, high, grads, out):
-    mine = grads[0:32].astype(BF16)
+    mine = grads[0:32]
     for j in range(ROWS):
         out[j, 0:T] = low[j] if j < HALF else high[j - HALF]
         out[j, T:] = mine
@@ -198,7 +214,8 @@
         rows = slice(16 * j, 16 * j + 16)
         grad_weight[rows, :T] = got[j, T : T + 16].astype(F32)
         grad_weight[rows, T:] = got[j, T + 16 :].astype(F32)
-    grad_bias[...] = jnp.concatenate([grads[32:33], grads[33:34]], axis=1)
+    bias = bias_of(grads)
+    grad_bias[...] = jnp.concatenate([bias[0:1], bias[1:2]], axis=1)
 
 
 def call(kernel, out, in_specs, scratch=(), flops=0, moved=1 << 20):
@@ -313,7 +330,7 @@
     (own,) = call(own_sums_kernel, [(tiles, F32)], [SMEM] + [VMEM] * 2, sums, work, 3 << 20)(
         meta, held, got
     )
-    (grads,) = call(pair_kernel, [((GRAD, T), F32)], [VMEM] * 2, (), PAIR_FLOPS)(mine, other)
+    (grads,) = call(pair_kernel, [((GRAD, T), BF16)], [VMEM] * 2, (), PAIR_FLOPS)(mine, other)
     groups = [swap(grads, bits) for bits in (4, 8, 12)]
     low, high = call(total_kernel, [(half, BF16), (half, BF16)], [VMEM] * 3)(own, near, far)
     sent_low, sent_high = low, high
@@ -321,10 +338,10 @@
     high = move(high, lambda b, r: (b - 4 * r, r ^ 2))
     anywhere = pl.BlockSpec(memory_space=pl.ANY)
     (grads,) = call(
-        group_kernel, [((GRAD, T), F32)], [VMEM] * 4 + [anywhere] * 2, (), GROUP_FLOPS
+        group_kernel, [((GRAD, T), BF16)], [VMEM] * 4 + [anywhere] * 2, (), GROUP_FLOPS
     )(grads, *groups, sent_low, sent_high)
     for bit in (2, 16):
-        grads = grads + swap(grads, bit)
+        (grads,) = call(add_kernel, [((GRAD, T), BF16)], [VMEM] * 2)(grads, swap(grads, bit))
     (send,) = call(gather_kernel, [((ROWS, T + 32, T), BF16)], [VMEM] * 3)(low, high, grads)
     got = exchange(send, REP)
     grad_features, grad_weight, grad_bias = call(

time: 111 us -> 111 us (level)
  no operation moved by 1% of the time
where the time goes in v12:
time: 111 us
  blocking collectives  52.5 us (47%)
  starting transfers between devices  28.1 us (25%)
  Pallas kernels  16 us (14%)
  waiting for transfers between devices  13 us (12%)
    all_to_all x3, blocking collectives, exchange(): return lax.all_to_all(value, axes, 0, 0, tiled=True)  52.5 us
    ppermute x18, starting transfers between devices, move(): return lax.ppermute(value, BLK + REP, pairs)  28.1 us
    ppermute x18, waiting for transfers between devices, move(): return lax.ppermute(value, BLK + REP, pairs)  13 us
    pallas_call x1, Pallas kernels, on_device(): call(load_kernel, [(edges.shape, BF16)], [HBM], [pltpu.SemaphoreType.DMA]...  2.82 us
  transfers between devices with their start and end apart: 18, of which 6 were waited for; matrix products, arithmetic and copies ran while one was open for 0% of the time, Pallas kernels for 8%

profile of v12, /device:TPU:32, one launch (start us, length us, event | category | flops | bytes accessed | tf_op | source)
XLA Modules:
  0.0 110.6 jit_solution(776010802347586527)
XLA Ops:
  0.6 1.7 %shard_map.111 = (bf16[4,128,128]{2,1,0:T(8,128)(2,1)S(1)}, bf16[4,128,128]{2,1,0:T(8,128)(2,1)S(1)}, f32[128,128]{1,0:T(8,128)S(1)}) custom-call(s32[1]{0:T(128)} %bitcast.rep, bf16[1024,128]{1,0:T(8,128)(2,1)} %features.1, s32[8,128]{1,0:T(8,128)} %bitcast.10), custom_call_target="tpu_custom_call" | custom-call | bytes 1048576 | tf_op jit(solution)/shard_map/pallas_call | solution.py:275
  3.0 9.1 %collective-permute-start.2 = (bf16[4,128,128]{2,1,0:T(8,128)(2,1)S(1)}, bf16[4,128,128]{2,1,0:T(8,128)(2,1)S(1)}, u32[]{:S(2)}, u32[]{:S(2)}) collective-permute-start(bf16[4,128,128]{2,1,0:T(8,128)(2,1)S(1)} %get-tuple-element.28), channel_id=1, source_target_pairs={{0,66},{1,231},{2,0},{3,165},{4,198},{5,99},{6,132},{7,33},{8,74},... | collective-permute-start | bytes 393224 | tf_op jit(solution)/shard_map/ppermute | solution.py:248
  12.2 2.8 %shard_map.112.held = bf16[8,4,6,128,128]{4,3,2,1,0:T(8,128)(2,1)S(1)} custom-call(bf16[8,4,6,128,128]{4,3,2,1,0:T(8,128)(2,1)} %edges.1), custom_call_target="tpu_custom_call" | custom-call | bytes 12582912 | tf_op jit(solution)/shard_map/pallas_call | solution.py:283
  15.1 1.7 %collective-permute-start.4 = (bf16[4,128,128]{2,1,0:T(8,128)(2,1)S(1)}, bf16[4,128,128]{2,1,0:T(8,128)(2,1)S(1)}, u32[]{:S(2)}, u32[]{:S(2)}) collective-permute-start(bf16[4,128,128]{2,1,0:T(8,128)(2,1)S(1)} %collective-permute-done.low), channel_id=1, source_target_pairs={{0,16},{1,17},{2,18},{3,19},{4,20},{5,21},{6,22},{7,23},{8,24},{9,... | collective-permute-start | bytes 393224 | tf_op jit(solution)/shard_map/ppermute | solution.py:248
  16.7 1.5 %collective-permute-start.6 = (bf16[4,128,128]{2,1,0:T(8,128)(2,1)S(1)}, bf16[4,128,128]{2,1,0:T(8,128)(2,1)S(1)}, u32[]{:S(2)}, u32[]{:S(2)}) collective-permute-start(bf16[4,128,128]{2,1,0:T(8,128)(2,1)S(1)} %collective-permute-done.2.high), channel_id=1, source_target_pairs={{0,16},{1,17},{2,18},{3,19},{4,20},{5,21},{6,22},{7,23},{8,24},{9,... | collective-permute-start | bytes 393224 | tf_op jit(solution)/shard_map/ppermute | solution.py:248
  18.3 1.4 %shard_map.113.total = f32[8,128,128]{2,1,0:T(8,128)S(1)} custom-call(s32[8,4,8]{2,1,0:T(4,128)S(1)} %pad_add_fusion.meta, bf16[8,4,6,128,128]{4,3,2,1,0:T(8,128)(2,1)S(1)} %shard_map.112.held, bf16[4,128,128]{2,1,0:T(8,128)(2,1)S(1)} %collective-permute-done.low, bf16[4,128,128]{2,1,0:T(8,128)(2,1)S(1)} %collective-permute-done.2.high), custom_call_target="tpu_custom_call" | custom-call | flops 201326592 | bytes 3145728 | tf_op jit(solution)/shard_map/pallas_call | solution.py:292
  19.7 1.9 %collective-permute-start.3 = (bf16[4,128,128]{2,1,0:T(8,128)(2,1)S(1)}, bf16[4,128,128]{2,1,0:T(8,128)(2,1)S(1)}, u32[]{:S(2)}, u32[]{:S(2)}) collective-permute-start(bf16[4,128,128]{2,1,0:T(8,128)(2,1)S(1)} %collective-permute-done.2.high), channel_id=1, source_target_pairs={{0,8},{1,9},{2,10},{3,11},{4,12},{5,13},{6,14},{7,15},{8,32},{9,33... | collective-permute-start | bytes 393224 | tf_op jit(solution)/shard_map/ppermute | solution.py:248
  21.6 1.2 %collective-permute-done.4.low = bf16[4,128,128]{2,1,0:T(8,128)(2,1)S(1)} collective-permute-done((bf16[4,128,128]{2,1,0:T(8,128)(2,1)S(1)}, bf16[4,128,128]{2,1,0:T(8,128)(2,1)S(1)}, u32[]{:S(2)}, u32[]{:S(2)}) %collective-permute-start.4) | collective-permute-done | bytes 131104 | tf_op jit(solution)/shard_map/ppermute | solution.py:248
  22.8 1.4 %collective-permute-done.6.high = bf16[4,128,128]{2,1,0:T(8,128)(2,1)S(1)} collective-permute-done((bf16[4,128,128]{2,1,0:T(8,128)(2,1)S(1)}, bf16[4,128,128]{2,1,0:T(8,128)(2,1)S(1)}, u32[]{:S(2)}, u32[]{:S(2)}) %collective-permute-start.6) | collective-permute-done | bytes 131104 | tf_op jit(solution)/shard_map/ppermute | solution.py:248
  24.2 1.4 %shard_map.114.total = f32[8,128,128]{2,1,0:T(8,128)S(1)} custom-call(s32[8,4,8]{2,1,0:T(4,128)S(1)} %pad_add_fusion.meta, bf16[8,4,6,128,128]{4,3,2,1,0:T(8,128)(2,1)S(1)} %shard_map.112.held, bf16[4,128,128]{2,1,0:T(8,128)(2,1)S(1)} %collective-permute-done.4.low, bf16[4,128,128]{2,1,0:T(8,128)(2,1)S(1)} %collective-permute-done.6.high, ...), custom_call_target="tpu_custom_call" | custom-call | flops 201326592 | bytes 3145728 | tf_op jit(solution)/shard_map/pallas_call | solution.py:298
  25.7 1.8 %shard_map.115 = bf16[8,128,128]{2,1,0:T(8,128)(2,1)S(1)} custom-call(s32[8,4,8]{2,1,0:T(4,128)S(1)} %pad_add_fusion.meta, bf16[8,4,6,128,128]{4,3,2,1,0:T(8,128)(2,1)S(1)} %shard_map.112.held, bf16[4,128,128]{2,1,0:T(8,128)(2,1)S(1)} %collective-permute-done.1.near_low, bf16[4,128,128]{2,1,0:T(8,128)(2,1)S(1)} %collective-permute-done.3.near_high, ...), custom_call_target="tpu_custom_call" | custom-call | flops 402653184 | bytes 6291456 | tf_op jit(solution)/shard_map/pallas_call | solution.py:301
  27.5 20.7 %all_to_all.15.parts = bf16[8,128,128]{2,1,0:T(8,128)(2,1)S(1)} all-to-all(bf16[8,128,128]{2,1,0:T(8,128)(2,1)S(1)} %shard_map.115), channel_id=1, replica_groups=mesh['z'=8,'yl'=2,'core'=2,'x'=4,'yh'=2] {'x','yh'}, dimensions={0} | all-to-all | bytes 524288 | tf_op jit(solution)/shard_map/all_to_all | solution.py:238
  49.0 12.2 %all_to_all.16.got = bf16[8,176,128]{2,1,0:T(8,128)(2,1)S(1)} all-to-all(bf16[8,176,128]{2,1,0:T(8,128)(2,1)S(1)} %get-tuple-element.33), channel_id=1, replica_groups=mesh['z'=8,'yl'=2,'core'=2,'x'=4,'yh'=2] {'x','yh'}, dimensions={0} | all-to-all | bytes 720896 | tf_op jit(solution)/shard_map/all_to_all | solution.py:238
  61.2 2.1 %shard_map.118 = (bf16[8,128,128]{2,1,0:T(8,128)(2,1)S(1)}, bf16[1120,128]{1,0:T(8,128)(2,1)S(1)}) custom-call(s32[8,4,8]{2,1,0:T(4,128)S(1)} %pad_add_fusion.meta, bf16[8,4,6,128,128]{4,3,2,1,0:T(8,128)(2,1)S(1)} %shard_map.112.held, bf16[8,176,128]{2,1,0:T(8,128)(2,1)S(1)} %all_to_all.16.got), custom_call_target="tpu_custom_call" | custom-call | flops 402653184 | bytes 6291456 | tf_op jit(solution)/shard_map/pallas_call | solution.py:314
  63.5 1.5 %shard_map.117.far = bf16[8,128,128]{2,1,0:T(8,128)(2,1)S(1)} custom-call(s32[8,4,8]{2,1,0:T(4,128)S(1)} %pad_add_fusion.meta, bf16[8,4,6,128,128]{4,3,2,1,0:T(8,128)(2,1)S(1)} %shard_map.112.held, bf16[8,176,128]{2,1,0:T(8,128)(2,1)S(1)} %all_to_all.16.got), custom_call_target="tpu_custom_call" | custom-call | flops 201326592 | bytes 3145728 | tf_op jit(solution)/shard_map/pallas_call | solution.py:324
  66.1 1.6 %collective-permute-start.13 = (bf16[48,128]{1,0:T(8,128)(2,1)S(1)}, bf16[48,128]{1,0:T(8,128)(2,1)S(1)}, u32[]{:S(2)}, u32[]{:S(2)}) collective-permute-start(bf16[48,128]{1,0:T(8,128)(2,1)S(1)} %shard_map.122.grads), channel_id=1, source_target_pairs={{0,32},{1,33},{2,34},{3,35},{4,36},{5,37},{6,38},{7,39},{8,40},{9,... | collective-permute-start | bytes 36872 | tf_op jit(solution)/shard_map/ppermute | solution.py:248
  69.7 1.5 %shard_map.120.own = f32[8,128,128]{2,1,0:T(8,128)S(1)} custom-call(s32[8,4,8]{2,1,0:T(4,128)S(1)} %pad_add_fusion.meta, bf16[8,4,6,128,128]{4,3,2,1,0:T(8,128)(2,1)S(1)} %shard_map.112.held, bf16[8,176,128]{2,1,0:T(8,128)(2,1)S(1)} %all_to_all.16.got), custom_call_target="tpu_custom_call" | custom-call | flops 201326592 | bytes 3145728 | tf_op jit(solution)/shard_map/pallas_call | solution.py:330
  71.2 2.6 %collective-permute-done.10.far = bf16[8,128,128]{2,1,0:T(8,128)(2,1)S(1)} collective-permute-done((bf16[8,128,128]{2,1,0:T(8,128)(2,1)S(1)}, bf16[8,128,128]{2,1,0:T(8,128)(2,1)S(1)}, u32[]{:S(2)}, u32[]{:S(2)}) %collective-permute-start.10) | collective-permute-done | bytes 262176 | tf_op jit(solution)/shard_map/ppermute | solution.py:248
  74.5 3.9 %collective-permute-start.12 = (bf16[4,128,128]{2,1,0:T(8,128)(2,1)S(1)}, bf16[4,128,128]{2,1,0:T(8,128)(2,1)S(1)}, u32[]{:S(2)}, u32[]{:S(2)}) collective-permute-start(bf16[4,128,128]{2,1,0:T(8,128)(2,1)S(1)} %get-tuple-element.39.high), channel_id=1, source_target_pairs={{0,2},{1,227},{2,192},{3,161},{4,134},{5,103},{6,68},{7,37},{8,10}... | collective-permute-start | bytes 393224 | tf_op jit(solution)/shard_map/ppermute | solution.py:248
  78.5 1.8 %collective-permute-start.16 = (bf16[48,128]{1,0:T(8,128)(2,1)S(1)}, bf16[48,128]{1,0:T(8,128)(2,1)S(1)}, u32[]{:S(2)}, u32[]{:S(2)}) collective-permute-start(bf16[48,128]{1,0:T(8,128)(2,1)S(1)} %shard_map.123.grads), channel_id=1, source_target_pairs={{0,16},{1,17},{2,18},{3,19},{4,20},{5,21},{6,22},{7,23},{8,24},{9,... | collective-permute-start | bytes 36872 | tf_op jit(solution)/shard_map/ppermute | solution.py:248
  80.2 2.0 %collective-permute-done.16.other = bf16[48,128]{1,0:T(8,128)(2,1)S(1)} collective-permute-done((bf16[48,128]{1,0:T(8,128)(2,1)S(1)}, bf16[48,128]{1,0:T(8,128)(2,1)S(1)}, u32[]{:S(2)}, u32[]{:S(2)}) %collective-permute-start.16) | collective-permute-done | bytes 12320 | tf_op jit(solution)/shard_map/ppermute | solution.py:248
  82.3 2.1 %collective-permute-start.17 = (bf16[48,128]{1,0:T(8,128)(2,1)S(1)}, bf16[48,128]{1,0:T(8,128)(2,1)S(1)}, u32[]{:S(2)}, u32[]{:S(2)}) collective-permute-start(bf16[48,128]{1,0:T(8,128)(2,1)S(1)} %shard_map.124.grads), channel_id=1, source_target_pairs={{0,128},{1,129},{2,130},{3,131},{4,132},{5,133},{6,134},{7,135},{8... | collective-permute-start | bytes 36872 | tf_op jit(solution)/shard_map/ppermute | solution.py:248
  84.3 5.6 %collective-permute-done.17.other = bf16[48,128]{1,0:T(8,128)(2,1)S(1)} collective-permute-done((bf16[48,128]{1,0:T(8,128)(2,1)S(1)}, bf16[48,128]{1,0:T(8,128)(2,1)S(1)}, u32[]{:S(2)}, u32[]{:S(2)}) %collective-permute-start.17) | collective-permute-done | bytes 12320 | tf_op jit(solution)/shard_map/ppermute | solution.py:248
  90.2 19.6 %all_to_all.17.got = bf16[8,160,128]{2,1,0:T(8,128)(2,1)S(1)} all-to-all(bf16[8,160,128]{2,1,0:T(8,128)(2,1)S(1)} %shard_map.126), channel_id=1, replica_groups=mesh['z'=8,'yl'=2,'core'=2,'x'=4,'yh'=2] {'x','yh'}, dimensions={0} | all-to-all | bytes 655360 | tf_op jit(solution)/shard_map/all_to_all | solution.py:238
  (45 shorter events, 6.6 us)
Async XLA Ops:
  2.4 12.7 %collective-permute-start = (bf16[4,128,128]{2,1,0:T(8,128)(2,1)S(1)}, bf16[4,128,128]{2,1,0:T(8,128)(2,1)S(1)}, u32[]{:S(2)}, u32[]{:S(2)}) collective-permute-start(bf16[4,128,128]{2,1,0:T(8,128)(2,1)S(1)} %get-tuple-element.24), channel_id=1, source_target_pairs={{0,0},{1,33},{2,66},{3,99},{4,132},{5,165},{6,198},{7,231},{8,8},{... | collective-permute-start | bytes 393224 | tf_op jit(solution)/shard_map/ppermute | solution.py:248
  3.0 13.7 %collective-permute-start.2 = (bf16[4,128,128]{2,1,0:T(8,128)(2,1)S(1)}, bf16[4,128,128]{2,1,0:T(8,128)(2,1)S(1)}, u32[]{:S(2)}, u32[]{:S(2)}) collective-permute-start(bf16[4,128,128]{2,1,0:T(8,128)(2,1)S(1)} %get-tuple-element.28), channel_id=1, source_target_pairs={{0,66},{1,231},{2,0},{3,165},{4,198},{5,99},{6,132},{7,33},{8,74},... | collective-permute-start | bytes 393224 | tf_op jit(solution)/shard_map/ppermute | solution.py:248
  12.2 2.8 %copy-start.3 = (s32[8,4,6]{0,1,2:T(4,128)S(1)}, s32[8,4,6]{0,1,2:T(4,128)}, u32[]{:S(2)}) copy-start(s32[8,4,6]{0,1,2:T(4,128)} %param.10) | copy-start | bytes 2308
  12.2 2.9 %copy-start.4 = (s32[8,4]{0,1:T(4,128)S(1)}, s32[8,4]{0,1:T(4,128)}, u32[]{:S(2)}) copy-start(s32[8,4]{0,1:T(4,128)} %param.11) | copy-start | bytes 388
  15.1 7.8 %collective-permute-start.4 = (bf16[4,128,128]{2,1,0:T(8,128)(2,1)S(1)}, bf16[4,128,128]{2,1,0:T(8,128)(2,1)S(1)}, u32[]{:S(2)}, u32[]{:S(2)}) collective-permute-start(bf16[4,128,128]{2,1,0:T(8,128)(2,1)S(1)} %collective-permute-done.low), channel_id=1, source_target_pairs={{0,16},{1,17},{2,18},{3,19},{4,20},{5,21},{6,22},{7,23},{8,24},{9,... | collective-permute-start | bytes 393224 | tf_op jit(solution)/shard_map/ppermute | solution.py:248
  16.7 7.5 %collective-permute-start.6 = (bf16[4,128,128]{2,1,0:T(8,128)(2,1)S(1)}, bf16[4,128,128]{2,1,0:T(8,128)(2,1)S(1)}, u32[]{:S(2)}, u32[]{:S(2)}) collective-permute-start(bf16[4,128,128]{2,1,0:T(8,128)(2,1)S(1)} %collective-permute-done.2.high), channel_id=1, source_target_pairs={{0,16},{1,17},{2,18},{3,19},{4,20},{5,21},{6,22},{7,23},{8,24},{9,... | collective-permute-start | bytes 393224 | tf_op jit(solution)/shard_map/ppermute | solution.py:248
  18.3 7.4 %collective-permute-start.1 = (bf16[4,128,128]{2,1,0:T(8,128)(2,1)S(1)}, bf16[4,128,128]{2,1,0:T(8,128)(2,1)S(1)}, u32[]{:S(2)}, u32[]{:S(2)}) collective-permute-start(bf16[4,128,128]{2,1,0:T(8,128)(2,1)S(1)} %collective-permute-done.low), channel_id=1, source_target_pairs={{0,8},{1,9},{2,10},{3,11},{4,12},{5,13},{6,14},{7,15},{8,32},{9,33... | collective-permute-start | bytes 393224 | tf_op jit(solution)/shard_map/ppermute | solution.py:248
  19.7 28.5 %copy-start = (bf16[128,256]{1,0:T(8,128)(2,1)S(1)}, bf16[128,256]{1,0:T(8,128)(2,1)}, u32[]{:S(2)}) copy-start(bf16[128,256]{1,0:T(8,128)(2,1)} %weight.1) | copy-start | bytes 196612
  19.7 28.5 %copy-start.1 = (bf16[128,256]{1,0:T(8,128)(2,1)S(1)}, bf16[128,256]{1,0:T(8,128)(2,1)}, u32[]{:S(2)}) copy-start(bf16[128,256]{1,0:T(8,128)(2,1)} %cot.1) | copy-start | bytes 196612
  19.7 28.5 %copy-start.2 = (f32[256]{0:T(256)S(1)}, f32[256]{0:T(256)}, u32[]{:S(2)}) copy-start(f32[256]{0:T(256)} %param.14) | copy-start | bytes 3076
  19.7 5.9 %collective-permute-start.3 = (bf16[4,128,128]{2,1,0:T(8,128)(2,1)S(1)}, bf16[4,128,128]{2,1,0:T(8,128)(2,1)S(1)}, u32[]{:S(2)}, u32[]{:S(2)}) collective-permute-start(bf16[4,128,128]{2,1,0:T(8,128)(2,1)S(1)} %collective-permute-done.2.high), channel_id=1, source_target_pairs={{0,8},{1,9},{2,10},{3,11},{4,12},{5,13},{6,14},{7,15},{8,32},{9,33... | collective-permute-start | bytes 393224 | tf_op jit(solution)/shard_map/ppermute | solution.py:248
  22.8 2.8 %collective-permute-start.5 = (bf16[4,128,128]{2,1,0:T(8,128)(2,1)S(1)}, bf16[4,128,128]{2,1,0:T(8,128)(2,1)S(1)}, u32[]{:S(2)}, u32[]{:S(2)}) collective-permute-start(bf16[4,128,128]{2,1,0:T(8,128)(2,1)S(1)} %collective-permute-done.4.low), channel_id=1, source_target_pairs={{0,8},{1,9},{2,10},{3,11},{4,12},{5,13},{6,14},{7,15},{8,0},{9,1},... | collective-permute-start | bytes 393224 | tf_op jit(solution)/shard_map/ppermute | solution.py:248
  24.2 1.4 %collective-permute-start.7 = (bf16[4,128,128]{2,1,0:T(8,128)(2,1)S(1)}, bf16[4,128,128]{2,1,0:T(8,128)(2,1)S(1)}, u32[]{:S(2)}, u32[]{:S(2)}) collective-permute-start(bf16[4,128,128]{2,1,0:T(8,128)(2,1)S(1)} %collective-permute-done.6.high), channel_id=1, source_target_pairs={{0,8},{1,9},{2,10},{3,11},{4,12},{5,13},{6,14},{7,15},{8,0},{9,1},... | collective-permute-start | bytes 393224 | tf_op jit(solution)/shard_map/ppermute | solution.py:248
  63.3 1.8 %collective-permute-start.8 = (bf16[1120,128]{1,0:T(8,128)(2,1)S(1)}, bf16[1120,128]{1,0:T(8,128)(2,1)S(1)}, u32[]{:S(2)}, u32[]{:S(2)}) collective-permute-start(bf16[1120,128]{1,0:T(8,128)(2,1)S(1)} %get-tuple-element.34.mine), channel_id=1, source_target_pairs={{0,8},{1,9},{2,10},{3,11},{4,12},{5,13},{6,14},{7,15},{8,0},{9,1},... | collective-permute-start | bytes 860168 | tf_op jit(solution)/shard_map/ppermute | solution.py:248
  63.4 7.8 %collective-permute-start.9 = (bf16[8,128,128]{2,1,0:T(8,128)(2,1)S(1)}, bf16[8,128,128]{2,1,0:T(8,128)(2,1)S(1)}, u32[]{:S(2)}, u32[]{:S(2)}) collective-permute-start(bf16[8,128,128]{2,1,0:T(8,128)(2,1)S(1)} %get-tuple-element.36), channel_id=1, source_target_pairs={{0,232},{1,233},{2,234},{3,235},{4,236},{5,237},{6,238},{7,239},{8... | collective-permute-start | bytes 786440 | tf_op jit(solution)/shard_map/ppermute | solution.py:248
  65.1 8.6 %collective-permute-start.10 = (bf16[8,128,128]{2,1,0:T(8,128)(2,1)S(1)}, bf16[8,128,128]{2,1,0:T(8,128)(2,1)S(1)}, u32[]{:S(2)}, u32[]{:S(2)}) collective-permute-start(bf16[8,128,128]{2,1,0:T(8,128)(2,1)S(1)} %shard_map.119), channel_id=1, source_target_pairs={{0,17},{1,18},{2,19},{3,20},{4,21},{5,22},{6,23},{7,16},{8,25},{9,... | collective-permute-start | bytes 786440 | tf_op jit(solution)/shard_map/ppermute | solution.py:248
  66.1 12.3 %collective-permute-start.13 = (bf16[48,128]{1,0:T(8,128)(2,1)S(1)}, bf16[48,128]{1,0:T(8,128)(2,1)S(1)}, u32[]{:S(2)}, u32[]{:S(2)}) collective-permute-start(bf16[48,128]{1,0:T(8,128)(2,1)S(1)} %shard_map.122.grads), channel_id=1, source_target_pairs={{0,32},{1,33},{2,34},{3,35},{4,36},{5,37},{6,38},{7,39},{8,40},{9,... | collective-permute-start | bytes 36872 | tf_op jit(solution)/shard_map/ppermute | solution.py:248
  67.7 10.7 %collective-permute-start.14 = (bf16[48,128]{1,0:T(8,128)(2,1)S(1)}, bf16[48,128]{1,0:T(8,128)(2,1)S(1)}, u32[]{:S(2)}, u32[]{:S(2)}) collective-permute-start(bf16[48,128]{1,0:T(8,128)(2,1)S(1)} %shard_map.122.grads), channel_id=1, source_target_pairs={{0,64},{1,65},{2,66},{3,67},{4,68},{5,69},{6,70},{7,71},{8,72},{9,... | collective-permute-start | bytes 36872 | tf_op jit(solution)/shard_map/ppermute | solution.py:248
  68.8 9.7 %collective-permute-start.15 = (bf16[48,128]{1,0:T(8,128)(2,1)S(1)}, bf16[48,128]{1,0:T(8,128)(2,1)S(1)}, u32[]{:S(2)}, u32[]{:S(2)}) collective-permute-start(bf16[48,128]{1,0:T(8,128)(2,1)S(1)} %shard_map.122.grads), channel_id=1, source_target_pairs={{0,96},{1,97},{2,98},{3,99},{4,100},{5,101},{6,102},{7,103},{8,104... | collective-permute-start | bytes 36872 | tf_op jit(solution)/shard_map/ppermute | solution.py:248
  73.9 16.1 %collective-permute-start.11 = (bf16[4,128,128]{2,1,0:T(8,128)(2,1)S(1)}, bf16[4,128,128]{2,1,0:T(8,128)(2,1)S(1)}, u32[]{:S(2)}, u32[]{:S(2)}) collective-permute-start(bf16[4,128,128]{2,1,0:T(8,128)(2,1)S(1)} %get-tuple-element.38.low), channel_id=1, source_target_pairs={{0,0},{1,225},{2,194},{3,163},{4,132},{5,101},{6,70},{7,39},{8,8},... | collective-permute-start | bytes 393224 | tf_op jit(solution)/shard_map/ppermute | solution.py:248
  74.5 15.6 %collective-permute-start.12 = (bf16[4,128,128]{2,1,0:T(8,128)(2,1)S(1)}, bf16[4,128,128]{2,1,0:T(8,128)(2,1)S(1)}, u32[]{:S(2)}, u32[]{:S(2)}) collective-permute-start(bf16[4,128,128]{2,1,0:T(8,128)(2,1)S(1)} %get-tuple-element.39.high), channel_id=1, source_target_pairs={{0,2},{1,227},{2,192},{3,161},{4,134},{5,103},{6,68},{7,37},{8,10}... | collective-permute-start | bytes 393224 | tf_op jit(solution)/shard_map/ppermute | solution.py:248
  78.5 3.8 %collective-permute-start.16 = (bf16[48,128]{1,0:T(8,128)(2,1)S(1)}, bf16[48,128]{1,0:T(8,128)(2,1)S(1)}, u32[]{:S(2)}, u32[]{:S(2)}) collective-permute-start(bf16[48,128]{1,0:T(8,128)(2,1)S(1)} %shard_map.123.grads), channel_id=1, source_target_pairs={{0,16},{1,17},{2,18},{3,19},{4,20},{5,21},{6,22},{7,23},{8,24},{9,... | collective-permute-start | bytes 36872 | tf_op jit(solution)/shard_map/ppermute | solution.py:248
  82.3 7.7 %collective-permute-start.17 = (bf16[48,128]{1,0:T(8,128)(2,1)S(1)}, bf16[48,128]{1,0:T(8,128)(2,1)S(1)}, u32[]{:S(2)}, u32[]{:S(2)}) collective-permute-start(bf16[48,128]{1,0:T(8,128)(2,1)S(1)} %shard_map.124.grads), channel_id=1, source_target_pairs={{0,128},{1,129},{2,130},{3,131},{4,132},{5,133},{6,134},{7,135},{8... | collective-permute-start | bytes 36872 | tf_op jit(solution)/shard_map/ppermute | solution.py:248

commit v13 on v11

--- a/solution.py
+++ b/solution.py
@@ -232,7 +232,7 @@
 
 
 def column(r):
-    return r ^ (6 if r % 2 else 2)
+    return r ^ (6 if r % 2 else 4)
 
 
 def far_out(b, r):

time: 111 us -> 111 us (level)
  blocking collectives: 52.7 us -> 51.1 us
    all_to_all x3, blocking collectives: 52.7 us -> 51.1 us  [exchange(): return lax.all_to_all(value, axes, 0, 0, tiled=True)]
  transfers between devices with their start and end apart: 18 -> 18, of which waited for: 6 -> 8; matrix products, arithmetic and copies ran while one was open for 0% -> 0% of each run, Pallas kernels for 8% -> 8%
where the time goes in v13:
time: 111 us; the launch traced here: 110 us
  blocking collectives  51.1 us (46%)
  starting transfers between devices  28.9 us (26%)
  Pallas kernels  16 us (14%)
  waiting for transfers between devices  13.6 us (12%)
    all_to_all x3, blocking collectives, exchange(): return lax.all_to_all(value, axes, 0, 0, tiled=True)  51.1 us
    ppermute x18, starting transfers between devices, move(): return lax.ppermute(value, BLK + REP, pairs)  28.9 us
    ppermute x18, waiting for transfers between devices, move(): return lax.ppermute(value, BLK + REP, pairs)  13.6 us
    pallas_call x1, Pallas kernels, on_device(): call(load_kernel, [(edges.shape, BF16)], [HBM], [pltpu.SemaphoreType.DMA]...  2.82 us
  transfers between devices with their start and end apart: 18, of which 8 were waited for; matrix products, arithmetic and copies ran while one was open for 0% of the time, Pallas kernels for 8%

profile of v13, /device:TPU:32, one launch (start us, length us, event | category | flops | bytes accessed | tf_op | source)
XLA Modules:
  0.0 110.4 jit_solution(8003759270707773781)
XLA Ops:
  0.6 1.7 %shard_map.111 = (bf16[4,128,128]{2,1,0:T(8,128)(2,1)S(1)}, bf16[4,128,128]{2,1,0:T(8,128)(2,1)S(1)}, f32[128,128]{1,0:T(8,128)S(1)}) custom-call(s32[1]{0:T(128)} %bitcast.rep, bf16[1024,128]{1,0:T(8,128)(2,1)} %features.1, s32[8,128]{1,0:T(8,128)} %bitcast.10), custom_call_target="tpu_custom_call" | custom-call | bytes 1048576 | tf_op jit(solution)/shard_map/pallas_call | solution.py:258
  3.0 10.1 %collective-permute-start.2 = (bf16[4,128,128]{2,1,0:T(8,128)(2,1)S(1)}, bf16[4,128,128]{2,1,0:T(8,128)(2,1)S(1)}, u32[]{:S(2)}, u32[]{:S(2)}) collective-permute-start(bf16[4,128,128]{2,1,0:T(8,128)(2,1)S(1)} %get-tuple-element.28), channel_id=1, source_target_pairs={{0,132},{1,231},{2,198},{3,165},{4,0},{5,99},{6,66},{7,33},{8,140}... | collective-permute-start | bytes 393224 | tf_op jit(solution)/shard_map/ppermute | solution.py:231
  13.2 2.8 %shard_map.112.held = bf16[8,4,6,128,128]{4,3,2,1,0:T(8,128)(2,1)S(1)} custom-call(bf16[8,4,6,128,128]{4,3,2,1,0:T(8,128)(2,1)} %edges.1), custom_call_target="tpu_custom_call" | custom-call | bytes 12582912 | tf_op jit(solution)/shard_map/pallas_call | solution.py:266
  16.0 1.7 %collective-permute-start.4 = (bf16[4,128,128]{2,1,0:T(8,128)(2,1)S(1)}, bf16[4,128,128]{2,1,0:T(8,128)(2,1)S(1)}, u32[]{:S(2)}, u32[]{:S(2)}) collective-permute-start(bf16[4,128,128]{2,1,0:T(8,128)(2,1)S(1)} %collective-permute-done.low), channel_id=1, source_target_pairs={{0,16},{1,17},{2,18},{3,19},{4,20},{5,21},{6,22},{7,23},{8,24},{9,... | collective-permute-start | bytes 393224 | tf_op jit(solution)/shard_map/ppermute | solution.py:231
  18.7 1.6 %collective-permute-start.6 = (bf16[4,128,128]{2,1,0:T(8,128)(2,1)S(1)}, bf16[4,128,128]{2,1,0:T(8,128)(2,1)S(1)}, u32[]{:S(2)}, u32[]{:S(2)}) collective-permute-start(bf16[4,128,128]{2,1,0:T(8,128)(2,1)S(1)} %collective-permute-done.2.high), channel_id=1, source_target_pairs={{0,16},{1,17},{2,18},{3,19},{4,20},{5,21},{6,22},{7,23},{8,24},{9,... | collective-permute-start | bytes 393224 | tf_op jit(solution)/shard_map/ppermute | solution.py:231
  20.3 1.4 %shard_map.113.total = f32[8,128,128]{2,1,0:T(8,128)S(1)} custom-call(s32[8,4,8]{2,1,0:T(4,128)S(1)} %pad_add_fusion.meta, bf16[8,4,6,128,128]{4,3,2,1,0:T(8,128)(2,1)S(1)} %shard_map.112.held, bf16[4,128,128]{2,1,0:T(8,128)(2,1)S(1)} %collective-permute-done.low, bf16[4,128,128]{2,1,0:T(8,128)(2,1)S(1)} %collective-permute-done.2.high), custom_call_target="tpu_custom_call" | custom-call | flops 201326592 | bytes 3145728 | tf_op jit(solution)/shard_map/pallas_call | solution.py:275
  21.7 1.4 %collective-permute-start.3 = (bf16[4,128,128]{2,1,0:T(8,128)(2,1)S(1)}, bf16[4,128,128]{2,1,0:T(8,128)(2,1)S(1)}, u32[]{:S(2)}, u32[]{:S(2)}) collective-permute-start(bf16[4,128,128]{2,1,0:T(8,128)(2,1)S(1)} %collective-permute-done.2.high), channel_id=1, source_target_pairs={{0,8},{1,9},{2,10},{3,11},{4,12},{5,13},{6,14},{7,15},{8,32},{9,33... | collective-permute-start | bytes 393224 | tf_op jit(solution)/shard_map/ppermute | solution.py:231
  23.7 1.4 %collective-permute-done.6.high = bf16[4,128,128]{2,1,0:T(8,128)(2,1)S(1)} collective-permute-done((bf16[4,128,128]{2,1,0:T(8,128)(2,1)S(1)}, bf16[4,128,128]{2,1,0:T(8,128)(2,1)S(1)}, u32[]{:S(2)}, u32[]{:S(2)}) %collective-permute-start.6) | collective-permute-done | bytes 131104 | tf_op jit(solution)/shard_map/ppermute | solution.py:231
  25.1 1.4 %shard_map.114.total = f32[8,128,128]{2,1,0:T(8,128)S(1)} custom-call(s32[8,4,8]{2,1,0:T(4,128)S(1)} %pad_add_fusion.meta, bf16[8,4,6,128,128]{4,3,2,1,0:T(8,128)(2,1)S(1)} %shard_map.112.held, bf16[4,128,128]{2,1,0:T(8,128)(2,1)S(1)} %collective-permute-done.4.low, bf16[4,128,128]{2,1,0:T(8,128)(2,1)S(1)} %collective-permute-done.6.high, ...), custom_call_target="tpu_custom_call" | custom-call | flops 201326592 | bytes 3145728 | tf_op jit(solution)/shard_map/pallas_call | solution.py:281
  27.1 1.8 %shard_map.115 = bf16[8,128,128]{2,1,0:T(8,128)(2,1)S(1)} custom-call(s32[8,4,8]{2,1,0:T(4,128)S(1)} %pad_add_fusion.meta, bf16[8,4,6,128,128]{4,3,2,1,0:T(8,128)(2,1)S(1)} %shard_map.112.held, bf16[4,128,128]{2,1,0:T(8,128)(2,1)S(1)} %collective-permute-done.1.near_low, bf16[4,128,128]{2,1,0:T(8,128)(2,1)S(1)} %collective-permute-done.3.near_high, ...), custom_call_target="tpu_custom_call" | custom-call | flops 402653184 | bytes 6291456 | tf_op jit(solution)/shard_map/pallas_call | solution.py:284
  28.9 19.3 %all_to_all.15.parts = bf16[8,128,128]{2,1,0:T(8,128)(2,1)S(1)} all-to-all(bf16[8,128,128]{2,1,0:T(8,128)(2,1)S(1)} %shard_map.115), channel_id=1, replica_groups=mesh['z'=8,'yl'=2,'core'=2,'x'=4,'yh'=2] {'x','yh'}, dimensions={0} | all-to-all | bytes 524288 | tf_op jit(solution)/shard_map/all_to_all | solution.py:221
  49.0 12.2 %all_to_all.16.got = bf16[8,176,128]{2,1,0:T(8,128)(2,1)S(1)} all-to-all(bf16[8,176,128]{2,1,0:T(8,128)(2,1)S(1)} %get-tuple-element.33), channel_id=1, replica_groups=mesh['z'=8,'yl'=2,'core'=2,'x'=4,'yh'=2] {'x','yh'}, dimensions={0} | all-to-all | bytes 720896 | tf_op jit(solution)/shard_map/all_to_all | solution.py:221
  61.2 2.1 %shard_map.118 = (bf16[8,128,128]{2,1,0:T(8,128)(2,1)S(1)}, bf16[1120,128]{1,0:T(8,128)(2,1)S(1)}) custom-call(s32[8,4,8]{2,1,0:T(4,128)S(1)} %pad_add_fusion.meta, bf16[8,4,6,128,128]{4,3,2,1,0:T(8,128)(2,1)S(1)} %shard_map.112.held, bf16[8,176,128]{2,1,0:T(8,128)(2,1)S(1)} %all_to_all.16.got), custom_call_target="tpu_custom_call" | custom-call | flops 402653184 | bytes 6291456 | tf_op jit(solution)/shard_map/pallas_call | solution.py:297
  63.4 1.5 %shard_map.117.far = bf16[8,128,128]{2,1,0:T(8,128)(2,1)S(1)} custom-call(s32[8,4,8]{2,1,0:T(4,128)S(1)} %pad_add_fusion.meta, bf16[8,4,6,128,128]{4,3,2,1,0:T(8,128)(2,1)S(1)} %shard_map.112.held, bf16[8,176,128]{2,1,0:T(8,128)(2,1)S(1)} %all_to_all.16.got), custom_call_target="tpu_custom_call" | custom-call | flops 201326592 | bytes 3145728 | tf_op jit(solution)/shard_map/pallas_call | solution.py:307
  65.0 2.0 %collective-permute-start.10 = (bf16[8,128,128]{2,1,0:T(8,128)(2,1)S(1)}, bf16[8,128,128]{2,1,0:T(8,128)(2,1)S(1)}, u32[]{:S(2)}, u32[]{:S(2)}) collective-permute-start(bf16[8,128,128]{2,1,0:T(8,128)(2,1)S(1)} %shard_map.119), channel_id=1, source_target_pairs={{0,17},{1,18},{2,19},{3,20},{4,21},{5,22},{6,23},{7,16},{8,25},{9,... | collective-permute-start | bytes 786440 | tf_op jit(solution)/shard_map/ppermute | solution.py:231
  67.2 1.8 %collective-permute-start.14 = (f32[48,128]{1,0:T(8,128)S(1)}, f32[48,128]{1,0:T(8,128)S(1)}, u32[]{:S(2)}, u32[]{:S(2)}) collective-permute-start(f32[48,128]{1,0:T(8,128)S(1)} %shard_map.122.grads), channel_id=1, source_target_pairs={{0,64},{1,65},{2,66},{3,67},{4,68},{5,69},{6,70},{7,71},{8,72},{9,... | collective-permute-start | bytes 73736 | tf_op jit(solution)/shard_map/ppermute | solution.py:231
  69.0 1.5 %collective-permute-start.15 = (f32[48,128]{1,0:T(8,128)S(1)}, f32[48,128]{1,0:T(8,128)S(1)}, u32[]{:S(2)}, u32[]{:S(2)}) collective-permute-start(f32[48,128]{1,0:T(8,128)S(1)} %shard_map.122.grads), channel_id=1, source_target_pairs={{0,96},{1,97},{2,98},{3,99},{4,100},{5,101},{6,102},{7,103},{8,104... | collective-permute-start | bytes 73736 | tf_op jit(solution)/shard_map/ppermute | solution.py:231
  70.5 1.5 %shard_map.120.own = f32[8,128,128]{2,1,0:T(8,128)S(1)} custom-call(s32[8,4,8]{2,1,0:T(4,128)S(1)} %pad_add_fusion.meta, bf16[8,4,6,128,128]{4,3,2,1,0:T(8,128)(2,1)S(1)} %shard_map.112.held, bf16[8,176,128]{2,1,0:T(8,128)(2,1)S(1)} %all_to_all.16.got), custom_call_target="tpu_custom_call" | custom-call | flops 201326592 | bytes 3145728 | tf_op jit(solution)/shard_map/pallas_call | solution.py:313
  72.1 1.7 %collective-permute-done.10.far = bf16[8,128,128]{2,1,0:T(8,128)(2,1)S(1)} collective-permute-done((bf16[8,128,128]{2,1,0:T(8,128)(2,1)S(1)}, bf16[8,128,128]{2,1,0:T(8,128)(2,1)S(1)}, u32[]{:S(2)}, u32[]{:S(2)}) %collective-permute-start.10) | collective-permute-done | bytes 262176 | tf_op jit(solution)/shard_map/ppermute | solution.py:231
  74.5 3.3 %collective-permute-start.12 = (bf16[4,128,128]{2,1,0:T(8,128)(2,1)S(1)}, bf16[4,128,128]{2,1,0:T(8,128)(2,1)S(1)}, u32[]{:S(2)}, u32[]{:S(2)}) collective-permute-start(bf16[4,128,128]{2,1,0:T(8,128)(2,1)S(1)} %get-tuple-element.39.high), channel_id=1, source_target_pairs={{0,2},{1,227},{2,192},{3,161},{4,134},{5,103},{6,68},{7,37},{8,10}... | collective-permute-start | bytes 393224 | tf_op jit(solution)/shard_map/ppermute | solution.py:231
  79.1 2.7 %collective-permute-done.16 = f32[48,128]{1,0:T(8,128)S(1)} collective-permute-done((f32[48,128]{1,0:T(8,128)S(1)}, f32[48,128]{1,0:T(8,128)S(1)}, u32[]{:S(2)}, u32[]{:S(2)}) %collective-permute-start.16) | collective-permute-done | bytes 24608 | tf_op jit(solution)/shard_map/ppermute | solution.py:231
  81.8 2.6 %collective-permute-start.17 = (f32[48,128]{1,0:T(8,128)S(1)}, f32[48,128]{1,0:T(8,128)S(1)}, u32[]{:S(2)}, u32[]{:S(2)}) collective-permute-start(f32[48,128]{1,0:T(8,128)S(1)} %add.10), channel_id=1, source_target_pairs={{0,128},{1,129},{2,130},{3,131},{4,132},{5,133},{6,134},{7,135},{8... | collective-permute-start | bytes 73736 | tf_op jit(solution)/shard_map/ppermute | solution.py:231
  84.3 5.2 %collective-permute-done.17 = f32[48,128]{1,0:T(8,128)S(1)} collective-permute-done((f32[48,128]{1,0:T(8,128)S(1)}, f32[48,128]{1,0:T(8,128)S(1)}, u32[]{:S(2)}, u32[]{:S(2)}) %collective-permute-start.17) | collective-permute-done | bytes 24608 | tf_op jit(solution)/shard_map/ppermute | solution.py:231
  90.0 19.7 %all_to_all.17.got = bf16[8,160,128]{2,1,0:T(8,128)(2,1)S(1)} all-to-all(bf16[8,160,128]{2,1,0:T(8,128)(2,1)S(1)} %shard_map.124), channel_id=1, replica_groups=mesh['z'=8,'yl'=2,'core'=2,'x'=4,'yh'=2] {'x','yh'}, dimensions={0} | all-to-all | bytes 655360 | tf_op jit(solution)/shard_map/all_to_all | solution.py:221
  (45 shorter events, 7.5 us)
Async XLA Ops:
  2.4 13.7 %collective-permute-start = (bf16[4,128,128]{2,1,0:T(8,128)(2,1)S(1)}, bf16[4,128,128]{2,1,0:T(8,128)(2,1)S(1)}, u32[]{:S(2)}, u32[]{:S(2)}) collective-permute-start(bf16[4,128,128]{2,1,0:T(8,128)(2,1)S(1)} %get-tuple-element.24), channel_id=1, source_target_pairs={{0,0},{1,33},{2,66},{3,99},{4,132},{5,165},{6,198},{7,231},{8,8},{... | collective-permute-start | bytes 393224 | tf_op jit(solution)/shard_map/ppermute | solution.py:231
  3.0 15.7 %collective-permute-start.2 = (bf16[4,128,128]{2,1,0:T(8,128)(2,1)S(1)}, bf16[4,128,128]{2,1,0:T(8,128)(2,1)S(1)}, u32[]{:S(2)}, u32[]{:S(2)}) collective-permute-start(bf16[4,128,128]{2,1,0:T(8,128)(2,1)S(1)} %get-tuple-element.28), channel_id=1, source_target_pairs={{0,132},{1,231},{2,198},{3,165},{4,0},{5,99},{6,66},{7,33},{8,140}... | collective-permute-start | bytes 393224 | tf_op jit(solution)/shard_map/ppermute | solution.py:231
  13.2 2.8 %copy-start.3 = (s32[8,4,6]{0,1,2:T(4,128)S(1)}, s32[8,4,6]{0,1,2:T(4,128)}, u32[]{:S(2)}) copy-start(s32[8,4,6]{0,1,2:T(4,128)} %param.10) | copy-start | bytes 2308
  13.2 2.9 %copy-start.4 = (s32[8,4]{0,1:T(4,128)S(1)}, s32[8,4]{0,1:T(4,128)}, u32[]{:S(2)}) copy-start(s32[8,4]{0,1:T(4,128)} %param.11) | copy-start | bytes 388
  16.0 7.6 %collective-permute-start.4 = (bf16[4,128,128]{2,1,0:T(8,128)(2,1)S(1)}, bf16[4,128,128]{2,1,0:T(8,128)(2,1)S(1)}, u32[]{:S(2)}, u32[]{:S(2)}) collective-permute-start(bf16[4,128,128]{2,1,0:T(8,128)(2,1)S(1)} %collective-permute-done.low), channel_id=1, source_target_pairs={{0,16},{1,17},{2,18},{3,19},{4,20},{5,21},{6,22},{7,23},{8,24},{9,... | collective-permute-start | bytes 393224 | tf_op jit(solution)/shard_map/ppermute | solution.py:231
  18.7 6.4 %collective-permute-start.6 = (bf16[4,128,128]{2,1,0:T(8,128)(2,1)S(1)}, bf16[4,128,128]{2,1,0:T(8,128)(2,1)S(1)}, u32[]{:S(2)}, u32[]{:S(2)}) collective-permute-start(bf16[4,128,128]{2,1,0:T(8,128)(2,1)S(1)} %collective-permute-done.2.high), channel_id=1, source_target_pairs={{0,16},{1,17},{2,18},{3,19},{4,20},{5,21},{6,22},{7,23},{8,24},{9,... | collective-permute-start | bytes 393224 | tf_op jit(solution)/shard_map/ppermute | solution.py:231
  20.3 6.8 %collective-permute-start.1 = (bf16[4,128,128]{2,1,0:T(8,128)(2,1)S(1)}, bf16[4,128,128]{2,1,0:T(8,128)(2,1)S(1)}, u32[]{:S(2)}, u32[]{:S(2)}) collective-permute-start(bf16[4,128,128]{2,1,0:T(8,128)(2,1)S(1)} %collective-permute-done.low), channel_id=1, source_target_pairs={{0,8},{1,9},{2,10},{3,11},{4,12},{5,13},{6,14},{7,15},{8,32},{9,33... | collective-permute-start | bytes 393224 | tf_op jit(solution)/shard_map/ppermute | solution.py:231
  21.7 26.5 %copy-start = (bf16[128,256]{1,0:T(8,128)(2,1)S(1)}, bf16[128,256]{1,0:T(8,128)(2,1)}, u32[]{:S(2)}) copy-start(bf16[128,256]{1,0:T(8,128)(2,1)} %weight.1) | copy-start | bytes 196612
  21.7 26.5 %copy-start.1 = (bf16[128,256]{1,0:T(8,128)(2,1)S(1)}, bf16[128,256]{1,0:T(8,128)(2,1)}, u32[]{:S(2)}) copy-start(bf16[128,256]{1,0:T(8,128)(2,1)} %cot.1) | copy-start | bytes 196612
  21.7 26.5 %copy-start.2 = (f32[256]{0:T(256)S(1)}, f32[256]{0:T(256)}, u32[]{:S(2)}) copy-start(f32[256]{0:T(256)} %param.14) | copy-start | bytes 3076
  21.7 5.4 %collective-permute-start.3 = (bf16[4,128,128]{2,1,0:T(8,128)(2,1)S(1)}, bf16[4,128,128]{2,1,0:T(8,128)(2,1)S(1)}, u32[]{:S(2)}, u32[]{:S(2)}) collective-permute-start(bf16[4,128,128]{2,1,0:T(8,128)(2,1)S(1)} %collective-permute-done.2.high), channel_id=1, source_target_pairs={{0,8},{1,9},{2,10},{3,11},{4,12},{5,13},{6,14},{7,15},{8,32},{9,33... | collective-permute-start | bytes 393224 | tf_op jit(solution)/shard_map/ppermute | solution.py:231
  23.7 3.4 %collective-permute-start.5 = (bf16[4,128,128]{2,1,0:T(8,128)(2,1)S(1)}, bf16[4,128,128]{2,1,0:T(8,128)(2,1)S(1)}, u32[]{:S(2)}, u32[]{:S(2)}) collective-permute-start(bf16[4,128,128]{2,1,0:T(8,128)(2,1)S(1)} %collective-permute-done.4.low), channel_id=1, source_target_pairs={{0,8},{1,9},{2,10},{3,11},{4,12},{5,13},{6,14},{7,15},{8,0},{9,1},... | collective-permute-start | bytes 393224 | tf_op jit(solution)/shard_map/ppermute | solution.py:231
  25.1 2.0 %collective-permute-start.7 = (bf16[4,128,128]{2,1,0:T(8,128)(2,1)S(1)}, bf16[4,128,128]{2,1,0:T(8,128)(2,1)S(1)}, u32[]{:S(2)}, u32[]{:S(2)}) collective-permute-start(bf16[4,128,128]{2,1,0:T(8,128)(2,1)S(1)} %collective-permute-done.6.high), channel_id=1, source_target_pairs={{0,8},{1,9},{2,10},{3,11},{4,12},{5,13},{6,14},{7,15},{8,0},{9,1},... | collective-permute-start | bytes 393224 | tf_op jit(solution)/shard_map/ppermute | solution.py:231
  63.3 1.7 %collective-permute-start.8 = (bf16[1120,128]{1,0:T(8,128)(2,1)S(1)}, bf16[1120,128]{1,0:T(8,128)(2,1)S(1)}, u32[]{:S(2)}, u32[]{:S(2)}) collective-permute-start(bf16[1120,128]{1,0:T(8,128)(2,1)S(1)} %get-tuple-element.34.mine), channel_id=1, source_target_pairs={{0,8},{1,9},{2,10},{3,11},{4,12},{5,13},{6,14},{7,15},{8,0},{9,1},... | collective-permute-start | bytes 860168 | tf_op jit(solution)/shard_map/ppermute | solution.py:231
  63.4 8.7 %collective-permute-start.9 = (bf16[8,128,128]{2,1,0:T(8,128)(2,1)S(1)}, bf16[8,128,128]{2,1,0:T(8,128)(2,1)S(1)}, u32[]{:S(2)}, u32[]{:S(2)}) collective-permute-start(bf16[8,128,128]{2,1,0:T(8,128)(2,1)S(1)} %get-tuple-element.36), channel_id=1, source_target_pairs={{0,232},{1,233},{2,234},{3,235},{4,236},{5,237},{6,238},{7,239},{8... | collective-permute-start | bytes 786440 | tf_op jit(solution)/shard_map/ppermute | solution.py:231
  65.0 8.8 %collective-permute-start.10 = (bf16[8,128,128]{2,1,0:T(8,128)(2,1)S(1)}, bf16[8,128,128]{2,1,0:T(8,128)(2,1)S(1)}, u32[]{:S(2)}, u32[]{:S(2)}) collective-permute-start(bf16[8,128,128]{2,1,0:T(8,128)(2,1)S(1)} %shard_map.119), channel_id=1, source_target_pairs={{0,17},{1,18},{2,19},{3,20},{4,21},{5,22},{6,23},{7,16},{8,25},{9,... | collective-permute-start | bytes 786440 | tf_op jit(solution)/shard_map/ppermute | solution.py:231
  67.0 10.9 %collective-permute-start.13 = (f32[48,128]{1,0:T(8,128)S(1)}, f32[48,128]{1,0:T(8,128)S(1)}, u32[]{:S(2)}, u32[]{:S(2)}) collective-permute-start(f32[48,128]{1,0:T(8,128)S(1)} %shard_map.122.grads), channel_id=1, source_target_pairs={{0,32},{1,33},{2,34},{3,35},{4,36},{5,37},{6,38},{7,39},{8,40},{9,... | collective-permute-start | bytes 73736 | tf_op jit(solution)/shard_map/ppermute | solution.py:231
  67.2 10.6 %collective-permute-start.14 = (f32[48,128]{1,0:T(8,128)S(1)}, f32[48,128]{1,0:T(8,128)S(1)}, u32[]{:S(2)}, u32[]{:S(2)}) collective-permute-start(f32[48,128]{1,0:T(8,128)S(1)} %shard_map.122.grads), channel_id=1, source_target_pairs={{0,64},{1,65},{2,66},{3,67},{4,68},{5,69},{6,70},{7,71},{8,72},{9,... | collective-permute-start | bytes 73736 | tf_op jit(solution)/shard_map/ppermute | solution.py:231
  69.0 8.8 %collective-permute-start.15 = (f32[48,128]{1,0:T(8,128)S(1)}, f32[48,128]{1,0:T(8,128)S(1)}, u32[]{:S(2)}, u32[]{:S(2)}) collective-permute-start(f32[48,128]{1,0:T(8,128)S(1)} %shard_map.122.grads), channel_id=1, source_target_pairs={{0,96},{1,97},{2,98},{3,99},{4,100},{5,101},{6,102},{7,103},{8,104... | collective-permute-start | bytes 73736 | tf_op jit(solution)/shard_map/ppermute | solution.py:231
  73.9 15.7 %collective-permute-start.11 = (bf16[4,128,128]{2,1,0:T(8,128)(2,1)S(1)}, bf16[4,128,128]{2,1,0:T(8,128)(2,1)S(1)}, u32[]{:S(2)}, u32[]{:S(2)}) collective-permute-start(bf16[4,128,128]{2,1,0:T(8,128)(2,1)S(1)} %get-tuple-element.38.low), channel_id=1, source_target_pairs={{0,0},{1,225},{2,194},{3,163},{4,132},{5,101},{6,70},{7,39},{8,8},... | collective-permute-start | bytes 393224 | tf_op jit(solution)/shard_map/ppermute | solution.py:231
  74.5 15.5 %collective-permute-start.12 = (bf16[4,128,128]{2,1,0:T(8,128)(2,1)S(1)}, bf16[4,128,128]{2,1,0:T(8,128)(2,1)S(1)}, u32[]{:S(2)}, u32[]{:S(2)}) collective-permute-start(bf16[4,128,128]{2,1,0:T(8,128)(2,1)S(1)} %get-tuple-element.39.high), channel_id=1, source_target_pairs={{0,2},{1,227},{2,192},{3,161},{4,134},{5,103},{6,68},{7,37},{8,10}... | collective-permute-start | bytes 393224 | tf_op jit(solution)/shard_map/ppermute | solution.py:231
  77.8 3.9 %collective-permute-start.16 = (f32[48,128]{1,0:T(8,128)S(1)}, f32[48,128]{1,0:T(8,128)S(1)}, u32[]{:S(2)}, u32[]{:S(2)}) collective-permute-start(f32[48,128]{1,0:T(8,128)S(1)} %shard_map.123), channel_id=1, source_target_pairs={{0,16},{1,17},{2,18},{3,19},{4,20},{5,21},{6,22},{7,23},{8,24},{9,... | collective-permute-start | bytes 73736 | tf_op jit(solution)/shard_map/ppermute | solution.py:231
  81.8 7.7 %collective-permute-start.17 = (f32[48,128]{1,0:T(8,128)S(1)}, f32[48,128]{1,0:T(8,128)S(1)}, u32[]{:S(2)}, u32[]{:S(2)}) collective-permute-start(f32[48,128]{1,0:T(8,128)S(1)} %add.10), channel_id=1, source_target_pairs={{0,128},{1,129},{2,130},{3,131},{4,132},{5,133},{6,134},{7,135},{8... | collective-permute-start | bytes 73736 | tf_op jit(solution)/shard_map/ppermute | solution.py:231
